TPU v7x, 128 devices: a whole 4x4x4 slice. The times are simulated.
128 devices in a mesh: gx: 8 (over x, core), gy: 16 (over y, z).
Axes of the slice: x: 4, y: 4, z: 4, core: 2. Of those that a mesh axis runs over, the one named last changes fastest.
Arguments:
- state: float32 [16, 512, 2048], P(None, 'gx', 'gy'), may hold values from -5.5 to 5.5
- kappa_x: float32 [16, 512, 2048], P(None, 'gx', 'gy'), may hold values from 300 to 30000
- kappa_y: float32 [16, 512, 2048], P(None, 'gx', 'gy'), may hold values from 300 to 30000
Outputs:
- updated: float32 [16, 512, 2048], P(None, 'gx', 'gy')
All inputs are finite; a program needn't handle non-finite values.
Results may differ from a plain program's by a relative error of at most 0.025.
Values sent between devices are 32-bit elements; how exact they have to be, the bound alone decides.
No kernel may reach another device: no remote copies, remote signals or barrier semaphores. Data moves between devices by JAX's collectives and lax.ppermute only.
A program may use at most 128 MiB of HBM per device.

v0:
```python
import jax
import jax.numpy as jnp
from jax import lax
from jax.sharding import PartitionSpec as P


def padded(cells, sides, width):
    for axis, dim in sides:
        count = lax.axis_size(axis)
        ends = count - 1
        head = lax.slice_in_dim(cells, 0, width, axis=dim)
        tail = lax.slice_in_dim(cells, cells.shape[dim] - width, cells.shape[dim], axis=dim)
        cells = jnp.concatenate(
            [
                lax.ppermute(tail, axis, [(i, (i + 1) % count) for i in range(ends)]),
                cells,
                lax.ppermute(head, axis, [((i + 1) % count, i) for i in range(ends)]),
            ],
            axis=dim,
        )
    return cells


def neighbor(values, step, axis):
    length = values.shape[axis]
    widths = [(0, 0)] * values.ndim
    if step > 0:
        part = lax.slice_in_dim(values, step, length, axis=axis)
        widths[axis] = (0, step)
    else:
        part = lax.slice_in_dim(values, 0, length + step, axis=axis)
        widths[axis] = (-step, 0)
    return jnp.pad(part, widths)


def reduce_lines(lower, diag, upper, sources, axis):
    lower = lower / diag
    upper = upper / diag
    sources = [entry / diag for entry in sources]
    length = diag.shape[axis]
    stride = 1
    while stride < length:
        low_prev = neighbor(lower, -stride, axis)
        up_prev = neighbor(upper, -stride, axis)
        low_next = neighbor(lower, stride, axis)
        up_next = neighbor(upper, stride, axis)
        pivot = 1.0 - lower * up_prev - upper * low_next
        sources = [
            (entry - lower * neighbor(entry, -stride, axis) - upper * neighbor(entry, stride, axis))
            / pivot
            for entry in sources
        ]
        lower, upper = (-lower * low_prev / pivot, -upper * up_next / pivot)
        stride = stride * 2
    return sources


def gathered_solve(allrows, position):
    sequence = jnp.moveaxis(allrows, 1, 0)
    zeros = jnp.zeros(allrows.shape[2:], jnp.float32)

    def forward(carry, row):
        prior_c, prior_d = carry
        pivot = row[1] - row[0] * prior_c
        next_c = row[2] / pivot
        next_d = (row[3] - row[0] * prior_d) / pivot
        return ((next_c, next_d), (next_c, next_d))

    final, (ratios, values) = lax.scan(forward, (zeros, zeros), sequence)

    def backward(later, pair):
        result = pair[1] - pair[0] * later
        return (result, result)

    final, solved = lax.scan(backward, zeros, (ratios, values), reverse=True)
    return lax.dynamic_slice_in_dim(solved, 2 * position, 2, 0)


def interface_x(rows):
    return gathered_solve(lax.all_gather(rows, "gx", axis=1, tiled=True), lax.axis_index("gx"))


def interface_y(rows):
    return gathered_solve(lax.all_gather(rows, "gy", axis=1, tiled=True), lax.axis_index("gy"))


def solve_line(left, right, source, axis, interface):
    lower = -left
    upper = -right
    diag = 1.0 + left + right
    length = diag.shape[axis]
    inner_lower = lax.slice_in_dim(lower, 1, length - 1, axis=axis)
    inner_diag = lax.slice_in_dim(diag, 1, length - 1, axis=axis)
    inner_upper = lax.slice_in_dim(upper, 1, length - 1, axis=axis)
    inner_source = lax.slice_in_dim(source, 1, length - 1, axis=axis)
    row_index = lax.broadcasted_iota(jnp.int32, inner_diag.shape, axis)
    first_row = row_index == 0
    last_row = row_index == length - 3
    zero = jnp.zeros_like(inner_diag)
    from_first = jnp.where(first_row, -inner_lower, zero)
    from_last = jnp.where(last_row, -inner_upper, zero)
    inner_lower = jnp.where(first_row, zero, inner_lower)
    inner_upper = jnp.where(last_row, zero, inner_upper)
    base, with_first, with_last = reduce_lines(
        inner_lower, inner_diag, inner_upper, [inner_source, from_first, from_last], axis
    )
    plane_shape = tuple((extent for position, extent in enumerate(diag.shape) if position != axis))

    def pick(values, position):
        return lax.index_in_dim(values, position, axis, keepdims=False).reshape(-1)

    lower_first, diag_first, upper_first, source_first = (
        pick(lower, 0),
        pick(diag, 0),
        pick(upper, 0),
        pick(source, 0),
    )
    lower_last, diag_last, upper_last, source_last = (
        pick(lower, length - 1),
        pick(diag, length - 1),
        pick(upper, length - 1),
        pick(source, length - 1),
    )
    coef_a = jnp.stack([lower_first, lower_last * pick(with_first, length - 3)])
    coef_b = jnp.stack(
        [
            diag_first + upper_first * pick(with_first, 0),
            diag_last + lower_last * pick(with_last, length - 3),
        ]
    )
    coef_c = jnp.stack([upper_first * pick(with_last, 0), upper_last])
    coef_d = jnp.stack(
        [
            source_first - upper_first * pick(base, 0),
            source_last - lower_last * pick(base, length - 3),
        ]
    )
    edges = interface(jnp.stack([coef_a, coef_b, coef_c, coef_d]))
    edge_first = jnp.expand_dims(edges[0].reshape(plane_shape), axis)
    edge_last = jnp.expand_dims(edges[1].reshape(plane_shape), axis)
    interior = base + with_first * edge_first + with_last * edge_last
    return jnp.concatenate([edge_first, interior, edge_last], axis=axis)


def on_device(state, kappa_x, kappa_y):
    wide_x = padded(jnp.stack([state, kappa_x]), (("gx", 2),), 1)
    field_x = wide_x[0]
    kappa_wx = wide_x[1]
    left_x = 0.5 * (kappa_wx[:, :-2] + kappa_wx[:, 1:-1])
    right_x = 0.5 * (kappa_wx[:, 1:-1] + kappa_wx[:, 2:])
    lap_x = right_x * (field_x[:, 2:] - state) - left_x * (state - field_x[:, :-2])
    wide_y = padded(jnp.stack([state, kappa_y]), (("gy", 3),), 1)
    field_y = wide_y[0]
    kappa_wy = wide_y[1]
    left_y = 0.5 * (kappa_wy[:, :, :-2] + kappa_wy[:, :, 1:-1])
    right_y = 0.5 * (kappa_wy[:, :, 1:-1] + kappa_wy[:, :, 2:])
    lap_y = right_y * (field_y[:, :, 2:] - state) - left_y * (state - field_y[:, :, :-2])
    source = state + lap_x + 2.0 * lap_y
    middle = solve_line(left_x, right_x, source, 1, interface_x)
    return solve_line(left_y, right_y, middle - lap_y, 2, interface_y)


def solution(mesh):
    return jax.shard_map(
        on_device,
        mesh=mesh,
        in_specs=(P(None, "gx", "gy"), P(None, "gx", "gy"), P(None, "gx", "gy")),
        out_specs=P(None, "gx", "gy"),
        check_vma=False,
    )
```

profile of v0, /device:TPU:0, one launch (start us, length us, event | category | flops | bytes accessed | tf_op | source)
XLA Modules:
  0.0 169.2 jit_solution(5999286894331950306)
XLA Ops:
  0.0 1.9 %copy_bitcast_fusion = (f32[1,16,64,128]{3,1,2,0:T(8,128)S(1)}, f32[1,16,64,128]{3,1,2,0:T(8,128)S(1)}) fusion(f32[16,64,128]{2,1,0:T(8,128)} %param.12, f32[16,64,128]{2,1,0:T(8,128)} %param.11), kind=kLoop, calls=%fused_computation.72 | loop fusion | bytes 2097152 | tf_op jit(solution)/shard_map/stack | solution.py:146
  6.2 1.7 copy.21
  7.8 4.3 %collective-permute-start = (f32[2,16,64,1]{2,1,3,0:T(8,128)S(1)}, f32[2,16,64,1]{2,1,3,0:T(8,128)S(1)}, u32[]{:S(2)}, u32[]{:S(2)}) collective-permute-start(f32[2,16,64,1]{2,1,3,0:T(8,128)S(1)} %copy.21), channel_id=1, source_target_pairs={{0,1},{1,2},{2,3},{3,4},{4,5},{5,6},{6,7},{7,8},{8,9},{9,10},{10,1... | collective-permute-start | bytes 24584 | tf_op jit(solution)/shard_map/ppermute | solution.py:15
  14.6 3.7 %collective-permute-done.1 = f32[2,16,64,1]{2,1,3,0:T(8,128)S(1)} collective-permute-done((f32[2,16,64,1]{2,1,3,0:T(8,128)S(1)}, f32[2,16,64,1]{2,1,3,0:T(8,128)S(1)}, u32[]{:S(2)}, u32[]{:S(2)}) %collective-permute-start.1) | collective-permute-done | bytes 8224 | tf_op jit(solution)/shard_map/ppermute | solution.py:17
  19.7 2.1 %pad_maximum_fusion = f32[2,16,64,130]{3,1,2,0:T(8,128)S(1)} fusion(f32[2,16,64,1]{3,1,2,0:T(8,128)} %copy.24, f32[1,16,64,128]{3,1,2,0:T(8,128)S(1)} %bitcast.119, f32[1,16,64,128]{3,1,2,0:T(8,128)S(1)} %get-tuple-element.675, f32[2,16,64,1]{3,1,2,0:T(8,128)S(1)} %copy.23), kind=kLoop, calls=%fused_computation.28 | loop fusion | flops 798720 | bytes 2129920 | tf_op jit(solution)/shard_map/concatenate | solution.py:13
  31.4 17.1 %all_gather.6 = f32[4,16,2048]{2,0,1:T(4,128)} all-gather(f32[4,2,2048]{2,0,1:T(4,128)S(1)} %copy.37), channel_id=1, replica_groups=mesh['gx'=8,'gy'=16] {'gx'}, dimensions={1}, use_global_device_ids=true | all-gather | bytes 589824 | tf_op jit(solution)/shard_map/all_gather | solution.py:80
  48.5 23.0 %while.68 = (s32[]{:T(128)}, f32[2048]{0:T(1024)S(1)}, f32[2048]{0:T(1024)S(1)}, f32[16,2048]{1,0:T(8,128)S(1)}, f32[16,2048]{1,0:T(8,128)S(1)}, /*index=5*/f32[...) while((s32[]{:T(128)}, f32[2048]{0:T(1024)S(1)}, f32[2048]{0:T(1024)S(1)}, ...), condition=%wide.region_1.2_spmd.clone, body=%wide.region_0.1_spmd.clone.sunk | while | flops 16390 | bytes 164019 | solution.py:69
  72.1 24.7 %while.69 = (s32[]{:T(128)}, f32[2048]{0:T(1024)S(1)}, f32[16,2048]{1,0:T(8,128)}, f32[16,2048]{1,0:T(8,128)S(1)}, f32[16,2048]{1,0:T(8,128)S(1)}, /*index=5*/s32[]{:T(128)}, s32[]{:T(128)}, s32[]{:T(128)}) while((s32[]{:T(128)}, f32[2048]{0:T(1024)S(1)}, f32[16,2048]{1,0:T(8,128)}, f32[16,2048]{1,0:T(8,128)S(1)}, ...), condition=%wide.region_3.4_spmd.clone, body=%wide.region_2.3_spmd.clone.sunk | while | flops 6148 | bytes 82035 | solution.py:75
  72.2 1.5 dynamic_update_slice.46
  73.7 1.5 dynamic_update_slice.46
  75.3 1.5 dynamic_update_slice.46
  76.8 1.5 dynamic_update_slice.46
  78.4 1.5 dynamic_update_slice.46
  79.9 1.5 dynamic_update_slice.46
  81.5 1.5 dynamic_update_slice.46
  83.0 1.5 dynamic_update_slice.46
  84.5 1.5 dynamic_update_slice.46
  86.1 1.5 dynamic_update_slice.46
  90.7 1.5 dynamic_update_slice.46
  93.8 1.5 dynamic_update_slice.46
  112.8 3.1 %fusion.12 = (f32[16,64,1]{2,0,1:T(8,128)}, f32[16,64,1]{2,0,1:T(8,128)}, f32[16,64,1]{2,0,1:T(8,128)}, f32[16,64,1]{2,0,1:T(8,128)}, f32[16,64,1]{2,0,1:T(8,128...) fusion(f32[16,64,126]{2,0,1:T(8,128)S(1)} %get-tuple-element.455, ...), kind=kLoop, calls=%fused_computation.42 | loop fusion | flops 10240 | bytes 90112 | tf_op jit(solution)/shard_map/sub | solution.py:134
  124.0 25.8 %all_gather.7 = f32[4,32,1024]{2,0,1:T(4,128)S(1)} all-gather(f32[4,2,1024]{2,0,1:T(4,128)S(1)} %copy.40), channel_id=1, replica_groups=mesh['gx'=8,'gy'=16] {'gy'}, dimensions={1}, use_global_device_ids=true | all-gather | bytes 557056 | tf_op jit(solution)/shard_map/all_gather | solution.py:84
  149.8 9.8 %while.70 = (s32[]{:T(128)}, f32[1024]{0:T(1024)S(1)}, f32[1024]{0:T(1024)S(1)}, f32[32,1024]{1,0:T(8,128)S(1)}, f32[32,1024]{1,0:T(8,128)S(1)}, /*index=5*/f32[...) while((s32[]{:T(128)}, f32[1024]{0:T(1024)S(1)}, ...), condition=%wide.region_5.6_spmd.clone, body=%wide.region_4.5_spmd.clone.sunk | while | flops 8198 | bytes 82099 | solution.py:69
  159.6 5.6 %while.71 = (s32[]{:T(128)}, f32[1024]{0:T(1024)S(1)}, f32[32,1024]{1,0:T(8,128)S(1)}, f32[32,1024]{1,0:T(8,128)S(1)}, f32[32,1024]{1,0:T(8,128)S(1)}, /*index=5*/s32[]{:T(128)}, s32[]{:T(128)}, s32[]{:T(128)}) while((s32[]{:T(128)}, f32[1024]{0:T(1024)S(1)}, f32[32,1024]{1,0:T(8,128)S(1)}, f32[32,1024]{1,0:T(8,128)S(1)}, ...), condition=%wide.region_7.8_spmd.clone, body=%wide.region_6.7_spmd.clone.sunk | while | flops 3076 | bytes 41075 | solution.py:75
  (502 shorter events, 86.9 us)
Async XLA Ops:
  0.0 4.5 %copy-start.5 = (f32[16,64,128]{2,1,0:T(8,128)S(1)}, f32[16,64,128]{2,1,0:T(8,128)}, u32[]{:S(2)}) copy-start(f32[16,64,128]{2,1,0:T(8,128)} %param.13) | copy-start | bytes 1572868
  1.9 20.1 %collective-permute-start.2 = (f32[2,16,1,128]{3,1,2,0:T(8,128)S(1)}, f32[2,16,1,128]{3,1,2,0:T(8,128)S(1)}, u32[]{:S(2)}, u32[]{:S(2)}) collective-permute-start(f32[2,16,1,128]{3,1,2,0:T(8,128)S(1)} %get-tuple-element.513), channel_id=1, source_target_pairs={{0,16},{16,32},{32,48},{48,64},{64,80},{80,96},{96,112},{1,17},{17... | collective-permute-start | bytes 49160 | tf_op jit(solution)/shard_map/ppermute | solution.py:15
  3.2 18.8 %collective-permute-start.3 = (f32[2,16,1,128]{3,1,2,0:T(8,128)S(1)}, f32[2,16,1,128]{3,1,2,0:T(8,128)S(1)}, u32[]{:S(2)}, u32[]{:S(2)}) collective-permute-start(f32[2,16,1,128]{3,1,2,0:T(8,128)S(1)} %get-tuple-element.514), channel_id=1, source_target_pairs={{16,0},{32,16},{48,32},{64,48},{80,64},{96,80},{112,96},{17,1},{33... | collective-permute-start | bytes 49160 | tf_op jit(solution)/shard_map/ppermute | solution.py:17
  7.8 6.2 %collective-permute-start = (f32[2,16,64,1]{2,1,3,0:T(8,128)S(1)}, f32[2,16,64,1]{2,1,3,0:T(8,128)S(1)}, u32[]{:S(2)}, u32[]{:S(2)}) collective-permute-start(f32[2,16,64,1]{2,1,3,0:T(8,128)S(1)} %copy.21), channel_id=1, source_target_pairs={{0,1},{1,2},{2,3},{3,4},{4,5},{5,6},{6,7},{7,8},{8,9},{9,10},{10,1... | collective-permute-start | bytes 24584 | tf_op jit(solution)/shard_map/ppermute | solution.py:15
  12.6 5.6 %collective-permute-start.1 = (f32[2,16,64,1]{2,1,3,0:T(8,128)S(1)}, f32[2,16,64,1]{2,1,3,0:T(8,128)S(1)}, u32[]{:S(2)}, u32[]{:S(2)}) collective-permute-start(f32[2,16,64,1]{2,1,3,0:T(8,128)S(1)} %copy.22), channel_id=1, source_target_pairs={{1,0},{2,1},{3,2},{4,3},{5,4},{6,5},{7,6},{8,7},{9,8},{10,9},{11,1... | collective-permute-start | bytes 24584 | tf_op jit(solution)/shard_map/ppermute | solution.py:17
  22.2 1.0 copy-start.4
  96.8 1.1 copy-start
  115.8 7.0 %copy-start.3 = (f32[16,64,1]{2,0,1:T(8,128)S(1)}, f32[16,64,1]{2,0,1:T(8,128)}, u32[]{:S(2)}) copy-start(f32[16,64,1]{2,0,1:T(8,128)} %get-tuple-element.559) | copy-start | bytes 12292
  115.8 7.3 %copy-start.2 = (f32[16,64,1]{2,0,1:T(8,128)S(1)}, f32[16,64,1]{2,0,1:T(8,128)}, u32[]{:S(2)}) copy-start(f32[16,64,1]{2,0,1:T(8,128)} %get-tuple-element.508) | copy-start | bytes 12292
  115.8 7.7 %copy-start.1 = (f32[16,64,1]{2,0,1:T(8,128)S(1)}, f32[16,64,1]{2,0,1:T(8,128)}, u32[]{:S(2)}) copy-start(f32[16,64,1]{2,0,1:T(8,128)} %get-tuple-element.509) | copy-start | bytes 12292
where the time goes:
time: 172 us; the launch traced here: 169 us
  local copies, waits for them, and re-layouts  87.4 us (51%)
  blocking collectives  42.8 us (25%)
  other arithmetic  22.4 us (13%)
  starting transfers between devices  8.21 us (5%)
  loops' own time  3.9 us (2%)
  waiting for transfers between devices  3.69 us (2%)
    dynamic_update_slice x144, local copies, waits for them, and re-layouts, gathered_solve(): final, (ratios, values) = lax.scan(forward, (zeros, zeros), sequence)  41.2 us
    all_gather x1, blocking collectives, interface_y(): lax.all_gather(rows, 'gy', axis=1, tiled=True)  25.8 us
    all_gather x1, blocking collectives, interface_x(): lax.all_gather(rows, 'gx', axis=1, tiled=True)  17.1 us
    slice x48, local copies, waits for them, and re-layouts, forward(): next_d = (row[3] - row[0] * prior_d) / pivot  16.4 us
    div x23, other arithmetic, reduce_lines(): (entry - lower * neighbor(entry, -stride, axis) - upper * neighbor(entry,...  11 us
    slice x52, local copies, waits for them, and re-layouts, neighbor(): part = lax.slice_in_dim(values, 0, length + step, axis=axis)  6.99 us
    ppermute x2, starting transfers between devices, padded(): lax.ppermute(tail, axis, [(i, (i + 1) % count) for i in range(ends)])  5.63 us
    ppermute x2, waiting for transfers between devices, padded(): lax.ppermute(head, axis, [((i + 1) % count, i) for i in range(ends)])  3.68 us
  transfers between devices with their start and end apart: 4, of which 1 were waited for; matrix products, arithmetic and copies ran while one was open for 5% of the time, Pallas kernels for 0%

commit v1 on v0

v1 whole, which is shorter than its diff:
```python
import jax
import jax.numpy as jnp
from jax import lax
from jax.experimental import pallas as pl
from jax.experimental.pallas import tpu as pltpu
from jax.sharding import PartitionSpec as P

F32 = jnp.float32
NZ, BX, BY = 16, 64, 128
ROWS = NZ * BX
GROUPS = ROWS // 128
LIMIT = 40 * 1024 * 1024


def inverse(x):
    guess = pl.reciprocal(x, approx=True)
    return guess * (2.0 - x * guess)


def load_kernel(st_hbm, kx_hbm, ky_hbm, st, kx, ky, ky_t, up, down, sems):
    moves = [
        pltpu.make_async_copy(src, dst, sems.at[n])
        for n, (src, dst) in enumerate(((ky_hbm, ky), (st_hbm, st), (kx_hbm, kx)))
    ]
    for move in moves:
        move.start()
    moves[0].wait()
    for g in range(GROUPS):
        ky_t[pl.ds(g, BY, stride=GROUPS), :] = ky[pl.ds(g * 128, 128), :].T
    moves[1].wait()
    for g in range(GROUPS):
        turned = st[pl.ds(g * 128, 128), :].T
        down[0, pl.ds(g, 1), :] = turned[0:1, :]
        up[0, pl.ds(g, 1), :] = turned[127:128, :]
    down[1] = ky_t[pl.ds(0, GROUPS), :]
    up[1] = ky_t[pl.ds((BY - 1) * GROUPS, GROUPS), :]
    moves[2].wait()


def matrix_kernel(st, kx, ky, ky_t, fx, ux, wf, wl, fy, uy, yf, yl, mx, my, source):
    def x_row(ref, i):
        return jnp.concatenate(
            [ref[pl.ds(i, 8, stride=BX), :], ref[pl.ds(8 * BX + i, 8, stride=BX), :]], axis=0
        )

    def y_row(ref, i):
        return ref[pl.ds(i * GROUPS, GROUPS), :]

    def chains(count, row, f, u, first, last, m):
        ahead = jnp.ones_like(row(0))
        back = jnp.ones_like(ahead)
        low, high = row(0), row(count - 1)
        m[3] = low
        m[4] = high
        for i in range(count - 1):
            nxt = row(i + 1)
            r = 0.5 * (low + nxt)
            low = nxt
            inv = inverse(r + ahead)
            ratio = r * inv
            ahead = 1.0 + ratio * ahead
            u[i] = inv
            f[i] = ratio
            j = count - 1 - i
            prev = row(j - 1)
            r = 0.5 * (high + prev)
            high = prev
            ratio = r * inverse(r + back)
            back = 1.0 + ratio * back
            first[j] = ratio
            yield
        start = inverse(back)
        end = inverse(ahead)
        m[0] = start
        m[2] = end
        first[0] = start
        last[count - 1] = end
        u[count - 1] = end
        f[count - 1] = jnp.zeros_like(end)
        for i in range(1, count):
            start = start * first[i]
            first[i] = start
            j = count - 1 - i
            end = end * f[j]
            last[j] = end
            yield
        m[1] = end

    running = [
        chains(BX, lambda i: x_row(kx, i), fx, ux, wf, wl, mx),
        chains(BY, lambda i: y_row(ky_t, i), fy, uy, yf, yl, my),
    ]
    while running:
        for chain in list(running):
            if next(chain, 0) == 0:
                running.remove(chain)
    lane = lax.broadcasted_iota(jnp.int32, (128, 128), 1)
    for g in range(GROUPS):
        rows = pl.ds(g * 128, 128)
        s = st[rows, :]
        k = ky[rows, :]
        flux = 0.5 * (k + pltpu.roll(k, 127, 1)) * (pltpu.roll(s, 127, 1) - s)
        flux = jnp.where(lane == 127, 0.0, flux)
        source[rows, :] = s + flux - pltpu.roll(flux, 1, 1)


def x_send_kernel(above, below, up, down, source, wf, wl, mx, s_out, send):
    flux_l = 0.5 * (below[1] + down[1]) * (down[0] - below[0])
    flux_r = 0.5 * (above[1] + up[1]) * (above[0] - up[0])
    both = jnp.concatenate([flux_l, flux_r], axis=0)
    turned = jnp.concatenate([both] * 8, axis=0).T
    lane = lax.broadcasted_iota(jnp.int32, (128, 128), 1)
    for g in range(GROUPS):
        rows = pl.ds(g * 128, 128)
        left = jnp.broadcast_to(turned[:, g : g + 1], (128, 128))
        right = jnp.broadcast_to(turned[:, 8 + g : 9 + g], (128, 128))
        extra = jnp.where(lane == 0, -left, jnp.where(lane == 127, right, 0.0))
        s_out[rows, :] = source[rows, :] + extra
    firsts = [jnp.zeros((NZ, BY), F32) for _ in range(2)]
    lasts = [jnp.zeros((NZ, BY), F32) for _ in range(2)]
    for i in range(BX):
        s = jnp.concatenate(
            [s_out[pl.ds(i, 8, stride=BX), :], s_out[pl.ds(8 * BX + i, 8, stride=BX), :]], axis=0
        )
        firsts[i % 2] = firsts[i % 2] + wf[i] * s
        lasts[i % 2] = lasts[i % 2] + wl[i] * s
    sums = (firsts[0] + firsts[1], lasts[0] + lasts[1])
    for p in range(send.shape[0]):
        send[p, 0:5] = mx[...]
        send[p, 5] = sums[0]
        send[p, 6] = sums[1]


def interface(got, slots, me):
    count = got.shape[0]
    zero = jnp.zeros_like(got[0, 0])
    gammas, rhos = [], []
    gamma, rho = zero, zero
    for i in range(count + 1):
        below = [got[i - 1, n] for n in range(7)] if i else [zero] * 7
        above = [got[i, n] for n in range(7)] if i < count else [zero] * 7
        pivot = 2.0 * inverse(below[4] + above[3]) + below[2] + above[0] - below[1] * gamma
        inv = inverse(pivot)
        rho = (below[6] - above[5] + below[1] * rho) * inv
        gamma = above[1] * inv
        gammas.append(gamma)
        rhos.append(rho)
    flow = rhos[count]
    slots[count] = flow
    for i in range(count - 1, -1, -1):
        flow = rhos[i] + gammas[i] * flow
        slots[i] = flow
    return slots[me], slots[me + 1]


def x_solve_kernel(got, s_in, st, fx, ux, wf, wl, yf, yl, my, v_t, send, slots, work, v):
    me = lax.axis_index("gx")
    q_l, q_r = interface(got, slots, me)

    def x_row(ref, i):
        return jnp.concatenate(
            [ref[pl.ds(i, 8, stride=BX), :], ref[pl.ds(8 * BX + i, 8, stride=BX), :]], axis=0
        )

    total = x_row(s_in, 0) + q_l
    work[0] = total
    for i in range(1, BX):
        total = x_row(s_in, i) + fx[i - 1] * total
        work[i] = total
    total = total - q_r
    x = jnp.zeros_like(total)
    for i in range(BX - 1, -1, -1):
        x = ux[i] * (total if i == BX - 1 else work[i]) + fx[i] * x
        d = x - x_row(st, i)
        v[pl.ds(i, 8, stride=BX), :] = d[:8]
        v[pl.ds(8 * BX + i, 8, stride=BX), :] = d[8:]
    for g in range(GROUPS):
        v_t[pl.ds(g, BY, stride=GROUPS), :] = v[pl.ds(g * 128, 128), :].T
    firsts = [jnp.zeros((GROUPS, 128), F32) for _ in range(4)]
    lasts = [jnp.zeros((GROUPS, 128), F32) for _ in range(4)]
    for j in range(BY):
        row = v_t[pl.ds(j * GROUPS, GROUPS), :]
        firsts[j % 4] = firsts[j % 4] + yf[j] * row
        lasts[j % 4] = lasts[j % 4] + yl[j] * row
    sums = (
        (firsts[0] + firsts[1]) + (firsts[2] + firsts[3]),
        (lasts[0] + lasts[1]) + (lasts[2] + lasts[3]),
    )
    for p in range(send.shape[0]):
        send[p, 0:5] = my[...]
        send[p, 5] = sums[0]
        send[p, 6] = sums[1]


def y_solve_kernel(got, v_t, st, fy, uy, out_hbm, slots, work, out, sems):
    me = lax.axis_index("gy")
    p_l, p_r = interface(got, slots, me)

    def y_row(ref, j):
        return ref[pl.ds(j * GROUPS, GROUPS), :]

    total = y_row(v_t, 0) + p_l
    work[pl.ds(0, GROUPS), :] = total
    for j in range(1, BY):
        total = y_row(v_t, j) + fy[j - 1] * total
        work[pl.ds(j * GROUPS, GROUPS), :] = total
    total = total - p_r
    x = jnp.zeros_like(total)
    for j in range(BY - 1, -1, -1):
        x = uy[j] * (total if j == BY - 1 else y_row(work, j)) + fy[j] * x
        work[pl.ds(j * GROUPS, GROUPS), :] = x
    moves = []
    for g in range(GROUPS):
        rows = pl.ds(g * 128, 128)
        out[rows, :] = st[rows, :] + 2.0 * work[pl.ds(g, BY, stride=GROUPS), :].T
        move = pltpu.make_async_copy(out.at[rows], out_hbm.at[rows], sems.at[g])
        move.start()
        moves.append(move)
    for move in moves:
        move.wait()


def call(kernel, outs, args, scratch=(), flops=0):
    vm = pl.BlockSpec(memory_space=pltpu.VMEM)
    anywhere = pl.BlockSpec(memory_space=pl.ANY)
    return pl.pallas_call(
        kernel,
        out_shape=[
            jax.ShapeDtypeStruct(shape, F32) if hbm else pltpu.VMEM(shape, F32)
            for shape, hbm in outs
        ],
        in_specs=[anywhere if hbm else vm for _, hbm in args],
        out_specs=[anywhere if hbm else vm for _, hbm in outs],
        scratch_shapes=list(scratch),
        compiler_params=pltpu.CompilerParams(vmem_limit_bytes=LIMIT),
        cost_estimate=pl.CostEstimate(flops=flops, bytes_accessed=flops, transcendentals=0),
    )(*[value for value, _ in args])


def inside(*shape):
    return (shape, False)


def on_device(state, kappa_x, kappa_y):
    flat = [a.reshape(ROWS, BY) for a in (state, kappa_x, kappa_y)]
    plane = inside(ROWS, BY)
    edge = inside(2, GROUPS, 128)
    st, kx, ky, ky_t, up, down = call(
        load_kernel,
        [plane, plane, plane, plane, edge, edge],
        [(a, True) for a in flat],
        [pltpu.SemaphoreType.DMA((3,))],
    )
    count = lax.axis_size("gy")
    below = lax.ppermute(up, "gy", [(i, i + 1) for i in range(count - 1)])
    above = lax.ppermute(down, "gy", [(i + 1, i) for i in range(count - 1)])
    xs = inside(BX, NZ, BY)
    ys = inside(BY, GROUPS, 128)
    fx, ux, wf, wl, fy, uy, yf, yl, mx, my, source = call(
        matrix_kernel,
        [xs] * 4 + [ys] * 4 + [inside(5, NZ, BY), inside(5, GROUPS, 128), plane],
        [(a, False) for a in (st, kx, ky, ky_t)],
        flops=10_000_000,
    )
    s, send = call(
        x_send_kernel,
        [plane, inside(lax.axis_size("gx"), 7, NZ, BY)],
        [(a, False) for a in (above, below, up, down, source, wf, wl, mx)],
    )
    got = lax.all_to_all(send, "gx", 0, 0)
    v_t, send = call(
        x_solve_kernel,
        [plane, inside(count, 7, GROUPS, 128)],
        [(a, False) for a in (got, s, st, fx, ux, wf, wl, yf, yl, my)],
        [
            pltpu.VMEM((lax.axis_size("gx") + 1, NZ, BY), F32),
            pltpu.VMEM((BX, NZ, BY), F32),
            pltpu.VMEM((ROWS, BY), F32),
        ],
    )
    got = lax.all_to_all(send, "gy", 0, 0)
    (out,) = call(
        y_solve_kernel,
        [((ROWS, BY), True)],
        [(a, False) for a in (got, v_t, st, fy, uy)],
        [
            pltpu.VMEM((count + 1, GROUPS, 128), F32),
            pltpu.VMEM((ROWS, BY), F32),
            pltpu.VMEM((ROWS, BY), F32),
            pltpu.SemaphoreType.DMA((GROUPS,)),
        ],
    )
    return out.reshape(state.shape)


def solution(mesh):
    spec = P(None, "gx", "gy")
    return jax.shard_map(
        on_device, mesh=mesh, in_specs=(spec, spec, spec), out_specs=spec, check_vma=False
    )
```

time: 172 us -> 50.6 us (0.29); the launches traced: 169 us -> 50.2 us
  local copies, waits for them, and re-layouts: 87.4 us -> 3.12 us
  other arithmetic: 22.4 us -> 0 us
  blocking collectives: 42.8 us -> 34.4 us
  Pallas kernels: 0 us -> 6.78 us
  loops' own time: 3.9 us -> 0 us
  waiting for transfers between devices: 3.69 us -> 0.01 us
  starting transfers between devices: 8.21 us -> 5.84 us
    all_gather x2 -> x0, blocking collectives: 42.8 us -> none  [the longest x1 25.8 us: interface_y(): lax.all_gather(rows, 'gy', axis=1, tiled=True)]
    dynamic_update_slice x144 -> x0, local copies, waits for them, and re-layouts: 41.2 us -> none  [gathered_solve(): final, (ratios, values) = lax.scan(forward, (zeros, zeros), sequence)]
    all_to_all x0 -> x2, blocking collectives: none -> 34.4 us  [the longest x1 20.5 us: on_device(): got = lax.all_to_all(send, 'gy', 0, 0)]
    slice x119 -> x0, local copies, waits for them, and re-layouts: 30.9 us -> none  [the longest x48 16.4 us: forward(): next_d = (row[3] - row[0] * prior_d) / pivot]
    div x74 -> x0, other arithmetic: 12.8 us -> none  [the longest x23 11 us: reduce_lines(): (entry - lower * neighbor(entry, -stride, axis) - upper * neighbor(entry,...]
    pallas_call x0 -> x5, Pallas kernels: none -> 6.78 us  [call(): pl.pallas_call(kernel, out_shape=[jax.ShapeDtypeStruct(shape, F32) if hbm...]
    another operation x4 -> x0, loops' own time: 3.9 us -> none  [the longest x2 2.31 us: gathered_solve(): final, (ratios, values) = lax.scan(forward, (zeros, zeros), sequence)]
    ppermute x4 -> x2, waiting for transfers between devices: 3.69 us -> 0.01 us  [the longest x1 0.01 us: on_device(): above = lax.ppermute(down, 'gy', [(i + 1, i) for i in range(count - 1)])]
  transfers between devices with their start and end apart: 4 -> 2, of which waited for: 1 -> 0; matrix products, arithmetic and copies ran while one was open for 5% -> 0% of each run, Pallas kernels for 0% -> 4%
where the time goes in v1:
time: 50.6 us; the launch traced here: 50.2 us
  blocking collectives  34.4 us (68%)
  Pallas kernels  6.78 us (13%)
  starting transfers between devices  5.84 us (12%)
  local copies, waits for them, and re-layouts  3.12 us (6%)
    all_to_all x1, blocking collectives, on_device(): got = lax.all_to_all(send, 'gy', 0, 0)  20.5 us
    all_to_all x1, blocking collectives, on_device(): got = lax.all_to_all(send, 'gx', 0, 0)  13.9 us
    pallas_call x5, Pallas kernels, call(): pl.pallas_call(kernel, out_shape=[jax.ShapeDtypeStruct(shape, F32) if hbm...  6.78 us
    ppermute x1, starting transfers between devices, on_device(): below = lax.ppermute(up, 'gy', [(i, i + 1) for i in range(count - 1)])  4.55 us
    unnamed x6, local copies, waits for them, and re-layouts  3.12 us
    ppermute x1, starting transfers between devices, on_device(): above = lax.ppermute(down, 'gy', [(i + 1, i) for i in range(count - 1)])  1.29 us
  transfers between devices with their start and end apart: 2, of which 0 were waited for; matrix products, arithmetic and copies ran while one was open for 0% of the time, Pallas kernels for 4%

profile of v1, /device:TPU:0, one launch (start us, length us, event | category | flops | bytes accessed | tf_op | source)
XLA Modules:
  0.0 50.2 jit_solution(10213720469811020700)
XLA Ops:
  0.0 0.0 copy-start
  0.0 1.0 %copy-done = f32[16,64,128]{2,1,0:T(8,128)S(1)} copy-done((f32[16,64,128]{2,1,0:T(8,128)S(1)}, f32[16,64,128]{2,1,0:T(8,128)}, u32[]{:S(2)}) %copy-start) | copy-done | bytes 524312
  1.0 0.0 copy-start.1
  1.0 1.0 %copy-done.1 = f32[16,64,128]{2,1,0:T(8,128)S(1)} copy-done((f32[16,64,128]{2,1,0:T(8,128)S(1)}, f32[16,64,128]{2,1,0:T(8,128)}, u32[]{:S(2)}) %copy-start.1) | copy-done | bytes 524312
  2.1 0.0 copy-start.2
  2.1 1.0 %copy-done.2 = f32[16,64,128]{2,1,0:T(8,128)S(1)} copy-done((f32[16,64,128]{2,1,0:T(8,128)S(1)}, f32[16,64,128]{2,1,0:T(8,128)}, u32[]{:S(2)}) %copy-start.2) | copy-done | bytes 524312
  3.1 0.5 %shard_map.37 = (f32[1024,128]{1,0:T(8,128)S(1)}, f32[1024,128]{1,0:T(8,128)S(1)}, f32[1024,128]{1,0:T(8,128)S(1)}, f32[1024,128]{1,0:T(8,128)S(1)}, f32[2,8,128]{2,1,0:T(8,128)S(1)}, /*index=5*/f32[2,8,128]{2,1,0:T(8,128)S(1)}) custom-call(f32[1024,128]{1,0:T(8,128)S(1)} %bitcast.4, f32[1024,128]{1,0:T(8,128)S(1)} %bitcast.5, f32[1024,128]{1,0:T(8,128)S(1)} %bitcast.6), custom_call_target="tpu_custom_call" | custom-call | tf_op jit(solution)/shard_map/pallas_call | solution.py:226
  3.7 1.3 %collective-permute-start = (f32[2,8,128]{2,1,0:T(8,128)S(1)}, f32[2,8,128]{2,1,0:T(8,128)S(1)}, u32[]{:S(2)}, u32[]{:S(2)}) collective-permute-start(f32[2,8,128]{2,1,0:T(8,128)S(1)} %get-tuple-element.26.down), channel_id=1, source_target_pairs={{1,0},{2,1},{3,2},{4,3},{5,4},{6,5},{7,6},{8,7},{9,8},{10,9},{11,1... | collective-permute-start | bytes 24584 | tf_op jit(solution)/shard_map/ppermute | solution.py:256
  5.0 4.5 %collective-permute-start.1 = (f32[2,8,128]{2,1,0:T(8,128)S(1)}, f32[2,8,128]{2,1,0:T(8,128)S(1)}, u32[]{:S(2)}, u32[]{:S(2)}) collective-permute-start(f32[2,8,128]{2,1,0:T(8,128)S(1)} %get-tuple-element.27.up), channel_id=1, source_target_pairs={{0,1},{1,2},{2,3},{3,4},{4,5},{5,6},{6,7},{7,8},{8,9},{9,10},{10,1... | collective-permute-start | bytes 24584 | tf_op jit(solution)/shard_map/ppermute | solution.py:255
  9.5 2.1 %shard_map.38 = (f32[64,16,128]{2,1,0:T(8,128)S(1)}, f32[64,16,128]{2,1,0:T(8,128)S(1)}, f32[64,16,128]{2,1,0:T(8,128)S(1)}, f32[64,16,128]{2,1,0:T(8,128)S(1)},...) custom-call(f32[1024,128]{1,0:T(8,128)S(1)} %get-tuple-element.28.st, ...), custom_call_target="tpu_custom_call" | custom-call | flops 10000000 | bytes 10000000 | tf_op jit(solution)/shard_map/pallas_call | solution.py:226
  11.6 0.0 collective-permute-done.above
  11.6 0.0 collective-permute-done.1.below
  11.6 0.9 %shard_map.39 = (f32[1024,128]{1,0:T(8,128)S(1)}, f32[8,7,16,128]{3,2,1,0:T(8,128)S(1)}) custom-call(f32[2,8,128]{2,1,0:T(8,128)S(1)} %collective-permute-done.above, f32[2,8,128]{2,1,0:T(8,128)S(1)} %collective-permute-done.1.below, f32[2,8,128]{2,1,0:T(8,128)S(1)} %get-tuple-element.27.up, f32[2,8,128]{2,1,0:T(8,128)S(1)} %get-tuple-element.26.down, ...), custom_call_target="tpu_custom_call" | custom-call | tf_op jit(solution)/shard_map/pallas_call | solution.py:226
  12.6 13.9 %all_to_all.10.got = f32[8,7,16,128]{3,2,1,0:T(8,128)S(1)} all-to-all(f32[8,7,16,128]{3,2,1,0:T(8,128)S(1)} %get-tuple-element.36), channel_id=1, replica_groups=mesh['gx'=8,'gy'=16] {'gx'}, dimensions={0} | all-to-all | bytes 917504 | tf_op jit(solution)/shard_map/all_to_all | solution.py:270
  26.5 1.5 %shard_map.40 = (f32[1024,128]{1,0:T(8,128)S(1)}, f32[16,7,8,128]{3,2,1,0:T(8,128)S(1)}) custom-call(f32[8,7,16,128]{3,2,1,0:T(8,128)S(1)} %all_to_all.10.got, f32[1024,128]{1,0:T(8,128)S(1)} %get-tuple-element.37.s_in, f32[1024,128]{1,0:T(8,128)S(1)} %get-tuple-element.28.st, f32[64,16,128]{2,1,0:T(8,128)S(1)} %get-tuple-element.38.fx, ...), custom_call_target="tpu_custom_call" | custom-call | tf_op jit(solution)/shard_map/pallas_call | solution.py:226
  27.9 20.5 %all_to_all.11.got = f32[16,7,8,128]{3,2,1,0:T(8,128)S(1)} all-to-all(f32[16,7,8,128]{3,2,1,0:T(8,128)S(1)} %get-tuple-element.43), channel_id=1, replica_groups=mesh['gx'=8,'gy'=16] {'gy'}, dimensions={0} | all-to-all | bytes 917504 | tf_op jit(solution)/shard_map/all_to_all | solution.py:281
  48.5 1.8 %shard_map.41 = f32[1024,128]{1,0:T(8,128)} custom-call(f32[16,7,8,128]{3,2,1,0:T(8,128)S(1)} %all_to_all.11.got, f32[1024,128]{1,0:T(8,128)S(1)} %get-tuple-element.44.v_t, f32[1024,128]{1,0:T(8,128)S(1)} %get-tuple-element.28.st, f32[128,8,128]{2,1,0:T(8,128)S(1)} %get-tuple-element.45.fy, f32[128,8,128]{2,1,0:T(8,128)S(1)} %get-tuple-element.46.uy), custom_call_target="tpu_custom_call" | custom-call | tf_op jit(solution)/shard_map/pallas_call | solution.py:226
Async XLA Ops:
  0.0 1.0 %copy-start = (f32[16,64,128]{2,1,0:T(8,128)S(1)}, f32[16,64,128]{2,1,0:T(8,128)}, u32[]{:S(2)}) copy-start(f32[16,64,128]{2,1,0:T(8,128)} %param.3) | copy-start | bytes 1572868
  1.0 1.0 %copy-start.1 = (f32[16,64,128]{2,1,0:T(8,128)S(1)}, f32[16,64,128]{2,1,0:T(8,128)}, u32[]{:S(2)}) copy-start(f32[16,64,128]{2,1,0:T(8,128)} %param.4) | copy-start | bytes 1572868
  2.1 1.0 %copy-start.2 = (f32[16,64,128]{2,1,0:T(8,128)S(1)}, f32[16,64,128]{2,1,0:T(8,128)}, u32[]{:S(2)}) copy-start(f32[16,64,128]{2,1,0:T(8,128)} %param.5) | copy-start | bytes 1572868
  3.7 7.9 %collective-permute-start = (f32[2,8,128]{2,1,0:T(8,128)S(1)}, f32[2,8,128]{2,1,0:T(8,128)S(1)}, u32[]{:S(2)}, u32[]{:S(2)}) collective-permute-start(f32[2,8,128]{2,1,0:T(8,128)S(1)} %get-tuple-element.26.down), channel_id=1, source_target_pairs={{1,0},{2,1},{3,2},{4,3},{5,4},{6,5},{7,6},{8,7},{9,8},{10,9},{11,1... | collective-permute-start | bytes 24584 | tf_op jit(solution)/shard_map/ppermute | solution.py:256
  5.0 6.6 %collective-permute-start.1 = (f32[2,8,128]{2,1,0:T(8,128)S(1)}, f32[2,8,128]{2,1,0:T(8,128)S(1)}, u32[]{:S(2)}, u32[]{:S(2)}) collective-permute-start(f32[2,8,128]{2,1,0:T(8,128)S(1)} %get-tuple-element.27.up), channel_id=1, source_target_pairs={{0,1},{1,2},{2,3},{3,4},{4,5},{5,6},{6,7},{7,8},{8,9},{9,10},{10,1... | collective-permute-start | bytes 24584 | tf_op jit(solution)/shard_map/ppermute | solution.py:255

commit v2 on v1

v2 whole, which is shorter than its diff:
```python
import jax
import jax.numpy as jnp
from jax import lax
from jax.experimental import pallas as pl
from jax.experimental.pallas import tpu as pltpu
from jax.sharding import PartitionSpec as P

F32 = jnp.float32
NZ, BX, BY = 16, 64, 128
ROWS = NZ * BX
GROUPS = ROWS // 128
LIMIT = 40 * 1024 * 1024
SIDE = 4


def inverse(x):
    guess = pl.reciprocal(x, approx=True)
    return guess * (2.0 - x * guess)


def x_row(ref, i):
    return jnp.concatenate(
        [ref[pl.ds(i, 8, stride=BX), :], ref[pl.ds(8 * BX + i, 8, stride=BX), :]], axis=0
    )


def y_row(ref, j):
    return ref[pl.ds(j * GROUPS, GROUPS), :]


def read(ref):
    return [ref[n] for n in range(7)]


def merge(low, high):
    inv = inverse(2.0 * inverse(low[4] + high[3]) + low[2] + high[0])
    e = (low[6] - high[5]) * inv
    a = low[1] * inv
    b = high[1] * inv
    joined = [
        low[0] - low[1] * a,
        low[1] * b,
        high[2] - high[1] * b,
        low[3],
        high[4],
        low[5] - low[1] * e,
        high[6] + high[1] * e,
    ]
    return joined, (e, a, b)


def chain_ends(blocks):
    zero = jnp.zeros_like(blocks[0][0])
    gammas, rhos = [], []
    gamma, rho = zero, zero
    count = len(blocks)
    for i in range(count + 1):
        below = blocks[i - 1] if i else [zero] * 7
        above = blocks[i] if i < count else [zero] * 7
        inv = inverse(2.0 * inverse(below[4] + above[3]) + below[2] + above[0] - below[1] * gamma)
        rho = (below[6] - above[5] + below[1] * rho) * inv
        gamma = above[1] * inv
        gammas.append(gamma)
        rhos.append(rho)
    flows = [rhos[count]]
    for i in range(count - 1, -1, -1):
        flows.append(rhos[i] + gammas[i] * flows[-1])
    return flows[::-1]


def arrange(own, others, place, slots):
    slots[place] = own[...]
    for k, other in enumerate(others):
        slots[lax.rem(place + SIDE - 1 - k, SIDE)] = other[...]
    return [[slots[c, n] for n in range(7)] for c in range(SIDE)]


def load_kernel(st_hbm, kx_hbm, ky_hbm, st, kx, ky, ky_t, up, down, sems):
    moves = [
        pltpu.make_async_copy(src, dst, sems.at[n])
        for n, (src, dst) in enumerate(((ky_hbm, ky), (st_hbm, st), (kx_hbm, kx)))
    ]
    for move in moves:
        move.start()
    moves[0].wait()
    for g in range(GROUPS):
        ky_t[pl.ds(g, BY, stride=GROUPS), :] = ky[pl.ds(g * 128, 128), :].T
    moves[1].wait()
    for g in range(GROUPS):
        turned = st[pl.ds(g * 128, 128), :].T
        down[0, pl.ds(g, 1), :] = turned[0:1, :]
        up[0, pl.ds(g, 1), :] = turned[127:128, :]
    down[1] = ky_t[pl.ds(0, GROUPS), :]
    up[1] = ky_t[pl.ds((BY - 1) * GROUPS, GROUPS), :]
    moves[2].wait()


def sweep(count, row, f, u, first, last, m):
    ahead = jnp.ones_like(row(0))
    back = jnp.ones_like(ahead)
    low, high = row(0), row(count - 1)
    m[3] = low
    m[4] = high
    for i in range(count - 1):
        nxt = row(i + 1)
        r = 0.5 * (low + nxt)
        low = nxt
        inv = inverse(r + ahead)
        ratio = r * inv
        ahead = 1.0 + ratio * ahead
        u[i] = inv
        f[i] = ratio
        j = count - 1 - i
        prev = row(j - 1)
        r = 0.5 * (high + prev)
        high = prev
        ratio = r * inverse(r + back)
        back = 1.0 + ratio * back
        first[j] = ratio
    start = inverse(back)
    end = inverse(ahead)
    m[0] = start
    m[2] = end
    first[0] = start
    last[count - 1] = end
    u[count - 1] = end
    f[count - 1] = jnp.zeros_like(end)
    for i in range(1, count):
        start = start * first[i]
        first[i] = start
        j = count - 1 - i
        end = end * f[j]
        last[j] = end
    m[1] = end


def x_matrix_kernel(st, kx, ky, fx, ux, wf, wl, mx, source):
    sweep(BX, lambda i: x_row(kx, i), fx, ux, wf, wl, mx)
    lane = lax.broadcasted_iota(jnp.int32, (128, 128), 1)
    for g in range(GROUPS):
        rows = pl.ds(g * 128, 128)
        s = st[rows, :]
        k = ky[rows, :]
        flux = 0.5 * (k + pltpu.roll(k, 127, 1)) * (pltpu.roll(s, 127, 1) - s)
        flux = jnp.where(lane == 127, 0.0, flux)
        source[rows, :] = s + flux - pltpu.roll(flux, 1, 1)


def y_matrix_kernel(ky_t, after, fy, uy, yf, yl, my):
    sweep(BY, lambda j: y_row(ky_t, j), fy, uy, yf, yl, my)


def x_ends_kernel(above, below, up, down, source, wf, wl, mx, s_out, send):
    flux_l = 0.5 * (below[1] + down[1]) * (down[0] - below[0])
    flux_r = 0.5 * (above[1] + up[1]) * (above[0] - up[0])
    both = jnp.concatenate([flux_l, flux_r], axis=0)
    turned = jnp.concatenate([both] * 8, axis=0).T
    lane = lax.broadcasted_iota(jnp.int32, (128, 128), 1)
    for g in range(GROUPS):
        rows = pl.ds(g * 128, 128)
        left = jnp.broadcast_to(turned[:, g : g + 1], (128, 128))
        right = jnp.broadcast_to(turned[:, 8 + g : 9 + g], (128, 128))
        extra = jnp.where(lane == 0, -left, jnp.where(lane == 127, right, 0.0))
        s_out[rows, :] = source[rows, :] + extra
    firsts = [jnp.zeros((NZ, BY), F32) for _ in range(2)]
    lasts = [jnp.zeros((NZ, BY), F32) for _ in range(2)]
    for i in range(BX):
        s = x_row(s_out, i)
        firsts[i % 2] = firsts[i % 2] + wf[i] * s
        lasts[i % 2] = lasts[i % 2] + wl[i] * s
    send[0:5] = mx[...]
    send[5] = firsts[0] + firsts[1]
    send[6] = lasts[0] + lasts[1]


def x_local_kernel(s_in, st, fx, ux, d):
    total = x_row(s_in, 0)
    d[0] = total
    for i in range(1, BX):
        total = x_row(s_in, i) + fx[i - 1] * total
        d[i] = total
    x = jnp.zeros_like(total)
    for i in range(BX - 1, -1, -1):
        x = ux[i] * d[i] + fx[i] * x
        d[i] = x - x_row(st, i)


def x_merge_kernel(own, other, send, coefs):
    core = lax.rem(lax.axis_index("gx"), 2)
    mine, theirs = read(own), read(other)
    low = [jnp.where(core == 0, a, b) for a, b in zip(mine, theirs)]
    high = [jnp.where(core == 0, b, a) for a, b in zip(mine, theirs)]
    joined, flow = merge(low, high)
    for n in range(7):
        send[n] = joined[n]
    for n in range(3):
        coefs[n] = flow[n]


def x_flow_kernel(own, other1, other2, other3, coefs, after, for_low, for_high, slots, ends):
    place = lax.div(lax.axis_index("gx"), 2)
    blocks = arrange(own, (other1, other2, other3), place, slots)
    for n, flow in enumerate(chain_ends(blocks)):
        ends[n] = flow
    enter, leave = ends[place], ends[place + 1]
    middle = coefs[0] + coefs[1] * enter + coefs[2] * leave
    for_low[0] = enter
    for_low[1] = middle
    for_high[0] = middle
    for_high[1] = leave


def y_ends_kernel(came, held, d, wf, wl, yf, yl, my, v_t, send, v):
    core = lax.rem(lax.axis_index("gx"), 2)
    enter = jnp.where(core == 0, came[0], held[0])
    leave = jnp.where(core == 0, came[1], held[1])
    for i in range(BX):
        part = d[i] + wf[i] * enter - wl[i] * leave
        v[pl.ds(i, 8, stride=BX), :] = part[:8]
        v[pl.ds(8 * BX + i, 8, stride=BX), :] = part[8:]
    for g in range(GROUPS):
        v_t[pl.ds(g, BY, stride=GROUPS), :] = v[pl.ds(g * 128, 128), :].T
    firsts = [jnp.zeros((GROUPS, 128), F32) for _ in range(4)]
    lasts = [jnp.zeros((GROUPS, 128), F32) for _ in range(4)]
    for j in range(BY):
        row = y_row(v_t, j)
        firsts[j % 4] = firsts[j % 4] + yf[j] * row
        lasts[j % 4] = lasts[j % 4] + yl[j] * row
    send[0:5] = my[...]
    send[5] = (firsts[0] + firsts[1]) + (firsts[2] + firsts[3])
    send[6] = (lasts[0] + lasts[1]) + (lasts[2] + lasts[3])


def y_pack_kernel(own, other, send):
    send[:, 0:GROUPS] = own[...]
    send[:, GROUPS : 2 * GROUPS] = other[...]


def y_local_kernel(v_t, fy, uy, after, g_t):
    total = y_row(v_t, 0)
    g_t[0] = total
    for j in range(1, BY):
        total = y_row(v_t, j) + fy[j - 1] * total
        g_t[j] = total
    x = jnp.zeros_like(total)
    for j in range(BY - 1, -1, -1):
        x = uy[j] * g_t[j] + fy[j] * x
        g_t[j] = x


def y_merge_kernel(own, other1, other2, other3, after, send, coefs, slots):
    place = lax.rem(lax.axis_index("gy"), SIDE)
    blocks = arrange(own, (other1, other2, other3), place, slots)
    joined = blocks[0]
    for c in range(1, SIDE):
        joined, flow = merge(joined, blocks[c])
        for n in range(3):
            coefs[c - 1, n] = flow[n]
    for n in range(7):
        send[n] = joined[n]


def y_flow_kernel(own, other1, other2, other3, coefs, for_low, for_high, slots, ends, inner):
    place = lax.div(lax.axis_index("gy"), SIDE)
    blocks = arrange(own, (other1, other2, other3), place, slots)
    for n, flow in enumerate(chain_ends(blocks)):
        ends[n] = flow
    enter, leave = ends[place], ends[place + 1]
    inner[0] = enter
    inner[SIDE] = leave
    flow = leave
    for c in range(SIDE - 1, 0, -1):
        flow = coefs[c - 1, 0] + coefs[c - 1, 1] * enter + coefs[c - 1, 2] * flow
        inner[c] = flow
    depth = lax.rem(lax.axis_index("gy"), SIDE)
    enter, leave = inner[depth], inner[depth + 1]
    for_high[0] = enter[:GROUPS]
    for_high[1] = leave[:GROUPS]
    for_low[0] = enter[GROUPS:]
    for_low[1] = leave[GROUPS:]


def y_solve_kernel(came, held, g_t, yf, yl, st, out_hbm, work, out, sems):
    core = lax.rem(lax.axis_index("gx"), 2)
    enter = jnp.where(core == 0, came[0], held[0])
    leave = jnp.where(core == 0, came[1], held[1])
    for j in range(BY):
        work[pl.ds(j * GROUPS, GROUPS), :] = 2.0 * (g_t[j] + yf[j] * enter - yl[j] * leave)
    moves = []
    for g in range(GROUPS):
        rows = pl.ds(g * 128, 128)
        out[rows, :] = st[rows, :] + work[pl.ds(g, BY, stride=GROUPS), :].T
        move = pltpu.make_async_copy(out.at[rows], out_hbm.at[rows], sems.at[g])
        move.start()
        moves.append(move)
    for move in moves:
        move.wait()


def call(kernel, outs, args, scratch=(), cost=100_000):
    vm = pl.BlockSpec(memory_space=pltpu.VMEM)
    hbm = pl.BlockSpec(memory_space=pltpu.HBM)
    return pl.pallas_call(
        kernel,
        out_shape=[
            jax.ShapeDtypeStruct(shape, F32) if far else pltpu.VMEM(shape, F32)
            for shape, far in outs
        ],
        in_specs=[hbm if far else vm for _, far in args],
        out_specs=[hbm if far else vm for _, far in outs],
        scratch_shapes=list(scratch),
        compiler_params=pltpu.CompilerParams(vmem_limit_bytes=LIMIT),
        cost_estimate=pl.CostEstimate(flops=cost, bytes_accessed=cost, transcendentals=0),
    )(*[value for value, _ in args])


def near(*values):
    return [(value, False) for value in values]


def on_device(state, kappa_x, kappa_y):
    flat = [a.reshape(ROWS, BY) for a in (state, kappa_x, kappa_y)]
    plane = (ROWS, BY)
    xs = (BX, NZ, BY)
    ys = (BY, GROUPS, 128)
    x_block = (7, NZ, BY)
    y_block = (7, GROUPS, 128)
    wide = (7, 2 * GROUPS, 128)
    edge = (2, GROUPS, 128)
    nx, ny = lax.axis_size("gx"), lax.axis_size("gy")

    def to_core(value, sources):
        return lax.ppermute(value, "gx", [(i, i ^ 1) for i in range(nx) if i % 2 in sources])

    def to_chips(value, target):
        return [
            lax.ppermute(
                value,
                ("gx", "gy"),
                [(i * ny + j, target(i, j, k)) for i in range(1, nx, 2) for j in range(ny)],
            )
            for k in range(1, SIDE)
        ]

    st, kx, ky, ky_t, up, down = call(
        load_kernel,
        near(plane, plane, plane, plane, edge, edge),
        [(a, True) for a in flat],
        [pltpu.SemaphoreType.DMA((3,))],
    )
    below = lax.ppermute(up, "gy", [(i, i + 1) for i in range(ny - 1)])
    above = lax.ppermute(down, "gy", [(i + 1, i) for i in range(ny - 1)])
    fx, ux, wf, wl, mx, source = call(
        x_matrix_kernel, near(xs, xs, xs, xs, (5, NZ, BY), plane), near(st, kx, ky), cost=5_000_000
    )
    s, ends = call(
        x_ends_kernel,
        near(plane, x_block),
        near(above, below, up, down, source, wf, wl, mx),
    )
    other = to_core(ends, (0, 1))
    (d,) = call(x_local_kernel, near(xs), near(s, st, fx, ux), cost=3_000_000)
    chip, coefs = call(x_merge_kernel, near(x_block, (3, NZ, BY)), near(ends, other))
    others = to_chips(chip, lambda i, j, k: (i + 2 * k) % nx * ny + j)
    fy, uy, yf, yl, my = call(
        y_matrix_kernel, near(ys, ys, ys, ys, (5, GROUPS, 128)), near(ky_t, coefs), cost=5_000_000
    )
    for_low, for_high = call(
        x_flow_kernel,
        near((2, NZ, BY), (2, NZ, BY)),
        near(chip, *others, coefs, my),
        [pltpu.VMEM((SIDE,) + x_block, F32), pltpu.VMEM((SIDE + 1, NZ, BY), F32)],
    )
    came = to_core(for_low, (1,))
    v_t, ends = call(
        y_ends_kernel,
        near(plane, y_block),
        near(came, for_high, d, wf, wl, yf, yl, my),
        [pltpu.VMEM(plane, F32)],
    )
    other = to_core(ends, (0,))
    (pair,) = call(y_pack_kernel, near(wide), near(ends, other))
    others = to_chips(pair, lambda i, j, k: i * ny + j // SIDE * SIDE + (j + k) % SIDE)
    (g_t,) = call(y_local_kernel, near(ys), near(v_t, fy, uy, pair), cost=5_000_000)
    quad, coefs = call(
        y_merge_kernel,
        near(wide, (SIDE - 1, 3, 2 * GROUPS, 128)),
        near(pair, *others, g_t),
        [pltpu.VMEM((SIDE,) + wide, F32)],
    )
    others = to_chips(quad, lambda i, j, k: i * ny + (j + SIDE * k) % ny)
    for_low, for_high = call(
        y_flow_kernel,
        near(edge, edge),
        near(quad, *others, coefs),
        [
            pltpu.VMEM((SIDE,) + wide, F32),
            pltpu.VMEM((SIDE + 1, 2 * GROUPS, 128), F32),
            pltpu.VMEM((SIDE + 1, 2 * GROUPS, 128), F32),
        ],
    )
    came = to_core(for_low, (1,))
    (out,) = call(
        y_solve_kernel,
        [(plane, True)],
        near(came, for_high, g_t, yf, yl, st),
        [
            pltpu.VMEM(plane, F32),
            pltpu.VMEM(plane, F32),
            pltpu.SemaphoreType.DMA((GROUPS,)),
        ],
    )
    return out.reshape(state.shape)


def solution(mesh):
    spec = P(None, "gx", "gy")
    return jax.shard_map(
        on_device, mesh=mesh, in_specs=(spec, spec, spec), out_specs=spec, check_vma=False
    )
```

time: 50.6 us -> 67.6 us (1.34)
  the two profiles are of different devices: /device:TPU:0 before, /device:TPU:1 now
where the time goes in v2:
time: 67.6 us; the launch traced here: 67 us
  starting transfers between devices  47.4 us (70%)
  waiting for transfers between devices  8.62 us (13%)
  Pallas kernels  7.69 us (11%)
  local copies, waits for them, and re-layouts  3.12 us (5%)
    ppermute x9, starting transfers between devices, to_chips(): lax.ppermute(value, ('gx', 'gy'), [(i * ny + j, target(i, j, k)) for i in...  36 us
    pallas_call x13, Pallas kernels, call(): pl.pallas_call(kernel, out_shape=[jax.ShapeDtypeStruct(shape, F32) if far...  7.69 us
    ppermute x4, starting transfers between devices, to_core(): lax.ppermute(value, 'gx', [(i, i ^ 1) for i in range(nx) if i % 2 in sour...  5.09 us
    ppermute x9, waiting for transfers between devices, to_chips(): lax.ppermute(value, ('gx', 'gy'), [(i * ny + j, target(i, j, k)) for i in...  5.01 us
    ppermute x1, starting transfers between devices, on_device(): below = lax.ppermute(up, 'gy', [(i, i + 1) for i in range(ny - 1)])  5 us
    ppermute x4, waiting for transfers between devices, to_core(): lax.ppermute(value, 'gx', [(i, i ^ 1) for i in range(nx) if i % 2 in sour...  3.6 us
    unnamed x6, local copies, waits for them, and re-layouts  3.12 us
  transfers between devices with their start and end apart: 15, of which 7 were waited for; matrix products, arithmetic and copies ran while one was open for 0% of the time, Pallas kernels for 6%

profile of v2, /device:TPU:1, one launch (start us, length us, event | category | flops | bytes accessed | tf_op | source)
XLA Modules:
  0.0 67.0 jit_solution(18205179570389107851)
XLA Ops:
  0.0 1.0 %copy-done = f32[16,64,128]{2,1,0:T(8,128)S(1)} copy-done((f32[16,64,128]{2,1,0:T(8,128)S(1)}, f32[16,64,128]{2,1,0:T(8,128)}, u32[]{:S(2)}) %copy-start) | copy-done | bytes 524312
  1.0 1.0 %copy-done.1 = f32[16,64,128]{2,1,0:T(8,128)S(1)} copy-done((f32[16,64,128]{2,1,0:T(8,128)S(1)}, f32[16,64,128]{2,1,0:T(8,128)}, u32[]{:S(2)}) %copy-start.1) | copy-done | bytes 524312
  2.1 1.0 %copy-done.2 = f32[16,64,128]{2,1,0:T(8,128)S(1)} copy-done((f32[16,64,128]{2,1,0:T(8,128)S(1)}, f32[16,64,128]{2,1,0:T(8,128)}, u32[]{:S(2)}) %copy-start.2) | copy-done | bytes 524312
  3.7 1.3 %collective-permute-start = (f32[2,8,128]{2,1,0:T(8,128)S(1)}, f32[2,8,128]{2,1,0:T(8,128)S(1)}, u32[]{:S(2)}, u32[]{:S(2)}) collective-permute-start(f32[2,8,128]{2,1,0:T(8,128)S(1)} %get-tuple-element.34.down), channel_id=1, source_target_pairs={{1,0},{2,1},{3,2},{4,3},{5,4},{6,5},{7,6},{8,7},{9,8},{10,9},{11,1... | collective-permute-start | bytes 24584 | tf_op jit(solution)/shard_map/ppermute | solution.py:352
  5.0 5.0 %collective-permute-start.1 = (f32[2,8,128]{2,1,0:T(8,128)S(1)}, f32[2,8,128]{2,1,0:T(8,128)S(1)}, u32[]{:S(2)}, u32[]{:S(2)}) collective-permute-start(f32[2,8,128]{2,1,0:T(8,128)S(1)} %get-tuple-element.35.up), channel_id=1, source_target_pairs={{0,1},{1,2},{2,3},{3,4},{4,5},{5,6},{6,7},{7,8},{8,9},{9,10},{10,1... | collective-permute-start | bytes 24584 | tf_op jit(solution)/shard_map/ppermute | solution.py:351
  10.0 1.1 %shard_map.38 = (f32[64,16,128]{2,1,0:T(8,128)S(1)}, f32[64,16,128]{2,1,0:T(8,128)S(1)}, f32[64,16,128]{2,1,0:T(8,128)S(1)}, f32[64,16,128]{2,1,0:T(8,128)S(1)},...) custom-call(f32[1024,128]{1,0:T(8,128)S(1)} %get-tuple-element.36.st, f32[1024,128]{1,0:T(8,128)S(1)} %get-tuple-element.37.kx, ...), custom_call_target="tpu_custom_call" | custom-call | flops 5000000 | bytes 5000000 | tf_op jit(solution)/shard_map/pallas_call | solution.py:303
  12.1 1.2 %collective-permute-start.2 = (f32[7,16,128]{2,1,0:T(8,128)S(1)}, f32[7,16,128]{2,1,0:T(8,128)S(1)}, u32[]{:S(2)}, u32[]{:S(2)}) collective-permute-start(f32[7,16,128]{2,1,0:T(8,128)S(1)} %get-tuple-element.43.own), channel_id=1, source_target_pairs={{0,16},{16,0},{32,48},{48,32},{64,80},{80,64},{96,112},{112,96},{1... | collective-permute-start | bytes 172040 | tf_op jit(solution)/shard_map/ppermute | solution.py:333
  14.2 3.2 %collective-permute-start.3 = (f32[7,16,128]{2,1,0:T(8,128)S(1)}, f32[7,16,128]{2,1,0:T(8,128)S(1)}, u32[]{:S(2)}, u32[]{:S(2)}) collective-permute-start(f32[7,16,128]{2,1,0:T(8,128)S(1)} %get-tuple-element.44.own), channel_id=1, source_target_pairs={{16,48},{17,49},{18,50},{19,51},{20,52},{21,53},{22,54},{23,55},{2... | collective-permute-start | bytes 172040 | tf_op jit(solution)/shard_map/ppermute | solution.py:337
  17.4 4.4 %collective-permute-start.4 = (f32[7,16,128]{2,1,0:T(8,128)S(1)}, f32[7,16,128]{2,1,0:T(8,128)S(1)}, u32[]{:S(2)}, u32[]{:S(2)}) collective-permute-start(f32[7,16,128]{2,1,0:T(8,128)S(1)} %get-tuple-element.44.own), channel_id=1, source_target_pairs={{16,80},{17,81},{18,82},{19,83},{20,84},{21,85},{22,86},{23,87},{2... | collective-permute-start | bytes 172040 | tf_op jit(solution)/shard_map/ppermute | solution.py:337
  21.8 3.1 %collective-permute-start.5 = (f32[7,16,128]{2,1,0:T(8,128)S(1)}, f32[7,16,128]{2,1,0:T(8,128)S(1)}, u32[]{:S(2)}, u32[]{:S(2)}) collective-permute-start(f32[7,16,128]{2,1,0:T(8,128)S(1)} %get-tuple-element.44.own), channel_id=1, source_target_pairs={{16,112},{17,113},{18,114},{19,115},{20,116},{21,117},{22,118},{23... | collective-permute-start | bytes 172040 | tf_op jit(solution)/shard_map/ppermute | solution.py:337
  24.9 1.8 %shard_map.41 = (f32[128,8,128]{2,1,0:T(8,128)S(1)}, f32[128,8,128]{2,1,0:T(8,128)S(1)}, f32[128,8,128]{2,1,0:T(8,128)S(1)}, f32[128,8,128]{2,1,0:T(8,128)S(1)}, f32[5,8,128]{2,1,0:T(8,128)S(1)}) custom-call(f32[1024,128]{1,0:T(8,128)S(1)} %get-tuple-element.46.ky_t, f32[3,16,128]{2,1,0:T(8,128)S(1)} %get-tuple-element.45.after.coefs), custom_call_target="tpu_custom_call" | custom-call | flops 5000000 | bytes 5000000 | tf_op jit(solution)/shard_map/pallas_call | solution.py:303
  26.8 1.3 %collective-permute-start.6 = (f32[2,16,128]{2,1,0:T(8,128)S(1)}, f32[2,16,128]{2,1,0:T(8,128)S(1)}, u32[]{:S(2)}, u32[]{:S(2)}) collective-permute-start(f32[2,16,128]{2,1,0:T(8,128)S(1)} %get-tuple-element.48), channel_id=1, source_target_pairs={{16,0},{48,32},{80,64},{112,96},{17,1},{49,33},{81,65},{113,97},{1... | collective-permute-start | bytes 49160 | tf_op jit(solution)/shard_map/ppermute | solution.py:333
  29.6 1.3 %collective-permute-start.7 = (f32[7,8,128]{2,1,0:T(8,128)S(1)}, f32[7,8,128]{2,1,0:T(8,128)S(1)}, u32[]{:S(2)}, u32[]{:S(2)}) collective-permute-start(f32[7,8,128]{2,1,0:T(8,128)S(1)} %get-tuple-element.55.own), channel_id=1, source_target_pairs={{0,16},{32,48},{64,80},{96,112},{1,17},{33,49},{65,81},{97,113},{2... | collective-permute-start | bytes 86024 | tf_op jit(solution)/shard_map/ppermute | solution.py:333
  30.9 1.8 %collective-permute-done.7.other = f32[7,8,128]{2,1,0:T(8,128)S(1)} collective-permute-done((f32[7,8,128]{2,1,0:T(8,128)S(1)}, f32[7,8,128]{2,1,0:T(8,128)S(1)}, u32[]{:S(2)}, u32[]{:S(2)}) %collective-permute-start.7) | collective-permute-done | bytes 28704 | tf_op jit(solution)/shard_map/ppermute | solution.py:333
  32.7 7.8 %collective-permute-start.10 = (f32[7,16,128]{2,1,0:T(8,128)S(1)}, f32[7,16,128]{2,1,0:T(8,128)S(1)}, u32[]{:S(2)}, u32[]{:S(2)}) collective-permute-start(f32[7,16,128]{2,1,0:T(8,128)S(1)} %shard_map.45.after.own), channel_id=1, source_target_pairs={{16,19},{17,16},{18,17},{19,18},{20,23},{21,20},{22,21},{23,22},{2... | collective-permute-start | bytes 172040 | tf_op jit(solution)/shard_map/ppermute | solution.py:337
  40.4 1.9 %collective-permute-start.8 = (f32[7,16,128]{2,1,0:T(8,128)S(1)}, f32[7,16,128]{2,1,0:T(8,128)S(1)}, u32[]{:S(2)}, u32[]{:S(2)}) collective-permute-start(f32[7,16,128]{2,1,0:T(8,128)S(1)} %shard_map.45.after.own), channel_id=1, source_target_pairs={{16,17},{17,18},{18,19},{19,16},{20,21},{21,22},{22,23},{23,20},{2... | collective-permute-start | bytes 172040 | tf_op jit(solution)/shard_map/ppermute | solution.py:337
  42.4 3.1 %collective-permute-start.9 = (f32[7,16,128]{2,1,0:T(8,128)S(1)}, f32[7,16,128]{2,1,0:T(8,128)S(1)}, u32[]{:S(2)}, u32[]{:S(2)}) collective-permute-start(f32[7,16,128]{2,1,0:T(8,128)S(1)} %shard_map.45.after.own), channel_id=1, source_target_pairs={{16,18},{17,19},{18,16},{19,17},{20,22},{21,23},{22,20},{23,21},{2... | collective-permute-start | bytes 172040 | tf_op jit(solution)/shard_map/ppermute | solution.py:337
  46.6 2.2 %collective-permute-done.9.other2 = f32[7,16,128]{2,1,0:T(8,128)S(1)} collective-permute-done((f32[7,16,128]{2,1,0:T(8,128)S(1)}, f32[7,16,128]{2,1,0:T(8,128)S(1)}, u32[]{:S(2)}, u32[]{:S(2)}) %collective-permute-start.9) | collective-permute-done | bytes 57376 | tf_op jit(solution)/shard_map/ppermute | solution.py:337
  48.9 5.1 %collective-permute-start.11 = (f32[7,16,128]{2,1,0:T(8,128)S(1)}, f32[7,16,128]{2,1,0:T(8,128)S(1)}, u32[]{:S(2)}, u32[]{:S(2)}) collective-permute-start(f32[7,16,128]{2,1,0:T(8,128)S(1)} %get-tuple-element.59.own), channel_id=1, source_target_pairs={{16,20},{17,21},{18,22},{19,23},{20,24},{21,25},{22,26},{23,27},{2... | collective-permute-start | bytes 172040 | tf_op jit(solution)/shard_map/ppermute | solution.py:337
  54.0 4.8 %collective-permute-start.12 = (f32[7,16,128]{2,1,0:T(8,128)S(1)}, f32[7,16,128]{2,1,0:T(8,128)S(1)}, u32[]{:S(2)}, u32[]{:S(2)}) collective-permute-start(f32[7,16,128]{2,1,0:T(8,128)S(1)} %get-tuple-element.59.own), channel_id=1, source_target_pairs={{16,24},{17,25},{18,26},{19,27},{20,28},{21,29},{22,30},{23,31},{2... | collective-permute-start | bytes 172040 | tf_op jit(solution)/shard_map/ppermute | solution.py:337
  58.8 2.7 %collective-permute-start.13 = (f32[7,16,128]{2,1,0:T(8,128)S(1)}, f32[7,16,128]{2,1,0:T(8,128)S(1)}, u32[]{:S(2)}, u32[]{:S(2)}) collective-permute-start(f32[7,16,128]{2,1,0:T(8,128)S(1)} %get-tuple-element.59.own), channel_id=1, source_target_pairs={{16,28},{17,29},{18,30},{19,31},{20,16},{21,17},{22,18},{23,19},{2... | collective-permute-start | bytes 172040 | tf_op jit(solution)/shard_map/ppermute | solution.py:337
  61.5 2.2 %collective-permute-done.13.other3 = f32[7,16,128]{2,1,0:T(8,128)S(1)} collective-permute-done((f32[7,16,128]{2,1,0:T(8,128)S(1)}, f32[7,16,128]{2,1,0:T(8,128)S(1)}, u32[]{:S(2)}, u32[]{:S(2)}) %collective-permute-start.13) | collective-permute-done | bytes 57376 | tf_op jit(solution)/shard_map/ppermute | solution.py:337
  63.9 1.3 %collective-permute-start.14 = (f32[2,8,128]{2,1,0:T(8,128)S(1)}, f32[2,8,128]{2,1,0:T(8,128)S(1)}, u32[]{:S(2)}, u32[]{:S(2)}) collective-permute-start(f32[2,8,128]{2,1,0:T(8,128)S(1)} %get-tuple-element.61), channel_id=1, source_target_pairs={{16,0},{48,32},{80,64},{112,96},{17,1},{49,33},{81,65},{113,97},{1... | collective-permute-start | bytes 24584 | tf_op jit(solution)/shard_map/ppermute | solution.py:333
  66.0 1.1 %shard_map.49 = f32[1024,128]{1,0:T(8,128)} custom-call(f32[2,8,128]{2,1,0:T(8,128)S(1)} %collective-permute-done.14.came, f32[2,8,128]{2,1,0:T(8,128)S(1)} %get-tuple-element.62.held, f32[128,8,128]{2,1,0:T(8,128)S(1)} %shard_map.46.after.g_t, f32[128,8,128]{2,1,0:T(8,128)S(1)} %get-tuple-element.53.yf, f32[128,8,128]{2,1,0:T(8,128)S(1)} %get-tuple-element.54.yl, ...), custom_call_target="tpu_custom_call" | custom-call | flops 100000 | bytes 100000 | tf_op jit(solution)/shard_map/pallas_call | solution.py:303
  (25 shorter events, 6.1 us)
Async XLA Ops:
  0.0 1.0 %copy-start = (f32[16,64,128]{2,1,0:T(8,128)S(1)}, f32[16,64,128]{2,1,0:T(8,128)}, u32[]{:S(2)}) copy-start(f32[16,64,128]{2,1,0:T(8,128)} %param.3) | copy-start | bytes 1572868
  1.0 1.0 %copy-start.1 = (f32[16,64,128]{2,1,0:T(8,128)S(1)}, f32[16,64,128]{2,1,0:T(8,128)}, u32[]{:S(2)}) copy-start(f32[16,64,128]{2,1,0:T(8,128)} %param.4) | copy-start | bytes 1572868
  2.1 1.0 %copy-start.2 = (f32[16,64,128]{2,1,0:T(8,128)S(1)}, f32[16,64,128]{2,1,0:T(8,128)}, u32[]{:S(2)}) copy-start(f32[16,64,128]{2,1,0:T(8,128)} %param.5) | copy-start | bytes 1572868
  3.7 7.5 %collective-permute-start = (f32[2,8,128]{2,1,0:T(8,128)S(1)}, f32[2,8,128]{2,1,0:T(8,128)S(1)}, u32[]{:S(2)}, u32[]{:S(2)}) collective-permute-start(f32[2,8,128]{2,1,0:T(8,128)S(1)} %get-tuple-element.34.down), channel_id=1, source_target_pairs={{1,0},{2,1},{3,2},{4,3},{5,4},{6,5},{7,6},{8,7},{9,8},{10,9},{11,1... | collective-permute-start | bytes 24584 | tf_op jit(solution)/shard_map/ppermute | solution.py:352
  5.0 6.2 %collective-permute-start.1 = (f32[2,8,128]{2,1,0:T(8,128)S(1)}, f32[2,8,128]{2,1,0:T(8,128)S(1)}, u32[]{:S(2)}, u32[]{:S(2)}) collective-permute-start(f32[2,8,128]{2,1,0:T(8,128)S(1)} %get-tuple-element.35.up), channel_id=1, source_target_pairs={{0,1},{1,2},{2,3},{3,4},{4,5},{5,6},{6,7},{7,8},{8,9},{9,10},{10,1... | collective-permute-start | bytes 24584 | tf_op jit(solution)/shard_map/ppermute | solution.py:351
  12.1 2.1 %collective-permute-start.2 = (f32[7,16,128]{2,1,0:T(8,128)S(1)}, f32[7,16,128]{2,1,0:T(8,128)S(1)}, u32[]{:S(2)}, u32[]{:S(2)}) collective-permute-start(f32[7,16,128]{2,1,0:T(8,128)S(1)} %get-tuple-element.43.own), channel_id=1, source_target_pairs={{0,16},{16,0},{32,48},{48,32},{64,80},{80,64},{96,112},{112,96},{1... | collective-permute-start | bytes 172040 | tf_op jit(solution)/shard_map/ppermute | solution.py:333
  14.2 12.5 %collective-permute-start.3 = (f32[7,16,128]{2,1,0:T(8,128)S(1)}, f32[7,16,128]{2,1,0:T(8,128)S(1)}, u32[]{:S(2)}, u32[]{:S(2)}) collective-permute-start(f32[7,16,128]{2,1,0:T(8,128)S(1)} %get-tuple-element.44.own), channel_id=1, source_target_pairs={{16,48},{17,49},{18,50},{19,51},{20,52},{21,53},{22,54},{23,55},{2... | collective-permute-start | bytes 172040 | tf_op jit(solution)/shard_map/ppermute | solution.py:337
  17.4 9.3 %collective-permute-start.4 = (f32[7,16,128]{2,1,0:T(8,128)S(1)}, f32[7,16,128]{2,1,0:T(8,128)S(1)}, u32[]{:S(2)}, u32[]{:S(2)}) collective-permute-start(f32[7,16,128]{2,1,0:T(8,128)S(1)} %get-tuple-element.44.own), channel_id=1, source_target_pairs={{16,80},{17,81},{18,82},{19,83},{20,84},{21,85},{22,86},{23,87},{2... | collective-permute-start | bytes 172040 | tf_op jit(solution)/shard_map/ppermute | solution.py:337
  21.8 4.9 %collective-permute-start.5 = (f32[7,16,128]{2,1,0:T(8,128)S(1)}, f32[7,16,128]{2,1,0:T(8,128)S(1)}, u32[]{:S(2)}, u32[]{:S(2)}) collective-permute-start(f32[7,16,128]{2,1,0:T(8,128)S(1)} %get-tuple-element.44.own), channel_id=1, source_target_pairs={{16,112},{17,113},{18,114},{19,115},{20,116},{21,117},{22,118},{23... | collective-permute-start | bytes 172040 | tf_op jit(solution)/shard_map/ppermute | solution.py:337
  26.8 2.1 %collective-permute-start.6 = (f32[2,16,128]{2,1,0:T(8,128)S(1)}, f32[2,16,128]{2,1,0:T(8,128)S(1)}, u32[]{:S(2)}, u32[]{:S(2)}) collective-permute-start(f32[2,16,128]{2,1,0:T(8,128)S(1)} %get-tuple-element.48), channel_id=1, source_target_pairs={{16,0},{48,32},{80,64},{112,96},{17,1},{49,33},{81,65},{113,97},{1... | collective-permute-start | bytes 49160 | tf_op jit(solution)/shard_map/ppermute | solution.py:333
  29.6 3.1 %collective-permute-start.7 = (f32[7,8,128]{2,1,0:T(8,128)S(1)}, f32[7,8,128]{2,1,0:T(8,128)S(1)}, u32[]{:S(2)}, u32[]{:S(2)}) collective-permute-start(f32[7,8,128]{2,1,0:T(8,128)S(1)} %get-tuple-element.55.own), channel_id=1, source_target_pairs={{0,16},{32,48},{64,80},{96,112},{1,17},{33,49},{65,81},{97,113},{2... | collective-permute-start | bytes 86024 | tf_op jit(solution)/shard_map/ppermute | solution.py:333
  32.7 13.3 %collective-permute-start.10 = (f32[7,16,128]{2,1,0:T(8,128)S(1)}, f32[7,16,128]{2,1,0:T(8,128)S(1)}, u32[]{:S(2)}, u32[]{:S(2)}) collective-permute-start(f32[7,16,128]{2,1,0:T(8,128)S(1)} %shard_map.45.after.own), channel_id=1, source_target_pairs={{16,19},{17,16},{18,17},{19,18},{20,23},{21,20},{22,21},{23,22},{2... | collective-permute-start | bytes 172040 | tf_op jit(solution)/shard_map/ppermute | solution.py:337
  40.4 6.1 %collective-permute-start.8 = (f32[7,16,128]{2,1,0:T(8,128)S(1)}, f32[7,16,128]{2,1,0:T(8,128)S(1)}, u32[]{:S(2)}, u32[]{:S(2)}) collective-permute-start(f32[7,16,128]{2,1,0:T(8,128)S(1)} %shard_map.45.after.own), channel_id=1, source_target_pairs={{16,17},{17,18},{18,19},{19,16},{20,21},{21,22},{22,23},{23,20},{2... | collective-permute-start | bytes 172040 | tf_op jit(solution)/shard_map/ppermute | solution.py:337
  42.4 6.4 %collective-permute-start.9 = (f32[7,16,128]{2,1,0:T(8,128)S(1)}, f32[7,16,128]{2,1,0:T(8,128)S(1)}, u32[]{:S(2)}, u32[]{:S(2)}) collective-permute-start(f32[7,16,128]{2,1,0:T(8,128)S(1)} %shard_map.45.after.own), channel_id=1, source_target_pairs={{16,18},{17,19},{18,16},{19,17},{20,22},{21,23},{22,20},{23,21},{2... | collective-permute-start | bytes 172040 | tf_op jit(solution)/shard_map/ppermute | solution.py:337
  48.9 12.6 %collective-permute-start.11 = (f32[7,16,128]{2,1,0:T(8,128)S(1)}, f32[7,16,128]{2,1,0:T(8,128)S(1)}, u32[]{:S(2)}, u32[]{:S(2)}) collective-permute-start(f32[7,16,128]{2,1,0:T(8,128)S(1)} %get-tuple-element.59.own), channel_id=1, source_target_pairs={{16,20},{17,21},{18,22},{19,23},{20,24},{21,25},{22,26},{23,27},{2... | collective-permute-start | bytes 172040 | tf_op jit(solution)/shard_map/ppermute | solution.py:337
  54.0 7.5 %collective-permute-start.12 = (f32[7,16,128]{2,1,0:T(8,128)S(1)}, f32[7,16,128]{2,1,0:T(8,128)S(1)}, u32[]{:S(2)}, u32[]{:S(2)}) collective-permute-start(f32[7,16,128]{2,1,0:T(8,128)S(1)} %get-tuple-element.59.own), channel_id=1, source_target_pairs={{16,24},{17,25},{18,26},{19,27},{20,28},{21,29},{22,30},{23,31},{2... | collective-permute-start | bytes 172040 | tf_op jit(solution)/shard_map/ppermute | solution.py:337
  58.8 4.9 %collective-permute-start.13 = (f32[7,16,128]{2,1,0:T(8,128)S(1)}, f32[7,16,128]{2,1,0:T(8,128)S(1)}, u32[]{:S(2)}, u32[]{:S(2)}) collective-permute-start(f32[7,16,128]{2,1,0:T(8,128)S(1)} %get-tuple-element.59.own), channel_id=1, source_target_pairs={{16,28},{17,29},{18,30},{19,31},{20,16},{21,17},{22,18},{23,19},{2... | collective-permute-start | bytes 172040 | tf_op jit(solution)/shard_map/ppermute | solution.py:337
  63.9 2.1 %collective-permute-start.14 = (f32[2,8,128]{2,1,0:T(8,128)S(1)}, f32[2,8,128]{2,1,0:T(8,128)S(1)}, u32[]{:S(2)}, u32[]{:S(2)}) collective-permute-start(f32[2,8,128]{2,1,0:T(8,128)S(1)} %get-tuple-element.61), channel_id=1, source_target_pairs={{16,0},{48,32},{80,64},{112,96},{17,1},{49,33},{81,65},{113,97},{1... | collective-permute-start | bytes 24584 | tf_op jit(solution)/shard_map/ppermute | solution.py:333

commit v3 on v2

v3 whole, which is shorter than its diff:
```python
import jax
import jax.numpy as jnp
from jax import lax
from jax.experimental import pallas as pl
from jax.experimental.pallas import tpu as pltpu
from jax.sharding import PartitionSpec as P

F32 = jnp.float32
NZ, BX, BY = 16, 64, 128
ROWS = NZ * BX
GROUPS = ROWS // 128
LIMIT = 40 * 1024 * 1024


def inverse(x):
    guess = pl.reciprocal(x, approx=True)
    return guess * (2.0 - x * guess)


def x_row(ref, i):
    return jnp.concatenate(
        [ref[pl.ds(i, 8, stride=BX), :], ref[pl.ds(8 * BX + i, 8, stride=BX), :]], axis=0
    )


def y_row(ref, j):
    return ref[pl.ds(j * GROUPS, GROUPS), :]


def place_rows(ref, i, value):
    ref[pl.ds(i, 8, stride=BX), :] = value[:8]
    ref[pl.ds(8 * BX + i, 8, stride=BX), :] = value[8:]


def interface(blocks, ends, slots, me):
    count = blocks.shape[0]
    zero = jnp.zeros_like(ends[0, 0])
    gammas, rhos = [], []
    gamma, rho = zero, zero
    for i in range(count + 1):
        below = [blocks[i - 1, n] for n in range(5)] if i else [zero] * 5
        above = [blocks[i, n] for n in range(5)] if i < count else [zero] * 5
        gain = (ends[i - 1, 1] if i else zero) - (ends[i, 0] if i < count else zero)
        inv = inverse(2.0 * inverse(below[4] + above[3]) + below[2] + above[0] - below[1] * gamma)
        rho = (gain + below[1] * rho) * inv
        gamma = above[1] * inv
        gammas.append(gamma)
        rhos.append(rho)
    flow = rhos[count]
    slots[count] = flow
    for i in range(count - 1, -1, -1):
        flow = rhos[i] + gammas[i] * flow
        slots[i] = flow
    return slots[me], slots[me + 1]


def sweep(count, row, f, u, first, last, m):
    ahead = jnp.ones_like(row(0))
    back = jnp.ones_like(ahead)
    low, high = row(0), row(count - 1)
    m[3] = low
    m[4] = high
    for i in range(count - 1):
        nxt = row(i + 1)
        r = 0.5 * (low + nxt)
        low = nxt
        inv = inverse(r + ahead)
        ratio = r * inv
        ahead = 1.0 + ratio * ahead
        u[i] = inv
        f[i] = ratio
        j = count - 1 - i
        prev = row(j - 1)
        r = 0.5 * (high + prev)
        high = prev
        ratio = r * inverse(r + back)
        back = 1.0 + ratio * back
        first[j] = ratio
    start = inverse(back)
    end = inverse(ahead)
    m[0] = start
    m[2] = end
    first[0] = start
    last[count - 1] = end
    u[count - 1] = end
    f[count - 1] = jnp.zeros_like(end)
    for i in range(1, count):
        start = start * first[i]
        first[i] = start
        j = count - 1 - i
        end = end * f[j]
        last[j] = end
    m[1] = end


def x_matrix_kernel(
    st_hbm, kx_hbm, ky_hbm, st, ky_t, up, down, fx, ux, wf, wl, mx, source, kx, ky, sems
):
    moves = [
        pltpu.make_async_copy(src, dst, sems.at[n])
        for n, (src, dst) in enumerate(((kx_hbm, kx), (ky_hbm, ky), (st_hbm, st)))
    ]
    for move in moves:
        move.start()
    moves[0].wait()
    sweep(BX, lambda i: x_row(kx, i), fx, ux, wf, wl, mx)
    moves[1].wait()
    for g in range(GROUPS):
        ky_t[pl.ds(g, BY, stride=GROUPS), :] = ky[pl.ds(g * 128, 128), :].T
    moves[2].wait()
    for g in range(GROUPS):
        turned = st[pl.ds(g * 128, 128), :].T
        down[0, pl.ds(g, 1), :] = turned[0:1, :]
        up[0, pl.ds(g, 1), :] = turned[127:128, :]
    down[1] = ky_t[pl.ds(0, GROUPS), :]
    up[1] = ky_t[pl.ds((BY - 1) * GROUPS, GROUPS), :]
    lane = lax.broadcasted_iota(jnp.int32, (128, 128), 1)
    for g in range(GROUPS):
        rows = pl.ds(g * 128, 128)
        s = st[rows, :]
        k = ky[rows, :]
        flux = 0.5 * (k + pltpu.roll(k, 127, 1)) * (pltpu.roll(s, 127, 1) - s)
        flux = jnp.where(lane == 127, 0.0, flux)
        source[rows, :] = s + flux - pltpu.roll(flux, 1, 1)


def y_matrix_kernel(ky_t, fy, uy, yf, yl, my):
    sweep(BY, lambda j: y_row(ky_t, j), fy, uy, yf, yl, my)


def x_ends_kernel(above, below, up, down, source, wf, wl, s_out, send):
    flux_l = 0.5 * (below[1] + down[1]) * (down[0] - below[0])
    flux_r = 0.5 * (above[1] + up[1]) * (above[0] - up[0])
    both = jnp.concatenate([flux_l, flux_r], axis=0)
    turned = jnp.concatenate([both] * 8, axis=0).T
    lane = lax.broadcasted_iota(jnp.int32, (128, 128), 1)
    for g in range(GROUPS):
        rows = pl.ds(g * 128, 128)
        left = jnp.broadcast_to(turned[:, g : g + 1], (128, 128))
        right = jnp.broadcast_to(turned[:, 8 + g : 9 + g], (128, 128))
        extra = jnp.where(lane == 0, -left, jnp.where(lane == 127, right, 0.0))
        s_out[rows, :] = source[rows, :] + extra
    firsts = [jnp.zeros((NZ, BY), F32) for _ in range(2)]
    lasts = [jnp.zeros((NZ, BY), F32) for _ in range(2)]
    for i in range(BX):
        s = x_row(s_out, i)
        firsts[i % 2] = firsts[i % 2] + wf[i] * s
        lasts[i % 2] = lasts[i % 2] + wl[i] * s
    first, last = firsts[0] + firsts[1], lasts[0] + lasts[1]
    for p in range(send.shape[0]):
        send[p, 0] = first
        send[p, 1] = last


def x_local_kernel(s_in, st, fx, ux, d):
    total = x_row(s_in, 0)
    d[0] = total
    for i in range(1, BX):
        total = x_row(s_in, i) + fx[i - 1] * total
        d[i] = total
    x = jnp.zeros_like(total)
    for i in range(BX - 1, -1, -1):
        x = ux[i] * d[i] + fx[i] * x
        d[i] = x - x_row(st, i)


def y_ends_kernel(blocks, ends, d, wf, wl, yf, yl, v_t, send, slots, v):
    enter, leave = interface(blocks, ends, slots, lax.axis_index("gx"))
    for i in range(BX):
        place_rows(v, i, d[i] + wf[i] * enter - wl[i] * leave)
    for g in range(GROUPS):
        v_t[pl.ds(g, BY, stride=GROUPS), :] = v[pl.ds(g * 128, 128), :].T
    firsts = [jnp.zeros((GROUPS, 128), F32) for _ in range(4)]
    lasts = [jnp.zeros((GROUPS, 128), F32) for _ in range(4)]
    for j in range(BY):
        row = y_row(v_t, j)
        firsts[j % 4] = firsts[j % 4] + yf[j] * row
        lasts[j % 4] = lasts[j % 4] + yl[j] * row
    first = (firsts[0] + firsts[1]) + (firsts[2] + firsts[3])
    last = (lasts[0] + lasts[1]) + (lasts[2] + lasts[3])
    for p in range(send.shape[0]):
        send[p, 0] = first
        send[p, 1] = last


def y_local_kernel(v_t, fy, uy, g_t):
    total = y_row(v_t, 0)
    g_t[0] = total
    for j in range(1, BY):
        total = y_row(v_t, j) + fy[j - 1] * total
        g_t[j] = total
    x = jnp.zeros_like(total)
    for j in range(BY - 1, -1, -1):
        x = uy[j] * g_t[j] + fy[j] * x
        g_t[j] = x


def y_solve_kernel(blocks, ends, g_t, yf, yl, st, out_hbm, slots, work, out, sems):
    enter, leave = interface(blocks, ends, slots, lax.axis_index("gy"))
    for j in range(BY):
        work[pl.ds(j * GROUPS, GROUPS), :] = 2.0 * (g_t[j] + yf[j] * enter - yl[j] * leave)
    moves = []
    for g in range(GROUPS):
        rows = pl.ds(g * 128, 128)
        out[rows, :] = st[rows, :] + work[pl.ds(g, BY, stride=GROUPS), :].T
        move = pltpu.make_async_copy(out.at[rows], out_hbm.at[rows], sems.at[g])
        move.start()
        moves.append(move)
    for move in moves:
        move.wait()


def call(kernel, outs, args, scratch=(), cost=100_000, limit=LIMIT):
    vm = pl.BlockSpec(memory_space=pltpu.VMEM)
    hbm = pl.BlockSpec(memory_space=pltpu.HBM)
    return pl.pallas_call(
        kernel,
        out_shape=[
            jax.ShapeDtypeStruct(shape, F32) if far else pltpu.VMEM(shape, F32)
            for shape, far in outs
        ],
        in_specs=[hbm if far else vm for _, far in args],
        out_specs=[hbm if far else vm for _, far in outs],
        scratch_shapes=list(scratch),
        compiler_params=pltpu.CompilerParams(vmem_limit_bytes=limit),
        cost_estimate=pl.CostEstimate(flops=cost, bytes_accessed=cost, transcendentals=0),
    )(*[value for value, _ in args])


def near(*values):
    return [(value, False) for value in values]


def on_device(state, kappa_x, kappa_y):
    flat = [a.reshape(ROWS, BY) for a in (state, kappa_x, kappa_y)]
    plane = (ROWS, BY)
    xs = (BX, NZ, BY)
    ys = (BY, GROUPS, 128)
    edge = (2, GROUPS, 128)
    nx, ny = lax.axis_size("gx"), lax.axis_size("gy")
    st, ky_t, up, down, fx, ux, wf, wl, mx, source = call(
        x_matrix_kernel,
        near(plane, plane, edge, edge, xs, xs, xs, xs, (5, NZ, BY), plane),
        [(a, True) for a in flat],
        [pltpu.VMEM(plane, F32), pltpu.VMEM(plane, F32), pltpu.SemaphoreType.DMA((3,))],
        limit=54 * 1024 * 1024,
    )
    x_blocks = lax.all_gather(mx, "gx")
    below = lax.ppermute(up, "gy", [(i, i + 1) for i in range(ny - 1)])
    above = lax.ppermute(down, "gy", [(i + 1, i) for i in range(ny - 1)])
    fy, uy, yf, yl, my = call(
        y_matrix_kernel, near(ys, ys, ys, ys, (5, GROUPS, 128)), near(ky_t), cost=5_000_000
    )
    y_blocks = lax.all_gather(my, "gy")
    s, send = call(
        x_ends_kernel,
        near(plane, (nx, 2, NZ, BY)),
        near(above, below, up, down, source, wf, wl),
    )
    x_ends = lax.all_to_all(send, "gx", 0, 0)
    (d,) = call(x_local_kernel, near(xs), near(s, st, fx, ux), cost=3_000_000)
    v_t, send = call(
        y_ends_kernel,
        near(plane, (ny, 2, GROUPS, 128)),
        near(x_blocks, x_ends, d, wf, wl, yf, yl),
        [pltpu.VMEM((nx + 1, NZ, BY), F32), pltpu.VMEM(plane, F32)],
    )
    y_ends = lax.all_to_all(send, "gy", 0, 0)
    (g_t,) = call(y_local_kernel, near(ys), near(v_t, fy, uy), cost=5_000_000)
    (out,) = call(
        y_solve_kernel,
        [(plane, True)],
        near(y_blocks, y_ends, g_t, yf, yl, st),
        [
            pltpu.VMEM((ny + 1, GROUPS, 128), F32),
            pltpu.VMEM(plane, F32),
            pltpu.VMEM(plane, F32),
            pltpu.SemaphoreType.DMA((GROUPS,)),
        ],
    )
    return out.reshape(state.shape)


def solution(mesh):
    spec = P(None, "gx", "gy")
    return jax.shard_map(
        on_device, mesh=mesh, in_specs=(spec, spec, spec), out_specs=spec, check_vma=False
    )
```

time: 67.6 us -> 78 us (1.15)
  the two profiles are of different devices: /device:TPU:1 before, /device:TPU:0 now
where the time goes in v3:
time: 78 us; the launch traced here: 77.4 us
  blocking collectives  38 us (49%)
  starting transfers between devices  20.5 us (26%)
  Pallas kernels  10.5 us (13%)
  local copies, waits for them, and re-layouts  8.26 us (11%)
    all_gather x1, blocking collectives, on_device(): y_blocks = lax.all_gather(my, 'gy')  24.2 us
    all_gather x1, blocking collectives, on_device(): x_blocks = lax.all_gather(mx, 'gx')  13.7 us
    pallas_call x7, Pallas kernels, call(): pl.pallas_call(kernel, out_shape=[jax.ShapeDtypeStruct(shape, F32) if far...  10.5 us
    all_to_all x1, starting transfers between devices, on_device(): y_ends = lax.all_to_all(send, 'gy', 0, 0)  10.3 us
    unnamed x26, local copies, waits for them, and re-layouts  8.26 us
    ppermute x1, starting transfers between devices, on_device(): below = lax.ppermute(up, 'gy', [(i, i + 1) for i in range(ny - 1)])  4.55 us
    all_to_all x1, starting transfers between devices, on_device(): x_ends = lax.all_to_all(send, 'gx', 0, 0)  4.38 us
  transfers between devices with their start and end apart: 4, of which 0 were waited for; matrix products, arithmetic and copies ran while one was open for 0% of the time, Pallas kernels for 4%

profile of v3, /device:TPU:0, one launch (start us, length us, event | category | flops | bytes accessed | tf_op | source)
XLA Modules:
  0.0 77.4 jit_solution(5928385205116461424)
XLA Ops:
  0.0 3.2 %shard_map.37 = (f32[1024,128]{1,0:T(8,128)S(1)}, f32[1024,128]{1,0:T(8,128)S(1)}, f32[2,8,128]{2,1,0:T(8,128)S(1)}, f32[2,8,128]{2,1,0:T(8,128)S(1)}, f32[64,16...) custom-call(f32[1024,128]{1,0:T(8,128)} %bitcast.8, ...), custom_call_target="tpu_custom_call" | custom-call | flops 100000 | bytes 100000 | tf_op jit(solution)/shard_map/pallas_call | solution.py:216
  3.2 1.3 %collective-permute-start = (f32[2,8,128]{2,1,0:T(8,128)S(1)}, f32[2,8,128]{2,1,0:T(8,128)S(1)}, u32[]{:S(2)}, u32[]{:S(2)}) collective-permute-start(f32[2,8,128]{2,1,0:T(8,128)S(1)} %get-tuple-element.27.down), channel_id=1, source_target_pairs={{1,0},{2,1},{3,2},{4,3},{5,4},{6,5},{7,6},{8,7},{9,8},{10,9},{11,1... | collective-permute-start | bytes 24584 | tf_op jit(solution)/shard_map/ppermute | solution.py:250
  4.5 4.5 %collective-permute-start.1 = (f32[2,8,128]{2,1,0:T(8,128)S(1)}, f32[2,8,128]{2,1,0:T(8,128)S(1)}, u32[]{:S(2)}, u32[]{:S(2)}) collective-permute-start(f32[2,8,128]{2,1,0:T(8,128)S(1)} %get-tuple-element.28.up), channel_id=1, source_target_pairs={{0,1},{1,2},{2,3},{3,4},{4,5},{5,6},{6,7},{7,8},{8,9},{9,10},{10,1... | collective-permute-start | bytes 24584 | tf_op jit(solution)/shard_map/ppermute | solution.py:249
  9.1 1.8 %shard_map.38 = (f32[128,8,128]{2,1,0:T(8,128)S(1)}, f32[128,8,128]{2,1,0:T(8,128)S(1)}, f32[128,8,128]{2,1,0:T(8,128)S(1)}, f32[128,8,128]{2,1,0:T(8,128)S(1)}, f32[5,8,128]{2,1,0:T(8,128)S(1)}) custom-call(f32[1024,128]{1,0:T(8,128)S(1)} %get-tuple-element.24.ky_t), custom_call_target="tpu_custom_call" | custom-call | flops 5000000 | bytes 5000000 | tf_op jit(solution)/shard_map/pallas_call | solution.py:216
  10.9 0.8 %copy-done.6 = f32[128,8,128]{2,1,0:T(8,128)} copy-done((f32[128,8,128]{2,1,0:T(8,128)}, f32[128,8,128]{2,1,0:T(8,128)S(1)}, u32[]{:S(2)}) %copy-start.6) | copy-done | bytes 524312
  11.7 0.0 collective-permute-done.above
  11.7 1.4 %shard_map.39 = (f32[1024,128]{1,0:T(8,128)S(1)}, f32[8,2,16,128]{3,2,1,0:T(8,128)}) custom-call(f32[2,8,128]{2,1,0:T(8,128)S(1)} %collective-permute-done.above, f32[2,8,128]{2,1,0:T(8,128)S(1)} %collective-permute-done.1.below, f32[2,8,128]{2,1,0:T(8,128)S(1)} %get-tuple-element.28.up, f32[2,8,128]{2,1,0:T(8,128)S(1)} %get-tuple-element.27.down, ...), custom_call_target="tpu_custom_call" | custom-call | flops 100000 | bytes 100000 | tf_op jit(solution)/shard_map/pallas_call | solution.py:216
  13.2 0.8 %copy-done.4 = f32[1024,128]{1,0:T(8,128)} copy-done((f32[1024,128]{1,0:T(8,128)}, f32[1024,128]{1,0:T(8,128)S(1)}, u32[]{:S(2)}) %copy-start.4) | copy-done | bytes 524312
  13.9 4.4 %all-to-all-start = ((f32[8,2,16,128]{3,2,1,0:T(8,128)}), f32[8,2,16,128]{3,2,1,0:T(8,128)}, u32[]{:S(2)}, u32[]{:S(2)}) async-start(f32[8,2,16,128]{3,2,1,0:T(8,128)} %get-tuple-element.32), calls=%async_computation | async-start | bytes 262144 | tf_op jit(solution)/shard_map/all_to_all | solution.py:260
  18.3 13.7 %all-gather.1 = f32[40,16,128]{2,1,0:T(8,128)S(1)} all-gather(f32[5,16,128]{2,1,0:T(8,128)S(1)} %get-tuple-element.26), channel_id=3, replica_groups=mesh['gx'=8,'gy'=16] {'gx'}, dimensions={0}, use_global_device_ids=true | all-gather | bytes 368640 | tf_op jit(solution)/shard_map/all_gather | solution.py:248
  32.1 1.0 %copy-done.1 = f32[64,16,128]{2,1,0:T(8,128)S(1)} copy-done((f32[64,16,128]{2,1,0:T(8,128)S(1)}, f32[64,16,128]{2,1,0:T(8,128)}, u32[]{:S(2)}) %copy-start.1) | copy-done | bytes 524312
  33.1 1.0 %copy-done.3 = f32[64,16,128]{2,1,0:T(8,128)S(1)} copy-done((f32[64,16,128]{2,1,0:T(8,128)S(1)}, f32[64,16,128]{2,1,0:T(8,128)}, u32[]{:S(2)}) %copy-start.3) | copy-done | bytes 524312
  34.2 1.0 %copy-done.5 = f32[1024,128]{1,0:T(8,128)S(1)} copy-done((f32[1024,128]{1,0:T(8,128)S(1)}, f32[1024,128]{1,0:T(8,128)}, u32[]{:S(2)}) %copy-start.5) | copy-done | bytes 524312
  35.2 0.7 shard_map.40.d
  35.9 1.6 %shard_map.41 = (f32[1024,128]{1,0:T(8,128)S(1)}, f32[16,2,8,128]{3,2,1,0:T(8,128)S(1)}) custom-call(f32[8,5,16,128]{3,2,1,0:T(8,128)S(1)} %bitcast.6, f32[8,2,16,128]{3,2,1,0:T(8,128)} %all-to-all-done.ends, f32[64,16,128]{2,1,0:T(8,128)S(1)} %shard_map.40.d, f32[64,16,128]{2,1,0:T(8,128)S(1)} %get-tuple-element.30.wf, ...), custom_call_target="tpu_custom_call" | custom-call | flops 100000 | bytes 100000 | tf_op jit(solution)/shard_map/pallas_call | solution.py:216
  37.5 0.0 copy-start.10
  37.5 0.8 %copy-done.10 = f32[1024,128]{1,0:T(8,128)} copy-done((f32[1024,128]{1,0:T(8,128)}, f32[1024,128]{1,0:T(8,128)S(1)}, u32[]{:S(2)}) %copy-start.10) | copy-done | bytes 524312
  38.3 0.7 copy-done.12
  38.9 10.3 %all-to-all-start.1 = ((f32[16,2,8,128]{3,2,1,0:T(8,128)}), f32[16,2,8,128]{3,2,1,0:T(8,128)S(1)}, u32[]{:S(2)}, u32[]{:S(2)}) async-start(f32[16,2,8,128]{3,2,1,0:T(8,128)} %copy-done.12), calls=%async_computation.1 | async-start | bytes 262144 | tf_op jit(solution)/shard_map/all_to_all | solution.py:268
  49.2 24.2 %all-gather = f32[80,8,128]{2,1,0:T(8,128)S(1)} all-gather(f32[5,8,128]{2,1,0:T(8,128)S(1)} %get-tuple-element.25), channel_id=2, replica_groups=mesh['gx'=8,'gy'=16] {'gy'}, dimensions={0}, use_global_device_ids=true | all-gather | bytes 348160 | tf_op jit(solution)/shard_map/all_gather | solution.py:254
  73.5 1.0 %copy-done.9 = f32[128,8,128]{2,1,0:T(8,128)S(1)} copy-done((f32[128,8,128]{2,1,0:T(8,128)S(1)}, f32[128,8,128]{2,1,0:T(8,128)}, u32[]{:S(2)}) %copy-start.9) | copy-done | bytes 524312
  74.5 1.0 %copy-done.11 = f32[1024,128]{1,0:T(8,128)S(1)} copy-done((f32[1024,128]{1,0:T(8,128)S(1)}, f32[1024,128]{1,0:T(8,128)}, u32[]{:S(2)}) %copy-start.11) | copy-done | bytes 524312
  75.6 0.5 shard_map.42.g_t
  76.1 1.3 %shard_map.43 = f32[1024,128]{1,0:T(8,128)} custom-call(f32[16,5,8,128]{3,2,1,0:T(8,128)S(1)} %bitcast.7, f32[16,2,8,128]{3,2,1,0:T(8,128)S(1)} %all-to-all-done.1.ends, f32[128,8,128]{2,1,0:T(8,128)S(1)} %shard_map.42.g_t, f32[128,8,128]{2,1,0:T(8,128)S(1)} %get-tuple-element.37.yf, f32[128,8,128]{2,1,0:T(8,128)S(1)} %get-tuple-element.38.yl, ...), custom_call_target="tpu_custom_call" | custom-call | flops 100000 | bytes 100000 | tf_op jit(solution)/shard_map/pallas_call | solution.py:216
  (19 shorter events, 0.0 us)
Async XLA Ops:
  3.2 10.0 %copy-start = (f32[64,16,128]{2,1,0:T(8,128)}, f32[64,16,128]{2,1,0:T(8,128)S(1)}, u32[]{:S(2)}) copy-start(f32[64,16,128]{2,1,0:T(8,128)S(1)} %get-tuple-element.35.fx) | copy-start | bytes 1572868
  3.2 9.9 %copy-start.2 = (f32[64,16,128]{2,1,0:T(8,128)}, f32[64,16,128]{2,1,0:T(8,128)S(1)}, u32[]{:S(2)}) copy-start(f32[64,16,128]{2,1,0:T(8,128)S(1)} %get-tuple-element.36.ux) | copy-start | bytes 1572868
  3.2 8.5 %collective-permute-start = (f32[2,8,128]{2,1,0:T(8,128)S(1)}, f32[2,8,128]{2,1,0:T(8,128)S(1)}, u32[]{:S(2)}, u32[]{:S(2)}) collective-permute-start(f32[2,8,128]{2,1,0:T(8,128)S(1)} %get-tuple-element.27.down), channel_id=1, source_target_pairs={{1,0},{2,1},{3,2},{4,3},{5,4},{6,5},{7,6},{8,7},{9,8},{10,9},{11,1... | collective-permute-start | bytes 24584 | tf_op jit(solution)/shard_map/ppermute | solution.py:250
  4.5 7.2 %collective-permute-start.1 = (f32[2,8,128]{2,1,0:T(8,128)S(1)}, f32[2,8,128]{2,1,0:T(8,128)S(1)}, u32[]{:S(2)}, u32[]{:S(2)}) collective-permute-start(f32[2,8,128]{2,1,0:T(8,128)S(1)} %get-tuple-element.28.up), channel_id=1, source_target_pairs={{0,1},{1,2},{2,3},{3,4},{4,5},{5,6},{6,7},{7,8},{8,9},{9,10},{10,1... | collective-permute-start | bytes 24584 | tf_op jit(solution)/shard_map/ppermute | solution.py:249
  10.9 0.8 %copy-start.6 = (f32[128,8,128]{2,1,0:T(8,128)}, f32[128,8,128]{2,1,0:T(8,128)S(1)}, u32[]{:S(2)}) copy-start(f32[128,8,128]{2,1,0:T(8,128)S(1)} %get-tuple-element.41.fy) | copy-start | bytes 1572868
  11.7 1.5 %copy-start.8 = (f32[128,8,128]{2,1,0:T(8,128)}, f32[128,8,128]{2,1,0:T(8,128)S(1)}, u32[]{:S(2)}) copy-start(f32[128,8,128]{2,1,0:T(8,128)S(1)} %get-tuple-element.42.uy) | copy-start | bytes 1572868
  13.1 0.8 %copy-start.4 = (f32[1024,128]{1,0:T(8,128)}, f32[1024,128]{1,0:T(8,128)S(1)}, u32[]{:S(2)}) copy-start(f32[1024,128]{1,0:T(8,128)S(1)} %get-tuple-element.33.s_in) | copy-start | bytes 1572868
  13.9 21.9 %all-to-all-start = ((f32[8,2,16,128]{3,2,1,0:T(8,128)}), f32[8,2,16,128]{3,2,1,0:T(8,128)}, u32[]{:S(2)}, u32[]{:S(2)}) async-start(f32[8,2,16,128]{3,2,1,0:T(8,128)} %get-tuple-element.32), calls=%async_computation | async-start | bytes 262144 | tf_op jit(solution)/shard_map/all_to_all | solution.py:260
  32.1 1.0 %copy-start.1 = (f32[64,16,128]{2,1,0:T(8,128)S(1)}, f32[64,16,128]{2,1,0:T(8,128)}, u32[]{:S(2)}) copy-start(f32[64,16,128]{2,1,0:T(8,128)} %copy-done) | copy-start | bytes 1572868
  33.1 1.0 %copy-start.3 = (f32[64,16,128]{2,1,0:T(8,128)S(1)}, f32[64,16,128]{2,1,0:T(8,128)}, u32[]{:S(2)}) copy-start(f32[64,16,128]{2,1,0:T(8,128)} %copy-done.2) | copy-start | bytes 1572868
  34.2 1.0 %copy-start.5 = (f32[1024,128]{1,0:T(8,128)S(1)}, f32[1024,128]{1,0:T(8,128)}, u32[]{:S(2)}) copy-start(f32[1024,128]{1,0:T(8,128)} %copy-done.4) | copy-start | bytes 1572868
  37.5 0.8 %copy-start.10 = (f32[1024,128]{1,0:T(8,128)}, f32[1024,128]{1,0:T(8,128)S(1)}, u32[]{:S(2)}) copy-start(f32[1024,128]{1,0:T(8,128)S(1)} %get-tuple-element.40.v_t) | copy-start | bytes 1572868
  38.3 0.7 copy-start.12
  38.9 34.5 %copy-start.7 = (f32[128,8,128]{2,1,0:T(8,128)S(1)}, f32[128,8,128]{2,1,0:T(8,128)}, u32[]{:S(2)}) copy-start(f32[128,8,128]{2,1,0:T(8,128)} %copy-done.6) | copy-start | bytes 1572868
  38.9 37.2 %all-to-all-start.1 = ((f32[16,2,8,128]{3,2,1,0:T(8,128)}), f32[16,2,8,128]{3,2,1,0:T(8,128)S(1)}, u32[]{:S(2)}, u32[]{:S(2)}) async-start(f32[16,2,8,128]{3,2,1,0:T(8,128)} %copy-done.12), calls=%async_computation.1 | async-start | bytes 262144 | tf_op jit(solution)/shard_map/all_to_all | solution.py:268
  73.5 1.0 %copy-start.9 = (f32[128,8,128]{2,1,0:T(8,128)S(1)}, f32[128,8,128]{2,1,0:T(8,128)}, u32[]{:S(2)}) copy-start(f32[128,8,128]{2,1,0:T(8,128)} %copy-done.8) | copy-start | bytes 1572868
  74.5 1.0 %copy-start.11 = (f32[1024,128]{1,0:T(8,128)S(1)}, f32[1024,128]{1,0:T(8,128)}, u32[]{:S(2)}) copy-start(f32[1024,128]{1,0:T(8,128)} %copy-done.10) | copy-start | bytes 1572868

commit v4 on v3

v4 whole, which is shorter than its diff:
```python
import jax
import jax.numpy as jnp
from jax import lax
from jax.experimental import pallas as pl
from jax.experimental.pallas import tpu as pltpu
from jax.sharding import PartitionSpec as P

F32 = jnp.float32
NZ, BX, BY = 16, 64, 128
ROWS = NZ * BX
GROUPS = ROWS // 128
LIMIT = 40 * 1024 * 1024


def inverse(x):
    guess = pl.reciprocal(x, approx=True)
    return guess * (2.0 - x * guess)


def x_row(ref, i):
    return jnp.concatenate(
        [ref[pl.ds(i, 8, stride=BX), :], ref[pl.ds(8 * BX + i, 8, stride=BX), :]], axis=0
    )


def y_row(ref, j):
    return ref[pl.ds(j * GROUPS, GROUPS), :]


def place_rows(ref, i, value):
    ref[pl.ds(i, 8, stride=BX), :] = value[:8]
    ref[pl.ds(8 * BX + i, 8, stride=BX), :] = value[8:]


def merge(low, high):
    inv = inverse(2.0 * inverse(low[4] + high[3]) + low[2] + high[0])
    e = (low[6] - high[5]) * inv
    a = low[1] * inv
    b = high[1] * inv
    joined = [
        low[0] - low[1] * a,
        low[1] * b,
        high[2] - high[1] * b,
        low[3],
        high[4],
        low[5] - low[1] * e,
        high[6] + high[1] * e,
    ]
    return joined, (e, a, b)


def flows_of(count, pivot, lower, upper, gain, slots):
    gamma = rho = None
    gammas, rhos = [], []
    for i in range(count + 1):
        if i == 0:
            inv = inverse(pivot(i))
            rho = gain(i) * inv
        else:
            inv = inverse(pivot(i) - lower(i) * gamma)
            rho = (gain(i) + lower(i) * rho) * inv
        if i < count:
            gamma = upper(i) * inv
            gammas.append(gamma)
        rhos.append(rho)
    flow = rhos[count]
    slots[count] = flow
    for i in range(count - 1, -1, -1):
        flow = rhos[i] + gammas[i] * flow
        slots[i] = flow


def x_flows(blocks, slots):
    count = blocks.shape[0]

    def pivot(i):
        if i == 0:
            return 2.0 * inverse(blocks[0, 3]) + blocks[0, 0]
        if i == count:
            return 2.0 * inverse(blocks[count - 1, 4]) + blocks[count - 1, 2]
        return 2.0 * inverse(blocks[i - 1, 4] + blocks[i, 3]) + blocks[i - 1, 2] + blocks[i, 0]

    def gain(i):
        if i == 0:
            return -blocks[0, 5]
        return blocks[i - 1, 6] - blocks[i, 5] if i < count else blocks[i - 1, 6]

    flows_of(count, pivot, lambda i: blocks[i - 1, 1], lambda i: blocks[i, 1], gain, slots)


def y_flows(blocks, slots):
    count = blocks.shape[0]

    def pivot(i):
        if i == 0:
            return blocks[0, 0]
        return blocks[i - 1, 2] + blocks[i, 0] if i < count else blocks[i - 1, 2]

    def gain(i):
        if i == 0:
            return -blocks[0, 3]
        return blocks[i - 1, 4] - blocks[i, 3] if i < count else blocks[i - 1, 4]

    flows_of(count, pivot, lambda i: blocks[i - 1, 1], lambda i: blocks[i, 1], gain, slots)


def load_kernel(st_hbm, kx_hbm, ky_hbm, st, kx, ky, ky_t, up, down, sems):
    moves = [
        pltpu.make_async_copy(src, dst, sems.at[n])
        for n, (src, dst) in enumerate(((ky_hbm, ky), (st_hbm, st), (kx_hbm, kx)))
    ]
    for move in moves:
        move.start()
    moves[0].wait()
    for g in range(GROUPS):
        ky_t[pl.ds(g, BY, stride=GROUPS), :] = ky[pl.ds(g * 128, 128), :].T
    moves[1].wait()
    for g in range(GROUPS):
        turned = st[pl.ds(g * 128, 128), :].T
        down[0, pl.ds(g, 1), :] = turned[0:1, :]
        up[0, pl.ds(g, 1), :] = turned[127:128, :]
    down[1] = ky_t[pl.ds(0, GROUPS), :]
    up[1] = ky_t[pl.ds((BY - 1) * GROUPS, GROUPS), :]
    moves[2].wait()


def sweep(count, row, f, u, first, last):
    ahead = jnp.ones_like(row(0))
    back = jnp.ones_like(ahead)
    low, high = row(0), row(count - 1)
    for i in range(count - 1):
        nxt = row(i + 1)
        r = 0.5 * (low + nxt)
        low = nxt
        inv = inverse(r + ahead)
        ratio = r * inv
        ahead = 1.0 + ratio * ahead
        u[i] = inv
        f[i] = ratio
        j = count - 1 - i
        prev = row(j - 1)
        r = 0.5 * (high + prev)
        high = prev
        ratio = r * inverse(r + back)
        back = 1.0 + ratio * back
        first[j] = ratio
    start = inverse(back)
    end = inverse(ahead)
    lead, trail = start, end
    first[0] = start
    last[count - 1] = end
    u[count - 1] = end
    f[count - 1] = jnp.zeros_like(end)
    for i in range(1, count):
        start = start * first[i]
        first[i] = start
        j = count - 1 - i
        end = end * f[j]
        last[j] = end
    return lead, end, trail


def x_matrix_kernel(st, kx, ky, fx, ux, wf, wl, mx, source):
    values = sweep(BX, lambda i: x_row(kx, i), fx, ux, wf, wl)
    for n, value in enumerate(values + (x_row(kx, 0), x_row(kx, BX - 1))):
        mx[n] = value
    lane = lax.broadcasted_iota(jnp.int32, (128, 128), 1)
    for g in range(GROUPS):
        rows = pl.ds(g * 128, 128)
        s = st[rows, :]
        k = ky[rows, :]
        flux = 0.5 * (k + pltpu.roll(k, 127, 1)) * (pltpu.roll(s, 127, 1) - s)
        flux = jnp.where(lane == 127, 0.0, flux)
        source[rows, :] = s + flux - pltpu.roll(flux, 1, 1)


def y_matrix_kernel(ky_t, came, after, fy, uy, yf, yl, my):
    me = lax.axis_index("gy")
    last = lax.axis_size("gy") - 1
    lead, across, trail = sweep(BY, lambda j: y_row(ky_t, j), fy, uy, yf, yl)
    below = jnp.where(me == 0, 0.0, came[1])
    my[0] = lead + 2.0 * inverse(below + y_row(ky_t, 0))
    my[1] = across
    my[2] = trail + jnp.where(me == last, 2.0 * inverse(y_row(ky_t, BY - 1)), 0.0)


def x_ends_kernel(from_above, from_below, up, down, source, wf, wl, mx, s_out, send):
    me = lax.axis_index("gy")
    below = jnp.where(me == 0, 0.0, from_below[...])
    above = jnp.where(me == lax.axis_size("gy") - 1, 0.0, from_above[...])
    flux_l = 0.5 * (below[1] + down[1]) * (down[0] - below[0])
    flux_r = 0.5 * (above[1] + up[1]) * (above[0] - up[0])
    both = jnp.concatenate([flux_l, flux_r], axis=0)
    turned = jnp.concatenate([both] * 8, axis=0).T
    lane = lax.broadcasted_iota(jnp.int32, (128, 128), 1)
    for g in range(GROUPS):
        rows = pl.ds(g * 128, 128)
        left = jnp.broadcast_to(turned[:, g : g + 1], (128, 128))
        right = jnp.broadcast_to(turned[:, 8 + g : 9 + g], (128, 128))
        extra = jnp.where(lane == 0, -left, jnp.where(lane == 127, right, 0.0))
        s_out[rows, :] = source[rows, :] + extra
    firsts = [jnp.zeros((NZ, BY), F32) for _ in range(2)]
    lasts = [jnp.zeros((NZ, BY), F32) for _ in range(2)]
    for i in range(BX):
        s = x_row(s_out, i)
        firsts[i % 2] = firsts[i % 2] + wf[i] * s
        lasts[i % 2] = lasts[i % 2] + wl[i] * s
    send[0:5] = mx[...]
    send[5] = firsts[0] + firsts[1]
    send[6] = lasts[0] + lasts[1]


def x_local_kernel(s_in, st, fx, ux, d):
    total = x_row(s_in, 0)
    d[0] = total
    for i in range(1, BX):
        total = x_row(s_in, i) + fx[i - 1] * total
        d[i] = total
    x = jnp.zeros_like(total)
    for i in range(BX - 1, -1, -1):
        x = ux[i] * d[i] + fx[i] * x
        d[i] = x - x_row(st, i)


def x_merge_kernel(own, other, send, coefs):
    core = lax.rem(lax.axis_index("gx"), 2)
    mine, theirs = [own[n] for n in range(7)], [other[n] for n in range(7)]
    low = [jnp.where(core == 0, a, b) for a, b in zip(mine, theirs)]
    high = [jnp.where(core == 0, b, a) for a, b in zip(mine, theirs)]
    joined, flow = merge(low, high)
    for p in range(send.shape[0]):
        for n in range(7):
            send[p, n] = joined[n]
    for n in range(3):
        coefs[n] = flow[n]


def y_ends_kernel(blocks, coefs, d, wf, wl, yf, yl, my, v_t, send, slots, v):
    me = lax.axis_index("gx")
    x_flows(blocks, slots)
    place = lax.div(me, 2)
    enter, leave = slots[place], slots[place + 1]
    middle = coefs[0] + coefs[1] * enter + coefs[2] * leave
    low = lax.rem(me, 2) == 0
    enter, leave = jnp.where(low, enter, middle), jnp.where(low, middle, leave)
    for i in range(BX):
        place_rows(v, i, d[i] + wf[i] * enter - wl[i] * leave)
    for g in range(GROUPS):
        v_t[pl.ds(g, BY, stride=GROUPS), :] = v[pl.ds(g * 128, 128), :].T
    firsts = [jnp.zeros((GROUPS, 128), F32) for _ in range(4)]
    lasts = [jnp.zeros((GROUPS, 128), F32) for _ in range(4)]
    for j in range(BY):
        row = y_row(v_t, j)
        firsts[j % 4] = firsts[j % 4] + yf[j] * row
        lasts[j % 4] = lasts[j % 4] + yl[j] * row
    first = (firsts[0] + firsts[1]) + (firsts[2] + firsts[3])
    last = (lasts[0] + lasts[1]) + (lasts[2] + lasts[3])
    for p in range(send.shape[0]):
        send[p, 0:3] = my[...]
        send[p, 3] = first
        send[p, 4] = last


def y_local_kernel(v_t, fy, uy, g_t):
    total = y_row(v_t, 0)
    g_t[0] = total
    for j in range(1, BY):
        total = y_row(v_t, j) + fy[j - 1] * total
        g_t[j] = total
    x = jnp.zeros_like(total)
    for j in range(BY - 1, -1, -1):
        x = uy[j] * g_t[j] + fy[j] * x
        g_t[j] = x


def y_solve_kernel(blocks, g_t, yf, yl, st, out_hbm, slots, work, out, sems):
    me = lax.axis_index("gy")
    y_flows(blocks, slots)
    enter, leave = slots[me], slots[me + 1]
    for j in range(BY):
        work[pl.ds(j * GROUPS, GROUPS), :] = 2.0 * (g_t[j] + yf[j] * enter - yl[j] * leave)
    moves = []
    for g in range(GROUPS):
        rows = pl.ds(g * 128, 128)
        out[rows, :] = st[rows, :] + work[pl.ds(g, BY, stride=GROUPS), :].T
        move = pltpu.make_async_copy(out.at[rows], out_hbm.at[rows], sems.at[g])
        move.start()
        moves.append(move)
    for move in moves:
        move.wait()


def call(kernel, outs, args, scratch=(), cost=100_000):
    vm = pl.BlockSpec(memory_space=pltpu.VMEM)
    hbm = pl.BlockSpec(memory_space=pltpu.HBM)
    return pl.pallas_call(
        kernel,
        out_shape=[
            jax.ShapeDtypeStruct(shape, F32) if far else pltpu.VMEM(shape, F32)
            for shape, far in outs
        ],
        in_specs=[hbm if far else vm for _, far in args],
        out_specs=[hbm if far else vm for _, far in outs],
        scratch_shapes=list(scratch),
        compiler_params=pltpu.CompilerParams(vmem_limit_bytes=LIMIT),
        cost_estimate=pl.CostEstimate(flops=cost, bytes_accessed=cost, transcendentals=0),
    )(*[value for value, _ in args])


def near(*values):
    return [(value, False) for value in values]


def on_device(state, kappa_x, kappa_y):
    flat = [
        pltpu.with_memory_space_constraint(a.reshape(ROWS, BY), pltpu.HBM)
        for a in (state, kappa_x, kappa_y)
    ]
    plane = (ROWS, BY)
    xs = (BX, NZ, BY)
    ys = (BY, GROUPS, 128)
    x_block = (7, NZ, BY)
    edge = (2, GROUPS, 128)
    nx, ny = lax.axis_size("gx"), lax.axis_size("gy")
    chips = nx // 2
    st, kx, ky, ky_t, up, down = call(
        load_kernel,
        near(plane, plane, plane, plane, edge, edge),
        [(a, True) for a in flat],
        [pltpu.SemaphoreType.DMA((3,))],
    )
    below = lax.ppermute(up, "gy", [(i, (i + 1) % ny) for i in range(ny)])
    above = lax.ppermute(down, "gy", [((i + 1) % ny, i) for i in range(ny)])
    fx, ux, wf, wl, mx, source = call(
        x_matrix_kernel, near(xs, xs, xs, xs, (5, NZ, BY), plane), near(st, kx, ky), cost=5_000_000
    )
    s, ends = call(
        x_ends_kernel, near(plane, x_block), near(above, below, up, down, source, wf, wl, mx)
    )
    other = lax.ppermute(ends, "gx", [(i, i ^ 1) for i in range(nx)])
    (d,) = call(x_local_kernel, near(xs), near(s, st, fx, ux), cost=3_000_000)
    send, coefs = call(x_merge_kernel, near((chips,) + x_block, (3, NZ, BY)), near(ends, other))
    groups = [list(range(c, nx, 2)) for c in range(2)]
    x_blocks = lax.all_to_all(send, "gx", 0, 0, axis_index_groups=groups)
    fy, uy, yf, yl, my = call(
        y_matrix_kernel,
        near(ys, ys, ys, ys, (3, GROUPS, 128)),
        near(ky_t, below, coefs),
        cost=5_000_000,
    )
    v_t, send = call(
        y_ends_kernel,
        near(plane, (ny, 5, GROUPS, 128)),
        near(x_blocks, coefs, d, wf, wl, yf, yl, my),
        [pltpu.VMEM((chips + 1, NZ, BY), F32), pltpu.VMEM(plane, F32)],
    )
    y_blocks = lax.all_to_all(send, "gy", 0, 0)
    (g_t,) = call(y_local_kernel, near(ys), near(v_t, fy, uy), cost=5_000_000)
    (out,) = call(
        y_solve_kernel,
        [(plane, True)],
        near(y_blocks, g_t, yf, yl, st),
        [
            pltpu.VMEM((ny + 1, GROUPS, 128), F32),
            pltpu.VMEM(plane, F32),
            pltpu.VMEM(plane, F32),
            pltpu.SemaphoreType.DMA((GROUPS,)),
        ],
    )
    return out.reshape(state.shape)


def solution(mesh):
    spec = P(None, "gx", "gy")
    return jax.shard_map(
        on_device, mesh=mesh, in_specs=(spec, spec, spec), out_specs=spec, check_vma=False
    )
```

time: 78 us -> 46.7 us (0.60)
  blocking collectives: 38 us -> 0 us
  waiting for transfers between devices: 0.01 us -> 14.4 us
  starting transfers between devices: 20.5 us -> 14.5 us
  Pallas kernels: 10.5 us -> 9.03 us
    all_gather x2 -> x0, blocking collectives: 38 us -> none  [the longest x1 24.2 us: on_device(): y_blocks = lax.all_gather(my, 'gy')]
    all_to_all x2, waiting for transfers between devices: 0.01 us -> 7.27 us  [the longest x1 6.13 us: on_device(): y_blocks = lax.all_to_all(send, 'gy', 0, 0)]
    ppermute x2 -> x3, waiting for transfers between devices: 0.01 us -> 7.09 us  [the longest x1 5.6 us: on_device(): below = lax.ppermute(up, 'gy', [(i, (i + 1) % ny) for i in range(ny)])]
    all_to_all x2, starting transfers between devices: 14.7 us -> 7.97 us  [the longest x1 4.29 us: on_device(): x_blocks = lax.all_to_all(send, 'gx', 0, 0, axis_index_groups=groups)]
    pallas_call x7 -> x9, Pallas kernels: 10.5 us -> 9.03 us  [call(): pl.pallas_call(kernel, out_shape=[jax.ShapeDtypeStruct(shape, F32) if far...]
    ppermute x2 -> x3, starting transfers between devices: 5.84 us -> 6.58 us  [the longest x1 6.57 us: on_device(): above = lax.ppermute(down, 'gy', [((i + 1) % ny, i) for i in range(ny)])]
    unnamed x26 -> x22, local copies, waits for them, and re-layouts: 8.26 us -> 8.19 us
  transfers between devices with their start and end apart: 4 -> 5, of which waited for: 0 -> 5; matrix products, arithmetic and copies ran while one was open for 0% -> 0% of each run, Pallas kernels for 4% -> 9%
where the time goes in v4:
time: 46.7 us; the launch traced here: 46.2 us
  starting transfers between devices  14.5 us (31%)
  waiting for transfers between devices  14.4 us (31%)
  Pallas kernels  9.03 us (19%)
  local copies, waits for them, and re-layouts  8.19 us (18%)
    pallas_call x9, Pallas kernels, call(): pl.pallas_call(kernel, out_shape=[jax.ShapeDtypeStruct(shape, F32) if far...  9.03 us
    unnamed x22, local copies, waits for them, and re-layouts  8.19 us
    ppermute x1, starting transfers between devices, on_device(): above = lax.ppermute(down, 'gy', [((i + 1) % ny, i) for i in range(ny)])  6.57 us
    all_to_all x1, waiting for transfers between devices, on_device(): y_blocks = lax.all_to_all(send, 'gy', 0, 0)  6.13 us
    ppermute x1, waiting for transfers between devices, on_device(): below = lax.ppermute(up, 'gy', [(i, (i + 1) % ny) for i in range(ny)])  5.6 us
    all_to_all x1, starting transfers between devices, on_device(): x_blocks = lax.all_to_all(send, 'gx', 0, 0, axis_index_groups=groups)  4.29 us
    all_to_all x1, starting transfers between devices, on_device(): y_blocks = lax.all_to_all(send, 'gy', 0, 0)  3.67 us
    ppermute x1, waiting for transfers between devices, on_device(): other = lax.ppermute(ends, 'gx', [(i, i ^ 1) for i in range(nx)])  1.24 us
  transfers between devices with their start and end apart: 5, of which 5 were waited for; matrix products, arithmetic and copies ran while one was open for 0% of the time, Pallas kernels for 9%

profile of v4, /device:TPU:0, one launch (start us, length us, event | category | flops | bytes accessed | tf_op | source)
XLA Modules:
  0.0 46.2 jit_solution(10477686716640045917)
XLA Ops:
  0.0 1.5 %shard_map.37 = (f32[1024,128]{1,0:T(8,128)S(1)}, f32[1024,128]{1,0:T(8,128)S(1)}, f32[1024,128]{1,0:T(8,128)S(1)}, f32[1024,128]{1,0:T(8,128)S(1)}, f32[2,8,128]{2,1,0:T(8,128)S(1)}, /*index=5*/f32[2,8,128]{2,1,0:T(8,128)S(1)}) custom-call(f32[1024,128]{1,0:T(8,128)} %bitcast.4, f32[1024,128]{1,0:T(8,128)} %bitcast.5, f32[1024,128]{1,0:T(8,128)} %bitcast.6), custom_call_target="tpu_custom_call" | custom-call | flops 100000 | bytes 100000 | tf_op jit(solution)/shard_map/pallas_call | solution.py:296
  1.5 0.8 %copy-done.2 = f32[1024,128]{1,0:T(8,128)} copy-done((f32[1024,128]{1,0:T(8,128)}, f32[1024,128]{1,0:T(8,128)S(1)}, u32[]{:S(2)}) %copy-start.2) | copy-done | bytes 524312
  2.3 6.6 %collective-permute-start = (f32[2,8,128]{2,1,0:T(8,128)S(1)}, f32[2,8,128]{2,1,0:T(8,128)S(1)}, u32[]{:S(2)}, u32[]{:S(2)}) collective-permute-start(f32[2,8,128]{2,1,0:T(8,128)S(1)} %get-tuple-element.28.down), channel_id=1, source_target_pairs={{1,0},{2,1},{3,2},{4,3},{5,4},{6,5},{7,6},{8,7},{9,8},{10,9},{11,1... | collective-permute-start | bytes 24584 | tf_op jit(solution)/shard_map/ppermute | solution.py:333
  8.9 1.1 %shard_map.38 = (f32[64,16,128]{2,1,0:T(8,128)S(1)}, f32[64,16,128]{2,1,0:T(8,128)S(1)}, f32[64,16,128]{2,1,0:T(8,128)S(1)}, f32[64,16,128]{2,1,0:T(8,128)S(1)},...) custom-call(f32[1024,128]{1,0:T(8,128)S(1)} %get-tuple-element.30.st, f32[1024,128]{1,0:T(8,128)S(1)} %get-tuple-element.31.kx, ...), custom_call_target="tpu_custom_call" | custom-call | flops 5000000 | bytes 5000000 | tf_op jit(solution)/shard_map/pallas_call | solution.py:296
  10.2 5.6 %collective-permute-done.1.from_below.came = f32[2,8,128]{2,1,0:T(8,128)S(1)} collective-permute-done((f32[2,8,128]{2,1,0:T(8,128)S(1)}, f32[2,8,128]{2,1,0:T(8,128)S(1)}, u32[]{:S(2)}, u32[]{:S(2)}) %collective-permute-start.1) | collective-permute-done | bytes 8224 | tf_op jit(solution)/shard_map/ppermute | solution.py:332
  15.8 0.8 %shard_map.39 = (f32[1024,128]{1,0:T(8,128)S(1)}, f32[7,16,128]{2,1,0:T(8,128)S(1)}) custom-call(f32[2,8,128]{2,1,0:T(8,128)S(1)} %collective-permute-done.from_above, f32[2,8,128]{2,1,0:T(8,128)S(1)} %collective-permute-done.1.from_below.came, f32[2,8,128]{2,1,0:T(8,128)S(1)} %get-tuple-element.29.up, f32[2,8,128]{2,1,0:T(8,128)S(1)} %get-tuple-element.28.down, ...), custom_call_target="tpu_custom_call" | custom-call | flops 100000 | bytes 100000 | tf_op jit(solution)/shard_map/pallas_call | solution.py:296
  16.6 0.8 %copy-done = f32[1024,128]{1,0:T(8,128)} copy-done((f32[1024,128]{1,0:T(8,128)}, f32[1024,128]{1,0:T(8,128)S(1)}, u32[]{:S(2)}) %copy-start) | copy-done | bytes 524312
  17.4 1.2 %collective-permute-done.2.other = f32[7,16,128]{2,1,0:T(8,128)S(1)} collective-permute-done((f32[7,16,128]{2,1,0:T(8,128)S(1)}, f32[7,16,128]{2,1,0:T(8,128)S(1)}, u32[]{:S(2)}, u32[]{:S(2)}) %collective-permute-start.2) | collective-permute-done | bytes 57376 | tf_op jit(solution)/shard_map/ppermute | solution.py:340
  18.7 0.7 %shard_map.40 = (f32[4,7,16,128]{3,2,1,0:T(8,128)}, f32[3,16,128]{2,1,0:T(8,128)S(1)}) custom-call(f32[7,16,128]{2,1,0:T(8,128)S(1)} %get-tuple-element.37.own, f32[7,16,128]{2,1,0:T(8,128)S(1)} %collective-permute-done.2.other), custom_call_target="tpu_custom_call" | custom-call | flops 100000 | bytes 100000 | tf_op jit(solution)/shard_map/pallas_call | solution.py:296
  19.4 4.3 %all-to-all-start = ((f32[4,7,16,128]{3,2,1,0:T(8,128)}), f32[4,7,16,128]{3,2,1,0:T(8,128)S(1)}, u32[]{:S(2)}, u32[]{:S(2)}) async-start(f32[4,7,16,128]{3,2,1,0:T(8,128)} %get-tuple-element.38), calls=%async_computation | async-start | bytes 458752 | tf_op jit(solution)/shard_map/all_to_all | solution.py:344
  23.7 1.0 %copy-done.1 = f32[1024,128]{1,0:T(8,128)S(1)} copy-done((f32[1024,128]{1,0:T(8,128)S(1)}, f32[1024,128]{1,0:T(8,128)}, u32[]{:S(2)}) %copy-start.1) | copy-done | bytes 524312
  24.7 0.7 %shard_map.41.d = f32[64,16,128]{2,1,0:T(8,128)S(1)} custom-call(f32[1024,128]{1,0:T(8,128)S(1)} %copy-done.1, f32[1024,128]{1,0:T(8,128)S(1)} %get-tuple-element.30.st, f32[64,16,128]{2,1,0:T(8,128)S(1)} %get-tuple-element.41.fx, f32[64,16,128]{2,1,0:T(8,128)S(1)} %get-tuple-element.42.ux), custom_call_target="tpu_custom_call" | custom-call | flops 3000000 | bytes 3000000 | tf_op jit(solution)/shard_map/pallas_call | solution.py:296
  25.8 1.8 %shard_map.42 = (f32[128,8,128]{2,1,0:T(8,128)S(1)}, f32[128,8,128]{2,1,0:T(8,128)S(1)}, f32[128,8,128]{2,1,0:T(8,128)S(1)}, f32[128,8,128]{2,1,0:T(8,128)S(1)}, f32[3,8,128]{2,1,0:T(8,128)S(1)}) custom-call(f32[1024,128]{1,0:T(8,128)S(1)} %copy-done.3, f32[2,8,128]{2,1,0:T(8,128)S(1)} %collective-permute-done.1.from_below.came, ...), custom_call_target="tpu_custom_call" | custom-call | flops 5000000 | bytes 5000000 | tf_op jit(solution)/shard_map/pallas_call | solution.py:296
  27.6 0.8 %copy-done.4 = f32[128,8,128]{2,1,0:T(8,128)} copy-done((f32[128,8,128]{2,1,0:T(8,128)}, f32[128,8,128]{2,1,0:T(8,128)S(1)}, u32[]{:S(2)}) %copy-start.4) | copy-done | bytes 524312
  28.4 0.8 %copy-done.6 = f32[128,8,128]{2,1,0:T(8,128)} copy-done((f32[128,8,128]{2,1,0:T(8,128)}, f32[128,8,128]{2,1,0:T(8,128)S(1)}, u32[]{:S(2)}) %copy-start.6) | copy-done | bytes 524312
  29.2 1.1 %all-to-all-done.blocks = f32[4,7,16,128]{3,2,1,0:T(8,128)S(1)} async-done(((f32[4,7,16,128]{3,2,1,0:T(8,128)}), f32[4,7,16,128]{3,2,1,0:T(8,128)S(1)}, u32[]{:S(2)}, u32[]{:S(2)}) %all-to-all-start) | async-done | bytes 229408 | tf_op jit(solution)/shard_map/all_to_all | solution.py:344
  30.3 0.6 %shard_map.43 = (f32[1024,128]{1,0:T(8,128)S(1)}, f32[16,5,8,128]{3,2,1,0:T(8,128)S(1)}) custom-call(f32[4,7,16,128]{3,2,1,0:T(8,128)S(1)} %all-to-all-done.blocks, f32[3,16,128]{2,1,0:T(8,128)S(1)} %get-tuple-element.39.after.coefs, f32[64,16,128]{2,1,0:T(8,128)S(1)} %shard_map.41.d, f32[64,16,128]{2,1,0:T(8,128)S(1)} %get-tuple-element.34.wf, ...), custom_call_target="tpu_custom_call" | custom-call | flops 100000 | bytes 100000 | tf_op jit(solution)/shard_map/pallas_call | solution.py:296
  31.0 0.8 %copy-done.8 = f32[1024,128]{1,0:T(8,128)} copy-done((f32[1024,128]{1,0:T(8,128)}, f32[1024,128]{1,0:T(8,128)S(1)}, u32[]{:S(2)}) %copy-start.8) | copy-done | bytes 524312
  31.8 0.7 %copy-done.10 = f32[16,5,8,128]{3,2,1,0:T(8,128)} copy-done((f32[16,5,8,128]{3,2,1,0:T(8,128)}, f32[16,5,8,128]{3,2,1,0:T(8,128)S(1)}, u32[]{:S(2)}) %copy-start.10) | copy-done | bytes 327704
  32.5 3.7 %all-to-all-start.1 = ((f32[16,5,8,128]{3,2,1,0:T(8,128)}), f32[16,5,8,128]{3,2,1,0:T(8,128)S(1)}, u32[]{:S(2)}, u32[]{:S(2)}) async-start(f32[16,5,8,128]{3,2,1,0:T(8,128)} %copy-done.10), calls=%async_computation.1 | async-start | bytes 655360 | tf_op jit(solution)/shard_map/all_to_all | solution.py:357
  36.2 1.0 %copy-done.7 = f32[128,8,128]{2,1,0:T(8,128)S(1)} copy-done((f32[128,8,128]{2,1,0:T(8,128)S(1)}, f32[128,8,128]{2,1,0:T(8,128)}, u32[]{:S(2)}) %copy-start.7) | copy-done | bytes 524312
  37.2 1.0 %copy-done.9 = f32[1024,128]{1,0:T(8,128)S(1)} copy-done((f32[1024,128]{1,0:T(8,128)S(1)}, f32[1024,128]{1,0:T(8,128)}, u32[]{:S(2)}) %copy-start.9) | copy-done | bytes 524312
  38.8 6.1 %all-to-all-done.1.blocks = f32[16,5,8,128]{3,2,1,0:T(8,128)S(1)} async-done(((f32[16,5,8,128]{3,2,1,0:T(8,128)}), f32[16,5,8,128]{3,2,1,0:T(8,128)S(1)}, u32[]{:S(2)}, u32[]{:S(2)}) %all-to-all-start.1) | async-done | bytes 327712 | tf_op jit(solution)/shard_map/all_to_all | solution.py:357
  44.9 1.3 %shard_map.45 = f32[1024,128]{1,0:T(8,128)} custom-call(f32[16,5,8,128]{3,2,1,0:T(8,128)S(1)} %all-to-all-done.1.blocks, f32[128,8,128]{2,1,0:T(8,128)S(1)} %shard_map.44.g_t, f32[128,8,128]{2,1,0:T(8,128)S(1)} %get-tuple-element.44.yf, f32[128,8,128]{2,1,0:T(8,128)S(1)} %get-tuple-element.45.yl, f32[1024,128]{1,0:T(8,128)S(1)} %get-tuple-element.30.st), custom_call_target="tpu_custom_call" | custom-call | flops 100000 | bytes 100000 | tf_op jit(solution)/shard_map/pallas_call | solution.py:296
  (17 shorter events, 1.2 us)
Async XLA Ops:
  1.5 0.8 %copy-start.2 = (f32[1024,128]{1,0:T(8,128)}, f32[1024,128]{1,0:T(8,128)S(1)}, u32[]{:S(2)}) copy-start(f32[1024,128]{1,0:T(8,128)S(1)} %get-tuple-element.43.ky_t) | copy-start | bytes 1572868
  2.3 7.9 %collective-permute-start = (f32[2,8,128]{2,1,0:T(8,128)S(1)}, f32[2,8,128]{2,1,0:T(8,128)S(1)}, u32[]{:S(2)}, u32[]{:S(2)}) collective-permute-start(f32[2,8,128]{2,1,0:T(8,128)S(1)} %get-tuple-element.28.down), channel_id=1, source_target_pairs={{1,0},{2,1},{3,2},{4,3},{5,4},{6,5},{7,6},{8,7},{9,8},{10,9},{11,1... | collective-permute-start | bytes 24584 | tf_op jit(solution)/shard_map/ppermute | solution.py:333
  8.9 7.0 %collective-permute-start.1 = (f32[2,8,128]{2,1,0:T(8,128)S(1)}, f32[2,8,128]{2,1,0:T(8,128)S(1)}, u32[]{:S(2)}, u32[]{:S(2)}) collective-permute-start(f32[2,8,128]{2,1,0:T(8,128)S(1)} %get-tuple-element.29.up), channel_id=1, source_target_pairs={{0,1},{1,2},{2,3},{3,4},{4,5},{5,6},{6,7},{7,8},{8,9},{9,10},{10,1... | collective-permute-start | bytes 24584 | tf_op jit(solution)/shard_map/ppermute | solution.py:332
  16.6 0.8 %copy-start = (f32[1024,128]{1,0:T(8,128)}, f32[1024,128]{1,0:T(8,128)S(1)}, u32[]{:S(2)}) copy-start(f32[1024,128]{1,0:T(8,128)S(1)} %get-tuple-element.40.s_in) | copy-start | bytes 1572868
  17.4 1.2 %collective-permute-start.2 = (f32[7,16,128]{2,1,0:T(8,128)S(1)}, f32[7,16,128]{2,1,0:T(8,128)S(1)}, u32[]{:S(2)}, u32[]{:S(2)}) collective-permute-start(f32[7,16,128]{2,1,0:T(8,128)S(1)} %get-tuple-element.37.own), channel_id=1, source_target_pairs={{0,16},{16,0},{32,48},{48,32},{64,80},{80,64},{96,112},{112,96},{1... | collective-permute-start | bytes 172040 | tf_op jit(solution)/shard_map/ppermute | solution.py:340
  19.4 10.9 %all-to-all-start = ((f32[4,7,16,128]{3,2,1,0:T(8,128)}), f32[4,7,16,128]{3,2,1,0:T(8,128)S(1)}, u32[]{:S(2)}, u32[]{:S(2)}) async-start(f32[4,7,16,128]{3,2,1,0:T(8,128)} %get-tuple-element.38), calls=%async_computation | async-start | bytes 458752 | tf_op jit(solution)/shard_map/all_to_all | solution.py:344
  23.7 1.0 %copy-start.1 = (f32[1024,128]{1,0:T(8,128)S(1)}, f32[1024,128]{1,0:T(8,128)}, u32[]{:S(2)}) copy-start(f32[1024,128]{1,0:T(8,128)} %copy-done) | copy-start | bytes 1572868
  24.7 1.0 %copy-start.3 = (f32[1024,128]{1,0:T(8,128)S(1)}, f32[1024,128]{1,0:T(8,128)}, u32[]{:S(2)}) copy-start(f32[1024,128]{1,0:T(8,128)} %copy-done.2) | copy-start | bytes 1572868
  27.6 0.8 %copy-start.4 = (f32[128,8,128]{2,1,0:T(8,128)}, f32[128,8,128]{2,1,0:T(8,128)S(1)}, u32[]{:S(2)}) copy-start(f32[128,8,128]{2,1,0:T(8,128)S(1)} %get-tuple-element.49.fy) | copy-start | bytes 1572868
  28.4 0.8 %copy-start.6 = (f32[128,8,128]{2,1,0:T(8,128)}, f32[128,8,128]{2,1,0:T(8,128)S(1)}, u32[]{:S(2)}) copy-start(f32[128,8,128]{2,1,0:T(8,128)S(1)} %get-tuple-element.50.uy) | copy-start | bytes 1572868
  31.0 0.8 %copy-start.8 = (f32[1024,128]{1,0:T(8,128)}, f32[1024,128]{1,0:T(8,128)S(1)}, u32[]{:S(2)}) copy-start(f32[1024,128]{1,0:T(8,128)S(1)} %get-tuple-element.48.v_t) | copy-start | bytes 1572868
  31.8 0.7 %copy-start.10 = (f32[16,5,8,128]{3,2,1,0:T(8,128)}, f32[16,5,8,128]{3,2,1,0:T(8,128)S(1)}, u32[]{:S(2)}) copy-start(f32[16,5,8,128]{3,2,1,0:T(8,128)S(1)} %get-tuple-element.47) | copy-start | bytes 983044
  32.5 3.7 %copy-start.5 = (f32[128,8,128]{2,1,0:T(8,128)S(1)}, f32[128,8,128]{2,1,0:T(8,128)}, u32[]{:S(2)}) copy-start(f32[128,8,128]{2,1,0:T(8,128)} %copy-done.4) | copy-start | bytes 1572868
  32.5 12.4 %all-to-all-start.1 = ((f32[16,5,8,128]{3,2,1,0:T(8,128)}), f32[16,5,8,128]{3,2,1,0:T(8,128)S(1)}, u32[]{:S(2)}, u32[]{:S(2)}) async-start(f32[16,5,8,128]{3,2,1,0:T(8,128)} %copy-done.10), calls=%async_computation.1 | async-start | bytes 655360 | tf_op jit(solution)/shard_map/all_to_all | solution.py:357
  36.2 1.0 %copy-start.7 = (f32[128,8,128]{2,1,0:T(8,128)S(1)}, f32[128,8,128]{2,1,0:T(8,128)}, u32[]{:S(2)}) copy-start(f32[128,8,128]{2,1,0:T(8,128)} %copy-done.6) | copy-start | bytes 1572868
  37.2 1.0 %copy-start.9 = (f32[1024,128]{1,0:T(8,128)S(1)}, f32[1024,128]{1,0:T(8,128)}, u32[]{:S(2)}) copy-start(f32[1024,128]{1,0:T(8,128)} %copy-done.8) | copy-start | bytes 1572868

commit v5 on v4

--- a/solution.py
+++ b/solution.py
@@ -9,7 +9,7 @@
 NZ, BX, BY = 16, 64, 128
 ROWS = NZ * BX
 GROUPS = ROWS // 128
-LIMIT = 40 * 1024 * 1024
+LIMIT = 8 * 1024 * 1024
 
 
 def inverse(x):
@@ -70,8 +70,11 @@
         slots[i] = flow
 
 
-def x_flows(blocks, slots):
+def x_flows(own, others, place, blocks, slots):
     count = blocks.shape[0]
+    blocks[place] = own[...]
+    for k, other in enumerate(others):
+        blocks[place ^ (k + 1)] = other[...]
 
     def pivot(i):
         if i == 0:
@@ -104,7 +107,7 @@
     flows_of(count, pivot, lambda i: blocks[i - 1, 1], lambda i: blocks[i, 1], gain, slots)
 
 
-def load_kernel(st_hbm, kx_hbm, ky_hbm, st, kx, ky, ky_t, up, down, sems):
+def load_kernel(st_hbm, kx_hbm, ky_hbm, st, kx, ky, ky_t, mine, first, second, sems):
     moves = [
         pltpu.make_async_copy(src, dst, sems.at[n])
         for n, (src, dst) in enumerate(((ky_hbm, ky), (st_hbm, st), (kx_hbm, kx)))
@@ -117,10 +120,14 @@
     moves[1].wait()
     for g in range(GROUPS):
         turned = st[pl.ds(g * 128, 128), :].T
-        down[0, pl.ds(g, 1), :] = turned[0:1, :]
-        up[0, pl.ds(g, 1), :] = turned[127:128, :]
-    down[1] = ky_t[pl.ds(0, GROUPS), :]
-    up[1] = ky_t[pl.ds((BY - 1) * GROUPS, GROUPS), :]
+        mine[0, pl.ds(g, 1), :] = turned[0:1, :]
+        mine[2, pl.ds(g, 1), :] = turned[127:128, :]
+    mine[1] = ky_t[pl.ds(0, GROUPS), :]
+    mine[3] = ky_t[pl.ds((BY - 1) * GROUPS, GROUPS), :]
+    even = lax.rem(lax.axis_index("gy"), 2) == 0
+    low, high = mine[0:2], mine[2:4]
+    first[...] = jnp.where(even, high, low)
+    second[...] = jnp.where(even, low, high)
     moves[2].wait()
 
 
@@ -174,22 +181,24 @@
         source[rows, :] = s + flux - pltpu.roll(flux, 1, 1)
 
 
-def y_matrix_kernel(ky_t, came, after, fy, uy, yf, yl, my):
+def y_matrix_kernel(ky_t, came1, came2, after, yf, yl, my, f, u):
     me = lax.axis_index("gy")
     last = lax.axis_size("gy") - 1
-    lead, across, trail = sweep(BY, lambda j: y_row(ky_t, j), fy, uy, yf, yl)
-    below = jnp.where(me == 0, 0.0, came[1])
+    lead, across, trail = sweep(BY, lambda j: y_row(ky_t, j), f, u, yf, yl)
+    below = jnp.where(lax.rem(me, 2) == 0, came2[1], came1[1])
+    below = jnp.where(me == 0, 0.0, below)
     my[0] = lead + 2.0 * inverse(below + y_row(ky_t, 0))
     my[1] = across
     my[2] = trail + jnp.where(me == last, 2.0 * inverse(y_row(ky_t, BY - 1)), 0.0)
 
 
-def x_ends_kernel(from_above, from_below, up, down, source, wf, wl, mx, s_out, send):
+def x_ends_kernel(came1, came2, mine, source, wf, wl, mx, s_out, send):
     me = lax.axis_index("gy")
-    below = jnp.where(me == 0, 0.0, from_below[...])
-    above = jnp.where(me == lax.axis_size("gy") - 1, 0.0, from_above[...])
-    flux_l = 0.5 * (below[1] + down[1]) * (down[0] - below[0])
-    flux_r = 0.5 * (above[1] + up[1]) * (above[0] - up[0])
+    even = lax.rem(me, 2) == 0
+    below = jnp.where(me == 0, 0.0, jnp.where(even, came2[...], came1[...]))
+    above = jnp.where(me == lax.axis_size("gy") - 1, 0.0, jnp.where(even, came1[...], came2[...]))
+    flux_l = 0.5 * (below[1] + mine[1]) * (mine[0] - below[0])
+    flux_r = 0.5 * (above[1] + mine[3]) * (above[0] - mine[2])
     both = jnp.concatenate([flux_l, flux_r], axis=0)
     turned = jnp.concatenate([both] * 8, axis=0).T
     lane = lax.broadcasted_iota(jnp.int32, (128, 128), 1)
@@ -222,23 +231,24 @@
         d[i] = x - x_row(st, i)
 
 
-def x_merge_kernel(own, other, send, coefs):
+def x_merge_kernel(own, other, after, send, coefs):
     core = lax.rem(lax.axis_index("gx"), 2)
     mine, theirs = [own[n] for n in range(7)], [other[n] for n in range(7)]
     low = [jnp.where(core == 0, a, b) for a, b in zip(mine, theirs)]
     high = [jnp.where(core == 0, b, a) for a, b in zip(mine, theirs)]
     joined, flow = merge(low, high)
-    for p in range(send.shape[0]):
-        for n in range(7):
-            send[p, n] = joined[n]
+    for n in range(7):
+        send[n] = joined[n]
     for n in range(3):
         coefs[n] = flow[n]
 
 
-def y_ends_kernel(blocks, coefs, d, wf, wl, yf, yl, my, v_t, send, slots, v):
+def y_ends_kernel(
+    own, other1, other2, other3, coefs, d, wf, wl, yf, yl, my, v_t, send, blocks, slots, v
+):
     me = lax.axis_index("gx")
-    x_flows(blocks, slots)
     place = lax.div(me, 2)
+    x_flows(own, (other1, other2, other3), place, blocks, slots)
     enter, leave = slots[place], slots[place + 1]
     middle = coefs[0] + coefs[1] * enter + coefs[2] * leave
     low = lax.rem(me, 2) == 0
@@ -261,16 +271,30 @@
         send[p, 4] = last
 
 
-def y_local_kernel(v_t, fy, uy, g_t):
+def y_local_kernel(v_t, ky_t, st_hbm, g_t, st, f, u, sem):
+    move = pltpu.make_async_copy(st_hbm, st, sem)
+    move.start()
     total = y_row(v_t, 0)
     g_t[0] = total
+    ahead = jnp.ones_like(total)
+    low = y_row(ky_t, 0)
     for j in range(1, BY):
-        total = y_row(v_t, j) + fy[j - 1] * total
+        high = y_row(ky_t, j)
+        r = 0.5 * (low + high)
+        low = high
+        inv = inverse(r + ahead)
+        ratio = r * inv
+        ahead = 1.0 + ratio * ahead
+        u[j - 1] = inv
+        f[j - 1] = ratio
+        total = y_row(v_t, j) + ratio * total
         g_t[j] = total
-    x = jnp.zeros_like(total)
-    for j in range(BY - 1, -1, -1):
-        x = uy[j] * g_t[j] + fy[j] * x
+    x = total * inverse(ahead)
+    g_t[BY - 1] = x
+    for j in range(BY - 2, -1, -1):
+        x = u[j] * g_t[j] + f[j] * x
         g_t[j] = x
+    move.wait()
 
 
 def y_solve_kernel(blocks, g_t, yf, yl, st, out_hbm, slots, work, out, sems):
@@ -323,39 +347,49 @@
     edge = (2, GROUPS, 128)
     nx, ny = lax.axis_size("gx"), lax.axis_size("gy")
     chips = nx // 2
-    st, kx, ky, ky_t, up, down = call(
+    st, kx, ky, ky_t, mine, first, second = call(
         load_kernel,
-        near(plane, plane, plane, plane, edge, edge),
+        near(plane, plane, plane, plane, (4, GROUPS, 128), edge, edge),
         [(a, True) for a in flat],
         [pltpu.SemaphoreType.DMA((3,))],
     )
-    below = lax.ppermute(up, "gy", [(i, (i + 1) % ny) for i in range(ny)])
-    above = lax.ppermute(down, "gy", [((i + 1) % ny, i) for i in range(ny)])
+    came1 = lax.ppermute(first, "gy", [(i, i ^ 1) for i in range(ny)])
+    came2 = lax.ppermute(second, "gy", [(i, (i + 2 * (i % 2) - 1) % ny) for i in range(ny)])
     fx, ux, wf, wl, mx, source = call(
         x_matrix_kernel, near(xs, xs, xs, xs, (5, NZ, BY), plane), near(st, kx, ky), cost=5_000_000
     )
     s, ends = call(
-        x_ends_kernel, near(plane, x_block), near(above, below, up, down, source, wf, wl, mx)
+        x_ends_kernel, near(plane, x_block), near(came1, came2, mine, source, wf, wl, mx)
     )
     other = lax.ppermute(ends, "gx", [(i, i ^ 1) for i in range(nx)])
     (d,) = call(x_local_kernel, near(xs), near(s, st, fx, ux), cost=3_000_000)
-    send, coefs = call(x_merge_kernel, near((chips,) + x_block, (3, NZ, BY)), near(ends, other))
-    groups = [list(range(c, nx, 2)) for c in range(2)]
-    x_blocks = lax.all_to_all(send, "gx", 0, 0, axis_index_groups=groups)
-    fy, uy, yf, yl, my = call(
+    chip, coefs = call(x_merge_kernel, near(x_block, (3, NZ, BY)), near(ends, other, d))
+    others = [lax.ppermute(chip, "gx", [(i, i ^ (2 * k)) for i in range(nx)]) for k in range(1, chips)]
+    yf, yl, my = call(
         y_matrix_kernel,
-        near(ys, ys, ys, ys, (3, GROUPS, 128)),
-        near(ky_t, below, coefs),
+        near(ys, ys, (3, GROUPS, 128)),
+        near(ky_t, came1, came2, coefs),
+        [pltpu.VMEM(ys, F32), pltpu.VMEM(ys, F32)],
         cost=5_000_000,
     )
     v_t, send = call(
         y_ends_kernel,
         near(plane, (ny, 5, GROUPS, 128)),
-        near(x_blocks, coefs, d, wf, wl, yf, yl, my),
-        [pltpu.VMEM((chips + 1, NZ, BY), F32), pltpu.VMEM(plane, F32)],
+        near(chip, *others, coefs, d, wf, wl, yf, yl, my),
+        [
+            pltpu.VMEM((chips,) + x_block, F32),
+            pltpu.VMEM((chips + 1, NZ, BY), F32),
+            pltpu.VMEM(plane, F32),
+        ],
     )
     y_blocks = lax.all_to_all(send, "gy", 0, 0)
-    (g_t,) = call(y_local_kernel, near(ys), near(v_t, fy, uy), cost=5_000_000)
+    g_t, st = call(
+        y_local_kernel,
+        near(ys, plane),
+        near(v_t, ky_t) + [(flat[0], True)],
+        [pltpu.VMEM(ys, F32), pltpu.VMEM(ys, F32), pltpu.SemaphoreType.DMA],
+        cost=5_000_000,
+    )
     (out,) = call(
         y_solve_kernel,
         [(plane, True)],

time: 46.7 us -> 39.6 us (0.85)
  local copies, waits for them, and re-layouts: 8.19 us -> 0 us
  waiting for transfers between devices: 14.4 us -> 10.8 us
  starting transfers between devices: 14.5 us -> 17.7 us
  Pallas kernels: 9.03 us -> 10.8 us
    unnamed x22 -> x0, local copies, waits for them, and re-layouts: 8.19 us -> none
    ppermute x2 -> x5, starting transfers between devices: 6.57 us -> 11.2 us  [the longest x1 4.97 us: on_device(): lax.ppermute(second, 'gy', [(i, (i + 2 * (i % 2) - 1) % ny) for i in rang...]
    all_to_all x1 -> x0, starting transfers between devices: 4.29 us -> none  [on_device(): x_blocks = lax.all_to_all(send, 'gx', 0, 0, axis_index_groups=groups)]
    all_to_all x1, starting transfers between devices: 3.67 us -> 6.35 us  [on_device(): y_blocks = lax.all_to_all(send, 'gy', 0, 0)]
    ppermute x2 -> x5, waiting for transfers between devices: 5.85 us -> 3.47 us  [the longest x3 2.66 us: on_device(): lax.ppermute(chip, 'gx', [(i, i ^ 2 * k) for i in range(nx)])]
    pallas_call x9, Pallas kernels: 9.03 us -> 10.8 us  [call(): pl.pallas_call(kernel, out_shape=[jax.ShapeDtypeStruct(shape, F32) if far...]
    all_to_all x1 -> x0, waiting for transfers between devices: 1.14 us -> none  [on_device(): x_blocks = lax.all_to_all(send, 'gx', 0, 0, axis_index_groups=groups)]
    ppermute x1, waiting for transfers between devices: 1.24 us -> 0.5 us  [on_device(): other = lax.ppermute(ends, 'gx', [(i, i ^ 1) for i in range(nx)])]
  transfers between devices with their start and end apart: 5 -> 7, of which waited for: 5 -> 4; matrix products, arithmetic and copies ran while one was open for 0% -> 0% of each run, Pallas kernels for 9% -> 14%
where the time goes in v5:
time: 39.6 us; the launch traced here: 39.4 us
  starting transfers between devices  17.7 us (45%)
  Pallas kernels  10.8 us (27%)
  waiting for transfers between devices  10.8 us (27%)
    pallas_call x9, Pallas kernels, call(): pl.pallas_call(kernel, out_shape=[jax.ShapeDtypeStruct(shape, F32) if far...  10.8 us
    all_to_all x1, waiting for transfers between devices, on_device(): y_blocks = lax.all_to_all(send, 'gy', 0, 0)  6.85 us
    all_to_all x1, starting transfers between devices, on_device(): y_blocks = lax.all_to_all(send, 'gy', 0, 0)  6.35 us
    ppermute x1, starting transfers between devices, on_device(): lax.ppermute(second, 'gy', [(i, (i + 2 * (i % 2) - 1) % ny) for i in rang...  4.97 us
    ppermute x3, starting transfers between devices, on_device(): lax.ppermute(chip, 'gx', [(i, i ^ 2 * k) for i in range(nx)])  4.17 us
    ppermute x3, waiting for transfers between devices, on_device(): lax.ppermute(chip, 'gx', [(i, i ^ 2 * k) for i in range(nx)])  2.66 us
    ppermute x1, starting transfers between devices, on_device(): came1 = lax.ppermute(first, 'gy', [(i, i ^ 1) for i in range(ny)])  2.08 us
    ppermute x1, waiting for transfers between devices, on_device(): lax.ppermute(second, 'gy', [(i, (i + 2 * (i % 2) - 1) % ny) for i in rang...  0.81 us
  transfers between devices with their start and end apart: 7, of which 4 were waited for; matrix products, arithmetic and copies ran while one was open for 0% of the time, Pallas kernels for 14%

profile of v5, /device:TPU:0, one launch (start us, length us, event | category | flops | bytes accessed | tf_op | source)
XLA Modules:
  0.0 39.4 jit_solution(8210776427724723518)
XLA Ops:
  0.0 1.5 %shard_map.37 = (f32[1024,128]{1,0:T(8,128)S(1)}, f32[1024,128]{1,0:T(8,128)S(1)}, f32[1024,128]{1,0:T(8,128)S(1)}, f32[1024,128]{1,0:T(8,128)S(1)}, f32[4,8,128...) custom-call(f32[1024,128]{1,0:T(8,128)} %bitcast.4, f32[1024,128]{1,0:T(8,128)} %bitcast.6, ...), custom_call_target="tpu_custom_call" | custom-call | flops 100000 | bytes 100000 | tf_op jit(solution)/shard_map/pallas_call | solution.py:320
  1.5 2.1 %collective-permute-start = (f32[2,8,128]{2,1,0:T(8,128)S(1)}, f32[2,8,128]{2,1,0:T(8,128)S(1)}, u32[]{:S(2)}, u32[]{:S(2)}) collective-permute-start(f32[2,8,128]{2,1,0:T(8,128)S(1)} %get-tuple-element.29), channel_id=1, source_target_pairs={{0,1},{1,0},{2,3},{3,2},{4,5},{5,4},{6,7},{7,6},{8,9},{9,8},{10,11... | collective-permute-start | bytes 24584 | tf_op jit(solution)/shard_map/ppermute | solution.py:356
  3.6 5.0 %collective-permute-start.1 = (f32[2,8,128]{2,1,0:T(8,128)S(1)}, f32[2,8,128]{2,1,0:T(8,128)S(1)}, u32[]{:S(2)}, u32[]{:S(2)}) collective-permute-start(f32[2,8,128]{2,1,0:T(8,128)S(1)} %get-tuple-element.30), channel_id=1, source_target_pairs={{0,15},{1,2},{2,1},{3,4},{4,3},{5,6},{6,5},{7,8},{8,7},{9,10},{10,... | collective-permute-start | bytes 24584 | tf_op jit(solution)/shard_map/ppermute | solution.py:357
  8.5 1.2 %shard_map.38 = (f32[64,16,128]{2,1,0:T(8,128)S(1)}, f32[64,16,128]{2,1,0:T(8,128)S(1)}, f32[64,16,128]{2,1,0:T(8,128)S(1)}, f32[64,16,128]{2,1,0:T(8,128)S(1)},...) custom-call(f32[1024,128]{1,0:T(8,128)S(1)} %get-tuple-element.32.st, f32[1024,128]{1,0:T(8,128)S(1)} %get-tuple-element.33.kx, ...), custom_call_target="tpu_custom_call" | custom-call | flops 5000000 | bytes 5000000 | tf_op jit(solution)/shard_map/pallas_call | solution.py:320
  9.7 0.0 collective-permute-done.came1
  9.7 0.8 %collective-permute-done.1.came2 = f32[2,8,128]{2,1,0:T(8,128)S(1)} collective-permute-done((f32[2,8,128]{2,1,0:T(8,128)S(1)}, f32[2,8,128]{2,1,0:T(8,128)S(1)}, u32[]{:S(2)}, u32[]{:S(2)}) %collective-permute-start.1) | collective-permute-done | bytes 8224 | tf_op jit(solution)/shard_map/ppermute | solution.py:357
  10.5 0.9 %shard_map.39 = (f32[1024,128]{1,0:T(8,128)S(1)}, f32[7,16,128]{2,1,0:T(8,128)S(1)}) custom-call(f32[2,8,128]{2,1,0:T(8,128)S(1)} %collective-permute-done.came1, f32[2,8,128]{2,1,0:T(8,128)S(1)} %collective-permute-done.1.came2, f32[4,8,128]{2,1,0:T(8,128)S(1)} %get-tuple-element.31.mine, f32[1024,128]{1,0:T(8,128)S(1)} %get-tuple-element.35.source, ...), custom_call_target="tpu_custom_call" | custom-call | flops 100000 | bytes 100000 | tf_op jit(solution)/shard_map/pallas_call | solution.py:320
  11.5 0.1 collective-permute-start.2
  11.5 0.7 %shard_map.40.after.d = f32[64,16,128]{2,1,0:T(8,128)S(1)} custom-call(f32[1024,128]{1,0:T(8,128)S(1)} %get-tuple-element.40.s_in, f32[1024,128]{1,0:T(8,128)S(1)} %get-tuple-element.32.st, f32[64,16,128]{2,1,0:T(8,128)S(1)} %get-tuple-element.41.fx, f32[64,16,128]{2,1,0:T(8,128)S(1)} %get-tuple-element.42.ux), custom_call_target="tpu_custom_call" | custom-call | flops 3000000 | bytes 3000000 | tf_op jit(solution)/shard_map/pallas_call | solution.py:320
  12.3 0.5 %collective-permute-done.2.other = f32[7,16,128]{2,1,0:T(8,128)S(1)} collective-permute-done((f32[7,16,128]{2,1,0:T(8,128)S(1)}, f32[7,16,128]{2,1,0:T(8,128)S(1)}, u32[]{:S(2)}, u32[]{:S(2)}) %collective-permute-start.2) | collective-permute-done | bytes 57376 | tf_op jit(solution)/shard_map/ppermute | solution.py:364
  12.8 2.8 %collective-permute-start.5 = (f32[7,16,128]{2,1,0:T(8,128)S(1)}, f32[7,16,128]{2,1,0:T(8,128)S(1)}, u32[]{:S(2)}, u32[]{:S(2)}) collective-permute-start(f32[7,16,128]{2,1,0:T(8,128)S(1)} %get-tuple-element.43.own), channel_id=1, source_target_pairs={{0,96},{16,112},{32,64},{48,80},{64,32},{80,48},{96,0},{112,16},{1... | collective-permute-start | bytes 172040 | tf_op jit(solution)/shard_map/ppermute | solution.py:367
  15.6 0.8 %collective-permute-start.4 = (f32[7,16,128]{2,1,0:T(8,128)S(1)}, f32[7,16,128]{2,1,0:T(8,128)S(1)}, u32[]{:S(2)}, u32[]{:S(2)}) collective-permute-start(f32[7,16,128]{2,1,0:T(8,128)S(1)} %get-tuple-element.43.own), channel_id=1, source_target_pairs={{0,64},{16,80},{32,96},{48,112},{64,0},{80,16},{96,32},{112,48},{1... | collective-permute-start | bytes 172040 | tf_op jit(solution)/shard_map/ppermute | solution.py:367
  16.4 0.5 %collective-permute-start.3 = (f32[7,16,128]{2,1,0:T(8,128)S(1)}, f32[7,16,128]{2,1,0:T(8,128)S(1)}, u32[]{:S(2)}, u32[]{:S(2)}) collective-permute-start(f32[7,16,128]{2,1,0:T(8,128)S(1)} %get-tuple-element.43.own), channel_id=1, source_target_pairs={{0,32},{16,48},{32,0},{48,16},{64,96},{80,112},{96,64},{112,80},{1... | collective-permute-start | bytes 172040 | tf_op jit(solution)/shard_map/ppermute | solution.py:367
  17.0 1.8 %shard_map.42 = (f32[128,8,128]{2,1,0:T(8,128)S(1)}, f32[128,8,128]{2,1,0:T(8,128)S(1)}, f32[3,8,128]{2,1,0:T(8,128)S(1)}) custom-call(f32[1024,128]{1,0:T(8,128)S(1)} %get-tuple-element.45.ky_t, f32[2,8,128]{2,1,0:T(8,128)S(1)} %collective-permute-done.came1, f32[2,8,128]{2,1,0:T(8,128)S(1)} %collective-permute-done.1.came2, ...), custom_call_target="tpu_custom_call" | custom-call | flops 5000000 | bytes 5000000 | tf_op jit(solution)/shard_map/pallas_call | solution.py:320
  18.8 0.0 collective-permute-done.5.other3
  18.8 2.7 %collective-permute-done.4.other2 = f32[7,16,128]{2,1,0:T(8,128)S(1)} collective-permute-done((f32[7,16,128]{2,1,0:T(8,128)S(1)}, f32[7,16,128]{2,1,0:T(8,128)S(1)}, u32[]{:S(2)}, u32[]{:S(2)}) %collective-permute-start.4) | collective-permute-done | bytes 57376 | tf_op jit(solution)/shard_map/ppermute | solution.py:367
  21.5 0.0 collective-permute-done.3.other1
  21.5 1.4 %shard_map.43 = (f32[1024,128]{1,0:T(8,128)S(1)}, f32[16,5,8,128]{3,2,1,0:T(8,128)}) custom-call(f32[7,16,128]{2,1,0:T(8,128)S(1)} %get-tuple-element.43.own, f32[7,16,128]{2,1,0:T(8,128)S(1)} %collective-permute-done.3.other1, f32[7,16,128]{2,1,0:T(8,128)S(1)} %collective-permute-done.4.other2, f32[7,16,128]{2,1,0:T(8,128)S(1)} %collective-permute-done.5.other3, ...), custom_call_target="tpu_custom_call" | custom-call | flops 100000 | bytes 100000 | tf_op jit(solution)/shard_map/pallas_call | solution.py:320
  22.9 6.4 %all-to-all-start = ((f32[16,5,8,128]{3,2,1,0:T(8,128)}), f32[16,5,8,128]{3,2,1,0:T(8,128)S(1)}, u32[]{:S(2)}, u32[]{:S(2)}) async-start(f32[16,5,8,128]{3,2,1,0:T(8,128)} %get-tuple-element.49), calls=%async_computation | async-start | bytes 655360 | tf_op jit(solution)/shard_map/all_to_all | solution.py:385
  29.2 2.0 %shard_map.44 = (f32[128,8,128]{2,1,0:T(8,128)S(1)}, f32[1024,128]{1,0:T(8,128)S(1)}) custom-call(f32[1024,128]{1,0:T(8,128)S(1)} %get-tuple-element.50.v_t, f32[1024,128]{1,0:T(8,128)S(1)} %get-tuple-element.45.ky_t, f32[1024,128]{1,0:T(8,128)} %bitcast.5), custom_call_target="tpu_custom_call" | custom-call | flops 5000000 | bytes 5000000 | tf_op jit(solution)/shard_map/pallas_call | solution.py:320
  31.2 6.8 %all-to-all-done.blocks = f32[16,5,8,128]{3,2,1,0:T(8,128)S(1)} async-done(((f32[16,5,8,128]{3,2,1,0:T(8,128)}), f32[16,5,8,128]{3,2,1,0:T(8,128)S(1)}, u32[]{:S(2)}, u32[]{:S(2)}) %all-to-all-start) | async-done | bytes 327712 | tf_op jit(solution)/shard_map/all_to_all | solution.py:385
  38.1 1.3 %shard_map.45 = f32[1024,128]{1,0:T(8,128)} custom-call(f32[16,5,8,128]{3,2,1,0:T(8,128)S(1)} %all-to-all-done.blocks, f32[128,8,128]{2,1,0:T(8,128)S(1)} %get-tuple-element.51.g_t, f32[128,8,128]{2,1,0:T(8,128)S(1)} %get-tuple-element.46.yf, f32[128,8,128]{2,1,0:T(8,128)S(1)} %get-tuple-element.47.yl, f32[1024,128]{1,0:T(8,128)S(1)} %get-tuple-element.52.st), custom_call_target="tpu_custom_call" | custom-call | flops 100000 | bytes 100000 | tf_op jit(solution)/shard_map/pallas_call | solution.py:320
  (1 shorter events, 0.0 us)
Async XLA Ops:
  1.5 8.2 %collective-permute-start = (f32[2,8,128]{2,1,0:T(8,128)S(1)}, f32[2,8,128]{2,1,0:T(8,128)S(1)}, u32[]{:S(2)}, u32[]{:S(2)}) collective-permute-start(f32[2,8,128]{2,1,0:T(8,128)S(1)} %get-tuple-element.29), channel_id=1, source_target_pairs={{0,1},{1,0},{2,3},{3,2},{4,5},{5,4},{6,7},{7,6},{8,9},{9,8},{10,11... | collective-permute-start | bytes 24584 | tf_op jit(solution)/shard_map/ppermute | solution.py:356
  3.6 7.0 %collective-permute-start.1 = (f32[2,8,128]{2,1,0:T(8,128)S(1)}, f32[2,8,128]{2,1,0:T(8,128)S(1)}, u32[]{:S(2)}, u32[]{:S(2)}) collective-permute-start(f32[2,8,128]{2,1,0:T(8,128)S(1)} %get-tuple-element.30), channel_id=1, source_target_pairs={{0,15},{1,2},{2,1},{3,4},{4,3},{5,6},{6,5},{7,8},{8,7},{9,10},{10,... | collective-permute-start | bytes 24584 | tf_op jit(solution)/shard_map/ppermute | solution.py:357
  11.5 1.3 %collective-permute-start.2 = (f32[7,16,128]{2,1,0:T(8,128)S(1)}, f32[7,16,128]{2,1,0:T(8,128)S(1)}, u32[]{:S(2)}, u32[]{:S(2)}) collective-permute-start(f32[7,16,128]{2,1,0:T(8,128)S(1)} %get-tuple-element.39.own), channel_id=1, source_target_pairs={{0,16},{16,0},{32,48},{48,32},{64,80},{80,64},{96,112},{112,96},{1... | collective-permute-start | bytes 172040 | tf_op jit(solution)/shard_map/ppermute | solution.py:364
  12.8 6.0 %collective-permute-start.5 = (f32[7,16,128]{2,1,0:T(8,128)S(1)}, f32[7,16,128]{2,1,0:T(8,128)S(1)}, u32[]{:S(2)}, u32[]{:S(2)}) collective-permute-start(f32[7,16,128]{2,1,0:T(8,128)S(1)} %get-tuple-element.43.own), channel_id=1, source_target_pairs={{0,96},{16,112},{32,64},{48,80},{64,32},{80,48},{96,0},{112,16},{1... | collective-permute-start | bytes 172040 | tf_op jit(solution)/shard_map/ppermute | solution.py:367
  15.6 5.8 %collective-permute-start.4 = (f32[7,16,128]{2,1,0:T(8,128)S(1)}, f32[7,16,128]{2,1,0:T(8,128)S(1)}, u32[]{:S(2)}, u32[]{:S(2)}) collective-permute-start(f32[7,16,128]{2,1,0:T(8,128)S(1)} %get-tuple-element.43.own), channel_id=1, source_target_pairs={{0,64},{16,80},{32,96},{48,112},{64,0},{80,16},{96,32},{112,48},{1... | collective-permute-start | bytes 172040 | tf_op jit(solution)/shard_map/ppermute | solution.py:367
  16.4 5.0 %collective-permute-start.3 = (f32[7,16,128]{2,1,0:T(8,128)S(1)}, f32[7,16,128]{2,1,0:T(8,128)S(1)}, u32[]{:S(2)}, u32[]{:S(2)}) collective-permute-start(f32[7,16,128]{2,1,0:T(8,128)S(1)} %get-tuple-element.43.own), channel_id=1, source_target_pairs={{0,32},{16,48},{32,0},{48,16},{64,96},{80,112},{96,64},{112,80},{1... | collective-permute-start | bytes 172040 | tf_op jit(solution)/shard_map/ppermute | solution.py:367
  22.9 15.2 %all-to-all-start = ((f32[16,5,8,128]{3,2,1,0:T(8,128)}), f32[16,5,8,128]{3,2,1,0:T(8,128)S(1)}, u32[]{:S(2)}, u32[]{:S(2)}) async-start(f32[16,5,8,128]{3,2,1,0:T(8,128)} %get-tuple-element.49), calls=%async_computation | async-start | bytes 655360 | tf_op jit(solution)/shard_map/all_to_all | solution.py:385

commit v6 on v5

--- a/solution.py
+++ b/solution.py
@@ -10,6 +10,7 @@
 ROWS = NZ * BX
 GROUPS = ROWS // 128
 LIMIT = 8 * 1024 * 1024
+CHUNKS = 4
 
 
 def inverse(x):
@@ -50,24 +51,39 @@
 
 
 def flows_of(count, pivot, lower, upper, gain, slots):
-    gamma = rho = None
-    gammas, rhos = [], []
-    for i in range(count + 1):
-        if i == 0:
-            inv = inverse(pivot(i))
-            rho = gain(i) * inv
-        else:
-            inv = inverse(pivot(i) - lower(i) * gamma)
-            rho = (gain(i) + lower(i) * rho) * inv
-        if i < count:
-            gamma = upper(i) * inv
-            gammas.append(gamma)
-        rhos.append(rho)
-    flow = rhos[count]
-    slots[count] = flow
-    for i in range(count - 1, -1, -1):
-        flow = rhos[i] + gammas[i] * flow
-        slots[i] = flow
+    half = (count + 1) // 2
+    up, down = {}, {}
+    for n in range(half + 1):
+        i = n
+        if i < half:
+            gain_i, pivot_i = gain(i), pivot(i)
+            if i:
+                gain_i = gain_i + lower(i) * up[i - 1][0]
+                pivot_i = pivot_i - lower(i) * up[i - 1][1]
+            inv = inverse(pivot_i)
+            up[i] = gain_i * inv, upper(i) * inv
+        i = count - n
+        if i > half:
+            gain_i, pivot_i = gain(i), pivot(i)
+            if n:
+                gain_i = gain_i + upper(i) * down[i + 1][0]
+                pivot_i = pivot_i - upper(i) * down[i + 1][1]
+            inv = inverse(pivot_i)
+            down[i] = gain_i * inv, lower(i) * inv
+    below, above = up[half - 1], down[half + 1]
+    low, high = lower(half), upper(half)
+    flow = (gain(half) + low * below[0] + high * above[0]) * inverse(
+        pivot(half) - low * below[1] - high * above[1]
+    )
+    slots[half] = flow
+    rising = flow
+    for n in range(1, half + 1):
+        if half - n >= 0:
+            flow = up[half - n][0] + up[half - n][1] * flow
+            slots[half - n] = flow
+        if half + n <= count:
+            rising = down[half + n][0] + down[half + n][1] * rising
+            slots[half + n] = rising
 
 
 def x_flows(own, others, place, blocks, slots):
@@ -108,18 +124,27 @@
 
 
 def load_kernel(st_hbm, kx_hbm, ky_hbm, st, kx, ky, ky_t, mine, first, second, sems):
-    moves = [
-        pltpu.make_async_copy(src, dst, sems.at[n])
-        for n, (src, dst) in enumerate(((ky_hbm, ky), (st_hbm, st), (kx_hbm, kx)))
-    ]
-    for move in moves:
-        move.start()
-    moves[0].wait()
+    chunk = ROWS // CHUNKS
+    waits = []
+    for c in range(CHUNKS):
+        rows = pl.ds(c * chunk, chunk)
+        waits.append(
+            [
+                pltpu.make_async_copy(src.at[rows], dst.at[rows], sems.at[2 * c + n])
+                for n, (src, dst) in enumerate(((ky_hbm, ky), (st_hbm, st)))
+            ]
+        )
+        for move in waits[-1]:
+            move.start()
+    rest = pltpu.make_async_copy(kx_hbm, kx, sems.at[2 * CHUNKS])
+    rest.start()
     for g in range(GROUPS):
-        ky_t[pl.ds(g, BY, stride=GROUPS), :] = ky[pl.ds(g * 128, 128), :].T
-    moves[1].wait()
-    for g in range(GROUPS):
-        turned = st[pl.ds(g * 128, 128), :].T
+        if g * CHUNKS % GROUPS == 0:
+            for move in waits[g * CHUNKS // GROUPS]:
+                move.wait()
+        rows = pl.ds(g * 128, 128)
+        ky_t[pl.ds(g, BY, stride=GROUPS), :] = ky[rows, :].T
+        turned = st[rows, :].T
         mine[0, pl.ds(g, 1), :] = turned[0:1, :]
         mine[2, pl.ds(g, 1), :] = turned[127:128, :]
     mine[1] = ky_t[pl.ds(0, GROUPS), :]
@@ -128,10 +153,10 @@
     low, high = mine[0:2], mine[2:4]
     first[...] = jnp.where(even, high, low)
     second[...] = jnp.where(even, low, high)
-    moves[2].wait()
-
-
-def sweep(count, row, f, u, first, last):
+    rest.wait()
+
+
+def sweep(count, row, f, u, ratios, put_first, put_last):
     ahead = jnp.ones_like(row(0))
     back = jnp.ones_like(ahead)
     low, high = row(0), row(count - 1)
@@ -150,27 +175,24 @@
         high = prev
         ratio = r * inverse(r + back)
         back = 1.0 + ratio * back
-        first[j] = ratio
+        ratios[j] = ratio
     start = inverse(back)
     end = inverse(ahead)
     lead, trail = start, end
-    first[0] = start
-    last[count - 1] = end
+    put_first(0, start)
+    put_last(count - 1, end)
     u[count - 1] = end
     f[count - 1] = jnp.zeros_like(end)
     for i in range(1, count):
-        start = start * first[i]
-        first[i] = start
+        start = start * ratios[i]
+        put_first(i, start)
         j = count - 1 - i
         end = end * f[j]
-        last[j] = end
+        put_last(j, end)
     return lead, end, trail
 
 
-def x_matrix_kernel(st, kx, ky, fx, ux, wf, wl, mx, source):
-    values = sweep(BX, lambda i: x_row(kx, i), fx, ux, wf, wl)
-    for n, value in enumerate(values + (x_row(kx, 0), x_row(kx, BX - 1))):
-        mx[n] = value
+def x_matrix_kernel(st, kx, ky, fx, ux, wf, wl, part, edges, source, ratios):
     lane = lax.broadcasted_iota(jnp.int32, (128, 128), 1)
     for g in range(GROUPS):
         rows = pl.ds(g * 128, 128)
@@ -179,12 +201,36 @@
         flux = 0.5 * (k + pltpu.roll(k, 127, 1)) * (pltpu.roll(s, 127, 1) - s)
         flux = jnp.where(lane == 127, 0.0, flux)
         source[rows, :] = s + flux - pltpu.roll(flux, 1, 1)
-
-
-def y_matrix_kernel(ky_t, came1, came2, after, yf, yl, my, f, u):
+    sums = [[jnp.zeros((NZ, BY), F32) for _ in range(2)] for _ in range(2)]
+
+    def put(ref, total):
+        def store(i, value):
+            place_rows(ref, i, value)
+            total[i % 2] = total[i % 2] + value * x_row(source, i)
+
+        return store
+
+    values = sweep(BX, lambda i: x_row(kx, i), fx, ux, ratios, put(wf, sums[0]), put(wl, sums[1]))
+    values += (x_row(kx, 0), x_row(kx, BX - 1), sums[0][0] + sums[0][1], sums[1][0] + sums[1][1])
+    for n, value in enumerate(values):
+        part[n] = value
+    for n, ref in enumerate((wf, wl)):
+        for g in range(GROUPS):
+            turned = ref[pl.ds(g * 128, 128), :].T
+            edges[2 * n, pl.ds(g, 1), :] = turned[0:1, :]
+            edges[2 * n + 1, pl.ds(g, 1), :] = turned[127:128, :]
+
+
+def y_matrix_kernel(ky_t, came2, came1, after, yf, yl, my, f, u, ratios):
+    def put(ref):
+        def store(j, value):
+            ref[j] = value
+
+        return store
+
     me = lax.axis_index("gy")
     last = lax.axis_size("gy") - 1
-    lead, across, trail = sweep(BY, lambda j: y_row(ky_t, j), f, u, yf, yl)
+    lead, across, trail = sweep(BY, lambda j: y_row(ky_t, j), f, u, ratios, put(yf), put(yl))
     below = jnp.where(lax.rem(me, 2) == 0, came2[1], came1[1])
     below = jnp.where(me == 0, 0.0, below)
     my[0] = lead + 2.0 * inverse(below + y_row(ky_t, 0))
@@ -192,14 +238,31 @@
     my[2] = trail + jnp.where(me == last, 2.0 * inverse(y_row(ky_t, BY - 1)), 0.0)
 
 
-def x_ends_kernel(came1, came2, mine, source, wf, wl, mx, s_out, send):
+def x_ends_kernel(came2, came1, mine, part, edges, send, flux, rows):
     me = lax.axis_index("gy")
     even = lax.rem(me, 2) == 0
     below = jnp.where(me == 0, 0.0, jnp.where(even, came2[...], came1[...]))
     above = jnp.where(me == lax.axis_size("gy") - 1, 0.0, jnp.where(even, came1[...], came2[...]))
-    flux_l = 0.5 * (below[1] + mine[1]) * (mine[0] - below[0])
-    flux_r = 0.5 * (above[1] + mine[3]) * (above[0] - mine[2])
-    both = jnp.concatenate([flux_l, flux_r], axis=0)
+    enter = 0.5 * (below[1] + mine[1]) * (mine[0] - below[0])
+    leave = 0.5 * (above[1] + mine[3]) * (above[0] - mine[2])
+    flux[0] = enter
+    flux[1] = leave
+    lane = lax.broadcasted_iota(jnp.int32, (GROUPS, 128), 1)
+    send[0:5] = part[0:5]
+    for n in range(2):
+        low = -edges[2 * n] * enter
+        high = edges[2 * n + 1] * leave
+        for h in range(2):
+            inside = lane // BX == h
+            at_low = jnp.sum(jnp.where(inside, low, 0.0), axis=1, keepdims=True)
+            at_high = jnp.sum(jnp.where(inside, high, 0.0), axis=1, keepdims=True)
+            value = jnp.where(lane == 0, at_low, jnp.where(lane == 127, at_high, 0.0))
+            rows[n, pl.ds(h, GROUPS, stride=2), :] = value
+        send[5 + n] = part[5 + n] + rows[n]
+
+
+def x_local_kernel(source, flux, st, fx, ux, d, s, work):
+    both = jnp.concatenate([flux[0], flux[1]], axis=0)
     turned = jnp.concatenate([both] * 8, axis=0).T
     lane = lax.broadcasted_iota(jnp.int32, (128, 128), 1)
     for g in range(GROUPS):
@@ -207,28 +270,16 @@
         left = jnp.broadcast_to(turned[:, g : g + 1], (128, 128))
         right = jnp.broadcast_to(turned[:, 8 + g : 9 + g], (128, 128))
         extra = jnp.where(lane == 0, -left, jnp.where(lane == 127, right, 0.0))
-        s_out[rows, :] = source[rows, :] + extra
-    firsts = [jnp.zeros((NZ, BY), F32) for _ in range(2)]
-    lasts = [jnp.zeros((NZ, BY), F32) for _ in range(2)]
-    for i in range(BX):
-        s = x_row(s_out, i)
-        firsts[i % 2] = firsts[i % 2] + wf[i] * s
-        lasts[i % 2] = lasts[i % 2] + wl[i] * s
-    send[0:5] = mx[...]
-    send[5] = firsts[0] + firsts[1]
-    send[6] = lasts[0] + lasts[1]
-
-
-def x_local_kernel(s_in, st, fx, ux, d):
-    total = x_row(s_in, 0)
-    d[0] = total
+        s[rows, :] = source[rows, :] + extra
+    total = x_row(s, 0)
+    work[0] = total
     for i in range(1, BX):
-        total = x_row(s_in, i) + fx[i - 1] * total
-        d[i] = total
+        total = x_row(s, i) + fx[i - 1] * total
+        work[i] = total
     x = jnp.zeros_like(total)
     for i in range(BX - 1, -1, -1):
-        x = ux[i] * d[i] + fx[i] * x
-        d[i] = x - x_row(st, i)
+        x = ux[i] * work[i] + fx[i] * x
+        place_rows(d, i, x - x_row(st, i))
 
 
 def x_merge_kernel(own, other, after, send, coefs):
@@ -244,7 +295,7 @@
 
 
 def y_ends_kernel(
-    own, other1, other2, other3, coefs, d, wf, wl, yf, yl, my, v_t, send, blocks, slots, v
+    own, other1, other2, other3, coefs, d, wf, wl, yf, yl, my, v_t, send, blocks, slots, flows
 ):
     me = lax.axis_index("gx")
     place = lax.div(me, 2)
@@ -252,11 +303,18 @@
     enter, leave = slots[place], slots[place + 1]
     middle = coefs[0] + coefs[1] * enter + coefs[2] * leave
     low = lax.rem(me, 2) == 0
-    enter, leave = jnp.where(low, enter, middle), jnp.where(low, middle, leave)
-    for i in range(BX):
-        place_rows(v, i, d[i] + wf[i] * enter - wl[i] * leave)
+    flows[0] = jnp.where(low, enter, middle)
+    flows[1] = jnp.where(low, middle, leave)
     for g in range(GROUPS):
-        v_t[pl.ds(g, BY, stride=GROUPS), :] = v[pl.ds(g * 128, 128), :].T
+        parts = []
+        for z in range(2 * g, 2 * g + 2):
+            rows = pl.ds(z * BX, BX)
+            parts.append(
+                d[rows, :]
+                + wf[rows, :] * flows[0, pl.ds(z, 1), :]
+                - wl[rows, :] * flows[1, pl.ds(z, 1), :]
+            )
+        v_t[pl.ds(g, BY, stride=GROUPS), :] = jnp.concatenate(parts, axis=0).T
     firsts = [jnp.zeros((GROUPS, 128), F32) for _ in range(4)]
     lasts = [jnp.zeros((GROUPS, 128), F32) for _ in range(4)]
     for j in range(BY):
@@ -351,25 +409,43 @@
         load_kernel,
         near(plane, plane, plane, plane, (4, GROUPS, 128), edge, edge),
         [(a, True) for a in flat],
-        [pltpu.SemaphoreType.DMA((3,))],
-    )
+        [pltpu.SemaphoreType.DMA((2 * CHUNKS + 1,))],
+    )
+    pairs = [
+        (i * ny + j, i * ny + j + 2 * (j % 2) - 1 if 0 < j < ny - 1 else (i ^ 1) * ny + j)
+        for i in range(nx)
+        for j in range(ny)
+    ]
+    came2 = lax.ppermute(second, ("gx", "gy"), pairs)
     came1 = lax.ppermute(first, "gy", [(i, i ^ 1) for i in range(ny)])
-    came2 = lax.ppermute(second, "gy", [(i, (i + 2 * (i % 2) - 1) % ny) for i in range(ny)])
-    fx, ux, wf, wl, mx, source = call(
-        x_matrix_kernel, near(xs, xs, xs, xs, (5, NZ, BY), plane), near(st, kx, ky), cost=5_000_000
-    )
-    s, ends = call(
-        x_ends_kernel, near(plane, x_block), near(came1, came2, mine, source, wf, wl, mx)
+    fx, ux, wf, wl, part, edges, source = call(
+        x_matrix_kernel,
+        near(xs, xs, plane, plane, x_block, (4, GROUPS, 128), plane),
+        near(st, kx, ky),
+        [pltpu.VMEM(xs, F32)],
+        cost=5_000_000,
+    )
+    ends, flux = call(
+        x_ends_kernel,
+        near(x_block, edge),
+        near(came2, came1, mine, part, edges),
+        [pltpu.VMEM((2, NZ, BY), F32)],
     )
     other = lax.ppermute(ends, "gx", [(i, i ^ 1) for i in range(nx)])
-    (d,) = call(x_local_kernel, near(xs), near(s, st, fx, ux), cost=3_000_000)
+    (d,) = call(
+        x_local_kernel,
+        near(plane),
+        near(source, flux, st, fx, ux),
+        [pltpu.VMEM(plane, F32), pltpu.VMEM(xs, F32)],
+        cost=3_000_000,
+    )
     chip, coefs = call(x_merge_kernel, near(x_block, (3, NZ, BY)), near(ends, other, d))
     others = [lax.ppermute(chip, "gx", [(i, i ^ (2 * k)) for i in range(nx)]) for k in range(1, chips)]
     yf, yl, my = call(
         y_matrix_kernel,
         near(ys, ys, (3, GROUPS, 128)),
-        near(ky_t, came1, came2, coefs),
-        [pltpu.VMEM(ys, F32), pltpu.VMEM(ys, F32)],
+        near(ky_t, came2, came1, coefs),
+        [pltpu.VMEM(ys, F32)] * 3,
         cost=5_000_000,
     )
     v_t, send = call(
@@ -379,7 +455,7 @@
         [
             pltpu.VMEM((chips,) + x_block, F32),
             pltpu.VMEM((chips + 1, NZ, BY), F32),
-            pltpu.VMEM(plane, F32),
+            pltpu.VMEM((2, NZ, BY), F32),
         ],
     )
     y_blocks = lax.all_to_all(send, "gy", 0, 0)

time: 39.6 us -> 37.6 us (0.949)
  starting transfers between devices: 17.7 us -> 15.3 us
  Pallas kernels: 10.8 us -> 12.1 us
  waiting for transfers between devices: 10.8 us -> 9.85 us
    ppermute x1, starting transfers between devices: 4.97 us -> 0.09 us  [on_device(): came2 = lax.ppermute(second, ('gx', 'gy'), pairs)]
    ppermute x1, starting transfers between devices: 2.08 us -> 3.91 us  [on_device(): came1 = lax.ppermute(first, 'gy', [(i, i ^ 1) for i in range(ny)])]
    pallas_call x9, Pallas kernels: 10.8 us -> 12.1 us  [call(): pl.pallas_call(kernel, out_shape=[jax.ShapeDtypeStruct(shape, F32) if far...]
    ppermute x1, waiting for transfers between devices: 0.81 us -> 0.01 us  [on_device(): came2 = lax.ppermute(second, ('gx', 'gy'), pairs)]
    all_to_all x1, starting transfers between devices: 6.35 us -> 7.13 us  [on_device(): y_blocks = lax.all_to_all(send, 'gy', 0, 0)]
    ppermute x1, waiting for transfers between devices: 0.5 us -> 0.01 us  [on_device(): other = lax.ppermute(ends, 'gx', [(i, i ^ 1) for i in range(nx)])]
  transfers between devices with their start and end apart: 7 -> 7, of which waited for: 4 -> 2; matrix products, arithmetic and copies ran while one was open for 0% -> 0% of each run, Pallas kernels for 14% -> 21%
where the time goes in v6:
time: 37.6 us; the launch traced here: 37.4 us
  starting transfers between devices  15.3 us (41%)
  Pallas kernels  12.1 us (32%)
  waiting for transfers between devices  9.85 us (26%)
    pallas_call x9, Pallas kernels, call(): pl.pallas_call(kernel, out_shape=[jax.ShapeDtypeStruct(shape, F32) if far...  12.1 us
    all_to_all x1, starting transfers between devices, on_device(): y_blocks = lax.all_to_all(send, 'gy', 0, 0)  7.13 us
    all_to_all x1, waiting for transfers between devices, on_device(): y_blocks = lax.all_to_all(send, 'gy', 0, 0)  6.85 us
    ppermute x3, starting transfers between devices, on_device(): lax.ppermute(chip, 'gx', [(i, i ^ 2 * k) for i in range(nx)])  4.17 us
    ppermute x1, starting transfers between devices, on_device(): came1 = lax.ppermute(first, 'gy', [(i, i ^ 1) for i in range(ny)])  3.91 us
    ppermute x3, waiting for transfers between devices, on_device(): lax.ppermute(chip, 'gx', [(i, i ^ 2 * k) for i in range(nx)])  2.99 us
  transfers between devices with their start and end apart: 7, of which 2 were waited for; matrix products, arithmetic and copies ran while one was open for 0% of the time, Pallas kernels for 21%

profile of v6, /device:TPU:0, one launch (start us, length us, event | category | flops | bytes accessed | tf_op | source)
XLA Modules:
  0.0 37.4 jit_solution(15491818750033782934)
XLA Ops:
  0.0 1.6 %shard_map.37 = (f32[1024,128]{1,0:T(8,128)S(1)}, f32[1024,128]{1,0:T(8,128)S(1)}, f32[1024,128]{1,0:T(8,128)S(1)}, f32[1024,128]{1,0:T(8,128)S(1)}, f32[4,8,128...) custom-call(f32[1024,128]{1,0:T(8,128)} %bitcast.4, f32[1024,128]{1,0:T(8,128)} %bitcast.6, ...), custom_call_target="tpu_custom_call" | custom-call | flops 100000 | bytes 100000 | tf_op jit(solution)/shard_map/pallas_call | solution.py:378
  1.7 0.1 collective-permute-start
  1.7 3.9 %collective-permute-start.1 = (f32[2,8,128]{2,1,0:T(8,128)S(1)}, f32[2,8,128]{2,1,0:T(8,128)S(1)}, u32[]{:S(2)}, u32[]{:S(2)}) collective-permute-start(f32[2,8,128]{2,1,0:T(8,128)S(1)} %get-tuple-element.31), channel_id=1, source_target_pairs={{0,1},{1,0},{2,3},{3,2},{4,5},{5,4},{6,7},{7,6},{8,9},{9,8},{10,11... | collective-permute-start | bytes 24584 | tf_op jit(solution)/shard_map/ppermute | solution.py:420
  5.7 2.8 %shard_map.38 = (f32[64,16,128]{2,1,0:T(8,128)S(1)}, f32[64,16,128]{2,1,0:T(8,128)S(1)}, f32[1024,128]{1,0:T(8,128)S(1)}, f32[1024,128]{1,0:T(8,128)S(1)}, f32[7...) custom-call(f32[1024,128]{1,0:T(8,128)S(1)} %get-tuple-element.33.st, ...), custom_call_target="tpu_custom_call" | custom-call | flops 5000000 | bytes 5000000 | tf_op jit(solution)/shard_map/pallas_call | solution.py:378
  8.5 0.0 collective-permute-done.came2
  8.5 0.0 collective-permute-done.1.came1
  8.5 0.1 shard_map.39
  8.6 0.0 collective-permute-start.2
  8.7 1.4 %shard_map.40.after.d = f32[1024,128]{1,0:T(8,128)S(1)} custom-call(f32[1024,128]{1,0:T(8,128)S(1)} %get-tuple-element.39.source, f32[2,8,128]{2,1,0:T(8,128)S(1)} %get-tuple-element.40.flux, f32[1024,128]{1,0:T(8,128)S(1)} %get-tuple-element.33.st, f32[64,16,128]{2,1,0:T(8,128)S(1)} %get-tuple-element.41.fx, f32[64,16,128]{2,1,0:T(8,128)S(1)} %get-tuple-element.42.ux), custom_call_target="tpu_custom_call" | custom-call | flops 3000000 | bytes 3000000 | tf_op jit(solution)/shard_map/pallas_call | solution.py:378
  10.1 0.0 collective-permute-done.2.other
  10.2 2.8 %collective-permute-start.5 = (f32[7,16,128]{2,1,0:T(8,128)S(1)}, f32[7,16,128]{2,1,0:T(8,128)S(1)}, u32[]{:S(2)}, u32[]{:S(2)}) collective-permute-start(f32[7,16,128]{2,1,0:T(8,128)S(1)} %get-tuple-element.43.own), channel_id=1, source_target_pairs={{0,96},{16,112},{32,64},{48,80},{64,32},{80,48},{96,0},{112,16},{1... | collective-permute-start | bytes 172040 | tf_op jit(solution)/shard_map/ppermute | solution.py:443
  13.0 0.8 %collective-permute-start.4 = (f32[7,16,128]{2,1,0:T(8,128)S(1)}, f32[7,16,128]{2,1,0:T(8,128)S(1)}, u32[]{:S(2)}, u32[]{:S(2)}) collective-permute-start(f32[7,16,128]{2,1,0:T(8,128)S(1)} %get-tuple-element.43.own), channel_id=1, source_target_pairs={{0,64},{16,80},{32,96},{48,112},{64,0},{80,16},{96,32},{112,48},{1... | collective-permute-start | bytes 172040 | tf_op jit(solution)/shard_map/ppermute | solution.py:443
  13.8 0.5 %collective-permute-start.3 = (f32[7,16,128]{2,1,0:T(8,128)S(1)}, f32[7,16,128]{2,1,0:T(8,128)S(1)}, u32[]{:S(2)}, u32[]{:S(2)}) collective-permute-start(f32[7,16,128]{2,1,0:T(8,128)S(1)} %get-tuple-element.43.own), channel_id=1, source_target_pairs={{0,32},{16,48},{32,0},{48,16},{64,96},{80,112},{96,64},{112,80},{1... | collective-permute-start | bytes 172040 | tf_op jit(solution)/shard_map/ppermute | solution.py:443
  14.3 1.8 %shard_map.42 = (f32[128,8,128]{2,1,0:T(8,128)S(1)}, f32[128,8,128]{2,1,0:T(8,128)S(1)}, f32[3,8,128]{2,1,0:T(8,128)S(1)}) custom-call(f32[1024,128]{1,0:T(8,128)S(1)} %get-tuple-element.47.ky_t, f32[2,8,128]{2,1,0:T(8,128)S(1)} %collective-permute-done.came2, f32[2,8,128]{2,1,0:T(8,128)S(1)} %collective-permute-done.1.came1, ...), custom_call_target="tpu_custom_call" | custom-call | flops 5000000 | bytes 5000000 | tf_op jit(solution)/shard_map/pallas_call | solution.py:378
  16.1 0.0 collective-permute-done.5.other3
  16.2 3.0 %collective-permute-done.4.other2 = f32[7,16,128]{2,1,0:T(8,128)S(1)} collective-permute-done((f32[7,16,128]{2,1,0:T(8,128)S(1)}, f32[7,16,128]{2,1,0:T(8,128)S(1)}, u32[]{:S(2)}, u32[]{:S(2)}) %collective-permute-start.4) | collective-permute-done | bytes 57376 | tf_op jit(solution)/shard_map/ppermute | solution.py:443
  19.1 0.0 collective-permute-done.3.other1
  19.1 1.1 %shard_map.43 = (f32[1024,128]{1,0:T(8,128)S(1)}, f32[16,5,8,128]{3,2,1,0:T(8,128)}) custom-call(f32[7,16,128]{2,1,0:T(8,128)S(1)} %get-tuple-element.43.own, f32[7,16,128]{2,1,0:T(8,128)S(1)} %collective-permute-done.3.other1, f32[7,16,128]{2,1,0:T(8,128)S(1)} %collective-permute-done.4.other2, f32[7,16,128]{2,1,0:T(8,128)S(1)} %collective-permute-done.5.other3, ...), custom_call_target="tpu_custom_call" | custom-call | flops 100000 | bytes 100000 | tf_op jit(solution)/shard_map/pallas_call | solution.py:378
  20.3 7.1 %all-to-all-start = ((f32[16,5,8,128]{3,2,1,0:T(8,128)}), f32[16,5,8,128]{3,2,1,0:T(8,128)S(1)}, u32[]{:S(2)}, u32[]{:S(2)}) async-start(f32[16,5,8,128]{3,2,1,0:T(8,128)} %get-tuple-element.51), calls=%async_computation | async-start | bytes 655360 | tf_op jit(solution)/shard_map/all_to_all | solution.py:461
  27.4 2.0 %shard_map.44 = (f32[128,8,128]{2,1,0:T(8,128)S(1)}, f32[1024,128]{1,0:T(8,128)S(1)}) custom-call(f32[1024,128]{1,0:T(8,128)S(1)} %get-tuple-element.52.v_t, f32[1024,128]{1,0:T(8,128)S(1)} %get-tuple-element.47.ky_t, f32[1024,128]{1,0:T(8,128)} %bitcast.5), custom_call_target="tpu_custom_call" | custom-call | flops 5000000 | bytes 5000000 | tf_op jit(solution)/shard_map/pallas_call | solution.py:378
  29.4 6.8 %all-to-all-done.blocks = f32[16,5,8,128]{3,2,1,0:T(8,128)S(1)} async-done(((f32[16,5,8,128]{3,2,1,0:T(8,128)}), f32[16,5,8,128]{3,2,1,0:T(8,128)S(1)}, u32[]{:S(2)}, u32[]{:S(2)}) %all-to-all-start) | async-done | bytes 327712 | tf_op jit(solution)/shard_map/all_to_all | solution.py:461
  36.2 1.2 %shard_map.45 = f32[1024,128]{1,0:T(8,128)} custom-call(f32[16,5,8,128]{3,2,1,0:T(8,128)S(1)} %all-to-all-done.blocks, f32[128,8,128]{2,1,0:T(8,128)S(1)} %get-tuple-element.53.g_t, f32[128,8,128]{2,1,0:T(8,128)S(1)} %get-tuple-element.48.yf, f32[128,8,128]{2,1,0:T(8,128)S(1)} %get-tuple-element.49.yl, f32[1024,128]{1,0:T(8,128)S(1)} %get-tuple-element.54.st), custom_call_target="tpu_custom_call" | custom-call | flops 100000 | bytes 100000 | tf_op jit(solution)/shard_map/pallas_call | solution.py:378
  (1 shorter events, 0.0 us)
Async XLA Ops:
  1.7 6.8 %collective-permute-start = (f32[2,8,128]{2,1,0:T(8,128)S(1)}, f32[2,8,128]{2,1,0:T(8,128)S(1)}, u32[]{:S(2)}, u32[]{:S(2)}) collective-permute-start(f32[2,8,128]{2,1,0:T(8,128)S(1)} %get-tuple-element.30), channel_id=1, source_target_pairs={{0,16},{1,2},{2,1},{3,4},{4,3},{5,6},{6,5},{7,8},{8,7},{9,10},{10,... | collective-permute-start | bytes 24584 | tf_op jit(solution)/shard_map/ppermute | solution.py:419
  1.7 6.7 %collective-permute-start.1 = (f32[2,8,128]{2,1,0:T(8,128)S(1)}, f32[2,8,128]{2,1,0:T(8,128)S(1)}, u32[]{:S(2)}, u32[]{:S(2)}) collective-permute-start(f32[2,8,128]{2,1,0:T(8,128)S(1)} %get-tuple-element.31), channel_id=1, source_target_pairs={{0,1},{1,0},{2,3},{3,2},{4,5},{5,4},{6,7},{7,6},{8,9},{9,8},{10,11... | collective-permute-start | bytes 24584 | tf_op jit(solution)/shard_map/ppermute | solution.py:420
  8.6 1.5 %collective-permute-start.2 = (f32[7,16,128]{2,1,0:T(8,128)S(1)}, f32[7,16,128]{2,1,0:T(8,128)S(1)}, u32[]{:S(2)}, u32[]{:S(2)}) collective-permute-start(f32[7,16,128]{2,1,0:T(8,128)S(1)} %get-tuple-element.38.own), channel_id=1, source_target_pairs={{0,16},{16,0},{32,48},{48,32},{64,80},{80,64},{96,112},{112,96},{1... | collective-permute-start | bytes 172040 | tf_op jit(solution)/shard_map/ppermute | solution.py:434
  10.2 6.0 %collective-permute-start.5 = (f32[7,16,128]{2,1,0:T(8,128)S(1)}, f32[7,16,128]{2,1,0:T(8,128)S(1)}, u32[]{:S(2)}, u32[]{:S(2)}) collective-permute-start(f32[7,16,128]{2,1,0:T(8,128)S(1)} %get-tuple-element.43.own), channel_id=1, source_target_pairs={{0,96},{16,112},{32,64},{48,80},{64,32},{80,48},{96,0},{112,16},{1... | collective-permute-start | bytes 172040 | tf_op jit(solution)/shard_map/ppermute | solution.py:443
  13.0 6.2 %collective-permute-start.4 = (f32[7,16,128]{2,1,0:T(8,128)S(1)}, f32[7,16,128]{2,1,0:T(8,128)S(1)}, u32[]{:S(2)}, u32[]{:S(2)}) collective-permute-start(f32[7,16,128]{2,1,0:T(8,128)S(1)} %get-tuple-element.43.own), channel_id=1, source_target_pairs={{0,64},{16,80},{32,96},{48,112},{64,0},{80,16},{96,32},{112,48},{1... | collective-permute-start | bytes 172040 | tf_op jit(solution)/shard_map/ppermute | solution.py:443
  13.8 5.4 %collective-permute-start.3 = (f32[7,16,128]{2,1,0:T(8,128)S(1)}, f32[7,16,128]{2,1,0:T(8,128)S(1)}, u32[]{:S(2)}, u32[]{:S(2)}) collective-permute-start(f32[7,16,128]{2,1,0:T(8,128)S(1)} %get-tuple-element.43.own), channel_id=1, source_target_pairs={{0,32},{16,48},{32,0},{48,16},{64,96},{80,112},{96,64},{112,80},{1... | collective-permute-start | bytes 172040 | tf_op jit(solution)/shard_map/ppermute | solution.py:443
  20.3 16.0 %all-to-all-start = ((f32[16,5,8,128]{3,2,1,0:T(8,128)}), f32[16,5,8,128]{3,2,1,0:T(8,128)S(1)}, u32[]{:S(2)}, u32[]{:S(2)}) async-start(f32[16,5,8,128]{3,2,1,0:T(8,128)} %get-tuple-element.51), calls=%async_computation | async-start | bytes 655360 | tf_op jit(solution)/shard_map/all_to_all | solution.py:461

commit v7 on v6

--- a/solution.py
+++ b/solution.py
@@ -10,7 +10,7 @@
 ROWS = NZ * BX
 GROUPS = ROWS // 128
 LIMIT = 8 * 1024 * 1024
-CHUNKS = 4
+CHUNKS = 1
 
 
 def inverse(x):
@@ -90,7 +90,7 @@
     count = blocks.shape[0]
     blocks[place] = own[...]
     for k, other in enumerate(others):
-        blocks[place ^ (k + 1)] = other[...]
+        blocks[place ^ (k + 1)] = other
 
     def pivot(i):
         if i == 0:
@@ -123,7 +123,20 @@
     flows_of(count, pivot, lambda i: blocks[i - 1, 1], lambda i: blocks[i, 1], gain, slots)
 
 
-def load_kernel(st_hbm, kx_hbm, ky_hbm, st, kx, ky, ky_t, mine, first, second, sems):
+def edge_columns(a, b, turned):
+    lane = lax.broadcasted_iota(jnp.int32, (1, 128), 1)
+    packed = jnp.zeros((128, 128), F32)
+    for g in range(GROUPS):
+        rows = pl.ds(g * 128, 128)
+        of_a = (lane == 4 * g) | (lane == 4 * g + 1)
+        of_b = (lane == 4 * g + 2) | (lane == 4 * g + 3)
+        packed = jnp.where(of_a, pltpu.roll(a[rows, :], 4 * g + 1, 1), packed)
+        packed = jnp.where(of_b, pltpu.roll(b[rows, :], 4 * g + 3, 1), packed)
+    turned[...] = packed.T
+    return [turned[pl.ds(n, GROUPS, stride=4), :] for n in range(4)]
+
+
+def load_kernel(st_hbm, kx_hbm, ky_hbm, st, kx, ky, mine, first, second, turned, sems):
     chunk = ROWS // CHUNKS
     waits = []
     for c in range(CHUNKS):
@@ -138,17 +151,10 @@
             move.start()
     rest = pltpu.make_async_copy(kx_hbm, kx, sems.at[2 * CHUNKS])
     rest.start()
-    for g in range(GROUPS):
-        if g * CHUNKS % GROUPS == 0:
-            for move in waits[g * CHUNKS // GROUPS]:
-                move.wait()
-        rows = pl.ds(g * 128, 128)
-        ky_t[pl.ds(g, BY, stride=GROUPS), :] = ky[rows, :].T
-        turned = st[rows, :].T
-        mine[0, pl.ds(g, 1), :] = turned[0:1, :]
-        mine[2, pl.ds(g, 1), :] = turned[127:128, :]
-    mine[1] = ky_t[pl.ds(0, GROUPS), :]
-    mine[3] = ky_t[pl.ds((BY - 1) * GROUPS, GROUPS), :]
+    for moves in waits:
+        for move in moves:
+            move.wait()
+    mine[2], mine[0], mine[3], mine[1] = edge_columns(st, ky, turned)
     even = lax.rem(lax.axis_index("gy"), 2) == 0
     low, high = mine[0:2], mine[2:4]
     first[...] = jnp.where(even, high, low)
@@ -192,7 +198,7 @@
     return lead, end, trail
 
 
-def x_matrix_kernel(st, kx, ky, fx, ux, wf, wl, part, edges, source, ratios):
+def x_matrix_kernel(st, kx, ky, fx, ux, wf, wl, part, edges, source, ratios, turned):
     lane = lax.broadcasted_iota(jnp.int32, (128, 128), 1)
     for g in range(GROUPS):
         rows = pl.ds(g * 128, 128)
@@ -214,14 +220,13 @@
     values += (x_row(kx, 0), x_row(kx, BX - 1), sums[0][0] + sums[0][1], sums[1][0] + sums[1][1])
     for n, value in enumerate(values):
         part[n] = value
-    for n, ref in enumerate((wf, wl)):
-        for g in range(GROUPS):
-            turned = ref[pl.ds(g * 128, 128), :].T
-            edges[2 * n, pl.ds(g, 1), :] = turned[0:1, :]
-            edges[2 * n + 1, pl.ds(g, 1), :] = turned[127:128, :]
-
-
-def y_matrix_kernel(ky_t, came2, came1, after, yf, yl, my, f, u, ratios):
+    edges[1], edges[0], edges[3], edges[2] = edge_columns(wf, wl, turned)
+
+
+def y_matrix_kernel(ky, after, ky_t, yf, yl, my, f, u, ratios):
+    for g in range(GROUPS):
+        ky_t[pl.ds(g, BY, stride=GROUPS), :] = ky[pl.ds(g * 128, 128), :].T
+
     def put(ref):
         def store(j, value):
             ref[j] = value
@@ -231,9 +236,7 @@
     me = lax.axis_index("gy")
     last = lax.axis_size("gy") - 1
     lead, across, trail = sweep(BY, lambda j: y_row(ky_t, j), f, u, ratios, put(yf), put(yl))
-    below = jnp.where(lax.rem(me, 2) == 0, came2[1], came1[1])
-    below = jnp.where(me == 0, 0.0, below)
-    my[0] = lead + 2.0 * inverse(below + y_row(ky_t, 0))
+    my[0] = lead
     my[1] = across
     my[2] = trail + jnp.where(me == last, 2.0 * inverse(y_row(ky_t, BY - 1)), 0.0)
 
@@ -247,6 +250,7 @@
     leave = 0.5 * (above[1] + mine[3]) * (above[0] - mine[2])
     flux[0] = enter
     flux[1] = leave
+    flux[2] = 2.0 * inverse(below[1] + mine[1])
     lane = lax.broadcasted_iota(jnp.int32, (GROUPS, 128), 1)
     send[0:5] = part[0:5]
     for n in range(2):
@@ -294,17 +298,23 @@
         coefs[n] = flow[n]
 
 
+def relay_kernel(value, after, out):
+    out[...] = value[...]
+
+
 def y_ends_kernel(
-    own, other1, other2, other3, coefs, d, wf, wl, yf, yl, my, v_t, send, blocks, slots, flows
+    own, far, near, shared, coefs, d, wf, wl, yf, yl, my, flux, v_t, send, blocks, slots, flows
 ):
     me = lax.axis_index("gx")
     place = lax.div(me, 2)
-    x_flows(own, (other1, other2, other3), place, blocks, slots)
+    on_low = lax.rem(me, 2) == 0
+    second = jnp.where(on_low, shared[...], far[...])
+    third = jnp.where(on_low, far[...], shared[...])
+    x_flows(own, (near[...], second, third), place, blocks, slots)
     enter, leave = slots[place], slots[place + 1]
     middle = coefs[0] + coefs[1] * enter + coefs[2] * leave
-    low = lax.rem(me, 2) == 0
-    flows[0] = jnp.where(low, enter, middle)
-    flows[1] = jnp.where(low, middle, leave)
+    flows[0] = jnp.where(on_low, enter, middle)
+    flows[1] = jnp.where(on_low, middle, leave)
     for g in range(GROUPS):
         parts = []
         for z in range(2 * g, 2 * g + 2):
@@ -323,8 +333,10 @@
         lasts[j % 4] = lasts[j % 4] + yl[j] * row
     first = (firsts[0] + firsts[1]) + (firsts[2] + firsts[3])
     last = (lasts[0] + lasts[1]) + (lasts[2] + lasts[3])
+    lead = my[0] + flux[2]
     for p in range(send.shape[0]):
-        send[p, 0:3] = my[...]
+        send[p, 0] = lead
+        send[p, 1:3] = my[1:3]
         send[p, 3] = first
         send[p, 4] = last
 
@@ -405,11 +417,11 @@
     edge = (2, GROUPS, 128)
     nx, ny = lax.axis_size("gx"), lax.axis_size("gy")
     chips = nx // 2
-    st, kx, ky, ky_t, mine, first, second = call(
+    st, kx, ky, mine, first, second = call(
         load_kernel,
-        near(plane, plane, plane, plane, (4, GROUPS, 128), edge, edge),
+        near(plane, plane, plane, (4, GROUPS, 128), edge, edge),
         [(a, True) for a in flat],
-        [pltpu.SemaphoreType.DMA((2 * CHUNKS + 1,))],
+        [pltpu.VMEM((128, 128), F32), pltpu.SemaphoreType.DMA((2 * CHUNKS + 1,))],
     )
     pairs = [
         (i * ny + j, i * ny + j + 2 * (j % 2) - 1 if 0 < j < ny - 1 else (i ^ 1) * ny + j)
@@ -422,12 +434,12 @@
         x_matrix_kernel,
         near(xs, xs, plane, plane, x_block, (4, GROUPS, 128), plane),
         near(st, kx, ky),
-        [pltpu.VMEM(xs, F32)],
+        [pltpu.VMEM(xs, F32), pltpu.VMEM((128, 128), F32)],
         cost=5_000_000,
     )
     ends, flux = call(
         x_ends_kernel,
-        near(x_block, edge),
+        near(x_block, (3, GROUPS, 128)),
         near(came2, came1, mine, part, edges),
         [pltpu.VMEM((2, NZ, BY), F32)],
     )
@@ -440,18 +452,21 @@
         cost=3_000_000,
     )
     chip, coefs = call(x_merge_kernel, near(x_block, (3, NZ, BY)), near(ends, other, d))
-    others = [lax.ppermute(chip, "gx", [(i, i ^ (2 * k)) for i in range(nx)]) for k in range(1, chips)]
-    yf, yl, my = call(
+    away = [lax.ppermute(chip, "gx", [(i, i ^ (6 - 2 * (i % 2))) for i in range(nx)])]
+    away.append(lax.ppermute(chip, "gx", [(i, i ^ 2) for i in range(nx)]))
+    ky_t, yf, yl, my = call(
         y_matrix_kernel,
-        near(ys, ys, (3, GROUPS, 128)),
-        near(ky_t, came2, came1, coefs),
+        near(plane, ys, ys, (3, GROUPS, 128)),
+        near(ky, coefs),
         [pltpu.VMEM(ys, F32)] * 3,
         cost=5_000_000,
     )
+    (relayed,) = call(relay_kernel, near(x_block), near(away[0], my))
+    away.append(lax.ppermute(relayed, "gx", [(i, i ^ 1) for i in range(nx)]))
     v_t, send = call(
         y_ends_kernel,
         near(plane, (ny, 5, GROUPS, 128)),
-        near(chip, *others, coefs, d, wf, wl, yf, yl, my),
+        near(chip, *away, coefs, d, wf, wl, yf, yl, my, flux),
         [
             pltpu.VMEM((chips,) + x_block, F32),
             pltpu.VMEM((chips + 1, NZ, BY), F32),

time: 37.6 us -> 36.4 us (0.968)
  starting transfers between devices: 15.3 us -> 14.3 us
    ppermute x3, starting transfers between devices: 4.17 us -> 3.06 us  [the longest x1 2.84 us: on_device(): lax.ppermute(chip, 'gx', [(i, i ^ 6 - 2 * (i % 2)) for i in range(nx)])]
    ppermute x3, waiting for transfers between devices: 2.99 us -> 2.02 us  [the longest x1 1.23 us: on_device(): away.append(lax.ppermute(chip, 'gx', [(i, i ^ 2) for i in range(nx)]))]
    all_to_all x1, waiting for transfers between devices: 6.85 us -> 7.51 us  [on_device(): y_blocks = lax.all_to_all(send, 'gy', 0, 0)]
    pallas_call x9 -> x10, Pallas kernels: 12.1 us -> 12.2 us  [call(): pl.pallas_call(kernel, out_shape=[jax.ShapeDtypeStruct(shape, F32) if far...]
  transfers between devices with their start and end apart: 7 -> 7, of which waited for: 2 -> 3; matrix products, arithmetic and copies ran while one was open for 0% -> 0% of each run, Pallas kernels for 21% -> 23%
where the time goes in v7:
time: 36.4 us; the launch traced here: 36.1 us
  starting transfers between devices  14.3 us (39%)
  Pallas kernels  12.2 us (34%)
  waiting for transfers between devices  9.54 us (26%)
    pallas_call x10, Pallas kernels, call(): pl.pallas_call(kernel, out_shape=[jax.ShapeDtypeStruct(shape, F32) if far...  12.2 us
    all_to_all x1, waiting for transfers between devices, on_device(): y_blocks = lax.all_to_all(send, 'gy', 0, 0)  7.51 us
    all_to_all x1, starting transfers between devices, on_device(): y_blocks = lax.all_to_all(send, 'gy', 0, 0)  7.23 us
    ppermute x1, starting transfers between devices, on_device(): came1 = lax.ppermute(first, 'gy', [(i, i ^ 1) for i in range(ny)])  3.91 us
    ppermute x1, starting transfers between devices, on_device(): lax.ppermute(chip, 'gx', [(i, i ^ 6 - 2 * (i % 2)) for i in range(nx)])  2.84 us
    ppermute x1, waiting for transfers between devices, on_device(): away.append(lax.ppermute(chip, 'gx', [(i, i ^ 2) for i in range(nx)]))  1.23 us
    ppermute x1, waiting for transfers between devices, on_device(): lax.ppermute(chip, 'gx', [(i, i ^ 6 - 2 * (i % 2)) for i in range(nx)])  0.78 us
  transfers between devices with their start and end apart: 7, of which 3 were waited for; matrix products, arithmetic and copies ran while one was open for 0% of the time, Pallas kernels for 23%

profile of v7, /device:TPU:0, one launch (start us, length us, event | category | flops | bytes accessed | tf_op | source)
XLA Modules:
  0.0 36.1 jit_solution(8755273929959247376)
XLA Ops:
  0.0 1.6 %shard_map.37 = (f32[1024,128]{1,0:T(8,128)S(1)}, f32[1024,128]{1,0:T(8,128)S(1)}, f32[1024,128]{1,0:T(8,128)S(1)}, f32[4,8,128]{2,1,0:T(8,128)S(1)}, f32[2,8,12...) custom-call(f32[1024,128]{1,0:T(8,128)} %bitcast.4, f32[1024,128]{1,0:T(8,128)} %bitcast.6, f32[1024,128]{1,0:T(8,128)} %bitcast.7), custom_call_target="tpu_custom_call" | custom-call | flops 100000 | bytes 100000 | tf_op jit(solution)/shard_map/pallas_call | solution.py:390
  1.6 0.1 collective-permute-start
  1.7 3.9 %collective-permute-start.1 = (f32[2,8,128]{2,1,0:T(8,128)S(1)}, f32[2,8,128]{2,1,0:T(8,128)S(1)}, u32[]{:S(2)}, u32[]{:S(2)}) collective-permute-start(f32[2,8,128]{2,1,0:T(8,128)S(1)} %get-tuple-element.31), channel_id=1, source_target_pairs={{0,1},{1,0},{2,3},{3,2},{4,5},{5,4},{6,7},{7,6},{8,9},{9,8},{10,11... | collective-permute-start | bytes 24584 | tf_op jit(solution)/shard_map/ppermute | solution.py:432
  5.6 2.7 %shard_map.38 = (f32[64,16,128]{2,1,0:T(8,128)S(1)}, f32[64,16,128]{2,1,0:T(8,128)S(1)}, f32[1024,128]{1,0:T(8,128)S(1)}, f32[1024,128]{1,0:T(8,128)S(1)}, f32[7...) custom-call(f32[1024,128]{1,0:T(8,128)S(1)} %get-tuple-element.33.st, ...), custom_call_target="tpu_custom_call" | custom-call | flops 5000000 | bytes 5000000 | tf_op jit(solution)/shard_map/pallas_call | solution.py:390
  8.4 0.0 collective-permute-done.came2
  8.4 0.0 collective-permute-done.1.came1
  8.4 0.1 shard_map.39
  8.5 0.0 collective-permute-start.2
  8.5 1.4 %shard_map.40.after.d = f32[1024,128]{1,0:T(8,128)S(1)} custom-call(f32[1024,128]{1,0:T(8,128)S(1)} %get-tuple-element.39.source, f32[3,8,128]{2,1,0:T(8,128)S(1)} %get-tuple-element.40.flux, f32[1024,128]{1,0:T(8,128)S(1)} %get-tuple-element.33.st, f32[64,16,128]{2,1,0:T(8,128)S(1)} %get-tuple-element.41.fx, f32[64,16,128]{2,1,0:T(8,128)S(1)} %get-tuple-element.42.ux), custom_call_target="tpu_custom_call" | custom-call | flops 3000000 | bytes 3000000 | tf_op jit(solution)/shard_map/pallas_call | solution.py:390
  9.9 0.0 collective-permute-done.2.other
  10.0 2.8 %collective-permute-start.3 = (f32[7,16,128]{2,1,0:T(8,128)S(1)}, f32[7,16,128]{2,1,0:T(8,128)S(1)}, u32[]{:S(2)}, u32[]{:S(2)}) collective-permute-start(f32[7,16,128]{2,1,0:T(8,128)S(1)} %get-tuple-element.43.own), channel_id=1, source_target_pairs={{0,96},{16,80},{32,64},{48,112},{64,32},{80,16},{96,0},{112,48},{1... | collective-permute-start | bytes 172040 | tf_op jit(solution)/shard_map/ppermute | solution.py:455
  12.8 0.2 collective-permute-start.4
  13.1 2.1 %shard_map.42 = (f32[1024,128]{1,0:T(8,128)S(1)}, f32[128,8,128]{2,1,0:T(8,128)S(1)}, f32[128,8,128]{2,1,0:T(8,128)S(1)}, f32[3,8,128]{2,1,0:T(8,128)S(1)}) custom-call(f32[1024,128]{1,0:T(8,128)S(1)} %get-tuple-element.35.ky, f32[3,16,128]{2,1,0:T(8,128)S(1)} %get-tuple-element.44.after.coefs), custom_call_target="tpu_custom_call" | custom-call | flops 5000000 | bytes 5000000 | tf_op jit(solution)/shard_map/pallas_call | solution.py:390
  15.1 0.8 %collective-permute-done.3.value.far = f32[7,16,128]{2,1,0:T(8,128)S(1)} collective-permute-done((f32[7,16,128]{2,1,0:T(8,128)S(1)}, f32[7,16,128]{2,1,0:T(8,128)S(1)}, u32[]{:S(2)}, u32[]{:S(2)}) %collective-permute-start.3) | collective-permute-done | bytes 57376 | tf_op jit(solution)/shard_map/ppermute | solution.py:455
  15.9 0.0 collective-permute-start.5
  15.9 1.2 %collective-permute-done.4.near = f32[7,16,128]{2,1,0:T(8,128)S(1)} collective-permute-done((f32[7,16,128]{2,1,0:T(8,128)S(1)}, f32[7,16,128]{2,1,0:T(8,128)S(1)}, u32[]{:S(2)}, u32[]{:S(2)}) %collective-permute-start.4) | collective-permute-done | bytes 57376 | tf_op jit(solution)/shard_map/ppermute | solution.py:456
  17.1 0.0 collective-permute-done.5.shared
  17.2 1.1 %shard_map.44 = (f32[1024,128]{1,0:T(8,128)S(1)}, f32[16,5,8,128]{3,2,1,0:T(8,128)}) custom-call(f32[7,16,128]{2,1,0:T(8,128)S(1)} %get-tuple-element.43.own, f32[7,16,128]{2,1,0:T(8,128)S(1)} %collective-permute-done.3.value.far, f32[7,16,128]{2,1,0:T(8,128)S(1)} %collective-permute-done.4.near, f32[7,16,128]{2,1,0:T(8,128)S(1)} %collective-permute-done.5.shared, ...), custom_call_target="tpu_custom_call" | custom-call | flops 100000 | bytes 100000 | tf_op jit(solution)/shard_map/pallas_call | solution.py:390
  18.2 7.2 %all-to-all-start = ((f32[16,5,8,128]{3,2,1,0:T(8,128)}), f32[16,5,8,128]{3,2,1,0:T(8,128)S(1)}, u32[]{:S(2)}, u32[]{:S(2)}) async-start(f32[16,5,8,128]{3,2,1,0:T(8,128)} %get-tuple-element.50), calls=%async_computation | async-start | bytes 655360 | tf_op jit(solution)/shard_map/all_to_all | solution.py:476
  25.5 2.0 %shard_map.45 = (f32[128,8,128]{2,1,0:T(8,128)S(1)}, f32[1024,128]{1,0:T(8,128)S(1)}) custom-call(f32[1024,128]{1,0:T(8,128)S(1)} %get-tuple-element.51.v_t, f32[1024,128]{1,0:T(8,128)S(1)} %get-tuple-element.52.ky_t, f32[1024,128]{1,0:T(8,128)} %bitcast.5), custom_call_target="tpu_custom_call" | custom-call | flops 5000000 | bytes 5000000 | tf_op jit(solution)/shard_map/pallas_call | solution.py:390
  27.4 7.5 %all-to-all-done.blocks = f32[16,5,8,128]{3,2,1,0:T(8,128)S(1)} async-done(((f32[16,5,8,128]{3,2,1,0:T(8,128)}), f32[16,5,8,128]{3,2,1,0:T(8,128)S(1)}, u32[]{:S(2)}, u32[]{:S(2)}) %all-to-all-start) | async-done | bytes 327712 | tf_op jit(solution)/shard_map/all_to_all | solution.py:476
  35.0 1.2 %shard_map.46 = f32[1024,128]{1,0:T(8,128)} custom-call(f32[16,5,8,128]{3,2,1,0:T(8,128)S(1)} %all-to-all-done.blocks, f32[128,8,128]{2,1,0:T(8,128)S(1)} %get-tuple-element.53.g_t, f32[128,8,128]{2,1,0:T(8,128)S(1)} %get-tuple-element.48.yf, f32[128,8,128]{2,1,0:T(8,128)S(1)} %get-tuple-element.49.yl, f32[1024,128]{1,0:T(8,128)S(1)} %get-tuple-element.54.st), custom_call_target="tpu_custom_call" | custom-call | flops 100000 | bytes 100000 | tf_op jit(solution)/shard_map/pallas_call | solution.py:390
  (2 shorter events, 0.0 us)
Async XLA Ops:
  1.6 6.7 %collective-permute-start = (f32[2,8,128]{2,1,0:T(8,128)S(1)}, f32[2,8,128]{2,1,0:T(8,128)S(1)}, u32[]{:S(2)}, u32[]{:S(2)}) collective-permute-start(f32[2,8,128]{2,1,0:T(8,128)S(1)} %get-tuple-element.30), channel_id=1, source_target_pairs={{0,16},{1,2},{2,1},{3,4},{4,3},{5,6},{6,5},{7,8},{8,7},{9,10},{10,... | collective-permute-start | bytes 24584 | tf_op jit(solution)/shard_map/ppermute | solution.py:431
  1.7 6.6 %collective-permute-start.1 = (f32[2,8,128]{2,1,0:T(8,128)S(1)}, f32[2,8,128]{2,1,0:T(8,128)S(1)}, u32[]{:S(2)}, u32[]{:S(2)}) collective-permute-start(f32[2,8,128]{2,1,0:T(8,128)S(1)} %get-tuple-element.31), channel_id=1, source_target_pairs={{0,1},{1,0},{2,3},{3,2},{4,5},{5,4},{6,7},{7,6},{8,9},{9,8},{10,11... | collective-permute-start | bytes 24584 | tf_op jit(solution)/shard_map/ppermute | solution.py:432
  8.5 1.5 %collective-permute-start.2 = (f32[7,16,128]{2,1,0:T(8,128)S(1)}, f32[7,16,128]{2,1,0:T(8,128)S(1)}, u32[]{:S(2)}, u32[]{:S(2)}) collective-permute-start(f32[7,16,128]{2,1,0:T(8,128)S(1)} %get-tuple-element.38.own), channel_id=1, source_target_pairs={{0,16},{16,0},{32,48},{48,32},{64,80},{80,64},{96,112},{112,96},{1... | collective-permute-start | bytes 172040 | tf_op jit(solution)/shard_map/ppermute | solution.py:446
  10.0 5.9 %collective-permute-start.3 = (f32[7,16,128]{2,1,0:T(8,128)S(1)}, f32[7,16,128]{2,1,0:T(8,128)S(1)}, u32[]{:S(2)}, u32[]{:S(2)}) collective-permute-start(f32[7,16,128]{2,1,0:T(8,128)S(1)} %get-tuple-element.43.own), channel_id=1, source_target_pairs={{0,96},{16,80},{32,64},{48,112},{64,32},{80,16},{96,0},{112,48},{1... | collective-permute-start | bytes 172040 | tf_op jit(solution)/shard_map/ppermute | solution.py:455
  12.8 4.3 %collective-permute-start.4 = (f32[7,16,128]{2,1,0:T(8,128)S(1)}, f32[7,16,128]{2,1,0:T(8,128)S(1)}, u32[]{:S(2)}, u32[]{:S(2)}) collective-permute-start(f32[7,16,128]{2,1,0:T(8,128)S(1)} %get-tuple-element.43.own), channel_id=1, source_target_pairs={{0,32},{16,48},{32,0},{48,16},{64,96},{80,112},{96,64},{112,80},{1... | collective-permute-start | bytes 172040 | tf_op jit(solution)/shard_map/ppermute | solution.py:456
  15.9 1.2 %collective-permute-start.5 = (f32[7,16,128]{2,1,0:T(8,128)S(1)}, f32[7,16,128]{2,1,0:T(8,128)S(1)}, u32[]{:S(2)}, u32[]{:S(2)}) collective-permute-start(f32[7,16,128]{2,1,0:T(8,128)S(1)} %shard_map.43), channel_id=1, source_target_pairs={{0,16},{16,0},{32,48},{48,32},{64,80},{80,64},{96,112},{112,96},{1... | collective-permute-start | bytes 172040 | tf_op jit(solution)/shard_map/ppermute | solution.py:465
  18.2 16.7 %all-to-all-start = ((f32[16,5,8,128]{3,2,1,0:T(8,128)}), f32[16,5,8,128]{3,2,1,0:T(8,128)S(1)}, u32[]{:S(2)}, u32[]{:S(2)}) async-start(f32[16,5,8,128]{3,2,1,0:T(8,128)} %get-tuple-element.50), calls=%async_computation | async-start | bytes 655360 | tf_op jit(solution)/shard_map/all_to_all | solution.py:476

commit v8 on v7

--- a/solution.py
+++ b/solution.py
@@ -10,17 +10,12 @@
 ROWS = NZ * BX
 GROUPS = ROWS // 128
 LIMIT = 8 * 1024 * 1024
-CHUNKS = 1
-
-
-def inverse(x):
-    guess = pl.reciprocal(x, approx=True)
-    return guess * (2.0 - x * guess)
+PITCH = 72
 
 
 def x_row(ref, i):
     return jnp.concatenate(
-        [ref[pl.ds(i, 8, stride=BX), :], ref[pl.ds(8 * BX + i, 8, stride=BX), :]], axis=0
+        [ref[pl.ds(i, 8, stride=PITCH), :], ref[pl.ds(8 * PITCH + i, 8, stride=PITCH), :]], axis=0
     )
 
 
@@ -29,12 +24,21 @@
 
 
 def place_rows(ref, i, value):
-    ref[pl.ds(i, 8, stride=BX), :] = value[:8]
-    ref[pl.ds(8 * BX + i, 8, stride=BX), :] = value[8:]
+    ref[pl.ds(i, 8, stride=PITCH), :] = value[:8]
+    ref[pl.ds(8 * PITCH + i, 8, stride=PITCH), :] = value[8:]
+
+
+def group(ref, g):
+    return jnp.concatenate([ref[pl.ds(z * PITCH, BX), :] for z in (2 * g, 2 * g + 1)], axis=0)
+
+
+def place_group(ref, g, value):
+    ref[pl.ds(2 * g * PITCH, BX), :] = value[:BX]
+    ref[pl.ds((2 * g + 1) * PITCH, BX), :] = value[BX:]
 
 
 def merge(low, high):
-    inv = inverse(2.0 * inverse(low[4] + high[3]) + low[2] + high[0])
+    inv = (1.0 / ((2.0 / (low[4] + high[3])) + low[2] + high[0]))
     e = (low[6] - high[5]) * inv
     a = low[1] * inv
     b = high[1] * inv
@@ -60,7 +64,7 @@
             if i:
                 gain_i = gain_i + lower(i) * up[i - 1][0]
                 pivot_i = pivot_i - lower(i) * up[i - 1][1]
-            inv = inverse(pivot_i)
+            inv = (1.0 / (pivot_i))
             up[i] = gain_i * inv, upper(i) * inv
         i = count - n
         if i > half:
@@ -68,13 +72,13 @@
             if n:
                 gain_i = gain_i + upper(i) * down[i + 1][0]
                 pivot_i = pivot_i - upper(i) * down[i + 1][1]
-            inv = inverse(pivot_i)
+            inv = (1.0 / (pivot_i))
             down[i] = gain_i * inv, lower(i) * inv
     below, above = up[half - 1], down[half + 1]
     low, high = lower(half), upper(half)
-    flow = (gain(half) + low * below[0] + high * above[0]) * inverse(
+    flow = (gain(half) + low * below[0] + high * above[0]) * (1.0 / (
         pivot(half) - low * below[1] - high * above[1]
-    )
+    ))
     slots[half] = flow
     rising = flow
     for n in range(1, half + 1):
@@ -94,10 +98,10 @@
 
     def pivot(i):
         if i == 0:
-            return 2.0 * inverse(blocks[0, 3]) + blocks[0, 0]
+            return (2.0 / (blocks[0, 3])) + blocks[0, 0]
         if i == count:
-            return 2.0 * inverse(blocks[count - 1, 4]) + blocks[count - 1, 2]
-        return 2.0 * inverse(blocks[i - 1, 4] + blocks[i, 3]) + blocks[i - 1, 2] + blocks[i, 0]
+            return (2.0 / (blocks[count - 1, 4])) + blocks[count - 1, 2]
+        return (2.0 / (blocks[i - 1, 4] + blocks[i, 3])) + blocks[i - 1, 2] + blocks[i, 0]
 
     def gain(i):
         if i == 0:
@@ -123,43 +127,32 @@
     flows_of(count, pivot, lambda i: blocks[i - 1, 1], lambda i: blocks[i, 1], gain, slots)
 
 
-def edge_columns(a, b, turned):
-    lane = lax.broadcasted_iota(jnp.int32, (1, 128), 1)
-    packed = jnp.zeros((128, 128), F32)
-    for g in range(GROUPS):
-        rows = pl.ds(g * 128, 128)
-        of_a = (lane == 4 * g) | (lane == 4 * g + 1)
-        of_b = (lane == 4 * g + 2) | (lane == 4 * g + 3)
-        packed = jnp.where(of_a, pltpu.roll(a[rows, :], 4 * g + 1, 1), packed)
-        packed = jnp.where(of_b, pltpu.roll(b[rows, :], 4 * g + 3, 1), packed)
-    turned[...] = packed.T
-    return [turned[pl.ds(n, GROUPS, stride=4), :] for n in range(4)]
-
-
-def load_kernel(st_hbm, kx_hbm, ky_hbm, st, kx, ky, mine, first, second, turned, sems):
-    chunk = ROWS // CHUNKS
-    waits = []
-    for c in range(CHUNKS):
-        rows = pl.ds(c * chunk, chunk)
-        waits.append(
-            [
-                pltpu.make_async_copy(src.at[rows], dst.at[rows], sems.at[2 * c + n])
-                for n, (src, dst) in enumerate(((ky_hbm, ky), (st_hbm, st)))
-            ]
+def load_kernel(st_hbm, kx_hbm, ky_hbm, st, kx, st_t, ky_t, mine, first, second, ky, sems):
+    inside = pl.ds(0, BX)
+    moves = [
+        pltpu.make_async_copy(src, dst, sems.at[n])
+        for n, (src, dst) in enumerate(
+            ((ky_hbm, ky), (st_hbm, st.at[:, inside, :]), (kx_hbm, kx.at[:, inside, :]))
         )
-        for move in waits[-1]:
-            move.start()
-    rest = pltpu.make_async_copy(kx_hbm, kx, sems.at[2 * CHUNKS])
-    rest.start()
-    for moves in waits:
-        for move in moves:
-            move.wait()
-    mine[2], mine[0], mine[3], mine[1] = edge_columns(st, ky, turned)
+    ]
+    for move in moves:
+        move.start()
+    moves[0].wait()
+    for g in range(GROUPS):
+        pair = jnp.concatenate([ky[2 * g], ky[2 * g + 1]], axis=0)
+        ky_t[pl.ds(g, BY, stride=GROUPS), :] = pair.T
+    moves[1].wait()
+    for g in range(GROUPS):
+        pair = jnp.concatenate([st[2 * g, inside, :], st[2 * g + 1, inside, :]], axis=0)
+        st_t[pl.ds(g, BY, stride=GROUPS), :] = pair.T
+    for n, ref in enumerate((st_t, ky_t)):
+        mine[n] = y_row(ref, 0)
+        mine[2 + n] = y_row(ref, BY - 1)
     even = lax.rem(lax.axis_index("gy"), 2) == 0
     low, high = mine[0:2], mine[2:4]
     first[...] = jnp.where(even, high, low)
     second[...] = jnp.where(even, low, high)
-    rest.wait()
+    moves[2].wait()
 
 
 def sweep(count, row, f, u, ratios, put_first, put_last):
@@ -170,7 +163,7 @@
         nxt = row(i + 1)
         r = 0.5 * (low + nxt)
         low = nxt
-        inv = inverse(r + ahead)
+        inv = (1.0 / (r + ahead))
         ratio = r * inv
         ahead = 1.0 + ratio * ahead
         u[i] = inv
@@ -179,11 +172,11 @@
         prev = row(j - 1)
         r = 0.5 * (high + prev)
         high = prev
-        ratio = r * inverse(r + back)
+        ratio = r * (1.0 / (r + back))
         back = 1.0 + ratio * back
         ratios[j] = ratio
-    start = inverse(back)
-    end = inverse(ahead)
+    start = (1.0 / (back))
+    end = (1.0 / (ahead))
     lead, trail = start, end
     put_first(0, start)
     put_last(count - 1, end)
@@ -198,15 +191,18 @@
     return lead, end, trail
 
 
-def x_matrix_kernel(st, kx, ky, fx, ux, wf, wl, part, edges, source, ratios, turned):
-    lane = lax.broadcasted_iota(jnp.int32, (128, 128), 1)
-    for g in range(GROUPS):
-        rows = pl.ds(g * 128, 128)
-        s = st[rows, :]
-        k = ky[rows, :]
-        flux = 0.5 * (k + pltpu.roll(k, 127, 1)) * (pltpu.roll(s, 127, 1) - s)
-        flux = jnp.where(lane == 127, 0.0, flux)
-        source[rows, :] = s + flux - pltpu.roll(flux, 1, 1)
+def x_matrix_kernel(st_t, kx, ky_t, fx, ux, wf, wl, part, edges, base_t, source, ratios):
+    here, k_here = y_row(st_t, 0), y_row(ky_t, 0)
+    value = here
+    for j in range(BY):
+        if j < BY - 1:
+            after, k_after = y_row(st_t, j + 1), y_row(ky_t, j + 1)
+            flux = 0.5 * (k_here + k_after) * (after - here)
+            value = value + flux
+        base_t[pl.ds(j * GROUPS, GROUPS), :] = value
+        here, k_here, value = after, k_after, after - flux
+    for g in range(GROUPS):
+        place_group(source, g, base_t[pl.ds(g, BY, stride=GROUPS), :].T)
     sums = [[jnp.zeros((NZ, BY), F32) for _ in range(2)] for _ in range(2)]
 
     def put(ref, total):
@@ -220,13 +216,14 @@
     values += (x_row(kx, 0), x_row(kx, BX - 1), sums[0][0] + sums[0][1], sums[1][0] + sums[1][1])
     for n, value in enumerate(values):
         part[n] = value
-    edges[1], edges[0], edges[3], edges[2] = edge_columns(wf, wl, turned)
-
-
-def y_matrix_kernel(ky, after, ky_t, yf, yl, my, f, u, ratios):
-    for g in range(GROUPS):
-        ky_t[pl.ds(g, BY, stride=GROUPS), :] = ky[pl.ds(g * 128, 128), :].T
-
+    for n, ref in enumerate((wf, wl)):
+        for g in range(GROUPS):
+            turned = group(ref, g).T
+            edges[2 * n, pl.ds(g, 1), :] = turned[0:1, :]
+            edges[2 * n + 1, pl.ds(g, 1), :] = turned[127:128, :]
+
+
+def y_matrix_kernel(ky_t, after, yf, yl, my, f, u, ratios):
     def put(ref):
         def store(j, value):
             ref[j] = value
@@ -238,7 +235,7 @@
     lead, across, trail = sweep(BY, lambda j: y_row(ky_t, j), f, u, ratios, put(yf), put(yl))
     my[0] = lead
     my[1] = across
-    my[2] = trail + jnp.where(me == last, 2.0 * inverse(y_row(ky_t, BY - 1)), 0.0)
+    my[2] = trail + jnp.where(me == last, (2.0 / (y_row(ky_t, BY - 1))), 0.0)
 
 
 def x_ends_kernel(came2, came1, mine, part, edges, send, flux, rows):
@@ -250,7 +247,7 @@
     leave = 0.5 * (above[1] + mine[3]) * (above[0] - mine[2])
     flux[0] = enter
     flux[1] = leave
-    flux[2] = 2.0 * inverse(below[1] + mine[1])
+    flux[2] = (2.0 / (below[1] + mine[1]))
     lane = lax.broadcasted_iota(jnp.int32, (GROUPS, 128), 1)
     send[0:5] = part[0:5]
     for n in range(2):
@@ -265,16 +262,12 @@
         send[5 + n] = part[5 + n] + rows[n]
 
 
-def x_local_kernel(source, flux, st, fx, ux, d, s, work):
-    both = jnp.concatenate([flux[0], flux[1]], axis=0)
-    turned = jnp.concatenate([both] * 8, axis=0).T
-    lane = lax.broadcasted_iota(jnp.int32, (128, 128), 1)
-    for g in range(GROUPS):
-        rows = pl.ds(g * 128, 128)
-        left = jnp.broadcast_to(turned[:, g : g + 1], (128, 128))
-        right = jnp.broadcast_to(turned[:, 8 + g : 9 + g], (128, 128))
-        extra = jnp.where(lane == 0, -left, jnp.where(lane == 127, right, 0.0))
-        s[rows, :] = source[rows, :] + extra
+def x_local_kernel(base_t, flux, st, fx, ux, d, s, work, work_t):
+    work_t[...] = base_t[...]
+    work_t[pl.ds(0, GROUPS), :] = y_row(base_t, 0) - flux[0]
+    work_t[pl.ds((BY - 1) * GROUPS, GROUPS), :] = y_row(base_t, BY - 1) + flux[1]
+    for g in range(GROUPS):
+        place_group(s, g, work_t[pl.ds(g, BY, stride=GROUPS), :].T)
     total = x_row(s, 0)
     work[0] = total
     for i in range(1, BX):
@@ -318,7 +311,7 @@
     for g in range(GROUPS):
         parts = []
         for z in range(2 * g, 2 * g + 2):
-            rows = pl.ds(z * BX, BX)
+            rows = pl.ds(z * PITCH, BX)
             parts.append(
                 d[rows, :]
                 + wf[rows, :] * flows[0, pl.ds(z, 1), :]
@@ -352,14 +345,14 @@
         high = y_row(ky_t, j)
         r = 0.5 * (low + high)
         low = high
-        inv = inverse(r + ahead)
+        inv = (1.0 / (r + ahead))
         ratio = r * inv
         ahead = 1.0 + ratio * ahead
         u[j - 1] = inv
         f[j - 1] = ratio
         total = y_row(v_t, j) + ratio * total
         g_t[j] = total
-    x = total * inverse(ahead)
+    x = total / ahead
     g_t[BY - 1] = x
     for j in range(BY - 2, -1, -1):
         x = u[j] * g_t[j] + f[j] * x
@@ -407,22 +400,24 @@
 
 def on_device(state, kappa_x, kappa_y):
     flat = [
-        pltpu.with_memory_space_constraint(a.reshape(ROWS, BY), pltpu.HBM)
-        for a in (state, kappa_x, kappa_y)
+        pltpu.with_memory_space_constraint(a, pltpu.HBM) for a in (state, kappa_x, kappa_y)
     ]
     plane = (ROWS, BY)
+    pitched = (NZ * PITCH, BY)
+    planes = (NZ, PITCH, BY)
     xs = (BX, NZ, BY)
     ys = (BY, GROUPS, 128)
     x_block = (7, NZ, BY)
     edge = (2, GROUPS, 128)
     nx, ny = lax.axis_size("gx"), lax.axis_size("gy")
     chips = nx // 2
-    st, kx, ky, mine, first, second = call(
+    st, kx, st_t, ky_t, mine, first, second = call(
         load_kernel,
-        near(plane, plane, plane, (4, GROUPS, 128), edge, edge),
+        near(planes, planes, plane, plane, (4, GROUPS, 128), edge, edge),
         [(a, True) for a in flat],
-        [pltpu.VMEM((128, 128), F32), pltpu.SemaphoreType.DMA((2 * CHUNKS + 1,))],
-    )
+        [pltpu.VMEM((NZ, BX, BY), F32), pltpu.SemaphoreType.DMA((3,))],
+    )
+    st, kx = st.reshape(pitched), kx.reshape(pitched)
     pairs = [
         (i * ny + j, i * ny + j + 2 * (j % 2) - 1 if 0 < j < ny - 1 else (i ^ 1) * ny + j)
         for i in range(nx)
@@ -430,11 +425,11 @@
     ]
     came2 = lax.ppermute(second, ("gx", "gy"), pairs)
     came1 = lax.ppermute(first, "gy", [(i, i ^ 1) for i in range(ny)])
-    fx, ux, wf, wl, part, edges, source = call(
+    fx, ux, wf, wl, part, edges, base_t = call(
         x_matrix_kernel,
-        near(xs, xs, plane, plane, x_block, (4, GROUPS, 128), plane),
-        near(st, kx, ky),
-        [pltpu.VMEM(xs, F32), pltpu.VMEM((128, 128), F32)],
+        near(xs, xs, pitched, pitched, x_block, (4, GROUPS, 128), plane),
+        near(st_t, kx, ky_t),
+        [pltpu.VMEM(pitched, F32), pltpu.VMEM(xs, F32)],
         cost=5_000_000,
     )
     ends, flux = call(
@@ -446,18 +441,18 @@
     other = lax.ppermute(ends, "gx", [(i, i ^ 1) for i in range(nx)])
     (d,) = call(
         x_local_kernel,
-        near(plane),
-        near(source, flux, st, fx, ux),
-        [pltpu.VMEM(plane, F32), pltpu.VMEM(xs, F32)],
+        near(pitched),
+        near(base_t, flux, st, fx, ux),
+        [pltpu.VMEM(pitched, F32), pltpu.VMEM(xs, F32), pltpu.VMEM(plane, F32)],
         cost=3_000_000,
     )
     chip, coefs = call(x_merge_kernel, near(x_block, (3, NZ, BY)), near(ends, other, d))
     away = [lax.ppermute(chip, "gx", [(i, i ^ (6 - 2 * (i % 2))) for i in range(nx)])]
     away.append(lax.ppermute(chip, "gx", [(i, i ^ 2) for i in range(nx)]))
-    ky_t, yf, yl, my = call(
+    yf, yl, my = call(
         y_matrix_kernel,
-        near(plane, ys, ys, (3, GROUPS, 128)),
-        near(ky, coefs),
+        near(ys, ys, (3, GROUPS, 128)),
+        near(ky_t, coefs),
         [pltpu.VMEM(ys, F32)] * 3,
         cost=5_000_000,
     )
@@ -476,7 +471,7 @@
     y_blocks = lax.all_to_all(send, "gy", 0, 0)
     g_t, st = call(
         y_local_kernel,
-        near(ys, plane),
+        near(ys, (NZ, BX, BY)),
         near(v_t, ky_t) + [(flat[0], True)],
         [pltpu.VMEM(ys, F32), pltpu.VMEM(ys, F32), pltpu.SemaphoreType.DMA],
         cost=5_000_000,
@@ -484,7 +479,7 @@
     (out,) = call(
         y_solve_kernel,
         [(plane, True)],
-        near(y_blocks, g_t, yf, yl, st),
+        near(y_blocks, g_t, yf, yl, st.reshape(plane)),
         [
             pltpu.VMEM((ny + 1, GROUPS, 128), F32),
             pltpu.VMEM(plane, F32),

time: 36.4 us -> 35.7 us (0.981)
  Pallas kernels: 12.2 us -> 8.75 us
  waiting for transfers between devices: 9.54 us -> 11.2 us
  starting transfers between devices: 14.3 us -> 15.4 us
    pallas_call x10, Pallas kernels: 12.2 us -> 8.75 us  [call(): pl.pallas_call(kernel, out_shape=[jax.ShapeDtypeStruct(shape, F32) if far...]
    all_to_all x1, starting transfers between devices: 7.23 us -> 8.35 us  [on_device(): y_blocks = lax.all_to_all(send, 'gy', 0, 0)]
    ppermute x1, waiting for transfers between devices: 0.01 us -> 0.67 us  [on_device(): other = lax.ppermute(ends, 'gx', [(i, i ^ 1) for i in range(nx)])]
  transfers between devices with their start and end apart: 7 -> 7, of which waited for: 3 -> 5; matrix products, arithmetic and copies ran while one was open for 0% -> 0% of each run, Pallas kernels for 23% -> 14%
where the time goes in v8:
time: 35.7 us; the launch traced here: 35.4 us
  starting transfers between devices  15.4 us (43%)
  waiting for transfers between devices  11.2 us (31%)
  Pallas kernels  8.75 us (25%)
    pallas_call x10, Pallas kernels, call(): pl.pallas_call(kernel, out_shape=[jax.ShapeDtypeStruct(shape, F32) if far...  8.75 us
    all_to_all x1, starting transfers between devices, on_device(): y_blocks = lax.all_to_all(send, 'gy', 0, 0)  8.35 us
    all_to_all x1, waiting for transfers between devices, on_device(): y_blocks = lax.all_to_all(send, 'gy', 0, 0)  7.71 us
    ppermute x1, starting transfers between devices, on_device(): came1 = lax.ppermute(first, 'gy', [(i, i ^ 1) for i in range(ny)])  3.91 us
    ppermute x1, starting transfers between devices, on_device(): lax.ppermute(chip, 'gx', [(i, i ^ 6 - 2 * (i % 2)) for i in range(nx)])  2.84 us
    ppermute x1, waiting for transfers between devices, on_device(): away.append(lax.ppermute(chip, 'gx', [(i, i ^ 2) for i in range(nx)]))  1.44 us
    ppermute x1, waiting for transfers between devices, on_device(): lax.ppermute(chip, 'gx', [(i, i ^ 6 - 2 * (i % 2)) for i in range(nx)])  1.09 us
  transfers between devices with their start and end apart: 7, of which 5 were waited for; matrix products, arithmetic and copies ran while one was open for 0% of the time, Pallas kernels for 14%

profile of v8, /device:TPU:0, one launch (start us, length us, event | category | flops | bytes accessed | tf_op | source)
XLA Modules:
  0.0 35.4 jit_solution(3881411044098157364)
XLA Ops:
  0.0 1.5 %shard_map.37 = (f32[16,72,128]{2,1,0:T(8,128)S(1)}, f32[16,72,128]{2,1,0:T(8,128)S(1)}, f32[1024,128]{1,0:T(8,128)S(1)}, f32[1024,128]{1,0:T(8,128)S(1)}, f32[4...) custom-call(f32[16,64,128]{2,1,0:T(8,128)} %st_hbm.3, f32[16,64,128]{2,1,0:T(8,128)} %kx_hbm.1, ...), custom_call_target="tpu_custom_call" | custom-call | flops 100000 | bytes 100000 | tf_op jit(solution)/shard_map/pallas_call | solution.py:383
  1.5 0.1 collective-permute-start
  1.6 3.9 %collective-permute-start.1 = (f32[2,8,128]{2,1,0:T(8,128)S(1)}, f32[2,8,128]{2,1,0:T(8,128)S(1)}, u32[]{:S(2)}, u32[]{:S(2)}) collective-permute-start(f32[2,8,128]{2,1,0:T(8,128)S(1)} %get-tuple-element.31), channel_id=1, source_target_pairs={{0,1},{1,0},{2,3},{3,2},{4,5},{5,4},{6,7},{7,6},{8,9},{9,8},{10,11... | collective-permute-start | bytes 24584 | tf_op jit(solution)/shard_map/ppermute | solution.py:427
  5.5 1.4 %shard_map.38 = (f32[64,16,128]{2,1,0:T(8,128)S(1)}, f32[64,16,128]{2,1,0:T(8,128)S(1)}, f32[1152,128]{1,0:T(8,128)S(1)}, f32[1152,128]{1,0:T(8,128)S(1)}, f32[7...) custom-call(f32[1024,128]{1,0:T(8,128)S(1)} %get-tuple-element.33.st_t, ...), custom_call_target="tpu_custom_call" | custom-call | flops 5000000 | bytes 5000000 | tf_op jit(solution)/shard_map/pallas_call | solution.py:383
  6.9 0.0 collective-permute-done.came2
  6.9 0.2 collective-permute-done.1.came1
  7.1 0.1 shard_map.39
  7.2 0.0 collective-permute-start.2
  7.3 0.6 %shard_map.40.after.d = f32[1152,128]{1,0:T(8,128)S(1)} custom-call(f32[1024,128]{1,0:T(8,128)S(1)} %get-tuple-element.39.base_t, f32[3,8,128]{2,1,0:T(8,128)S(1)} %get-tuple-element.40.flux, f32[1152,128]{1,0:T(8,128)S(1)} %bitcast.5, f32[64,16,128]{2,1,0:T(8,128)S(1)} %get-tuple-element.42.fx, f32[64,16,128]{2,1,0:T(8,128)S(1)} %get-tuple-element.43.ux), custom_call_target="tpu_custom_call" | custom-call | flops 3000000 | bytes 3000000 | tf_op jit(solution)/shard_map/pallas_call | solution.py:383
  7.8 0.7 %collective-permute-done.2.other = f32[7,16,128]{2,1,0:T(8,128)S(1)} collective-permute-done((f32[7,16,128]{2,1,0:T(8,128)S(1)}, f32[7,16,128]{2,1,0:T(8,128)S(1)}, u32[]{:S(2)}, u32[]{:S(2)}) %collective-permute-start.2) | collective-permute-done | bytes 57376 | tf_op jit(solution)/shard_map/ppermute | solution.py:441
  8.5 2.8 %collective-permute-start.3 = (f32[7,16,128]{2,1,0:T(8,128)S(1)}, f32[7,16,128]{2,1,0:T(8,128)S(1)}, u32[]{:S(2)}, u32[]{:S(2)}) collective-permute-start(f32[7,16,128]{2,1,0:T(8,128)S(1)} %get-tuple-element.44.own), channel_id=1, source_target_pairs={{0,96},{16,80},{32,64},{48,112},{64,32},{80,16},{96,0},{112,48},{1... | collective-permute-start | bytes 172040 | tf_op jit(solution)/shard_map/ppermute | solution.py:450
  11.4 0.2 collective-permute-start.4
  11.6 1.4 %shard_map.42 = (f32[128,8,128]{2,1,0:T(8,128)S(1)}, f32[128,8,128]{2,1,0:T(8,128)S(1)}, f32[3,8,128]{2,1,0:T(8,128)S(1)}) custom-call(f32[1024,128]{1,0:T(8,128)S(1)} %get-tuple-element.35.ky_t, f32[3,16,128]{2,1,0:T(8,128)S(1)} %get-tuple-element.45.after.coefs), custom_call_target="tpu_custom_call" | custom-call | flops 5000000 | bytes 5000000 | tf_op jit(solution)/shard_map/pallas_call | solution.py:383
  13.0 1.1 %collective-permute-done.3.value.far = f32[7,16,128]{2,1,0:T(8,128)S(1)} collective-permute-done((f32[7,16,128]{2,1,0:T(8,128)S(1)}, f32[7,16,128]{2,1,0:T(8,128)S(1)}, u32[]{:S(2)}, u32[]{:S(2)}) %collective-permute-start.3) | collective-permute-done | bytes 57376 | tf_op jit(solution)/shard_map/ppermute | solution.py:450
  14.1 0.0 collective-permute-start.5
  14.1 1.4 %collective-permute-done.4.near = f32[7,16,128]{2,1,0:T(8,128)S(1)} collective-permute-done((f32[7,16,128]{2,1,0:T(8,128)S(1)}, f32[7,16,128]{2,1,0:T(8,128)S(1)}, u32[]{:S(2)}, u32[]{:S(2)}) %collective-permute-start.4) | collective-permute-done | bytes 57376 | tf_op jit(solution)/shard_map/ppermute | solution.py:451
  15.5 0.0 collective-permute-done.5.shared
  15.6 1.1 %shard_map.44 = (f32[1024,128]{1,0:T(8,128)S(1)}, f32[16,5,8,128]{3,2,1,0:T(8,128)}) custom-call(f32[7,16,128]{2,1,0:T(8,128)S(1)} %get-tuple-element.44.own, f32[7,16,128]{2,1,0:T(8,128)S(1)} %collective-permute-done.3.value.far, f32[7,16,128]{2,1,0:T(8,128)S(1)} %collective-permute-done.4.near, f32[7,16,128]{2,1,0:T(8,128)S(1)} %collective-permute-done.5.shared, ...), custom_call_target="tpu_custom_call" | custom-call | flops 100000 | bytes 100000 | tf_op jit(solution)/shard_map/pallas_call | solution.py:383
  16.7 8.3 %all-to-all-start = ((f32[16,5,8,128]{3,2,1,0:T(8,128)}), f32[16,5,8,128]{3,2,1,0:T(8,128)S(1)}, u32[]{:S(2)}, u32[]{:S(2)}) async-start(f32[16,5,8,128]{3,2,1,0:T(8,128)} %get-tuple-element.51), calls=%async_computation | async-start | bytes 655360 | tf_op jit(solution)/shard_map/all_to_all | solution.py:471
  25.0 1.6 %shard_map.45 = (f32[128,8,128]{2,1,0:T(8,128)S(1)}, f32[16,64,128]{2,1,0:T(8,128)S(1)}) custom-call(f32[1024,128]{1,0:T(8,128)S(1)} %get-tuple-element.52.v_t, f32[1024,128]{1,0:T(8,128)S(1)} %get-tuple-element.35.ky_t, f32[16,64,128]{2,1,0:T(8,128)} %st_hbm.3), custom_call_target="tpu_custom_call" | custom-call | flops 5000000 | bytes 5000000 | tf_op jit(solution)/shard_map/pallas_call | solution.py:383
  26.6 7.7 %all-to-all-done.blocks = f32[16,5,8,128]{3,2,1,0:T(8,128)S(1)} async-done(((f32[16,5,8,128]{3,2,1,0:T(8,128)}), f32[16,5,8,128]{3,2,1,0:T(8,128)S(1)}, u32[]{:S(2)}, u32[]{:S(2)}) %all-to-all-start) | async-done | bytes 327712 | tf_op jit(solution)/shard_map/all_to_all | solution.py:471
  34.3 1.1 %shard_map.46 = f32[1024,128]{1,0:T(8,128)} custom-call(f32[16,5,8,128]{3,2,1,0:T(8,128)S(1)} %all-to-all-done.blocks, f32[128,8,128]{2,1,0:T(8,128)S(1)} %get-tuple-element.53.g_t, f32[128,8,128]{2,1,0:T(8,128)S(1)} %get-tuple-element.49.yf, f32[128,8,128]{2,1,0:T(8,128)S(1)} %get-tuple-element.50.yl, f32[1024,128]{1,0:T(8,128)S(1)} %bitcast.6), custom_call_target="tpu_custom_call" | custom-call | flops 100000 | bytes 100000 | tf_op jit(solution)/shard_map/pallas_call | solution.py:383
  (2 shorter events, 0.0 us)
Async XLA Ops:
  1.5 5.4 %collective-permute-start = (f32[2,8,128]{2,1,0:T(8,128)S(1)}, f32[2,8,128]{2,1,0:T(8,128)S(1)}, u32[]{:S(2)}, u32[]{:S(2)}) collective-permute-start(f32[2,8,128]{2,1,0:T(8,128)S(1)} %get-tuple-element.30), channel_id=1, source_target_pairs={{0,16},{1,2},{2,1},{3,4},{4,3},{5,6},{6,5},{7,8},{8,7},{9,10},{10,... | collective-permute-start | bytes 24584 | tf_op jit(solution)/shard_map/ppermute | solution.py:426
  1.6 5.5 %collective-permute-start.1 = (f32[2,8,128]{2,1,0:T(8,128)S(1)}, f32[2,8,128]{2,1,0:T(8,128)S(1)}, u32[]{:S(2)}, u32[]{:S(2)}) collective-permute-start(f32[2,8,128]{2,1,0:T(8,128)S(1)} %get-tuple-element.31), channel_id=1, source_target_pairs={{0,1},{1,0},{2,3},{3,2},{4,5},{5,4},{6,7},{7,6},{8,9},{9,8},{10,11... | collective-permute-start | bytes 24584 | tf_op jit(solution)/shard_map/ppermute | solution.py:427
  7.2 1.3 %collective-permute-start.2 = (f32[7,16,128]{2,1,0:T(8,128)S(1)}, f32[7,16,128]{2,1,0:T(8,128)S(1)}, u32[]{:S(2)}, u32[]{:S(2)}) collective-permute-start(f32[7,16,128]{2,1,0:T(8,128)S(1)} %get-tuple-element.38.own), channel_id=1, source_target_pairs={{0,16},{16,0},{32,48},{48,32},{64,80},{80,64},{96,112},{112,96},{1... | collective-permute-start | bytes 172040 | tf_op jit(solution)/shard_map/ppermute | solution.py:441
  8.5 5.6 %collective-permute-start.3 = (f32[7,16,128]{2,1,0:T(8,128)S(1)}, f32[7,16,128]{2,1,0:T(8,128)S(1)}, u32[]{:S(2)}, u32[]{:S(2)}) collective-permute-start(f32[7,16,128]{2,1,0:T(8,128)S(1)} %get-tuple-element.44.own), channel_id=1, source_target_pairs={{0,96},{16,80},{32,64},{48,112},{64,32},{80,16},{96,0},{112,48},{1... | collective-permute-start | bytes 172040 | tf_op jit(solution)/shard_map/ppermute | solution.py:450
  11.4 4.2 %collective-permute-start.4 = (f32[7,16,128]{2,1,0:T(8,128)S(1)}, f32[7,16,128]{2,1,0:T(8,128)S(1)}, u32[]{:S(2)}, u32[]{:S(2)}) collective-permute-start(f32[7,16,128]{2,1,0:T(8,128)S(1)} %get-tuple-element.44.own), channel_id=1, source_target_pairs={{0,32},{16,48},{32,0},{48,16},{64,96},{80,112},{96,64},{112,80},{1... | collective-permute-start | bytes 172040 | tf_op jit(solution)/shard_map/ppermute | solution.py:451
  14.1 1.4 %collective-permute-start.5 = (f32[7,16,128]{2,1,0:T(8,128)S(1)}, f32[7,16,128]{2,1,0:T(8,128)S(1)}, u32[]{:S(2)}, u32[]{:S(2)}) collective-permute-start(f32[7,16,128]{2,1,0:T(8,128)S(1)} %shard_map.43), channel_id=1, source_target_pairs={{0,16},{16,0},{32,48},{48,32},{64,80},{80,64},{96,112},{112,96},{1... | collective-permute-start | bytes 172040 | tf_op jit(solution)/shard_map/ppermute | solution.py:460
  16.7 17.6 %all-to-all-start = ((f32[16,5,8,128]{3,2,1,0:T(8,128)}), f32[16,5,8,128]{3,2,1,0:T(8,128)S(1)}, u32[]{:S(2)}, u32[]{:S(2)}) async-start(f32[16,5,8,128]{3,2,1,0:T(8,128)} %get-tuple-element.51), calls=%async_computation | async-start | bytes 655360 | tf_op jit(solution)/shard_map/all_to_all | solution.py:471

commit v9 on v8

--- a/solution.py
+++ b/solution.py
@@ -10,6 +10,7 @@
 ROWS = NZ * BX
 GROUPS = ROWS // 128
 LIMIT = 8 * 1024 * 1024
+SIDE = 4
 PITCH = 72
 
 
@@ -90,11 +91,8 @@
             slots[half + n] = rising
 
 
-def x_flows(own, others, place, blocks, slots):
+def x_flows(blocks, slots):
     count = blocks.shape[0]
-    blocks[place] = own[...]
-    for k, other in enumerate(others):
-        blocks[place ^ (k + 1)] = other
 
     def pivot(i):
         if i == 0:
@@ -109,6 +107,29 @@
         return blocks[i - 1, 6] - blocks[i, 5] if i < count else blocks[i - 1, 6]
 
     flows_of(count, pivot, lambda i: blocks[i - 1, 1], lambda i: blocks[i, 1], gain, slots)
+
+
+def y_merge(low, high):
+    inv = 1.0 / (low[2] + high[0])
+    e = (low[4] - high[3]) * inv
+    a = low[1] * inv
+    b = high[1] * inv
+    joined = [
+        low[0] - low[1] * a,
+        low[1] * b,
+        high[2] - high[1] * b,
+        low[3] - low[1] * e,
+        high[4] + high[1] * e,
+    ]
+    return joined, (e, a, b)
+
+
+def arrange(own, far, near, shared, place, blocks):
+    on_low = lax.rem(lax.axis_index("gx"), 2) == 0
+    blocks[place] = own[...]
+    blocks[place ^ 1] = near[...]
+    blocks[place ^ 2] = jnp.where(on_low, shared[...], far[...])
+    blocks[place ^ 3] = jnp.where(on_low, far[...], shared[...])
 
 
 def y_flows(blocks, slots):
@@ -223,7 +244,7 @@
             edges[2 * n + 1, pl.ds(g, 1), :] = turned[127:128, :]
 
 
-def y_matrix_kernel(ky_t, after, yf, yl, my, f, u, ratios):
+def y_matrix_kernel(ky_t, after, f, u, yf, yl, my, ratios):
     def put(ref):
         def store(j, value):
             ref[j] = value
@@ -301,9 +322,8 @@
     me = lax.axis_index("gx")
     place = lax.div(me, 2)
     on_low = lax.rem(me, 2) == 0
-    second = jnp.where(on_low, shared[...], far[...])
-    third = jnp.where(on_low, far[...], shared[...])
-    x_flows(own, (near[...], second, third), place, blocks, slots)
+    arrange(own, far, near, shared, place, blocks)
+    x_flows(blocks, slots)
     enter, leave = slots[place], slots[place + 1]
     middle = coefs[0] + coefs[1] * enter + coefs[2] * leave
     flows[0] = jnp.where(on_low, enter, middle)
@@ -326,50 +346,62 @@
         lasts[j % 4] = lasts[j % 4] + yl[j] * row
     first = (firsts[0] + firsts[1]) + (firsts[2] + firsts[3])
     last = (lasts[0] + lasts[1]) + (lasts[2] + lasts[3])
-    lead = my[0] + flux[2]
-    for p in range(send.shape[0]):
-        send[p, 0] = lead
-        send[p, 1:3] = my[1:3]
-        send[p, 3] = first
-        send[p, 4] = last
-
-
-def y_local_kernel(v_t, ky_t, st_hbm, g_t, st, f, u, sem):
-    move = pltpu.make_async_copy(st_hbm, st, sem)
-    move.start()
+    send[0] = my[0] + flux[2]
+    send[1:3] = my[1:3]
+    send[3] = first
+    send[4] = last
+
+
+def y_pack_kernel(own, other, both):
+    on_low = lax.rem(lax.axis_index("gx"), 2) == 0
+    both[:, 0:GROUPS] = jnp.where(on_low, own[...], other[...])
+    both[:, GROUPS : 2 * GROUPS] = jnp.where(on_low, other[...], own[...])
+
+
+def y_local_kernel(v_t, f, u, after, g_t):
     total = y_row(v_t, 0)
     g_t[0] = total
-    ahead = jnp.ones_like(total)
-    low = y_row(ky_t, 0)
     for j in range(1, BY):
-        high = y_row(ky_t, j)
-        r = 0.5 * (low + high)
-        low = high
-        inv = (1.0 / (r + ahead))
-        ratio = r * inv
-        ahead = 1.0 + ratio * ahead
-        u[j - 1] = inv
-        f[j - 1] = ratio
-        total = y_row(v_t, j) + ratio * total
+        total = y_row(v_t, j) + f[j - 1] * total
         g_t[j] = total
-    x = total / ahead
-    g_t[BY - 1] = x
-    for j in range(BY - 2, -1, -1):
+    x = jnp.zeros_like(total)
+    for j in range(BY - 1, -1, -1):
         x = u[j] * g_t[j] + f[j] * x
         g_t[j] = x
-    move.wait()
-
-
-def y_solve_kernel(blocks, g_t, yf, yl, st, out_hbm, slots, work, out, sems):
+
+
+def y_merge_kernel(own, far, near, shared, quad, coefs, blocks):
+    arrange(own, far, near, shared, lax.rem(lax.axis_index("gy"), SIDE), blocks)
+    joined = [blocks[0, n] for n in range(5)]
+    for c in range(1, SIDE):
+        joined, flow = y_merge(joined, [blocks[c, n] for n in range(5)])
+        for n in range(3):
+            coefs[c - 1, n] = flow[n]
+    for n in range(5):
+        quad[n] = joined[n]
+
+
+def y_solve_kernel(
+    own, far, near, shared, coefs, g_t, yf, yl, st, out_hbm, blocks, slots, inner, work, out, sems
+):
     me = lax.axis_index("gy")
+    place, depth = lax.div(me, SIDE), lax.rem(me, SIDE)
+    arrange(own, far, near, shared, place, blocks)
     y_flows(blocks, slots)
-    enter, leave = slots[me], slots[me + 1]
+    enter, flow = slots[place], slots[place + 1]
+    inner[0] = enter
+    inner[SIDE] = flow
+    for c in range(SIDE - 1, 0, -1):
+        flow = coefs[c - 1, 0] + coefs[c - 1, 1] * enter + coefs[c - 1, 2] * flow
+        inner[c] = flow
+    rows = pl.ds(pl.multiple_of(lax.rem(lax.axis_index("gx"), 2) * GROUPS, GROUPS), GROUPS)
+    enter, leave = inner[depth, rows, :], inner[depth + 1, rows, :]
     for j in range(BY):
         work[pl.ds(j * GROUPS, GROUPS), :] = 2.0 * (g_t[j] + yf[j] * enter - yl[j] * leave)
     moves = []
     for g in range(GROUPS):
         rows = pl.ds(g * 128, 128)
-        out[rows, :] = st[rows, :] + work[pl.ds(g, BY, stride=GROUPS), :].T
+        out[rows, :] = group(st, g) + work[pl.ds(g, BY, stride=GROUPS), :].T
         move = pltpu.make_async_copy(out.at[rows], out_hbm.at[rows], sems.at[g])
         move.start()
         moves.append(move)
@@ -410,7 +442,7 @@
     x_block = (7, NZ, BY)
     edge = (2, GROUPS, 128)
     nx, ny = lax.axis_size("gx"), lax.axis_size("gy")
-    chips = nx // 2
+    wide = (5, 2 * GROUPS, 128)
     st, kx, st_t, ky_t, mine, first, second = call(
         load_kernel,
         near(planes, planes, plane, plane, (4, GROUPS, 128), edge, edge),
@@ -447,41 +479,61 @@
         cost=3_000_000,
     )
     chip, coefs = call(x_merge_kernel, near(x_block, (3, NZ, BY)), near(ends, other, d))
-    away = [lax.ppermute(chip, "gx", [(i, i ^ (6 - 2 * (i % 2))) for i in range(nx)])]
-    away.append(lax.ppermute(chip, "gx", [(i, i ^ 2) for i in range(nx)]))
-    yf, yl, my = call(
+    def swap(axes, bits, value):
+        return lax.ppermute(
+            value,
+            ("gx", "gy"),
+            [
+                (i * ny + j, (i ^ (2 * bits[i % 2])) * ny + j if axes == "x" else i * ny + (j ^ bits[i % 2]))
+                for i in range(nx)
+                for j in range(ny)
+            ],
+        )
+
+    def share(value):
+        return lax.ppermute(value, "gx", [(i, i ^ 1) for i in range(nx)])
+
+    far = swap("x", (3, 2), chip)
+    near_x = swap("x", (1, 1), chip)
+    f, u, yf, yl, my = call(
         y_matrix_kernel,
-        near(ys, ys, (3, GROUPS, 128)),
+        near(ys, ys, ys, ys, (3, GROUPS, 128)),
         near(ky_t, coefs),
-        [pltpu.VMEM(ys, F32)] * 3,
+        [pltpu.VMEM(ys, F32)],
         cost=5_000_000,
     )
-    (relayed,) = call(relay_kernel, near(x_block), near(away[0], my))
-    away.append(lax.ppermute(relayed, "gx", [(i, i ^ 1) for i in range(nx)]))
-    v_t, send = call(
+    (relayed,) = call(relay_kernel, near(x_block), near(far, my))
+    v_t, own = call(
         y_ends_kernel,
-        near(plane, (ny, 5, GROUPS, 128)),
-        near(chip, *away, coefs, d, wf, wl, yf, yl, my, flux),
+        near(plane, (5, GROUPS, 128)),
+        near(chip, far, near_x, share(relayed), coefs, d, wf, wl, yf, yl, my, flux),
         [
-            pltpu.VMEM((chips,) + x_block, F32),
-            pltpu.VMEM((chips + 1, NZ, BY), F32),
+            pltpu.VMEM((SIDE,) + x_block, F32),
+            pltpu.VMEM((SIDE + 1, NZ, BY), F32),
             pltpu.VMEM((2, NZ, BY), F32),
         ],
     )
-    y_blocks = lax.all_to_all(send, "gy", 0, 0)
-    g_t, st = call(
-        y_local_kernel,
-        near(ys, (NZ, BX, BY)),
-        near(v_t, ky_t) + [(flat[0], True)],
-        [pltpu.VMEM(ys, F32), pltpu.VMEM(ys, F32), pltpu.SemaphoreType.DMA],
-        cost=5_000_000,
-    )
+    (both,) = call(y_pack_kernel, near(wide), near(own, share(own)))
+    far = swap("y", (3, 2), both)
+    near_y = swap("y", (1, 1), both)
+    (g_t,) = call(y_local_kernel, near(ys), near(v_t, f, u, both), cost=3_000_000)
+    (relayed,) = call(relay_kernel, near(wide), near(far, g_t))
+    quad, coefs = call(
+        y_merge_kernel,
+        near(wide, (SIDE - 1, 3, 2 * GROUPS, 128)),
+        near(both, far, near_y, share(relayed)),
+        [pltpu.VMEM((SIDE,) + wide, F32)],
+    )
+    far = swap("y", (12, 8), quad)
+    near_y = swap("y", (4, 4), quad)
     (out,) = call(
         y_solve_kernel,
         [(plane, True)],
-        near(y_blocks, g_t, yf, yl, st.reshape(plane)),
+        near(quad, far, near_y, share(far), coefs, g_t, yf, yl, st),
         [
-            pltpu.VMEM((ny + 1, GROUPS, 128), F32),
+            pltpu.VMEM((SIDE,) + wide, F32),
+            pltpu.VMEM((SIDE + 1, 2 * GROUPS, 128), F32),
+            pltpu.VMEM((SIDE + 1, 2 * GROUPS, 128), F32),
             pltpu.VMEM(plane, F32),
             pltpu.VMEM(plane, F32),
             pltpu.SemaphoreType.DMA((GROUPS,)),

time: 35.7 us -> 34.8 us (0.975)
  Pallas kernels: 8.75 us -> 7.03 us
  waiting for transfers between devices: 11.2 us -> 12.1 us
    ppermute x3 -> x10, waiting for transfers between devices: 2.53 us -> 11.2 us  [the longest x6 9.97 us: swap(): lax.ppermute(value, ('gx', 'gy'), [(i * ny + j, (i ^ 2 * bits[i % 2]) * n...]
    all_to_all x1 -> x0, starting transfers between devices: 8.35 us -> none  [on_device(): y_blocks = lax.all_to_all(send, 'gy', 0, 0)]
    ppermute x3 -> x10, starting transfers between devices: 3.06 us -> 11.2 us  [the longest x6 11.1 us: swap(): lax.ppermute(value, ('gx', 'gy'), [(i * ny + j, (i ^ 2 * bits[i % 2]) * n...]
    all_to_all x1 -> x0, waiting for transfers between devices: 7.71 us -> none  [on_device(): y_blocks = lax.all_to_all(send, 'gy', 0, 0)]
    pallas_call x10 -> x13, Pallas kernels: 8.75 us -> 7.03 us  [call(): pl.pallas_call(kernel, out_shape=[jax.ShapeDtypeStruct(shape, F32) if far...]
  transfers between devices with their start and end apart: 7 -> 13, of which waited for: 5 -> 9; matrix products, arithmetic and copies ran while one was open for 0% -> 0% of each run, Pallas kernels for 14% -> 11%
where the time goes in v9:
time: 34.8 us; the launch traced here: 34.4 us
  starting transfers between devices  15.2 us (44%)
  waiting for transfers between devices  12.1 us (35%)
  Pallas kernels  7.03 us (20%)
    ppermute x6, starting transfers between devices, swap(): lax.ppermute(value, ('gx', 'gy'), [(i * ny + j, (i ^ 2 * bits[i % 2]) * n...  11.1 us
    ppermute x6, waiting for transfers between devices, swap(): lax.ppermute(value, ('gx', 'gy'), [(i * ny + j, (i ^ 2 * bits[i % 2]) * n...  9.97 us
    pallas_call x13, Pallas kernels, call(): pl.pallas_call(kernel, out_shape=[jax.ShapeDtypeStruct(shape, F32) if far...  7.03 us
    ppermute x1, starting transfers between devices, on_device(): came1 = lax.ppermute(first, 'gy', [(i, i ^ 1) for i in range(ny)])  3.91 us
    ppermute x4, waiting for transfers between devices, share(): return lax.ppermute(value, 'gx', [(i, i ^ 1) for i in range(nx)])  1.18 us
  transfers between devices with their start and end apart: 13, of which 9 were waited for; matrix products, arithmetic and copies ran while one was open for 0% of the time, Pallas kernels for 11%

profile of v9, /device:TPU:0, one launch (start us, length us, event | category | flops | bytes accessed | tf_op | source)
XLA Modules:
  0.0 34.4 jit_solution(2541853824150308045)
XLA Ops:
  0.0 1.5 %shard_map.37 = (f32[16,72,128]{2,1,0:T(8,128)S(1)}, f32[16,72,128]{2,1,0:T(8,128)S(1)}, f32[1024,128]{1,0:T(8,128)S(1)}, f32[1024,128]{1,0:T(8,128)S(1)}, f32[4...) custom-call(f32[16,64,128]{2,1,0:T(8,128)} %st_hbm.1, f32[16,64,128]{2,1,0:T(8,128)} %kx_hbm.1, ...), custom_call_target="tpu_custom_call" | custom-call | flops 100000 | bytes 100000 | tf_op jit(solution)/shard_map/pallas_call | solution.py:415
  1.5 0.1 collective-permute-start
  1.6 3.9 %collective-permute-start.1 = (f32[2,8,128]{2,1,0:T(8,128)S(1)}, f32[2,8,128]{2,1,0:T(8,128)S(1)}, u32[]{:S(2)}, u32[]{:S(2)}) collective-permute-start(f32[2,8,128]{2,1,0:T(8,128)S(1)} %get-tuple-element.33), channel_id=1, source_target_pairs={{0,1},{1,0},{2,3},{3,2},{4,5},{5,4},{6,7},{7,6},{8,9},{9,8},{10,11... | collective-permute-start | bytes 24584 | tf_op jit(solution)/shard_map/ppermute | solution.py:459
  5.5 1.4 %shard_map.38 = (f32[64,16,128]{2,1,0:T(8,128)S(1)}, f32[64,16,128]{2,1,0:T(8,128)S(1)}, f32[1152,128]{1,0:T(8,128)S(1)}, f32[1152,128]{1,0:T(8,128)S(1)}, f32[7...) custom-call(f32[1024,128]{1,0:T(8,128)S(1)} %get-tuple-element.35.st_t, ...), custom_call_target="tpu_custom_call" | custom-call | flops 5000000 | bytes 5000000 | tf_op jit(solution)/shard_map/pallas_call | solution.py:415
  6.9 0.3 collective-permute-done.1.came1
  7.1 0.1 shard_map.39
  7.3 0.5 %shard_map.40.after.d = f32[1152,128]{1,0:T(8,128)S(1)} custom-call(f32[1024,128]{1,0:T(8,128)S(1)} %get-tuple-element.41.base_t, f32[3,8,128]{2,1,0:T(8,128)S(1)} %get-tuple-element.42.flux, f32[1152,128]{1,0:T(8,128)S(1)} %bitcast.3, f32[64,16,128]{2,1,0:T(8,128)S(1)} %get-tuple-element.44.fx, f32[64,16,128]{2,1,0:T(8,128)S(1)} %get-tuple-element.45.ux), custom_call_target="tpu_custom_call" | custom-call | flops 3000000 | bytes 3000000 | tf_op jit(solution)/shard_map/pallas_call | solution.py:415
  7.8 0.7 %collective-permute-done.2.other = f32[7,16,128]{2,1,0:T(8,128)S(1)} collective-permute-done((f32[7,16,128]{2,1,0:T(8,128)S(1)}, f32[7,16,128]{2,1,0:T(8,128)S(1)}, u32[]{:S(2)}, u32[]{:S(2)}) %collective-permute-start.2) | collective-permute-done | bytes 57376 | tf_op jit(solution)/shard_map/ppermute | solution.py:473
  8.5 2.8 %collective-permute-start.3 = (f32[7,16,128]{2,1,0:T(8,128)S(1)}, f32[7,16,128]{2,1,0:T(8,128)S(1)}, u32[]{:S(2)}, u32[]{:S(2)}) collective-permute-start(f32[7,16,128]{2,1,0:T(8,128)S(1)} %get-tuple-element.46.own), channel_id=1, source_target_pairs={{0,96},{1,97},{2,98},{3,99},{4,100},{5,101},{6,102},{7,103},{8,104... | collective-permute-start | bytes 172040 | tf_op jit(solution)/shard_map/ppermute | solution.py:483
  11.4 0.2 collective-permute-start.4
  11.6 1.4 %shard_map.42 = (f32[128,8,128]{2,1,0:T(8,128)S(1)}, f32[128,8,128]{2,1,0:T(8,128)S(1)}, f32[128,8,128]{2,1,0:T(8,128)S(1)}, f32[128,8,128]{2,1,0:T(8,128)S(1)}, f32[3,8,128]{2,1,0:T(8,128)S(1)}) custom-call(f32[1024,128]{1,0:T(8,128)S(1)} %get-tuple-element.37.ky_t, f32[3,16,128]{2,1,0:T(8,128)S(1)} %get-tuple-element.47.after.coefs), custom_call_target="tpu_custom_call" | custom-call | flops 5000000 | bytes 5000000 | tf_op jit(solution)/shard_map/pallas_call | solution.py:415
  13.0 1.1 %collective-permute-done.3.value.far = f32[7,16,128]{2,1,0:T(8,128)S(1)} collective-permute-done((f32[7,16,128]{2,1,0:T(8,128)S(1)}, f32[7,16,128]{2,1,0:T(8,128)S(1)}, u32[]{:S(2)}, u32[]{:S(2)}) %collective-permute-start.3) | collective-permute-done | bytes 57376 | tf_op jit(solution)/shard_map/ppermute | solution.py:483
  14.1 1.4 %collective-permute-done.4.near = f32[7,16,128]{2,1,0:T(8,128)S(1)} collective-permute-done((f32[7,16,128]{2,1,0:T(8,128)S(1)}, f32[7,16,128]{2,1,0:T(8,128)S(1)}, u32[]{:S(2)}, u32[]{:S(2)}) %collective-permute-start.4) | collective-permute-done | bytes 57376 | tf_op jit(solution)/shard_map/ppermute | solution.py:483
  15.6 0.4 %shard_map.44 = (f32[1024,128]{1,0:T(8,128)S(1)}, f32[5,8,128]{2,1,0:T(8,128)S(1)}) custom-call(f32[7,16,128]{2,1,0:T(8,128)S(1)} %get-tuple-element.46.own, f32[7,16,128]{2,1,0:T(8,128)S(1)} %collective-permute-done.3.value.far, f32[7,16,128]{2,1,0:T(8,128)S(1)} %collective-permute-done.4.near, f32[7,16,128]{2,1,0:T(8,128)S(1)} %collective-permute-done.5.shared, ...), custom_call_target="tpu_custom_call" | custom-call | flops 100000 | bytes 100000 | tf_op jit(solution)/shard_map/pallas_call | solution.py:415
  16.0 0.1 collective-permute-start.6
  16.1 1.2 %collective-permute-done.6.other = f32[5,8,128]{2,1,0:T(8,128)S(1)} collective-permute-done((f32[5,8,128]{2,1,0:T(8,128)S(1)}, f32[5,8,128]{2,1,0:T(8,128)S(1)}, u32[]{:S(2)}, u32[]{:S(2)}) %collective-permute-start.6) | collective-permute-done | bytes 20512 | tf_op jit(solution)/shard_map/ppermute | solution.py:494
  17.2 4.4 %collective-permute-start.7 = (f32[5,16,128]{2,1,0:T(8,128)S(1)}, f32[5,16,128]{2,1,0:T(8,128)S(1)}, u32[]{:S(2)}, u32[]{:S(2)}) collective-permute-start(f32[5,16,128]{2,1,0:T(8,128)S(1)} %shard_map.45.after.own), channel_id=1, source_target_pairs={{0,3},{1,2},{2,1},{3,0},{4,7},{5,6},{6,5},{7,4},{8,11},{9,10},{10,... | collective-permute-start | bytes 122888 | tf_op jit(solution)/shard_map/ppermute | solution.py:483
  21.7 0.5 %shard_map.46.after.g_t = f32[128,8,128]{2,1,0:T(8,128)S(1)} custom-call(f32[1024,128]{1,0:T(8,128)S(1)} %get-tuple-element.54.v_t, f32[128,8,128]{2,1,0:T(8,128)S(1)} %get-tuple-element.55.f, f32[128,8,128]{2,1,0:T(8,128)S(1)} %get-tuple-element.56.u, f32[5,16,128]{2,1,0:T(8,128)S(1)} %shard_map.45.after.own), custom_call_target="tpu_custom_call" | custom-call | flops 3000000 | bytes 3000000 | tf_op jit(solution)/shard_map/pallas_call | solution.py:415
  22.2 1.4 %collective-permute-done.7.value.far = f32[5,16,128]{2,1,0:T(8,128)S(1)} collective-permute-done((f32[5,16,128]{2,1,0:T(8,128)S(1)}, f32[5,16,128]{2,1,0:T(8,128)S(1)}, u32[]{:S(2)}, u32[]{:S(2)}) %collective-permute-start.7) | collective-permute-done | bytes 40992 | tf_op jit(solution)/shard_map/ppermute | solution.py:483
  23.6 2.0 %collective-permute-done.8.near = f32[5,16,128]{2,1,0:T(8,128)S(1)} collective-permute-done((f32[5,16,128]{2,1,0:T(8,128)S(1)}, f32[5,16,128]{2,1,0:T(8,128)S(1)}, u32[]{:S(2)}, u32[]{:S(2)}) %collective-permute-start.8) | collective-permute-done | bytes 40992 | tf_op jit(solution)/shard_map/ppermute | solution.py:483
  25.7 3.6 %collective-permute-start.10 = (f32[5,16,128]{2,1,0:T(8,128)S(1)}, f32[5,16,128]{2,1,0:T(8,128)S(1)}, u32[]{:S(2)}, u32[]{:S(2)}) collective-permute-start(f32[5,16,128]{2,1,0:T(8,128)S(1)} %get-tuple-element.57.own), channel_id=1, source_target_pairs={{0,12},{1,13},{2,14},{3,15},{4,8},{5,9},{6,10},{7,11},{8,4},{9,5},... | collective-permute-start | bytes 122888 | tf_op jit(solution)/shard_map/ppermute | solution.py:483
  29.3 2.0 %collective-permute-done.10.far = f32[5,16,128]{2,1,0:T(8,128)S(1)} collective-permute-done((f32[5,16,128]{2,1,0:T(8,128)S(1)}, f32[5,16,128]{2,1,0:T(8,128)S(1)}, u32[]{:S(2)}, u32[]{:S(2)}) %collective-permute-start.10) | collective-permute-done | bytes 40992 | tf_op jit(solution)/shard_map/ppermute | solution.py:483
  31.3 2.0 %collective-permute-done.11.near = f32[5,16,128]{2,1,0:T(8,128)S(1)} collective-permute-done((f32[5,16,128]{2,1,0:T(8,128)S(1)}, f32[5,16,128]{2,1,0:T(8,128)S(1)}, u32[]{:S(2)}, u32[]{:S(2)}) %collective-permute-start.11) | collective-permute-done | bytes 40992 | tf_op jit(solution)/shard_map/ppermute | solution.py:483
  33.3 1.1 %shard_map.49 = f32[1024,128]{1,0:T(8,128)} custom-call(f32[5,16,128]{2,1,0:T(8,128)S(1)} %get-tuple-element.57.own, f32[5,16,128]{2,1,0:T(8,128)S(1)} %collective-permute-done.10.far, f32[5,16,128]{2,1,0:T(8,128)S(1)} %collective-permute-done.11.near, f32[5,16,128]{2,1,0:T(8,128)S(1)} %collective-permute-done.12.shared, ...), custom_call_target="tpu_custom_call" | custom-call | flops 100000 | bytes 100000 | tf_op jit(solution)/shard_map/pallas_call | solution.py:415
  (15 shorter events, 0.2 us)
Async XLA Ops:
  1.5 5.4 %collective-permute-start = (f32[2,8,128]{2,1,0:T(8,128)S(1)}, f32[2,8,128]{2,1,0:T(8,128)S(1)}, u32[]{:S(2)}, u32[]{:S(2)}) collective-permute-start(f32[2,8,128]{2,1,0:T(8,128)S(1)} %get-tuple-element.32), channel_id=1, source_target_pairs={{0,16},{1,2},{2,1},{3,4},{4,3},{5,6},{6,5},{7,8},{8,7},{9,10},{10,... | collective-permute-start | bytes 24584 | tf_op jit(solution)/shard_map/ppermute | solution.py:458
  1.6 5.5 %collective-permute-start.1 = (f32[2,8,128]{2,1,0:T(8,128)S(1)}, f32[2,8,128]{2,1,0:T(8,128)S(1)}, u32[]{:S(2)}, u32[]{:S(2)}) collective-permute-start(f32[2,8,128]{2,1,0:T(8,128)S(1)} %get-tuple-element.33), channel_id=1, source_target_pairs={{0,1},{1,0},{2,3},{3,2},{4,5},{5,4},{6,7},{7,6},{8,9},{9,8},{10,11... | collective-permute-start | bytes 24584 | tf_op jit(solution)/shard_map/ppermute | solution.py:459
  7.2 1.3 %collective-permute-start.2 = (f32[7,16,128]{2,1,0:T(8,128)S(1)}, f32[7,16,128]{2,1,0:T(8,128)S(1)}, u32[]{:S(2)}, u32[]{:S(2)}) collective-permute-start(f32[7,16,128]{2,1,0:T(8,128)S(1)} %get-tuple-element.40.own), channel_id=1, source_target_pairs={{0,16},{16,0},{32,48},{48,32},{64,80},{80,64},{96,112},{112,96},{1... | collective-permute-start | bytes 172040 | tf_op jit(solution)/shard_map/ppermute | solution.py:473
  8.5 5.6 %collective-permute-start.3 = (f32[7,16,128]{2,1,0:T(8,128)S(1)}, f32[7,16,128]{2,1,0:T(8,128)S(1)}, u32[]{:S(2)}, u32[]{:S(2)}) collective-permute-start(f32[7,16,128]{2,1,0:T(8,128)S(1)} %get-tuple-element.46.own), channel_id=1, source_target_pairs={{0,96},{1,97},{2,98},{3,99},{4,100},{5,101},{6,102},{7,103},{8,104... | collective-permute-start | bytes 172040 | tf_op jit(solution)/shard_map/ppermute | solution.py:483
  11.4 4.2 %collective-permute-start.4 = (f32[7,16,128]{2,1,0:T(8,128)S(1)}, f32[7,16,128]{2,1,0:T(8,128)S(1)}, u32[]{:S(2)}, u32[]{:S(2)}) collective-permute-start(f32[7,16,128]{2,1,0:T(8,128)S(1)} %get-tuple-element.46.own), channel_id=1, source_target_pairs={{0,32},{1,33},{2,34},{3,35},{4,36},{5,37},{6,38},{7,39},{8,40},{9,... | collective-permute-start | bytes 172040 | tf_op jit(solution)/shard_map/ppermute | solution.py:483
  14.1 1.4 %collective-permute-start.5 = (f32[7,16,128]{2,1,0:T(8,128)S(1)}, f32[7,16,128]{2,1,0:T(8,128)S(1)}, u32[]{:S(2)}, u32[]{:S(2)}) collective-permute-start(f32[7,16,128]{2,1,0:T(8,128)S(1)} %shard_map.43), channel_id=1, source_target_pairs={{0,16},{16,0},{32,48},{48,32},{64,80},{80,64},{96,112},{112,96},{1... | collective-permute-start | bytes 172040 | tf_op jit(solution)/shard_map/ppermute | solution.py:494
  16.0 1.3 %collective-permute-start.6 = (f32[5,8,128]{2,1,0:T(8,128)S(1)}, f32[5,8,128]{2,1,0:T(8,128)S(1)}, u32[]{:S(2)}, u32[]{:S(2)}) collective-permute-start(f32[5,8,128]{2,1,0:T(8,128)S(1)} %get-tuple-element.53.own), channel_id=1, source_target_pairs={{0,16},{16,0},{32,48},{48,32},{64,80},{80,64},{96,112},{112,96},{1... | collective-permute-start | bytes 61448 | tf_op jit(solution)/shard_map/ppermute | solution.py:494
  17.2 6.4 %collective-permute-start.7 = (f32[5,16,128]{2,1,0:T(8,128)S(1)}, f32[5,16,128]{2,1,0:T(8,128)S(1)}, u32[]{:S(2)}, u32[]{:S(2)}) collective-permute-start(f32[5,16,128]{2,1,0:T(8,128)S(1)} %shard_map.45.after.own), channel_id=1, source_target_pairs={{0,3},{1,2},{2,1},{3,0},{4,7},{5,6},{6,5},{7,4},{8,11},{9,10},{10,... | collective-permute-start | bytes 122888 | tf_op jit(solution)/shard_map/ppermute | solution.py:483
  21.7 4.0 %collective-permute-start.8 = (f32[5,16,128]{2,1,0:T(8,128)S(1)}, f32[5,16,128]{2,1,0:T(8,128)S(1)}, u32[]{:S(2)}, u32[]{:S(2)}) collective-permute-start(f32[5,16,128]{2,1,0:T(8,128)S(1)} %shard_map.45.after.own), channel_id=1, source_target_pairs={{0,1},{1,0},{2,3},{3,2},{4,5},{5,4},{6,7},{7,6},{8,9},{9,8},{10,11... | collective-permute-start | bytes 122888 | tf_op jit(solution)/shard_map/ppermute | solution.py:483
  23.6 2.0 %collective-permute-start.9 = (f32[5,16,128]{2,1,0:T(8,128)S(1)}, f32[5,16,128]{2,1,0:T(8,128)S(1)}, u32[]{:S(2)}, u32[]{:S(2)}) collective-permute-start(f32[5,16,128]{2,1,0:T(8,128)S(1)} %shard_map.47), channel_id=1, source_target_pairs={{0,16},{16,0},{32,48},{48,32},{64,80},{80,64},{96,112},{112,96},{1... | collective-permute-start | bytes 122888 | tf_op jit(solution)/shard_map/ppermute | solution.py:494
  25.7 5.6 %collective-permute-start.10 = (f32[5,16,128]{2,1,0:T(8,128)S(1)}, f32[5,16,128]{2,1,0:T(8,128)S(1)}, u32[]{:S(2)}, u32[]{:S(2)}) collective-permute-start(f32[5,16,128]{2,1,0:T(8,128)S(1)} %get-tuple-element.57.own), channel_id=1, source_target_pairs={{0,12},{1,13},{2,14},{3,15},{4,8},{5,9},{6,10},{7,11},{8,4},{9,5},... | collective-permute-start | bytes 122888 | tf_op jit(solution)/shard_map/ppermute | solution.py:483
  29.3 4.0 %collective-permute-start.11 = (f32[5,16,128]{2,1,0:T(8,128)S(1)}, f32[5,16,128]{2,1,0:T(8,128)S(1)}, u32[]{:S(2)}, u32[]{:S(2)}) collective-permute-start(f32[5,16,128]{2,1,0:T(8,128)S(1)} %get-tuple-element.57.own), channel_id=1, source_target_pairs={{0,4},{1,5},{2,6},{3,7},{4,0},{5,1},{6,2},{7,3},{8,12},{9,13},{10,... | collective-permute-start | bytes 122888 | tf_op jit(solution)/shard_map/ppermute | solution.py:483
  31.3 2.0 %collective-permute-start.12 = (f32[5,16,128]{2,1,0:T(8,128)S(1)}, f32[5,16,128]{2,1,0:T(8,128)S(1)}, u32[]{:S(2)}, u32[]{:S(2)}) collective-permute-start(f32[5,16,128]{2,1,0:T(8,128)S(1)} %collective-permute-done.10.far), channel_id=1, source_target_pairs={{0,16},{16,0},{32,48},{48,32},{64,80},{80,64},{96,112},{112,96},{1... | collective-permute-start | bytes 122888 | tf_op jit(solution)/shard_map/ppermute | solution.py:494

commit v10 on v9

--- a/solution.py
+++ b/solution.py
@@ -127,9 +127,9 @@
 def arrange(own, far, near, shared, place, blocks):
     on_low = lax.rem(lax.axis_index("gx"), 2) == 0
     blocks[place] = own[...]
-    blocks[place ^ 1] = near[...]
+    blocks[place ^ 3] = near[...]
     blocks[place ^ 2] = jnp.where(on_low, shared[...], far[...])
-    blocks[place ^ 3] = jnp.where(on_low, far[...], shared[...])
+    blocks[place ^ 1] = jnp.where(on_low, far[...], shared[...])
 
 
 def y_flows(blocks, slots):
@@ -259,7 +259,7 @@
     my[2] = trail + jnp.where(me == last, (2.0 / (y_row(ky_t, BY - 1))), 0.0)
 
 
-def x_ends_kernel(came2, came1, mine, part, edges, send, flux, rows):
+def x_ends_kernel(came1, came2, mine, part, edges, send, flux, rows):
     me = lax.axis_index("gy")
     even = lax.rem(me, 2) == 0
     below = jnp.where(me == 0, 0.0, jnp.where(even, came2[...], came1[...]))
@@ -370,7 +370,21 @@
         g_t[j] = x
 
 
-def y_merge_kernel(own, far, near, shared, quad, coefs, blocks):
+def own_rows():
+    start = lax.rem(lax.axis_index("gx"), 2) * GROUPS
+    return pl.ds(pl.multiple_of(start, GROUPS), GROUPS)
+
+
+def other_rows():
+    start = (1 - lax.rem(lax.axis_index("gx"), 2)) * GROUPS
+    return pl.ds(pl.multiple_of(start, GROUPS), GROUPS)
+
+
+def pick_kernel(value, out):
+    out[...] = value[:, other_rows(), :]
+
+
+def y_merge_kernel(own, far, near, shared, quad, mine, coefs, blocks):
     arrange(own, far, near, shared, lax.rem(lax.axis_index("gy"), SIDE), blocks)
     joined = [blocks[0, n] for n in range(5)]
     for c in range(1, SIDE):
@@ -379,23 +393,25 @@
             coefs[c - 1, n] = flow[n]
     for n in range(5):
         quad[n] = joined[n]
+    mine[...] = quad[:, own_rows(), :]
 
 
 def y_solve_kernel(
-    own, far, near, shared, coefs, g_t, yf, yl, st, out_hbm, blocks, slots, inner, work, out, sems
+    mine, far, near, shared, coefs, g_t, yf, yl, st, out_hbm, blocks, slots, inner, work, out, sems
 ):
     me = lax.axis_index("gy")
     place, depth = lax.div(me, SIDE), lax.rem(me, SIDE)
-    arrange(own, far, near, shared, place, blocks)
+    rows = own_rows()
+    arrange(mine, far.at[:, rows, :], near, shared, place, blocks)
     y_flows(blocks, slots)
     enter, flow = slots[place], slots[place + 1]
     inner[0] = enter
     inner[SIDE] = flow
     for c in range(SIDE - 1, 0, -1):
-        flow = coefs[c - 1, 0] + coefs[c - 1, 1] * enter + coefs[c - 1, 2] * flow
+        e, a, b = [coefs[c - 1, n, rows, :] for n in range(3)]
+        flow = e + a * enter + b * flow
         inner[c] = flow
-    rows = pl.ds(pl.multiple_of(lax.rem(lax.axis_index("gx"), 2) * GROUPS, GROUPS), GROUPS)
-    enter, leave = inner[depth, rows, :], inner[depth + 1, rows, :]
+    enter, leave = inner[depth], inner[depth + 1]
     for j in range(BY):
         work[pl.ds(j * GROUPS, GROUPS), :] = 2.0 * (g_t[j] + yf[j] * enter - yl[j] * leave)
     moves = []
@@ -467,7 +483,7 @@
     ends, flux = call(
         x_ends_kernel,
         near(x_block, (3, GROUPS, 128)),
-        near(came2, came1, mine, part, edges),
+        near(came1, came2, mine, part, edges),
         [pltpu.VMEM((2, NZ, BY), F32)],
     )
     other = lax.ppermute(ends, "gx", [(i, i ^ 1) for i in range(nx)])
@@ -493,8 +509,8 @@
     def share(value):
         return lax.ppermute(value, "gx", [(i, i ^ 1) for i in range(nx)])
 
-    far = swap("x", (3, 2), chip)
-    near_x = swap("x", (1, 1), chip)
+    far = swap("x", (1, 2), chip)
+    near_x = swap("x", (3, 3), chip)
     f, u, yf, yl, my = call(
         y_matrix_kernel,
         near(ys, ys, ys, ys, (3, GROUPS, 128)),
@@ -514,26 +530,27 @@
         ],
     )
     (both,) = call(y_pack_kernel, near(wide), near(own, share(own)))
-    far = swap("y", (3, 2), both)
-    near_y = swap("y", (1, 1), both)
+    far = swap("y", (1, 2), both)
+    near_y = swap("y", (3, 3), both)
     (g_t,) = call(y_local_kernel, near(ys), near(v_t, f, u, both), cost=3_000_000)
     (relayed,) = call(relay_kernel, near(wide), near(far, g_t))
-    quad, coefs = call(
+    quad, mine, coefs = call(
         y_merge_kernel,
-        near(wide, (SIDE - 1, 3, 2 * GROUPS, 128)),
+        near(wide, (5, GROUPS, 128), (SIDE - 1, 3, 2 * GROUPS, 128)),
         near(both, far, near_y, share(relayed)),
         [pltpu.VMEM((SIDE,) + wide, F32)],
     )
-    far = swap("y", (12, 8), quad)
-    near_y = swap("y", (4, 4), quad)
+    far = swap("y", (4, 8), quad)
+    near_y = swap("y", (12, 12), mine)
+    (picked,) = call(pick_kernel, near((5, GROUPS, 128)), near(far))
     (out,) = call(
         y_solve_kernel,
         [(plane, True)],
-        near(quad, far, near_y, share(far), coefs, g_t, yf, yl, st),
+        near(mine, far, near_y, share(picked), coefs, g_t, yf, yl, st),
         [
-            pltpu.VMEM((SIDE,) + wide, F32),
-            pltpu.VMEM((SIDE + 1, 2 * GROUPS, 128), F32),
-            pltpu.VMEM((SIDE + 1, 2 * GROUPS, 128), F32),
+            pltpu.VMEM((SIDE, 5, GROUPS, 128), F32),
+            pltpu.VMEM((SIDE + 1, GROUPS, 128), F32),
+            pltpu.VMEM((SIDE + 1, GROUPS, 128), F32),
             pltpu.VMEM(plane, F32),
             pltpu.VMEM(plane, F32),
             pltpu.SemaphoreType.DMA((GROUPS,)),

time: 34.8 us -> 34.5 us (level)
  the two profiles are of different devices: /device:TPU:0 before, /device:TPU:1 now
where the time goes in v10:
time: 34.5 us; the launch traced here: 34.4 us
  starting transfers between devices  19.5 us (57%)
  waiting for transfers between devices  7.76 us (22%)
  Pallas kernels  7.06 us (20%)
    ppermute x6, starting transfers between devices, swap(): lax.ppermute(value, ('gx', 'gy'), [(i * ny + j, (i ^ 2 * bits[i % 2]) * n...  14.2 us
    pallas_call x14, Pallas kernels, call(): pl.pallas_call(kernel, out_shape=[jax.ShapeDtypeStruct(shape, F32) if far...  7.06 us
    ppermute x6, waiting for transfers between devices, swap(): lax.ppermute(value, ('gx', 'gy'), [(i * ny + j, (i ^ 2 * bits[i % 2]) * n...  6.44 us
    ppermute x1, starting transfers between devices, on_device(): came1 = lax.ppermute(first, 'gy', [(i, i ^ 1) for i in range(ny)])  2.55 us
    ppermute x4, starting transfers between devices, share(): return lax.ppermute(value, 'gx', [(i, i ^ 1) for i in range(nx)])  1.51 us
    ppermute x1, starting transfers between devices, on_device(): came2 = lax.ppermute(second, ('gx', 'gy'), pairs)  0.96 us
    ppermute x4, waiting for transfers between devices, share(): return lax.ppermute(value, 'gx', [(i, i ^ 1) for i in range(nx)])  0.87 us
  transfers between devices with their start and end apart: 13, of which 6 were waited for; matrix products, arithmetic and copies ran while one was open for 0% of the time, Pallas kernels for 11%

profile of v10, /device:TPU:1, one launch (start us, length us, event | category | flops | bytes accessed | tf_op | source)
XLA Modules:
  0.0 34.4 jit_solution(9619141537696803852)
XLA Ops:
  0.0 1.5 %shard_map.37 = (f32[16,72,128]{2,1,0:T(8,128)S(1)}, f32[16,72,128]{2,1,0:T(8,128)S(1)}, f32[1024,128]{1,0:T(8,128)S(1)}, f32[1024,128]{1,0:T(8,128)S(1)}, f32[4...) custom-call(f32[16,64,128]{2,1,0:T(8,128)} %st_hbm.1, f32[16,64,128]{2,1,0:T(8,128)} %kx_hbm.1, ...), custom_call_target="tpu_custom_call" | custom-call | flops 100000 | bytes 100000 | tf_op jit(solution)/shard_map/pallas_call | solution.py:431
  1.5 2.5 %collective-permute-start = (f32[2,8,128]{2,1,0:T(8,128)S(1)}, f32[2,8,128]{2,1,0:T(8,128)S(1)}, u32[]{:S(2)}, u32[]{:S(2)}) collective-permute-start(f32[2,8,128]{2,1,0:T(8,128)S(1)} %get-tuple-element.33), channel_id=1, source_target_pairs={{0,1},{1,0},{2,3},{3,2},{4,5},{5,4},{6,7},{7,6},{8,9},{9,8},{10,11... | collective-permute-start | bytes 24584 | tf_op jit(solution)/shard_map/ppermute | solution.py:475
  4.0 1.0 %collective-permute-start.1 = (f32[2,8,128]{2,1,0:T(8,128)S(1)}, f32[2,8,128]{2,1,0:T(8,128)S(1)}, u32[]{:S(2)}, u32[]{:S(2)}) collective-permute-start(f32[2,8,128]{2,1,0:T(8,128)S(1)} %get-tuple-element.34), channel_id=1, source_target_pairs={{0,16},{1,2},{2,1},{3,4},{4,3},{5,6},{6,5},{7,8},{8,7},{9,10},{10,... | collective-permute-start | bytes 24584 | tf_op jit(solution)/shard_map/ppermute | solution.py:474
  5.0 1.4 %shard_map.38 = (f32[64,16,128]{2,1,0:T(8,128)S(1)}, f32[64,16,128]{2,1,0:T(8,128)S(1)}, f32[1152,128]{1,0:T(8,128)S(1)}, f32[1152,128]{1,0:T(8,128)S(1)}, f32[7...) custom-call(f32[1024,128]{1,0:T(8,128)S(1)} %get-tuple-element.36.st_t, ...), custom_call_target="tpu_custom_call" | custom-call | flops 5000000 | bytes 5000000 | tf_op jit(solution)/shard_map/pallas_call | solution.py:431
  6.8 0.5 %shard_map.40.after.d = f32[1152,128]{1,0:T(8,128)S(1)} custom-call(f32[1024,128]{1,0:T(8,128)S(1)} %get-tuple-element.42.base_t, f32[3,8,128]{2,1,0:T(8,128)S(1)} %get-tuple-element.43.flux, f32[1152,128]{1,0:T(8,128)S(1)} %bitcast.3, f32[64,16,128]{2,1,0:T(8,128)S(1)} %get-tuple-element.45.fx, f32[64,16,128]{2,1,0:T(8,128)S(1)} %get-tuple-element.46.ux), custom_call_target="tpu_custom_call" | custom-call | flops 3000000 | bytes 3000000 | tf_op jit(solution)/shard_map/pallas_call | solution.py:431
  7.3 0.4 %collective-permute-done.2.other = f32[7,16,128]{2,1,0:T(8,128)S(1)} collective-permute-done((f32[7,16,128]{2,1,0:T(8,128)S(1)}, f32[7,16,128]{2,1,0:T(8,128)S(1)}, u32[]{:S(2)}, u32[]{:S(2)}) %collective-permute-start.2) | collective-permute-done | bytes 57376 | tf_op jit(solution)/shard_map/ppermute | solution.py:489
  7.8 2.8 %collective-permute-start.3 = (f32[7,16,128]{2,1,0:T(8,128)S(1)}, f32[7,16,128]{2,1,0:T(8,128)S(1)}, u32[]{:S(2)}, u32[]{:S(2)}) collective-permute-start(f32[7,16,128]{2,1,0:T(8,128)S(1)} %get-tuple-element.47.own), channel_id=1, source_target_pairs={{0,32},{1,33},{2,34},{3,35},{4,36},{5,37},{6,38},{7,39},{8,40},{9,... | collective-permute-start | bytes 172040 | tf_op jit(solution)/shard_map/ppermute | solution.py:499
  10.6 0.9 %collective-permute-start.4 = (f32[7,16,128]{2,1,0:T(8,128)S(1)}, f32[7,16,128]{2,1,0:T(8,128)S(1)}, u32[]{:S(2)}, u32[]{:S(2)}) collective-permute-start(f32[7,16,128]{2,1,0:T(8,128)S(1)} %get-tuple-element.47.own), channel_id=1, source_target_pairs={{0,96},{1,97},{2,98},{3,99},{4,100},{5,101},{6,102},{7,103},{8,104... | collective-permute-start | bytes 172040 | tf_op jit(solution)/shard_map/ppermute | solution.py:499
  11.5 1.4 %shard_map.42 = (f32[128,8,128]{2,1,0:T(8,128)S(1)}, f32[128,8,128]{2,1,0:T(8,128)S(1)}, f32[128,8,128]{2,1,0:T(8,128)S(1)}, f32[128,8,128]{2,1,0:T(8,128)S(1)}, f32[3,8,128]{2,1,0:T(8,128)S(1)}) custom-call(f32[1024,128]{1,0:T(8,128)S(1)} %get-tuple-element.38.ky_t, f32[3,16,128]{2,1,0:T(8,128)S(1)} %get-tuple-element.48.after.coefs), custom_call_target="tpu_custom_call" | custom-call | flops 5000000 | bytes 5000000 | tf_op jit(solution)/shard_map/pallas_call | solution.py:431
  12.9 0.4 %collective-permute-start.5 = (f32[7,16,128]{2,1,0:T(8,128)S(1)}, f32[7,16,128]{2,1,0:T(8,128)S(1)}, u32[]{:S(2)}, u32[]{:S(2)}) collective-permute-start(f32[7,16,128]{2,1,0:T(8,128)S(1)} %shard_map.43), channel_id=1, source_target_pairs={{0,16},{16,0},{32,48},{48,32},{64,80},{80,64},{96,112},{112,96},{1... | collective-permute-start | bytes 172040 | tf_op jit(solution)/shard_map/ppermute | solution.py:510
  13.3 1.7 %collective-permute-done.4.near = f32[7,16,128]{2,1,0:T(8,128)S(1)} collective-permute-done((f32[7,16,128]{2,1,0:T(8,128)S(1)}, f32[7,16,128]{2,1,0:T(8,128)S(1)}, u32[]{:S(2)}, u32[]{:S(2)}) %collective-permute-start.4) | collective-permute-done | bytes 57376 | tf_op jit(solution)/shard_map/ppermute | solution.py:499
  15.0 0.4 %shard_map.44 = (f32[1024,128]{1,0:T(8,128)S(1)}, f32[5,8,128]{2,1,0:T(8,128)S(1)}) custom-call(f32[7,16,128]{2,1,0:T(8,128)S(1)} %get-tuple-element.47.own, f32[7,16,128]{2,1,0:T(8,128)S(1)} %collective-permute-done.3.value.far, f32[7,16,128]{2,1,0:T(8,128)S(1)} %collective-permute-done.4.near, f32[7,16,128]{2,1,0:T(8,128)S(1)} %collective-permute-done.5.shared, ...), custom_call_target="tpu_custom_call" | custom-call | flops 100000 | bytes 100000 | tf_op jit(solution)/shard_map/pallas_call | solution.py:431
  15.4 0.4 %collective-permute-start.6 = (f32[5,8,128]{2,1,0:T(8,128)S(1)}, f32[5,8,128]{2,1,0:T(8,128)S(1)}, u32[]{:S(2)}, u32[]{:S(2)}) collective-permute-start(f32[5,8,128]{2,1,0:T(8,128)S(1)} %get-tuple-element.54.own), channel_id=1, source_target_pairs={{0,16},{16,0},{32,48},{48,32},{64,80},{80,64},{96,112},{112,96},{1... | collective-permute-start | bytes 61448 | tf_op jit(solution)/shard_map/ppermute | solution.py:510
  15.8 0.9 %collective-permute-done.6.other = f32[5,8,128]{2,1,0:T(8,128)S(1)} collective-permute-done((f32[5,8,128]{2,1,0:T(8,128)S(1)}, f32[5,8,128]{2,1,0:T(8,128)S(1)}, u32[]{:S(2)}, u32[]{:S(2)}) %collective-permute-start.6) | collective-permute-done | bytes 20512 | tf_op jit(solution)/shard_map/ppermute | solution.py:510
  16.7 5.3 %collective-permute-start.7 = (f32[5,16,128]{2,1,0:T(8,128)S(1)}, f32[5,16,128]{2,1,0:T(8,128)S(1)}, u32[]{:S(2)}, u32[]{:S(2)}) collective-permute-start(f32[5,16,128]{2,1,0:T(8,128)S(1)} %shard_map.45.after.own), channel_id=1, source_target_pairs={{0,1},{1,0},{2,3},{3,2},{4,5},{5,4},{6,7},{7,6},{8,9},{9,8},{10,11... | collective-permute-start | bytes 122888 | tf_op jit(solution)/shard_map/ppermute | solution.py:499
  22.0 1.1 %collective-permute-start.8 = (f32[5,16,128]{2,1,0:T(8,128)S(1)}, f32[5,16,128]{2,1,0:T(8,128)S(1)}, u32[]{:S(2)}, u32[]{:S(2)}) collective-permute-start(f32[5,16,128]{2,1,0:T(8,128)S(1)} %shard_map.45.after.own), channel_id=1, source_target_pairs={{0,3},{1,2},{2,1},{3,0},{4,7},{5,6},{6,5},{7,4},{8,11},{9,10},{10,... | collective-permute-start | bytes 122888 | tf_op jit(solution)/shard_map/ppermute | solution.py:499
  23.2 0.5 %shard_map.46.after.g_t = f32[128,8,128]{2,1,0:T(8,128)S(1)} custom-call(f32[1024,128]{1,0:T(8,128)S(1)} %get-tuple-element.55.v_t, f32[128,8,128]{2,1,0:T(8,128)S(1)} %get-tuple-element.56.f, f32[128,8,128]{2,1,0:T(8,128)S(1)} %get-tuple-element.57.u, f32[5,16,128]{2,1,0:T(8,128)S(1)} %shard_map.45.after.own), custom_call_target="tpu_custom_call" | custom-call | flops 3000000 | bytes 3000000 | tf_op jit(solution)/shard_map/pallas_call | solution.py:431
  23.7 0.7 %collective-permute-start.9 = (f32[5,16,128]{2,1,0:T(8,128)S(1)}, f32[5,16,128]{2,1,0:T(8,128)S(1)}, u32[]{:S(2)}, u32[]{:S(2)}) collective-permute-start(f32[5,16,128]{2,1,0:T(8,128)S(1)} %shard_map.47), channel_id=1, source_target_pairs={{0,16},{16,0},{32,48},{48,32},{64,80},{80,64},{96,112},{112,96},{1... | collective-permute-start | bytes 122888 | tf_op jit(solution)/shard_map/ppermute | solution.py:510
  24.4 1.7 %collective-permute-done.8.near = f32[5,16,128]{2,1,0:T(8,128)S(1)} collective-permute-done((f32[5,16,128]{2,1,0:T(8,128)S(1)}, f32[5,16,128]{2,1,0:T(8,128)S(1)}, u32[]{:S(2)}, u32[]{:S(2)}) %collective-permute-start.8) | collective-permute-done | bytes 40992 | tf_op jit(solution)/shard_map/ppermute | solution.py:499
  26.1 3.3 %collective-permute-start.10 = (f32[5,16,128]{2,1,0:T(8,128)S(1)}, f32[5,16,128]{2,1,0:T(8,128)S(1)}, u32[]{:S(2)}, u32[]{:S(2)}) collective-permute-start(f32[5,16,128]{2,1,0:T(8,128)S(1)} %get-tuple-element.59), channel_id=1, source_target_pairs={{0,4},{1,5},{2,6},{3,7},{4,0},{5,1},{6,2},{7,3},{8,12},{9,13},{10,... | collective-permute-start | bytes 122888 | tf_op jit(solution)/shard_map/ppermute | solution.py:499
  29.4 0.8 %collective-permute-start.11 = (f32[5,8,128]{2,1,0:T(8,128)S(1)}, f32[5,8,128]{2,1,0:T(8,128)S(1)}, u32[]{:S(2)}, u32[]{:S(2)}) collective-permute-start(f32[5,8,128]{2,1,0:T(8,128)S(1)} %get-tuple-element.58.mine), channel_id=1, source_target_pairs={{0,12},{1,13},{2,14},{3,15},{4,8},{5,9},{6,10},{7,11},{8,4},{9,5},... | collective-permute-start | bytes 61448 | tf_op jit(solution)/shard_map/ppermute | solution.py:499
  30.2 0.6 %collective-permute-done.10.value.far = f32[5,16,128]{2,1,0:T(8,128)S(1)} collective-permute-done((f32[5,16,128]{2,1,0:T(8,128)S(1)}, f32[5,16,128]{2,1,0:T(8,128)S(1)}, u32[]{:S(2)}, u32[]{:S(2)}) %collective-permute-start.10) | collective-permute-done | bytes 40992 | tf_op jit(solution)/shard_map/ppermute | solution.py:499
  30.8 2.4 %collective-permute-done.11.near = f32[5,8,128]{2,1,0:T(8,128)S(1)} collective-permute-done((f32[5,8,128]{2,1,0:T(8,128)S(1)}, f32[5,8,128]{2,1,0:T(8,128)S(1)}, u32[]{:S(2)}, u32[]{:S(2)}) %collective-permute-start.11) | collective-permute-done | bytes 20512 | tf_op jit(solution)/shard_map/ppermute | solution.py:499
  33.3 1.1 %shard_map.50 = f32[1024,128]{1,0:T(8,128)} custom-call(f32[5,8,128]{2,1,0:T(8,128)S(1)} %get-tuple-element.58.mine, f32[5,16,128]{2,1,0:T(8,128)S(1)} %collective-permute-done.10.value.far, f32[5,8,128]{2,1,0:T(8,128)S(1)} %collective-permute-done.11.near, f32[5,8,128]{2,1,0:T(8,128)S(1)} %collective-permute-done.12.shared, ...), custom_call_target="tpu_custom_call" | custom-call | flops 100000 | bytes 100000 | tf_op jit(solution)/shard_map/pallas_call | solution.py:431
  (16 shorter events, 0.5 us)
Async XLA Ops:
  1.5 4.9 %collective-permute-start = (f32[2,8,128]{2,1,0:T(8,128)S(1)}, f32[2,8,128]{2,1,0:T(8,128)S(1)}, u32[]{:S(2)}, u32[]{:S(2)}) collective-permute-start(f32[2,8,128]{2,1,0:T(8,128)S(1)} %get-tuple-element.33), channel_id=1, source_target_pairs={{0,1},{1,0},{2,3},{3,2},{4,5},{5,4},{6,7},{7,6},{8,9},{9,8},{10,11... | collective-permute-start | bytes 24584 | tf_op jit(solution)/shard_map/ppermute | solution.py:475
  4.0 2.3 %collective-permute-start.1 = (f32[2,8,128]{2,1,0:T(8,128)S(1)}, f32[2,8,128]{2,1,0:T(8,128)S(1)}, u32[]{:S(2)}, u32[]{:S(2)}) collective-permute-start(f32[2,8,128]{2,1,0:T(8,128)S(1)} %get-tuple-element.34), channel_id=1, source_target_pairs={{0,16},{1,2},{2,1},{3,4},{4,3},{5,6},{6,5},{7,8},{8,7},{9,10},{10,... | collective-permute-start | bytes 24584 | tf_op jit(solution)/shard_map/ppermute | solution.py:474
  6.5 1.3 %collective-permute-start.2 = (f32[7,16,128]{2,1,0:T(8,128)S(1)}, f32[7,16,128]{2,1,0:T(8,128)S(1)}, u32[]{:S(2)}, u32[]{:S(2)}) collective-permute-start(f32[7,16,128]{2,1,0:T(8,128)S(1)} %get-tuple-element.41.own), channel_id=1, source_target_pairs={{0,16},{16,0},{32,48},{48,32},{64,80},{80,64},{96,112},{112,96},{1... | collective-permute-start | bytes 172040 | tf_op jit(solution)/shard_map/ppermute | solution.py:489
  7.8 5.1 %collective-permute-start.3 = (f32[7,16,128]{2,1,0:T(8,128)S(1)}, f32[7,16,128]{2,1,0:T(8,128)S(1)}, u32[]{:S(2)}, u32[]{:S(2)}) collective-permute-start(f32[7,16,128]{2,1,0:T(8,128)S(1)} %get-tuple-element.47.own), channel_id=1, source_target_pairs={{0,32},{1,33},{2,34},{3,35},{4,36},{5,37},{6,38},{7,39},{8,40},{9,... | collective-permute-start | bytes 172040 | tf_op jit(solution)/shard_map/ppermute | solution.py:499
  10.6 4.4 %collective-permute-start.4 = (f32[7,16,128]{2,1,0:T(8,128)S(1)}, f32[7,16,128]{2,1,0:T(8,128)S(1)}, u32[]{:S(2)}, u32[]{:S(2)}) collective-permute-start(f32[7,16,128]{2,1,0:T(8,128)S(1)} %get-tuple-element.47.own), channel_id=1, source_target_pairs={{0,96},{1,97},{2,98},{3,99},{4,100},{5,101},{6,102},{7,103},{8,104... | collective-permute-start | bytes 172040 | tf_op jit(solution)/shard_map/ppermute | solution.py:499
  12.9 2.1 %collective-permute-start.5 = (f32[7,16,128]{2,1,0:T(8,128)S(1)}, f32[7,16,128]{2,1,0:T(8,128)S(1)}, u32[]{:S(2)}, u32[]{:S(2)}) collective-permute-start(f32[7,16,128]{2,1,0:T(8,128)S(1)} %shard_map.43), channel_id=1, source_target_pairs={{0,16},{16,0},{32,48},{48,32},{64,80},{80,64},{96,112},{112,96},{1... | collective-permute-start | bytes 172040 | tf_op jit(solution)/shard_map/ppermute | solution.py:510
  15.4 1.3 %collective-permute-start.6 = (f32[5,8,128]{2,1,0:T(8,128)S(1)}, f32[5,8,128]{2,1,0:T(8,128)S(1)}, u32[]{:S(2)}, u32[]{:S(2)}) collective-permute-start(f32[5,8,128]{2,1,0:T(8,128)S(1)} %get-tuple-element.54.own), channel_id=1, source_target_pairs={{0,16},{16,0},{32,48},{48,32},{64,80},{80,64},{96,112},{112,96},{1... | collective-permute-start | bytes 61448 | tf_op jit(solution)/shard_map/ppermute | solution.py:510
  16.7 7.0 %collective-permute-start.7 = (f32[5,16,128]{2,1,0:T(8,128)S(1)}, f32[5,16,128]{2,1,0:T(8,128)S(1)}, u32[]{:S(2)}, u32[]{:S(2)}) collective-permute-start(f32[5,16,128]{2,1,0:T(8,128)S(1)} %shard_map.45.after.own), channel_id=1, source_target_pairs={{0,1},{1,0},{2,3},{3,2},{4,5},{5,4},{6,7},{7,6},{8,9},{9,8},{10,11... | collective-permute-start | bytes 122888 | tf_op jit(solution)/shard_map/ppermute | solution.py:499
  22.0 4.1 %collective-permute-start.8 = (f32[5,16,128]{2,1,0:T(8,128)S(1)}, f32[5,16,128]{2,1,0:T(8,128)S(1)}, u32[]{:S(2)}, u32[]{:S(2)}) collective-permute-start(f32[5,16,128]{2,1,0:T(8,128)S(1)} %shard_map.45.after.own), channel_id=1, source_target_pairs={{0,3},{1,2},{2,1},{3,0},{4,7},{5,6},{6,5},{7,4},{8,11},{9,10},{10,... | collective-permute-start | bytes 122888 | tf_op jit(solution)/shard_map/ppermute | solution.py:499
  23.7 2.4 %collective-permute-start.9 = (f32[5,16,128]{2,1,0:T(8,128)S(1)}, f32[5,16,128]{2,1,0:T(8,128)S(1)}, u32[]{:S(2)}, u32[]{:S(2)}) collective-permute-start(f32[5,16,128]{2,1,0:T(8,128)S(1)} %shard_map.47), channel_id=1, source_target_pairs={{0,16},{16,0},{32,48},{48,32},{64,80},{80,64},{96,112},{112,96},{1... | collective-permute-start | bytes 122888 | tf_op jit(solution)/shard_map/ppermute | solution.py:510
  26.1 4.7 %collective-permute-start.10 = (f32[5,16,128]{2,1,0:T(8,128)S(1)}, f32[5,16,128]{2,1,0:T(8,128)S(1)}, u32[]{:S(2)}, u32[]{:S(2)}) collective-permute-start(f32[5,16,128]{2,1,0:T(8,128)S(1)} %get-tuple-element.59), channel_id=1, source_target_pairs={{0,4},{1,5},{2,6},{3,7},{4,0},{5,1},{6,2},{7,3},{8,12},{9,13},{10,... | collective-permute-start | bytes 122888 | tf_op jit(solution)/shard_map/ppermute | solution.py:499
  29.4 3.8 %collective-permute-start.11 = (f32[5,8,128]{2,1,0:T(8,128)S(1)}, f32[5,8,128]{2,1,0:T(8,128)S(1)}, u32[]{:S(2)}, u32[]{:S(2)}) collective-permute-start(f32[5,8,128]{2,1,0:T(8,128)S(1)} %get-tuple-element.58.mine), channel_id=1, source_target_pairs={{0,12},{1,13},{2,14},{3,15},{4,8},{5,9},{6,10},{7,11},{8,4},{9,5},... | collective-permute-start | bytes 61448 | tf_op jit(solution)/shard_map/ppermute | solution.py:499
  30.8 2.5 %collective-permute-start.12 = (f32[5,8,128]{2,1,0:T(8,128)S(1)}, f32[5,8,128]{2,1,0:T(8,128)S(1)}, u32[]{:S(2)}, u32[]{:S(2)}) collective-permute-start(f32[5,8,128]{2,1,0:T(8,128)S(1)} %shard_map.49), channel_id=1, source_target_pairs={{0,16},{16,0},{32,48},{48,32},{64,80},{80,64},{96,112},{112,96},{1... | collective-permute-start | bytes 61448 | tf_op jit(solution)/shard_map/ppermute | solution.py:510

commit v11 on v10

--- a/solution.py
+++ b/solution.py
@@ -39,18 +39,16 @@
 
 
 def merge(low, high):
-    inv = (1.0 / ((2.0 / (low[4] + high[3])) + low[2] + high[0]))
-    e = (low[6] - high[5]) * inv
+    inv = 1.0 / (low[2] + high[0])
+    e = (low[4] - high[3]) * inv
     a = low[1] * inv
     b = high[1] * inv
     joined = [
         low[0] - low[1] * a,
         low[1] * b,
         high[2] - high[1] * b,
-        low[3],
-        high[4],
-        low[5] - low[1] * e,
-        high[6] + high[1] * e,
+        low[3] - low[1] * e,
+        high[4] + high[1] * e,
     ]
     return joined, (e, a, b)
 
@@ -91,39 +89,6 @@
             slots[half + n] = rising
 
 
-def x_flows(blocks, slots):
-    count = blocks.shape[0]
-
-    def pivot(i):
-        if i == 0:
-            return (2.0 / (blocks[0, 3])) + blocks[0, 0]
-        if i == count:
-            return (2.0 / (blocks[count - 1, 4])) + blocks[count - 1, 2]
-        return (2.0 / (blocks[i - 1, 4] + blocks[i, 3])) + blocks[i - 1, 2] + blocks[i, 0]
-
-    def gain(i):
-        if i == 0:
-            return -blocks[0, 5]
-        return blocks[i - 1, 6] - blocks[i, 5] if i < count else blocks[i - 1, 6]
-
-    flows_of(count, pivot, lambda i: blocks[i - 1, 1], lambda i: blocks[i, 1], gain, slots)
-
-
-def y_merge(low, high):
-    inv = 1.0 / (low[2] + high[0])
-    e = (low[4] - high[3]) * inv
-    a = low[1] * inv
-    b = high[1] * inv
-    joined = [
-        low[0] - low[1] * a,
-        low[1] * b,
-        high[2] - high[1] * b,
-        low[3] - low[1] * e,
-        high[4] + high[1] * e,
-    ]
-    return joined, (e, a, b)
-
-
 def arrange(own, far, near, shared, place, blocks):
     on_low = lax.rem(lax.axis_index("gx"), 2) == 0
     blocks[place] = own[...]
@@ -132,7 +97,7 @@
     blocks[place ^ 1] = jnp.where(on_low, far[...], shared[...])
 
 
-def y_flows(blocks, slots):
+def line_flows(blocks, slots):
     count = blocks.shape[0]
 
     def pivot(i):
@@ -148,7 +113,7 @@
     flows_of(count, pivot, lambda i: blocks[i - 1, 1], lambda i: blocks[i, 1], gain, slots)
 
 
-def load_kernel(st_hbm, kx_hbm, ky_hbm, st, kx, st_t, ky_t, mine, first, second, ky, sems):
+def load_kernel(st_hbm, kx_hbm, ky_hbm, st, kx, st_t, ky_t, mine, first, second, last, ky, sems):
     inside = pl.ds(0, BX)
     moves = [
         pltpu.make_async_copy(src, dst, sems.at[n])
@@ -174,6 +139,8 @@
     first[...] = jnp.where(even, high, low)
     second[...] = jnp.where(even, low, high)
     moves[2].wait()
+    for z in range(NZ):
+        last[pl.ds(z, 1), :] = kx[z, pl.ds(BX - 1, 1), :]
 
 
 def sweep(count, row, f, u, ratios, put_first, put_last):
@@ -234,7 +201,10 @@
         return store
 
     values = sweep(BX, lambda i: x_row(kx, i), fx, ux, ratios, put(wf, sums[0]), put(wl, sums[1]))
-    values += (x_row(kx, 0), x_row(kx, BX - 1), sums[0][0] + sums[0][1], sums[1][0] + sums[1][1])
+    lead, across, trail = values
+    last = lax.axis_index("gx") == lax.axis_size("gx") - 1
+    trail = trail + jnp.where(last, 2.0 / x_row(kx, BX - 1), 0.0)
+    values = (lead, across, trail, sums[0][0] + sums[0][1], sums[1][0] + sums[1][1], x_row(kx, 0))
     for n, value in enumerate(values):
         part[n] = value
     for n, ref in enumerate((wf, wl)):
@@ -259,7 +229,7 @@
     my[2] = trail + jnp.where(me == last, (2.0 / (y_row(ky_t, BY - 1))), 0.0)
 
 
-def x_ends_kernel(came1, came2, mine, part, edges, send, flux, rows):
+def x_ends_kernel(came1, came2, below_x, mine, part, edges, send, flux, rows):
     me = lax.axis_index("gy")
     even = lax.rem(me, 2) == 0
     below = jnp.where(me == 0, 0.0, jnp.where(even, came2[...], came1[...]))
@@ -270,7 +240,9 @@
     flux[1] = leave
     flux[2] = (2.0 / (below[1] + mine[1]))
     lane = lax.broadcasted_iota(jnp.int32, (GROUPS, 128), 1)
-    send[0:5] = part[0:5]
+    below_x = jnp.where(lax.axis_index("gx") == 0, 0.0, below_x[...])
+    send[0] = part[0] + 2.0 / (below_x + part[5])
+    send[1:3] = part[1:3]
     for n in range(2):
         low = -edges[2 * n] * enter
         high = edges[2 * n + 1] * leave
@@ -280,7 +252,7 @@
             at_high = jnp.sum(jnp.where(inside, high, 0.0), axis=1, keepdims=True)
             value = jnp.where(lane == 0, at_low, jnp.where(lane == 127, at_high, 0.0))
             rows[n, pl.ds(h, GROUPS, stride=2), :] = value
-        send[5 + n] = part[5 + n] + rows[n]
+        send[3 + n] = part[3 + n] + rows[n]
 
 
 def x_local_kernel(base_t, flux, st, fx, ux, d, s, work, work_t):
@@ -302,11 +274,11 @@
 
 def x_merge_kernel(own, other, after, send, coefs):
     core = lax.rem(lax.axis_index("gx"), 2)
-    mine, theirs = [own[n] for n in range(7)], [other[n] for n in range(7)]
+    mine, theirs = [own[n] for n in range(5)], [other[n] for n in range(5)]
     low = [jnp.where(core == 0, a, b) for a, b in zip(mine, theirs)]
     high = [jnp.where(core == 0, b, a) for a, b in zip(mine, theirs)]
     joined, flow = merge(low, high)
-    for n in range(7):
+    for n in range(5):
         send[n] = joined[n]
     for n in range(3):
         coefs[n] = flow[n]
@@ -323,7 +295,7 @@
     place = lax.div(me, 2)
     on_low = lax.rem(me, 2) == 0
     arrange(own, far, near, shared, place, blocks)
-    x_flows(blocks, slots)
+    line_flows(blocks, slots)
     enter, leave = slots[place], slots[place + 1]
     middle = coefs[0] + coefs[1] * enter + coefs[2] * leave
     flows[0] = jnp.where(on_low, enter, middle)
@@ -388,7 +360,7 @@
     arrange(own, far, near, shared, lax.rem(lax.axis_index("gy"), SIDE), blocks)
     joined = [blocks[0, n] for n in range(5)]
     for c in range(1, SIDE):
-        joined, flow = y_merge(joined, [blocks[c, n] for n in range(5)])
+        joined, flow = merge(joined, [blocks[c, n] for n in range(5)])
         for n in range(3):
             coefs[c - 1, n] = flow[n]
     for n in range(5):
@@ -397,13 +369,13 @@
 
 
 def y_solve_kernel(
-    mine, far, near, shared, coefs, g_t, yf, yl, st, out_hbm, blocks, slots, inner, work, out, sems
+    mine, far, near, shared, coefs, g_t, yf, yl, st, out_hbm, blocks, slots, inner, work, out, sem
 ):
     me = lax.axis_index("gy")
     place, depth = lax.div(me, SIDE), lax.rem(me, SIDE)
     rows = own_rows()
     arrange(mine, far.at[:, rows, :], near, shared, place, blocks)
-    y_flows(blocks, slots)
+    line_flows(blocks, slots)
     enter, flow = slots[place], slots[place + 1]
     inner[0] = enter
     inner[SIDE] = flow
@@ -414,15 +386,11 @@
     enter, leave = inner[depth], inner[depth + 1]
     for j in range(BY):
         work[pl.ds(j * GROUPS, GROUPS), :] = 2.0 * (g_t[j] + yf[j] * enter - yl[j] * leave)
-    moves = []
     for g in range(GROUPS):
         rows = pl.ds(g * 128, 128)
         out[rows, :] = group(st, g) + work[pl.ds(g, BY, stride=GROUPS), :].T
-        move = pltpu.make_async_copy(out.at[rows], out_hbm.at[rows], sems.at[g])
-        move.start()
-        moves.append(move)
-    for move in moves:
-        move.wait()
+        pltpu.make_async_copy(out.at[rows], out_hbm.at[rows], sem).start()
+    pltpu.make_async_copy(out, out_hbm, sem).wait()
 
 
 def call(kernel, outs, args, scratch=(), cost=100_000):
@@ -455,13 +423,13 @@
     planes = (NZ, PITCH, BY)
     xs = (BX, NZ, BY)
     ys = (BY, GROUPS, 128)
-    x_block = (7, NZ, BY)
+    x_block = (5, NZ, BY)
     edge = (2, GROUPS, 128)
     nx, ny = lax.axis_size("gx"), lax.axis_size("gy")
     wide = (5, 2 * GROUPS, 128)
-    st, kx, st_t, ky_t, mine, first, second = call(
+    st, kx, st_t, ky_t, mine, first, second, last = call(
         load_kernel,
-        near(planes, planes, plane, plane, (4, GROUPS, 128), edge, edge),
+        near(planes, planes, plane, plane, (4, GROUPS, 128), edge, edge, (NZ, BY)),
         [(a, True) for a in flat],
         [pltpu.VMEM((NZ, BX, BY), F32), pltpu.SemaphoreType.DMA((3,))],
     )
@@ -473,9 +441,10 @@
     ]
     came2 = lax.ppermute(second, ("gx", "gy"), pairs)
     came1 = lax.ppermute(first, "gy", [(i, i ^ 1) for i in range(ny)])
+    below_x = lax.ppermute(last, "gx", [(i, (i + 1) % nx) for i in range(nx)])
     fx, ux, wf, wl, part, edges, base_t = call(
         x_matrix_kernel,
-        near(xs, xs, pitched, pitched, x_block, (4, GROUPS, 128), plane),
+        near(xs, xs, pitched, pitched, (6, NZ, BY), (4, GROUPS, 128), plane),
         near(st_t, kx, ky_t),
         [pltpu.VMEM(pitched, F32), pltpu.VMEM(xs, F32)],
         cost=5_000_000,
@@ -483,7 +452,7 @@
     ends, flux = call(
         x_ends_kernel,
         near(x_block, (3, GROUPS, 128)),
-        near(came1, came2, mine, part, edges),
+        near(came1, came2, below_x, mine, part, edges),
         [pltpu.VMEM((2, NZ, BY), F32)],
     )
     other = lax.ppermute(ends, "gx", [(i, i ^ 1) for i in range(nx)])
@@ -553,7 +522,7 @@
             pltpu.VMEM((SIDE + 1, GROUPS, 128), F32),
             pltpu.VMEM(plane, F32),
             pltpu.VMEM(plane, F32),
-            pltpu.SemaphoreType.DMA((GROUPS,)),
+            pltpu.SemaphoreType.DMA,
         ],
     )
     return out.reshape(state.shape)

time: 34.5 us -> 34.3 us (level)
  starting transfers between devices: 19.5 us -> 19.1 us
  waiting for transfers between devices: 7.76 us -> 8.11 us
    ppermute x6, starting transfers between devices: 14.2 us -> 12 us  [swap(): lax.ppermute(value, ('gx', 'gy'), [(i * ny + j, (i ^ 2 * bits[i % 2]) * n...]
    ppermute x1, starting transfers between devices: 0.31 us -> 1.87 us  [on_device(): other = lax.ppermute(ends, 'gx', [(i, i ^ 1) for i in range(nx)])]
    ppermute x0 -> x1, starting transfers between devices: none -> 1.1 us  [on_device(): below_x = lax.ppermute(last, 'gx', [(i, (i + 1) % nx) for i in range(nx)])]
    ppermute x4, starting transfers between devices: 1.51 us -> 0.69 us  [share(): return lax.ppermute(value, 'gx', [(i, i ^ 1) for i in range(nx)])]
  transfers between devices with their start and end apart: 13 -> 14, of which waited for: 6 -> 8; matrix products, arithmetic and copies ran while one was open for 0% -> 0% of each run, Pallas kernels for 11% -> 11%
where the time goes in v11:
time: 34.3 us; the launch traced here: 34.2 us
  starting transfers between devices  19.1 us (56%)
  waiting for transfers between devices  8.11 us (24%)
  Pallas kernels  6.87 us (20%)
    ppermute x6, starting transfers between devices, swap(): lax.ppermute(value, ('gx', 'gy'), [(i * ny + j, (i ^ 2 * bits[i % 2]) * n...  12 us
    pallas_call x14, Pallas kernels, call(): pl.pallas_call(kernel, out_shape=[jax.ShapeDtypeStruct(shape, F32) if far...  6.87 us
    ppermute x6, waiting for transfers between devices, swap(): lax.ppermute(value, ('gx', 'gy'), [(i * ny + j, (i ^ 2 * bits[i % 2]) * n...  6.6 us
    ppermute x1, starting transfers between devices, on_device(): came1 = lax.ppermute(first, 'gy', [(i, i ^ 1) for i in range(ny)])  2.55 us
    ppermute x1, starting transfers between devices, on_device(): other = lax.ppermute(ends, 'gx', [(i, i ^ 1) for i in range(nx)])  1.87 us
    ppermute x4, waiting for transfers between devices, share(): return lax.ppermute(value, 'gx', [(i, i ^ 1) for i in range(nx)])  1.17 us
    ppermute x1, starting transfers between devices, on_device(): below_x = lax.ppermute(last, 'gx', [(i, (i + 1) % nx) for i in range(nx)])  1.1 us
    ppermute x1, starting transfers between devices, on_device(): came2 = lax.ppermute(second, ('gx', 'gy'), pairs)  0.96 us
  transfers between devices with their start and end apart: 14, of which 8 were waited for; matrix products, arithmetic and copies ran while one was open for 0% of the time, Pallas kernels for 11%

profile of v11, /device:TPU:1, one launch (start us, length us, event | category | flops | bytes accessed | tf_op | source)
XLA Modules:
  0.0 34.2 jit_solution(9511757061852651512)
XLA Ops:
  0.0 1.5 %shard_map.37 = (f32[16,72,128]{2,1,0:T(8,128)S(1)}, f32[16,72,128]{2,1,0:T(8,128)S(1)}, f32[1024,128]{1,0:T(8,128)S(1)}, f32[1024,128]{1,0:T(8,128)S(1)}, f32[4...) custom-call(f32[16,64,128]{2,1,0:T(8,128)} %st_hbm.1, ...), custom_call_target="tpu_custom_call" | custom-call | flops 100000 | bytes 100000 | tf_op jit(solution)/shard_map/pallas_call | solution.py:399
  1.5 2.5 %collective-permute-start = (f32[2,8,128]{2,1,0:T(8,128)S(1)}, f32[2,8,128]{2,1,0:T(8,128)S(1)}, u32[]{:S(2)}, u32[]{:S(2)}) collective-permute-start(f32[2,8,128]{2,1,0:T(8,128)S(1)} %get-tuple-element.34), channel_id=1, source_target_pairs={{0,1},{1,0},{2,3},{3,2},{4,5},{5,4},{6,7},{7,6},{8,9},{9,8},{10,11... | collective-permute-start | bytes 24584 | tf_op jit(solution)/shard_map/ppermute | solution.py:443
  4.0 1.0 %collective-permute-start.1 = (f32[2,8,128]{2,1,0:T(8,128)S(1)}, f32[2,8,128]{2,1,0:T(8,128)S(1)}, u32[]{:S(2)}, u32[]{:S(2)}) collective-permute-start(f32[2,8,128]{2,1,0:T(8,128)S(1)} %get-tuple-element.35), channel_id=1, source_target_pairs={{0,16},{1,2},{2,1},{3,4},{4,3},{5,6},{6,5},{7,8},{8,7},{9,10},{10,... | collective-permute-start | bytes 24584 | tf_op jit(solution)/shard_map/ppermute | solution.py:442
  5.0 1.1 %collective-permute-start.2 = (f32[16,128]{1,0:T(8,128)S(1)}, f32[16,128]{1,0:T(8,128)S(1)}, u32[]{:S(2)}, u32[]{:S(2)}) collective-permute-start(f32[16,128]{1,0:T(8,128)S(1)} %get-tuple-element.36), channel_id=1, source_target_pairs={{0,16},{16,32},{32,48},{48,64},{64,80},{80,96},{96,112},{112,0},{1... | collective-permute-start | bytes 24584 | tf_op jit(solution)/shard_map/ppermute | solution.py:444
  6.1 1.3 %shard_map.38 = (f32[64,16,128]{2,1,0:T(8,128)S(1)}, f32[64,16,128]{2,1,0:T(8,128)S(1)}, f32[1152,128]{1,0:T(8,128)S(1)}, f32[1152,128]{1,0:T(8,128)S(1)}, f32[6...) custom-call(f32[1024,128]{1,0:T(8,128)S(1)} %get-tuple-element.38.st_t, ...), custom_call_target="tpu_custom_call" | custom-call | flops 5000000 | bytes 5000000 | tf_op jit(solution)/shard_map/pallas_call | solution.py:399
  7.6 1.9 %collective-permute-start.3 = (f32[5,16,128]{2,1,0:T(8,128)S(1)}, f32[5,16,128]{2,1,0:T(8,128)S(1)}, u32[]{:S(2)}, u32[]{:S(2)}) collective-permute-start(f32[5,16,128]{2,1,0:T(8,128)S(1)} %get-tuple-element.43.own), channel_id=1, source_target_pairs={{0,16},{16,0},{32,48},{48,32},{64,80},{80,64},{96,112},{112,96},{1... | collective-permute-start | bytes 122888 | tf_op jit(solution)/shard_map/ppermute | solution.py:458
  9.4 0.5 %shard_map.40.after.d = f32[1152,128]{1,0:T(8,128)S(1)} custom-call(f32[1024,128]{1,0:T(8,128)S(1)} %get-tuple-element.44.base_t, f32[3,8,128]{2,1,0:T(8,128)S(1)} %get-tuple-element.45.flux, f32[1152,128]{1,0:T(8,128)S(1)} %bitcast.3, f32[64,16,128]{2,1,0:T(8,128)S(1)} %get-tuple-element.47.fx, f32[64,16,128]{2,1,0:T(8,128)S(1)} %get-tuple-element.48.ux), custom_call_target="tpu_custom_call" | custom-call | flops 3000000 | bytes 3000000 | tf_op jit(solution)/shard_map/pallas_call | solution.py:399
  10.0 0.3 collective-permute-done.3.other
  10.3 1.6 %collective-permute-start.4 = (f32[5,16,128]{2,1,0:T(8,128)S(1)}, f32[5,16,128]{2,1,0:T(8,128)S(1)}, u32[]{:S(2)}, u32[]{:S(2)}) collective-permute-start(f32[5,16,128]{2,1,0:T(8,128)S(1)} %get-tuple-element.49.own), channel_id=1, source_target_pairs={{0,32},{1,33},{2,34},{3,35},{4,36},{5,37},{6,38},{7,39},{8,40},{9,... | collective-permute-start | bytes 122888 | tf_op jit(solution)/shard_map/ppermute | solution.py:468
  11.9 0.9 %collective-permute-start.5 = (f32[5,16,128]{2,1,0:T(8,128)S(1)}, f32[5,16,128]{2,1,0:T(8,128)S(1)}, u32[]{:S(2)}, u32[]{:S(2)}) collective-permute-start(f32[5,16,128]{2,1,0:T(8,128)S(1)} %get-tuple-element.49.own), channel_id=1, source_target_pairs={{0,96},{1,97},{2,98},{3,99},{4,100},{5,101},{6,102},{7,103},{8,104... | collective-permute-start | bytes 122888 | tf_op jit(solution)/shard_map/ppermute | solution.py:468
  12.8 1.4 %shard_map.42 = (f32[128,8,128]{2,1,0:T(8,128)S(1)}, f32[128,8,128]{2,1,0:T(8,128)S(1)}, f32[128,8,128]{2,1,0:T(8,128)S(1)}, f32[128,8,128]{2,1,0:T(8,128)S(1)}, f32[3,8,128]{2,1,0:T(8,128)S(1)}) custom-call(f32[1024,128]{1,0:T(8,128)S(1)} %get-tuple-element.40.ky_t, f32[3,16,128]{2,1,0:T(8,128)S(1)} %get-tuple-element.50.after.coefs), custom_call_target="tpu_custom_call" | custom-call | flops 5000000 | bytes 5000000 | tf_op jit(solution)/shard_map/pallas_call | solution.py:399
  14.2 0.7 %collective-permute-done.4.value.far = f32[5,16,128]{2,1,0:T(8,128)S(1)} collective-permute-done((f32[5,16,128]{2,1,0:T(8,128)S(1)}, f32[5,16,128]{2,1,0:T(8,128)S(1)}, u32[]{:S(2)}, u32[]{:S(2)}) %collective-permute-start.4) | collective-permute-done | bytes 40992 | tf_op jit(solution)/shard_map/ppermute | solution.py:468
  14.9 1.1 %collective-permute-done.5.near = f32[5,16,128]{2,1,0:T(8,128)S(1)} collective-permute-done((f32[5,16,128]{2,1,0:T(8,128)S(1)}, f32[5,16,128]{2,1,0:T(8,128)S(1)}, u32[]{:S(2)}, u32[]{:S(2)}) %collective-permute-start.5) | collective-permute-done | bytes 40992 | tf_op jit(solution)/shard_map/ppermute | solution.py:468
  16.7 1.0 %collective-permute-done.7.other = f32[5,8,128]{2,1,0:T(8,128)S(1)} collective-permute-done((f32[5,8,128]{2,1,0:T(8,128)S(1)}, f32[5,8,128]{2,1,0:T(8,128)S(1)}, u32[]{:S(2)}, u32[]{:S(2)}) %collective-permute-start.7) | collective-permute-done | bytes 20512 | tf_op jit(solution)/shard_map/ppermute | solution.py:479
  17.7 3.8 %collective-permute-start.8 = (f32[5,16,128]{2,1,0:T(8,128)S(1)}, f32[5,16,128]{2,1,0:T(8,128)S(1)}, u32[]{:S(2)}, u32[]{:S(2)}) collective-permute-start(f32[5,16,128]{2,1,0:T(8,128)S(1)} %shard_map.45.after.own), channel_id=1, source_target_pairs={{0,1},{1,0},{2,3},{3,2},{4,5},{5,4},{6,7},{7,6},{8,9},{9,8},{10,11... | collective-permute-start | bytes 122888 | tf_op jit(solution)/shard_map/ppermute | solution.py:468
  21.6 1.9 %collective-permute-start.9 = (f32[5,16,128]{2,1,0:T(8,128)S(1)}, f32[5,16,128]{2,1,0:T(8,128)S(1)}, u32[]{:S(2)}, u32[]{:S(2)}) collective-permute-start(f32[5,16,128]{2,1,0:T(8,128)S(1)} %shard_map.45.after.own), channel_id=1, source_target_pairs={{0,3},{1,2},{2,1},{3,0},{4,7},{5,6},{6,5},{7,4},{8,11},{9,10},{10,... | collective-permute-start | bytes 122888 | tf_op jit(solution)/shard_map/ppermute | solution.py:468
  23.5 0.5 %shard_map.46.after.g_t = f32[128,8,128]{2,1,0:T(8,128)S(1)} custom-call(f32[1024,128]{1,0:T(8,128)S(1)} %get-tuple-element.57.v_t, f32[128,8,128]{2,1,0:T(8,128)S(1)} %get-tuple-element.58.f, f32[128,8,128]{2,1,0:T(8,128)S(1)} %get-tuple-element.59.u, f32[5,16,128]{2,1,0:T(8,128)S(1)} %shard_map.45.after.own), custom_call_target="tpu_custom_call" | custom-call | flops 3000000 | bytes 3000000 | tf_op jit(solution)/shard_map/pallas_call | solution.py:399
  24.1 1.9 %collective-permute-done.9.near = f32[5,16,128]{2,1,0:T(8,128)S(1)} collective-permute-done((f32[5,16,128]{2,1,0:T(8,128)S(1)}, f32[5,16,128]{2,1,0:T(8,128)S(1)}, u32[]{:S(2)}, u32[]{:S(2)}) %collective-permute-start.9) | collective-permute-done | bytes 40992 | tf_op jit(solution)/shard_map/ppermute | solution.py:468
  26.1 3.0 %collective-permute-start.11 = (f32[5,16,128]{2,1,0:T(8,128)S(1)}, f32[5,16,128]{2,1,0:T(8,128)S(1)}, u32[]{:S(2)}, u32[]{:S(2)}) collective-permute-start(f32[5,16,128]{2,1,0:T(8,128)S(1)} %get-tuple-element.61), channel_id=1, source_target_pairs={{0,4},{1,5},{2,6},{3,7},{4,0},{5,1},{6,2},{7,3},{8,12},{9,13},{10,... | collective-permute-start | bytes 122888 | tf_op jit(solution)/shard_map/ppermute | solution.py:468
  29.1 0.8 %collective-permute-start.12 = (f32[5,8,128]{2,1,0:T(8,128)S(1)}, f32[5,8,128]{2,1,0:T(8,128)S(1)}, u32[]{:S(2)}, u32[]{:S(2)}) collective-permute-start(f32[5,8,128]{2,1,0:T(8,128)S(1)} %get-tuple-element.60.mine), channel_id=1, source_target_pairs={{0,12},{1,13},{2,14},{3,15},{4,8},{5,9},{6,10},{7,11},{8,4},{9,5},... | collective-permute-start | bytes 61448 | tf_op jit(solution)/shard_map/ppermute | solution.py:468
  29.9 0.7 %collective-permute-done.11.value.far = f32[5,16,128]{2,1,0:T(8,128)S(1)} collective-permute-done((f32[5,16,128]{2,1,0:T(8,128)S(1)}, f32[5,16,128]{2,1,0:T(8,128)S(1)}, u32[]{:S(2)}, u32[]{:S(2)}) %collective-permute-start.11) | collective-permute-done | bytes 40992 | tf_op jit(solution)/shard_map/ppermute | solution.py:468
  30.6 0.4 %collective-permute-start.13 = (f32[5,8,128]{2,1,0:T(8,128)S(1)}, f32[5,8,128]{2,1,0:T(8,128)S(1)}, u32[]{:S(2)}, u32[]{:S(2)}) collective-permute-start(f32[5,8,128]{2,1,0:T(8,128)S(1)} %shard_map.49), channel_id=1, source_target_pairs={{0,16},{16,0},{32,48},{48,32},{64,80},{80,64},{96,112},{112,96},{1... | collective-permute-start | bytes 61448 | tf_op jit(solution)/shard_map/ppermute | solution.py:479
  30.9 2.2 %collective-permute-done.12.near = f32[5,8,128]{2,1,0:T(8,128)S(1)} collective-permute-done((f32[5,8,128]{2,1,0:T(8,128)S(1)}, f32[5,8,128]{2,1,0:T(8,128)S(1)}, u32[]{:S(2)}, u32[]{:S(2)}) %collective-permute-start.12) | collective-permute-done | bytes 20512 | tf_op jit(solution)/shard_map/ppermute | solution.py:468
  33.1 1.1 %shard_map.50 = f32[1024,128]{1,0:T(8,128)} custom-call(f32[5,8,128]{2,1,0:T(8,128)S(1)} %get-tuple-element.60.mine, f32[5,16,128]{2,1,0:T(8,128)S(1)} %collective-permute-done.11.value.far, f32[5,8,128]{2,1,0:T(8,128)S(1)} %collective-permute-done.12.near, f32[5,8,128]{2,1,0:T(8,128)S(1)} %collective-permute-done.13.shared, ...), custom_call_target="tpu_custom_call" | custom-call | flops 100000 | bytes 100000 | tf_op jit(solution)/shard_map/pallas_call | solution.py:399
  (18 shorter events, 1.0 us)
Async XLA Ops:
  1.5 5.9 %collective-permute-start = (f32[2,8,128]{2,1,0:T(8,128)S(1)}, f32[2,8,128]{2,1,0:T(8,128)S(1)}, u32[]{:S(2)}, u32[]{:S(2)}) collective-permute-start(f32[2,8,128]{2,1,0:T(8,128)S(1)} %get-tuple-element.34), channel_id=1, source_target_pairs={{0,1},{1,0},{2,3},{3,2},{4,5},{5,4},{6,7},{7,6},{8,9},{9,8},{10,11... | collective-permute-start | bytes 24584 | tf_op jit(solution)/shard_map/ppermute | solution.py:443
  4.0 3.4 %collective-permute-start.1 = (f32[2,8,128]{2,1,0:T(8,128)S(1)}, f32[2,8,128]{2,1,0:T(8,128)S(1)}, u32[]{:S(2)}, u32[]{:S(2)}) collective-permute-start(f32[2,8,128]{2,1,0:T(8,128)S(1)} %get-tuple-element.35), channel_id=1, source_target_pairs={{0,16},{1,2},{2,1},{3,4},{4,3},{5,6},{6,5},{7,8},{8,7},{9,10},{10,... | collective-permute-start | bytes 24584 | tf_op jit(solution)/shard_map/ppermute | solution.py:442
  5.0 2.4 %collective-permute-start.2 = (f32[16,128]{1,0:T(8,128)S(1)}, f32[16,128]{1,0:T(8,128)S(1)}, u32[]{:S(2)}, u32[]{:S(2)}) collective-permute-start(f32[16,128]{1,0:T(8,128)S(1)} %get-tuple-element.36), channel_id=1, source_target_pairs={{0,16},{16,32},{32,48},{48,64},{64,80},{80,96},{96,112},{112,0},{1... | collective-permute-start | bytes 24584 | tf_op jit(solution)/shard_map/ppermute | solution.py:444
  7.6 2.7 %collective-permute-start.3 = (f32[5,16,128]{2,1,0:T(8,128)S(1)}, f32[5,16,128]{2,1,0:T(8,128)S(1)}, u32[]{:S(2)}, u32[]{:S(2)}) collective-permute-start(f32[5,16,128]{2,1,0:T(8,128)S(1)} %get-tuple-element.43.own), channel_id=1, source_target_pairs={{0,16},{16,0},{32,48},{48,32},{64,80},{80,64},{96,112},{112,96},{1... | collective-permute-start | bytes 122888 | tf_op jit(solution)/shard_map/ppermute | solution.py:458
  10.3 4.6 %collective-permute-start.4 = (f32[5,16,128]{2,1,0:T(8,128)S(1)}, f32[5,16,128]{2,1,0:T(8,128)S(1)}, u32[]{:S(2)}, u32[]{:S(2)}) collective-permute-start(f32[5,16,128]{2,1,0:T(8,128)S(1)} %get-tuple-element.49.own), channel_id=1, source_target_pairs={{0,32},{1,33},{2,34},{3,35},{4,36},{5,37},{6,38},{7,39},{8,40},{9,... | collective-permute-start | bytes 122888 | tf_op jit(solution)/shard_map/ppermute | solution.py:468
  11.9 4.1 %collective-permute-start.5 = (f32[5,16,128]{2,1,0:T(8,128)S(1)}, f32[5,16,128]{2,1,0:T(8,128)S(1)}, u32[]{:S(2)}, u32[]{:S(2)}) collective-permute-start(f32[5,16,128]{2,1,0:T(8,128)S(1)} %get-tuple-element.49.own), channel_id=1, source_target_pairs={{0,96},{1,97},{2,98},{3,99},{4,100},{5,101},{6,102},{7,103},{8,104... | collective-permute-start | bytes 122888 | tf_op jit(solution)/shard_map/ppermute | solution.py:468
  14.9 1.2 %collective-permute-start.6 = (f32[5,16,128]{2,1,0:T(8,128)S(1)}, f32[5,16,128]{2,1,0:T(8,128)S(1)}, u32[]{:S(2)}, u32[]{:S(2)}) collective-permute-start(f32[5,16,128]{2,1,0:T(8,128)S(1)} %shard_map.43), channel_id=1, source_target_pairs={{0,16},{16,0},{32,48},{48,32},{64,80},{80,64},{96,112},{112,96},{1... | collective-permute-start | bytes 122888 | tf_op jit(solution)/shard_map/ppermute | solution.py:479
  16.5 1.3 %collective-permute-start.7 = (f32[5,8,128]{2,1,0:T(8,128)S(1)}, f32[5,8,128]{2,1,0:T(8,128)S(1)}, u32[]{:S(2)}, u32[]{:S(2)}) collective-permute-start(f32[5,8,128]{2,1,0:T(8,128)S(1)} %get-tuple-element.56.own), channel_id=1, source_target_pairs={{0,16},{16,0},{32,48},{48,32},{64,80},{80,64},{96,112},{112,96},{1... | collective-permute-start | bytes 61448 | tf_op jit(solution)/shard_map/ppermute | solution.py:479
  17.7 6.3 %collective-permute-start.8 = (f32[5,16,128]{2,1,0:T(8,128)S(1)}, f32[5,16,128]{2,1,0:T(8,128)S(1)}, u32[]{:S(2)}, u32[]{:S(2)}) collective-permute-start(f32[5,16,128]{2,1,0:T(8,128)S(1)} %shard_map.45.after.own), channel_id=1, source_target_pairs={{0,1},{1,0},{2,3},{3,2},{4,5},{5,4},{6,7},{7,6},{8,9},{9,8},{10,11... | collective-permute-start | bytes 122888 | tf_op jit(solution)/shard_map/ppermute | solution.py:468
  21.6 4.5 %collective-permute-start.9 = (f32[5,16,128]{2,1,0:T(8,128)S(1)}, f32[5,16,128]{2,1,0:T(8,128)S(1)}, u32[]{:S(2)}, u32[]{:S(2)}) collective-permute-start(f32[5,16,128]{2,1,0:T(8,128)S(1)} %shard_map.45.after.own), channel_id=1, source_target_pairs={{0,3},{1,2},{2,1},{3,0},{4,7},{5,6},{6,5},{7,4},{8,11},{9,10},{10,... | collective-permute-start | bytes 122888 | tf_op jit(solution)/shard_map/ppermute | solution.py:468
  24.0 2.0 %collective-permute-start.10 = (f32[5,16,128]{2,1,0:T(8,128)S(1)}, f32[5,16,128]{2,1,0:T(8,128)S(1)}, u32[]{:S(2)}, u32[]{:S(2)}) collective-permute-start(f32[5,16,128]{2,1,0:T(8,128)S(1)} %shard_map.47), channel_id=1, source_target_pairs={{0,16},{16,0},{32,48},{48,32},{64,80},{80,64},{96,112},{112,96},{1... | collective-permute-start | bytes 122888 | tf_op jit(solution)/shard_map/ppermute | solution.py:479
  26.1 4.4 %collective-permute-start.11 = (f32[5,16,128]{2,1,0:T(8,128)S(1)}, f32[5,16,128]{2,1,0:T(8,128)S(1)}, u32[]{:S(2)}, u32[]{:S(2)}) collective-permute-start(f32[5,16,128]{2,1,0:T(8,128)S(1)} %get-tuple-element.61), channel_id=1, source_target_pairs={{0,4},{1,5},{2,6},{3,7},{4,0},{5,1},{6,2},{7,3},{8,12},{9,13},{10,... | collective-permute-start | bytes 122888 | tf_op jit(solution)/shard_map/ppermute | solution.py:468
  29.1 4.0 %collective-permute-start.12 = (f32[5,8,128]{2,1,0:T(8,128)S(1)}, f32[5,8,128]{2,1,0:T(8,128)S(1)}, u32[]{:S(2)}, u32[]{:S(2)}) collective-permute-start(f32[5,8,128]{2,1,0:T(8,128)S(1)} %get-tuple-element.60.mine), channel_id=1, source_target_pairs={{0,12},{1,13},{2,14},{3,15},{4,8},{5,9},{6,10},{7,11},{8,4},{9,5},... | collective-permute-start | bytes 61448 | tf_op jit(solution)/shard_map/ppermute | solution.py:468
  30.6 2.6 %collective-permute-start.13 = (f32[5,8,128]{2,1,0:T(8,128)S(1)}, f32[5,8,128]{2,1,0:T(8,128)S(1)}, u32[]{:S(2)}, u32[]{:S(2)}) collective-permute-start(f32[5,8,128]{2,1,0:T(8,128)S(1)} %shard_map.49), channel_id=1, source_target_pairs={{0,16},{16,0},{32,48},{48,32},{64,80},{80,64},{96,112},{112,96},{1... | collective-permute-start | bytes 61448 | tf_op jit(solution)/shard_map/ppermute | solution.py:479

commit v12 on v11

--- a/solution.py
+++ b/solution.py
@@ -229,7 +229,7 @@
     my[2] = trail + jnp.where(me == last, (2.0 / (y_row(ky_t, BY - 1))), 0.0)
 
 
-def x_ends_kernel(came1, came2, below_x, mine, part, edges, send, flux, rows):
+def x_ends_kernel(came2, came1, below_x, mine, part, edges, send, flux, rows):
     me = lax.axis_index("gy")
     even = lax.rem(me, 2) == 0
     below = jnp.where(me == 0, 0.0, jnp.where(even, came2[...], came1[...]))
@@ -324,13 +324,13 @@
     send[4] = last
 
 
-def y_pack_kernel(own, other, both):
+def y_pack_kernel(own, other, after, both):
     on_low = lax.rem(lax.axis_index("gx"), 2) == 0
     both[:, 0:GROUPS] = jnp.where(on_low, own[...], other[...])
     both[:, GROUPS : 2 * GROUPS] = jnp.where(on_low, other[...], own[...])
 
 
-def y_local_kernel(v_t, f, u, after, g_t):
+def y_local_kernel(v_t, f, u, g_t):
     total = y_row(v_t, 0)
     g_t[0] = total
     for j in range(1, BY):
@@ -452,7 +452,7 @@
     ends, flux = call(
         x_ends_kernel,
         near(x_block, (3, GROUPS, 128)),
-        near(came1, came2, below_x, mine, part, edges),
+        near(came2, came1, below_x, mine, part, edges),
         [pltpu.VMEM((2, NZ, BY), F32)],
     )
     other = lax.ppermute(ends, "gx", [(i, i ^ 1) for i in range(nx)])
@@ -498,15 +498,14 @@
             pltpu.VMEM((2, NZ, BY), F32),
         ],
     )
-    (both,) = call(y_pack_kernel, near(wide), near(own, share(own)))
+    (g_t,) = call(y_local_kernel, near(ys), near(v_t, f, u), cost=3_000_000)
+    (both,) = call(y_pack_kernel, near(wide), near(own, share(own), g_t))
     far = swap("y", (1, 2), both)
     near_y = swap("y", (3, 3), both)
-    (g_t,) = call(y_local_kernel, near(ys), near(v_t, f, u, both), cost=3_000_000)
-    (relayed,) = call(relay_kernel, near(wide), near(far, g_t))
     quad, mine, coefs = call(
         y_merge_kernel,
         near(wide, (5, GROUPS, 128), (SIDE - 1, 3, 2 * GROUPS, 128)),
-        near(both, far, near_y, share(relayed)),
+        near(both, far, near_y, share(far)),
         [pltpu.VMEM((SIDE,) + wide, F32)],
     )
     far = swap("y", (4, 8), quad)

time: 34.3 us -> 33.9 us (0.988)
  the two profiles are of different devices: /device:TPU:1 before, /device:TPU:0 now
where the time goes in v12:
time: 33.9 us; the launch traced here: 33.6 us
  starting transfers between devices  16.7 us (49%)
  waiting for transfers between devices  9.92 us (29%)
  Pallas kernels  6.86 us (20%)
    ppermute x6, starting transfers between devices, swap(): lax.ppermute(value, ('gx', 'gy'), [(i * ny + j, (i ^ 2 * bits[i % 2]) * n...  10.9 us
    pallas_call x13, Pallas kernels, call(): pl.pallas_call(kernel, out_shape=[jax.ShapeDtypeStruct(shape, F32) if far...  6.86 us
    ppermute x6, waiting for transfers between devices, swap(): lax.ppermute(value, ('gx', 'gy'), [(i * ny + j, (i ^ 2 * bits[i % 2]) * n...  5.94 us
    ppermute x1, starting transfers between devices, on_device(): came1 = lax.ppermute(first, 'gy', [(i, i ^ 1) for i in range(ny)])  3.91 us
    ppermute x1, waiting for transfers between devices, on_device(): below_x = lax.ppermute(last, 'gx', [(i, (i + 1) % nx) for i in range(nx)])  2.66 us
    ppermute x4, starting transfers between devices, share(): return lax.ppermute(value, 'gx', [(i, i ^ 1) for i in range(nx)])  1.79 us
  transfers between devices with their start and end apart: 14, of which 9 were waited for; matrix products, arithmetic and copies ran while one was open for 0% of the time, Pallas kernels for 11%

profile of v12, /device:TPU:0, one launch (start us, length us, event | category | flops | bytes accessed | tf_op | source)
XLA Modules:
  0.0 33.6 jit_solution(5444968333696239039)
XLA Ops:
  0.0 1.5 %shard_map.37 = (f32[16,72,128]{2,1,0:T(8,128)S(1)}, f32[16,72,128]{2,1,0:T(8,128)S(1)}, f32[1024,128]{1,0:T(8,128)S(1)}, f32[1024,128]{1,0:T(8,128)S(1)}, f32[4...) custom-call(f32[16,64,128]{2,1,0:T(8,128)} %st_hbm.1, ...), custom_call_target="tpu_custom_call" | custom-call | flops 100000 | bytes 100000 | tf_op jit(solution)/shard_map/pallas_call | solution.py:399
  1.6 3.9 %collective-permute-start.1 = (f32[2,8,128]{2,1,0:T(8,128)S(1)}, f32[2,8,128]{2,1,0:T(8,128)S(1)}, u32[]{:S(2)}, u32[]{:S(2)}) collective-permute-start(f32[2,8,128]{2,1,0:T(8,128)S(1)} %get-tuple-element.35), channel_id=1, source_target_pairs={{0,1},{1,0},{2,3},{3,2},{4,5},{5,4},{6,7},{7,6},{8,9},{9,8},{10,11... | collective-permute-start | bytes 24584 | tf_op jit(solution)/shard_map/ppermute | solution.py:443
  5.5 1.3 %shard_map.38 = (f32[64,16,128]{2,1,0:T(8,128)S(1)}, f32[64,16,128]{2,1,0:T(8,128)S(1)}, f32[1152,128]{1,0:T(8,128)S(1)}, f32[1152,128]{1,0:T(8,128)S(1)}, f32[6...) custom-call(f32[1024,128]{1,0:T(8,128)S(1)} %get-tuple-element.38.st_t, ...), custom_call_target="tpu_custom_call" | custom-call | flops 5000000 | bytes 5000000 | tf_op jit(solution)/shard_map/pallas_call | solution.py:399
  7.1 2.7 %collective-permute-done.2.below_x = f32[16,128]{1,0:T(8,128)S(1)} collective-permute-done((f32[16,128]{1,0:T(8,128)S(1)}, f32[16,128]{1,0:T(8,128)S(1)}, u32[]{:S(2)}, u32[]{:S(2)}) %collective-permute-start.2) | collective-permute-done | bytes 8224 | tf_op jit(solution)/shard_map/ppermute | solution.py:444
  9.9 0.5 %shard_map.40.after.d = f32[1152,128]{1,0:T(8,128)S(1)} custom-call(f32[1024,128]{1,0:T(8,128)S(1)} %get-tuple-element.44.base_t, f32[3,8,128]{2,1,0:T(8,128)S(1)} %get-tuple-element.45.flux, f32[1152,128]{1,0:T(8,128)S(1)} %bitcast.3, f32[64,16,128]{2,1,0:T(8,128)S(1)} %get-tuple-element.47.fx, f32[64,16,128]{2,1,0:T(8,128)S(1)} %get-tuple-element.48.ux), custom_call_target="tpu_custom_call" | custom-call | flops 3000000 | bytes 3000000 | tf_op jit(solution)/shard_map/pallas_call | solution.py:399
  10.5 0.7 %collective-permute-done.3.other = f32[5,16,128]{2,1,0:T(8,128)S(1)} collective-permute-done((f32[5,16,128]{2,1,0:T(8,128)S(1)}, f32[5,16,128]{2,1,0:T(8,128)S(1)}, u32[]{:S(2)}, u32[]{:S(2)}) %collective-permute-start.3) | collective-permute-done | bytes 40992 | tf_op jit(solution)/shard_map/ppermute | solution.py:458
  11.2 0.4 %collective-permute-start.4 = (f32[5,16,128]{2,1,0:T(8,128)S(1)}, f32[5,16,128]{2,1,0:T(8,128)S(1)}, u32[]{:S(2)}, u32[]{:S(2)}) collective-permute-start(f32[5,16,128]{2,1,0:T(8,128)S(1)} %get-tuple-element.49.own), channel_id=1, source_target_pairs={{0,32},{1,33},{2,34},{3,35},{4,36},{5,37},{6,38},{7,39},{8,40},{9,... | collective-permute-start | bytes 122888 | tf_op jit(solution)/shard_map/ppermute | solution.py:468
  11.5 2.1 %collective-permute-start.5 = (f32[5,16,128]{2,1,0:T(8,128)S(1)}, f32[5,16,128]{2,1,0:T(8,128)S(1)}, u32[]{:S(2)}, u32[]{:S(2)}) collective-permute-start(f32[5,16,128]{2,1,0:T(8,128)S(1)} %get-tuple-element.49.own), channel_id=1, source_target_pairs={{0,96},{1,97},{2,98},{3,99},{4,100},{5,101},{6,102},{7,103},{8,104... | collective-permute-start | bytes 122888 | tf_op jit(solution)/shard_map/ppermute | solution.py:468
  13.6 1.4 %shard_map.42 = (f32[128,8,128]{2,1,0:T(8,128)S(1)}, f32[128,8,128]{2,1,0:T(8,128)S(1)}, f32[128,8,128]{2,1,0:T(8,128)S(1)}, f32[128,8,128]{2,1,0:T(8,128)S(1)}, f32[3,8,128]{2,1,0:T(8,128)S(1)}) custom-call(f32[1024,128]{1,0:T(8,128)S(1)} %get-tuple-element.40.ky_t, f32[3,16,128]{2,1,0:T(8,128)S(1)} %get-tuple-element.50.after.coefs), custom_call_target="tpu_custom_call" | custom-call | flops 5000000 | bytes 5000000 | tf_op jit(solution)/shard_map/pallas_call | solution.py:399
  15.3 0.7 %collective-permute-start.6 = (f32[5,16,128]{2,1,0:T(8,128)S(1)}, f32[5,16,128]{2,1,0:T(8,128)S(1)}, u32[]{:S(2)}, u32[]{:S(2)}) collective-permute-start(f32[5,16,128]{2,1,0:T(8,128)S(1)} %shard_map.43), channel_id=1, source_target_pairs={{0,16},{16,0},{32,48},{48,32},{64,80},{80,64},{96,112},{112,96},{1... | collective-permute-start | bytes 122888 | tf_op jit(solution)/shard_map/ppermute | solution.py:479
  15.9 0.8 %collective-permute-done.5.near = f32[5,16,128]{2,1,0:T(8,128)S(1)} collective-permute-done((f32[5,16,128]{2,1,0:T(8,128)S(1)}, f32[5,16,128]{2,1,0:T(8,128)S(1)}, u32[]{:S(2)}, u32[]{:S(2)}) %collective-permute-start.5) | collective-permute-done | bytes 40992 | tf_op jit(solution)/shard_map/ppermute | solution.py:468
  16.8 0.3 shard_map.44
  17.1 0.4 %collective-permute-start.7 = (f32[5,8,128]{2,1,0:T(8,128)S(1)}, f32[5,8,128]{2,1,0:T(8,128)S(1)}, u32[]{:S(2)}, u32[]{:S(2)}) collective-permute-start(f32[5,8,128]{2,1,0:T(8,128)S(1)} %get-tuple-element.56.own), channel_id=1, source_target_pairs={{0,16},{16,0},{32,48},{48,32},{64,80},{80,64},{96,112},{112,96},{1... | collective-permute-start | bytes 61448 | tf_op jit(solution)/shard_map/ppermute | solution.py:479
  17.6 0.5 %shard_map.45.after.g_t = f32[128,8,128]{2,1,0:T(8,128)S(1)} custom-call(f32[1024,128]{1,0:T(8,128)S(1)} %get-tuple-element.57.v_t, f32[128,8,128]{2,1,0:T(8,128)S(1)} %get-tuple-element.58.f, f32[128,8,128]{2,1,0:T(8,128)S(1)} %get-tuple-element.59.u), custom_call_target="tpu_custom_call" | custom-call | flops 3000000 | bytes 3000000 | tf_op jit(solution)/shard_map/pallas_call | solution.py:399
  18.1 0.3 collective-permute-done.7.other
  18.4 0.6 %collective-permute-start.8 = (f32[5,16,128]{2,1,0:T(8,128)S(1)}, f32[5,16,128]{2,1,0:T(8,128)S(1)}, u32[]{:S(2)}, u32[]{:S(2)}) collective-permute-start(f32[5,16,128]{2,1,0:T(8,128)S(1)} %shard_map.46.own), channel_id=1, source_target_pairs={{0,1},{1,0},{2,3},{3,2},{4,5},{5,4},{6,7},{7,6},{8,9},{9,8},{10,11... | collective-permute-start | bytes 122888 | tf_op jit(solution)/shard_map/ppermute | solution.py:468
  19.0 2.4 %collective-permute-start.9 = (f32[5,16,128]{2,1,0:T(8,128)S(1)}, f32[5,16,128]{2,1,0:T(8,128)S(1)}, u32[]{:S(2)}, u32[]{:S(2)}) collective-permute-start(f32[5,16,128]{2,1,0:T(8,128)S(1)} %shard_map.46.own), channel_id=1, source_target_pairs={{0,3},{1,2},{2,1},{3,0},{4,7},{5,6},{6,5},{7,4},{8,11},{9,10},{10,... | collective-permute-start | bytes 122888 | tf_op jit(solution)/shard_map/ppermute | solution.py:468
  21.4 1.1 %collective-permute-done.8.far = f32[5,16,128]{2,1,0:T(8,128)S(1)} collective-permute-done((f32[5,16,128]{2,1,0:T(8,128)S(1)}, f32[5,16,128]{2,1,0:T(8,128)S(1)}, u32[]{:S(2)}, u32[]{:S(2)}) %collective-permute-start.8) | collective-permute-done | bytes 40992 | tf_op jit(solution)/shard_map/ppermute | solution.py:468
  22.5 0.7 %collective-permute-start.10 = (f32[5,16,128]{2,1,0:T(8,128)S(1)}, f32[5,16,128]{2,1,0:T(8,128)S(1)}, u32[]{:S(2)}, u32[]{:S(2)}) collective-permute-start(f32[5,16,128]{2,1,0:T(8,128)S(1)} %collective-permute-done.8.far), channel_id=1, source_target_pairs={{0,16},{16,0},{32,48},{48,32},{64,80},{80,64},{96,112},{112,96},{1... | collective-permute-start | bytes 122888 | tf_op jit(solution)/shard_map/ppermute | solution.py:479
  23.2 1.0 %collective-permute-done.9.near = f32[5,16,128]{2,1,0:T(8,128)S(1)} collective-permute-done((f32[5,16,128]{2,1,0:T(8,128)S(1)}, f32[5,16,128]{2,1,0:T(8,128)S(1)}, u32[]{:S(2)}, u32[]{:S(2)}) %collective-permute-start.9) | collective-permute-done | bytes 40992 | tf_op jit(solution)/shard_map/ppermute | solution.py:468
  24.3 3.2 %collective-permute-start.11 = (f32[5,16,128]{2,1,0:T(8,128)S(1)}, f32[5,16,128]{2,1,0:T(8,128)S(1)}, u32[]{:S(2)}, u32[]{:S(2)}) collective-permute-start(f32[5,16,128]{2,1,0:T(8,128)S(1)} %get-tuple-element.61), channel_id=1, source_target_pairs={{0,4},{1,5},{2,6},{3,7},{4,0},{5,1},{6,2},{7,3},{8,12},{9,13},{10,... | collective-permute-start | bytes 122888 | tf_op jit(solution)/shard_map/ppermute | solution.py:468
  27.5 2.2 %collective-permute-start.12 = (f32[5,8,128]{2,1,0:T(8,128)S(1)}, f32[5,8,128]{2,1,0:T(8,128)S(1)}, u32[]{:S(2)}, u32[]{:S(2)}) collective-permute-start(f32[5,8,128]{2,1,0:T(8,128)S(1)} %get-tuple-element.60.mine), channel_id=1, source_target_pairs={{0,12},{1,13},{2,14},{3,15},{4,8},{5,9},{6,10},{7,11},{8,4},{9,5},... | collective-permute-start | bytes 61448 | tf_op jit(solution)/shard_map/ppermute | solution.py:468
  29.7 2.8 %collective-permute-done.12.near = f32[5,8,128]{2,1,0:T(8,128)S(1)} collective-permute-done((f32[5,8,128]{2,1,0:T(8,128)S(1)}, f32[5,8,128]{2,1,0:T(8,128)S(1)}, u32[]{:S(2)}, u32[]{:S(2)}) %collective-permute-start.12) | collective-permute-done | bytes 20512 | tf_op jit(solution)/shard_map/ppermute | solution.py:468
  32.5 1.1 %shard_map.49 = f32[1024,128]{1,0:T(8,128)} custom-call(f32[5,8,128]{2,1,0:T(8,128)S(1)} %get-tuple-element.60.mine, f32[5,16,128]{2,1,0:T(8,128)S(1)} %collective-permute-done.11.value.far, f32[5,8,128]{2,1,0:T(8,128)S(1)} %collective-permute-done.12.near, f32[5,8,128]{2,1,0:T(8,128)S(1)} %collective-permute-done.13.shared, ...), custom_call_target="tpu_custom_call" | custom-call | flops 100000 | bytes 100000 | tf_op jit(solution)/shard_map/pallas_call | solution.py:399
  (17 shorter events, 0.9 us)
Async XLA Ops:
  1.5 5.3 %collective-permute-start = (f32[2,8,128]{2,1,0:T(8,128)S(1)}, f32[2,8,128]{2,1,0:T(8,128)S(1)}, u32[]{:S(2)}, u32[]{:S(2)}) collective-permute-start(f32[2,8,128]{2,1,0:T(8,128)S(1)} %get-tuple-element.34), channel_id=1, source_target_pairs={{0,16},{1,2},{2,1},{3,4},{4,3},{5,6},{6,5},{7,8},{8,7},{9,10},{10,... | collective-permute-start | bytes 24584 | tf_op jit(solution)/shard_map/ppermute | solution.py:442
  1.6 5.5 %collective-permute-start.1 = (f32[2,8,128]{2,1,0:T(8,128)S(1)}, f32[2,8,128]{2,1,0:T(8,128)S(1)}, u32[]{:S(2)}, u32[]{:S(2)}) collective-permute-start(f32[2,8,128]{2,1,0:T(8,128)S(1)} %get-tuple-element.35), channel_id=1, source_target_pairs={{0,1},{1,0},{2,3},{3,2},{4,5},{5,4},{6,7},{7,6},{8,9},{9,8},{10,11... | collective-permute-start | bytes 24584 | tf_op jit(solution)/shard_map/ppermute | solution.py:443
  5.5 4.3 %collective-permute-start.2 = (f32[16,128]{1,0:T(8,128)S(1)}, f32[16,128]{1,0:T(8,128)S(1)}, u32[]{:S(2)}, u32[]{:S(2)}) collective-permute-start(f32[16,128]{1,0:T(8,128)S(1)} %get-tuple-element.36), channel_id=1, source_target_pairs={{0,16},{16,32},{32,48},{48,64},{64,80},{80,96},{96,112},{112,0},{1... | collective-permute-start | bytes 24584 | tf_op jit(solution)/shard_map/ppermute | solution.py:444
  9.9 1.3 %collective-permute-start.3 = (f32[5,16,128]{2,1,0:T(8,128)S(1)}, f32[5,16,128]{2,1,0:T(8,128)S(1)}, u32[]{:S(2)}, u32[]{:S(2)}) collective-permute-start(f32[5,16,128]{2,1,0:T(8,128)S(1)} %get-tuple-element.43.own), channel_id=1, source_target_pairs={{0,16},{16,0},{32,48},{48,32},{64,80},{80,64},{96,112},{112,96},{1... | collective-permute-start | bytes 122888 | tf_op jit(solution)/shard_map/ppermute | solution.py:458
  11.2 4.1 %collective-permute-start.4 = (f32[5,16,128]{2,1,0:T(8,128)S(1)}, f32[5,16,128]{2,1,0:T(8,128)S(1)}, u32[]{:S(2)}, u32[]{:S(2)}) collective-permute-start(f32[5,16,128]{2,1,0:T(8,128)S(1)} %get-tuple-element.49.own), channel_id=1, source_target_pairs={{0,32},{1,33},{2,34},{3,35},{4,36},{5,37},{6,38},{7,39},{8,40},{9,... | collective-permute-start | bytes 122888 | tf_op jit(solution)/shard_map/ppermute | solution.py:468
  11.5 5.2 %collective-permute-start.5 = (f32[5,16,128]{2,1,0:T(8,128)S(1)}, f32[5,16,128]{2,1,0:T(8,128)S(1)}, u32[]{:S(2)}, u32[]{:S(2)}) collective-permute-start(f32[5,16,128]{2,1,0:T(8,128)S(1)} %get-tuple-element.49.own), channel_id=1, source_target_pairs={{0,96},{1,97},{2,98},{3,99},{4,100},{5,101},{6,102},{7,103},{8,104... | collective-permute-start | bytes 122888 | tf_op jit(solution)/shard_map/ppermute | solution.py:468
  15.3 1.5 %collective-permute-start.6 = (f32[5,16,128]{2,1,0:T(8,128)S(1)}, f32[5,16,128]{2,1,0:T(8,128)S(1)}, u32[]{:S(2)}, u32[]{:S(2)}) collective-permute-start(f32[5,16,128]{2,1,0:T(8,128)S(1)} %shard_map.43), channel_id=1, source_target_pairs={{0,16},{16,0},{32,48},{48,32},{64,80},{80,64},{96,112},{112,96},{1... | collective-permute-start | bytes 122888 | tf_op jit(solution)/shard_map/ppermute | solution.py:479
  17.1 1.3 %collective-permute-start.7 = (f32[5,8,128]{2,1,0:T(8,128)S(1)}, f32[5,8,128]{2,1,0:T(8,128)S(1)}, u32[]{:S(2)}, u32[]{:S(2)}) collective-permute-start(f32[5,8,128]{2,1,0:T(8,128)S(1)} %get-tuple-element.56.own), channel_id=1, source_target_pairs={{0,16},{16,0},{32,48},{48,32},{64,80},{80,64},{96,112},{112,96},{1... | collective-permute-start | bytes 61448 | tf_op jit(solution)/shard_map/ppermute | solution.py:479
  18.4 4.1 %collective-permute-start.8 = (f32[5,16,128]{2,1,0:T(8,128)S(1)}, f32[5,16,128]{2,1,0:T(8,128)S(1)}, u32[]{:S(2)}, u32[]{:S(2)}) collective-permute-start(f32[5,16,128]{2,1,0:T(8,128)S(1)} %shard_map.46.own), channel_id=1, source_target_pairs={{0,1},{1,0},{2,3},{3,2},{4,5},{5,4},{6,7},{7,6},{8,9},{9,8},{10,11... | collective-permute-start | bytes 122888 | tf_op jit(solution)/shard_map/ppermute | solution.py:468
  19.0 5.2 %collective-permute-start.9 = (f32[5,16,128]{2,1,0:T(8,128)S(1)}, f32[5,16,128]{2,1,0:T(8,128)S(1)}, u32[]{:S(2)}, u32[]{:S(2)}) collective-permute-start(f32[5,16,128]{2,1,0:T(8,128)S(1)} %shard_map.46.own), channel_id=1, source_target_pairs={{0,3},{1,2},{2,1},{3,0},{4,7},{5,6},{6,5},{7,4},{8,11},{9,10},{10,... | collective-permute-start | bytes 122888 | tf_op jit(solution)/shard_map/ppermute | solution.py:468
  22.5 1.7 %collective-permute-start.10 = (f32[5,16,128]{2,1,0:T(8,128)S(1)}, f32[5,16,128]{2,1,0:T(8,128)S(1)}, u32[]{:S(2)}, u32[]{:S(2)}) collective-permute-start(f32[5,16,128]{2,1,0:T(8,128)S(1)} %collective-permute-done.8.far), channel_id=1, source_target_pairs={{0,16},{16,0},{32,48},{48,32},{64,80},{80,64},{96,112},{112,96},{1... | collective-permute-start | bytes 122888 | tf_op jit(solution)/shard_map/ppermute | solution.py:479
  24.3 5.4 %collective-permute-start.11 = (f32[5,16,128]{2,1,0:T(8,128)S(1)}, f32[5,16,128]{2,1,0:T(8,128)S(1)}, u32[]{:S(2)}, u32[]{:S(2)}) collective-permute-start(f32[5,16,128]{2,1,0:T(8,128)S(1)} %get-tuple-element.61), channel_id=1, source_target_pairs={{0,4},{1,5},{2,6},{3,7},{4,0},{5,1},{6,2},{7,3},{8,12},{9,13},{10,... | collective-permute-start | bytes 122888 | tf_op jit(solution)/shard_map/ppermute | solution.py:468
  27.5 5.0 %collective-permute-start.12 = (f32[5,8,128]{2,1,0:T(8,128)S(1)}, f32[5,8,128]{2,1,0:T(8,128)S(1)}, u32[]{:S(2)}, u32[]{:S(2)}) collective-permute-start(f32[5,8,128]{2,1,0:T(8,128)S(1)} %get-tuple-element.60.mine), channel_id=1, source_target_pairs={{0,12},{1,13},{2,14},{3,15},{4,8},{5,9},{6,10},{7,11},{8,4},{9,5},... | collective-permute-start | bytes 61448 | tf_op jit(solution)/shard_map/ppermute | solution.py:468
  29.7 2.8 %collective-permute-start.13 = (f32[5,8,128]{2,1,0:T(8,128)S(1)}, f32[5,8,128]{2,1,0:T(8,128)S(1)}, u32[]{:S(2)}, u32[]{:S(2)}) collective-permute-start(f32[5,8,128]{2,1,0:T(8,128)S(1)} %shard_map.48), channel_id=1, source_target_pairs={{0,16},{16,0},{32,48},{48,32},{64,80},{80,64},{96,112},{112,96},{1... | collective-permute-start | bytes 61448 | tf_op jit(solution)/shard_map/ppermute | solution.py:479

commit v13 on v12

--- a/solution.py
+++ b/solution.py
@@ -229,7 +229,7 @@
     my[2] = trail + jnp.where(me == last, (2.0 / (y_row(ky_t, BY - 1))), 0.0)
 
 
-def x_ends_kernel(came2, came1, below_x, mine, part, edges, send, flux, rows):
+def x_ends_kernel(came2, below_x, came1, mine, part, edges, send, flux, rows):
     me = lax.axis_index("gy")
     even = lax.rem(me, 2) == 0
     below = jnp.where(me == 0, 0.0, jnp.where(even, came2[...], came1[...]))
@@ -452,7 +452,7 @@
     ends, flux = call(
         x_ends_kernel,
         near(x_block, (3, GROUPS, 128)),
-        near(came2, came1, below_x, mine, part, edges),
+        near(came2, below_x, came1, mine, part, edges),
         [pltpu.VMEM((2, NZ, BY), F32)],
     )
     other = lax.ppermute(ends, "gx", [(i, i ^ 1) for i in range(nx)])

time: 33.9 us -> 34.1 us (level)
  the two profiles are of different devices: /device:TPU:0 before, /device:TPU:1 now
where the time goes in v13:
time: 34.1 us; the launch traced here: 34 us
  starting transfers between devices  19.4 us (57%)
  waiting for transfers between devices  7.66 us (22%)
  Pallas kernels  6.86 us (20%)
    ppermute x6, starting transfers between devices, swap(): lax.ppermute(value, ('gx', 'gy'), [(i * ny + j, (i ^ 2 * bits[i % 2]) * n...  12.6 us
    pallas_call x13, Pallas kernels, call(): pl.pallas_call(kernel, out_shape=[jax.ShapeDtypeStruct(shape, F32) if far...  6.86 us
    ppermute x6, waiting for transfers between devices, swap(): lax.ppermute(value, ('gx', 'gy'), [(i * ny + j, (i ^ 2 * bits[i % 2]) * n...  6.67 us
    ppermute x1, starting transfers between devices, on_device(): came1 = lax.ppermute(first, 'gy', [(i, i ^ 1) for i in range(ny)])  3.53 us
    ppermute x1, starting transfers between devices, on_device(): came2 = lax.ppermute(second, ('gx', 'gy'), pairs)  1.5 us
    ppermute x1, starting transfers between devices, on_device(): below_x = lax.ppermute(last, 'gx', [(i, (i + 1) % nx) for i in range(nx)])  1.2 us
  transfers between devices with their start and end apart: 14, of which 7 were waited for; matrix products, arithmetic and copies ran while one was open for 0% of the time, Pallas kernels for 11%

profile of v13, /device:TPU:1, one launch (start us, length us, event | category | flops | bytes accessed | tf_op | source)
XLA Modules:
  0.0 34.0 jit_solution(16997697178899252336)
XLA Ops:
  0.0 1.5 %shard_map.37 = (f32[16,72,128]{2,1,0:T(8,128)S(1)}, f32[16,72,128]{2,1,0:T(8,128)S(1)}, f32[1024,128]{1,0:T(8,128)S(1)}, f32[1024,128]{1,0:T(8,128)S(1)}, f32[4...) custom-call(f32[16,64,128]{2,1,0:T(8,128)} %st_hbm.1, ...), custom_call_target="tpu_custom_call" | custom-call | flops 100000 | bytes 100000 | tf_op jit(solution)/shard_map/pallas_call | solution.py:399
  1.5 1.5 %collective-permute-start = (f32[2,8,128]{2,1,0:T(8,128)S(1)}, f32[2,8,128]{2,1,0:T(8,128)S(1)}, u32[]{:S(2)}, u32[]{:S(2)}) collective-permute-start(f32[2,8,128]{2,1,0:T(8,128)S(1)} %get-tuple-element.34), channel_id=1, source_target_pairs={{0,16},{1,2},{2,1},{3,4},{4,3},{5,6},{6,5},{7,8},{8,7},{9,10},{10,... | collective-permute-start | bytes 24584 | tf_op jit(solution)/shard_map/ppermute | solution.py:442
  3.0 1.2 %collective-permute-start.1 = (f32[16,128]{1,0:T(8,128)S(1)}, f32[16,128]{1,0:T(8,128)S(1)}, u32[]{:S(2)}, u32[]{:S(2)}) collective-permute-start(f32[16,128]{1,0:T(8,128)S(1)} %get-tuple-element.35), channel_id=1, source_target_pairs={{0,16},{16,32},{32,48},{48,64},{64,80},{80,96},{96,112},{112,0},{1... | collective-permute-start | bytes 24584 | tf_op jit(solution)/shard_map/ppermute | solution.py:444
  4.2 3.5 %collective-permute-start.2 = (f32[2,8,128]{2,1,0:T(8,128)S(1)}, f32[2,8,128]{2,1,0:T(8,128)S(1)}, u32[]{:S(2)}, u32[]{:S(2)}) collective-permute-start(f32[2,8,128]{2,1,0:T(8,128)S(1)} %get-tuple-element.36), channel_id=1, source_target_pairs={{0,1},{1,0},{2,3},{3,2},{4,5},{5,4},{6,7},{7,6},{8,9},{9,8},{10,11... | collective-permute-start | bytes 24584 | tf_op jit(solution)/shard_map/ppermute | solution.py:443
  7.7 1.3 %shard_map.38 = (f32[64,16,128]{2,1,0:T(8,128)S(1)}, f32[64,16,128]{2,1,0:T(8,128)S(1)}, f32[1152,128]{1,0:T(8,128)S(1)}, f32[1152,128]{1,0:T(8,128)S(1)}, f32[6...) custom-call(f32[1024,128]{1,0:T(8,128)S(1)} %get-tuple-element.38.st_t, ...), custom_call_target="tpu_custom_call" | custom-call | flops 5000000 | bytes 5000000 | tf_op jit(solution)/shard_map/pallas_call | solution.py:399
  9.3 0.5 %shard_map.40.after.d = f32[1152,128]{1,0:T(8,128)S(1)} custom-call(f32[1024,128]{1,0:T(8,128)S(1)} %get-tuple-element.44.base_t, f32[3,8,128]{2,1,0:T(8,128)S(1)} %get-tuple-element.45.flux, f32[1152,128]{1,0:T(8,128)S(1)} %bitcast.3, f32[64,16,128]{2,1,0:T(8,128)S(1)} %get-tuple-element.47.fx, f32[64,16,128]{2,1,0:T(8,128)S(1)} %get-tuple-element.48.ux), custom_call_target="tpu_custom_call" | custom-call | flops 3000000 | bytes 3000000 | tf_op jit(solution)/shard_map/pallas_call | solution.py:399
  9.8 0.7 %collective-permute-done.3.other = f32[5,16,128]{2,1,0:T(8,128)S(1)} collective-permute-done((f32[5,16,128]{2,1,0:T(8,128)S(1)}, f32[5,16,128]{2,1,0:T(8,128)S(1)}, u32[]{:S(2)}, u32[]{:S(2)}) %collective-permute-start.3) | collective-permute-done | bytes 40992 | tf_op jit(solution)/shard_map/ppermute | solution.py:458
  10.5 2.5 %collective-permute-start.4 = (f32[5,16,128]{2,1,0:T(8,128)S(1)}, f32[5,16,128]{2,1,0:T(8,128)S(1)}, u32[]{:S(2)}, u32[]{:S(2)}) collective-permute-start(f32[5,16,128]{2,1,0:T(8,128)S(1)} %get-tuple-element.49.own), channel_id=1, source_target_pairs={{0,32},{1,33},{2,34},{3,35},{4,36},{5,37},{6,38},{7,39},{8,40},{9,... | collective-permute-start | bytes 122888 | tf_op jit(solution)/shard_map/ppermute | solution.py:468
  13.0 1.2 %collective-permute-start.5 = (f32[5,16,128]{2,1,0:T(8,128)S(1)}, f32[5,16,128]{2,1,0:T(8,128)S(1)}, u32[]{:S(2)}, u32[]{:S(2)}) collective-permute-start(f32[5,16,128]{2,1,0:T(8,128)S(1)} %get-tuple-element.49.own), channel_id=1, source_target_pairs={{0,96},{1,97},{2,98},{3,99},{4,100},{5,101},{6,102},{7,103},{8,104... | collective-permute-start | bytes 122888 | tf_op jit(solution)/shard_map/ppermute | solution.py:468
  14.2 1.4 %shard_map.42 = (f32[128,8,128]{2,1,0:T(8,128)S(1)}, f32[128,8,128]{2,1,0:T(8,128)S(1)}, f32[128,8,128]{2,1,0:T(8,128)S(1)}, f32[128,8,128]{2,1,0:T(8,128)S(1)}, f32[3,8,128]{2,1,0:T(8,128)S(1)}) custom-call(f32[1024,128]{1,0:T(8,128)S(1)} %get-tuple-element.40.ky_t, f32[3,16,128]{2,1,0:T(8,128)S(1)} %get-tuple-element.50.after.coefs), custom_call_target="tpu_custom_call" | custom-call | flops 5000000 | bytes 5000000 | tf_op jit(solution)/shard_map/pallas_call | solution.py:399
  15.7 1.5 %collective-permute-done.5.near = f32[5,16,128]{2,1,0:T(8,128)S(1)} collective-permute-done((f32[5,16,128]{2,1,0:T(8,128)S(1)}, f32[5,16,128]{2,1,0:T(8,128)S(1)}, u32[]{:S(2)}, u32[]{:S(2)}) %collective-permute-start.5) | collective-permute-done | bytes 40992 | tf_op jit(solution)/shard_map/ppermute | solution.py:468
  17.2 0.3 shard_map.44
  17.5 0.4 %collective-permute-start.7 = (f32[5,8,128]{2,1,0:T(8,128)S(1)}, f32[5,8,128]{2,1,0:T(8,128)S(1)}, u32[]{:S(2)}, u32[]{:S(2)}) collective-permute-start(f32[5,8,128]{2,1,0:T(8,128)S(1)} %get-tuple-element.56.own), channel_id=1, source_target_pairs={{0,16},{16,0},{32,48},{48,32},{64,80},{80,64},{96,112},{112,96},{1... | collective-permute-start | bytes 61448 | tf_op jit(solution)/shard_map/ppermute | solution.py:479
  17.9 0.5 %shard_map.45.after.g_t = f32[128,8,128]{2,1,0:T(8,128)S(1)} custom-call(f32[1024,128]{1,0:T(8,128)S(1)} %get-tuple-element.57.v_t, f32[128,8,128]{2,1,0:T(8,128)S(1)} %get-tuple-element.58.f, f32[128,8,128]{2,1,0:T(8,128)S(1)} %get-tuple-element.59.u), custom_call_target="tpu_custom_call" | custom-call | flops 3000000 | bytes 3000000 | tf_op jit(solution)/shard_map/pallas_call | solution.py:399
  18.5 0.3 collective-permute-done.7.other
  18.8 1.7 %collective-permute-start.8 = (f32[5,16,128]{2,1,0:T(8,128)S(1)}, f32[5,16,128]{2,1,0:T(8,128)S(1)}, u32[]{:S(2)}, u32[]{:S(2)}) collective-permute-start(f32[5,16,128]{2,1,0:T(8,128)S(1)} %shard_map.46.own), channel_id=1, source_target_pairs={{0,1},{1,0},{2,3},{3,2},{4,5},{5,4},{6,7},{7,6},{8,9},{9,8},{10,11... | collective-permute-start | bytes 122888 | tf_op jit(solution)/shard_map/ppermute | solution.py:468
  20.5 1.9 %collective-permute-start.9 = (f32[5,16,128]{2,1,0:T(8,128)S(1)}, f32[5,16,128]{2,1,0:T(8,128)S(1)}, u32[]{:S(2)}, u32[]{:S(2)}) collective-permute-start(f32[5,16,128]{2,1,0:T(8,128)S(1)} %shard_map.46.own), channel_id=1, source_target_pairs={{0,3},{1,2},{2,1},{3,0},{4,7},{5,6},{6,5},{7,4},{8,11},{9,10},{10,... | collective-permute-start | bytes 122888 | tf_op jit(solution)/shard_map/ppermute | solution.py:468
  22.4 0.8 %collective-permute-done.8.far = f32[5,16,128]{2,1,0:T(8,128)S(1)} collective-permute-done((f32[5,16,128]{2,1,0:T(8,128)S(1)}, f32[5,16,128]{2,1,0:T(8,128)S(1)}, u32[]{:S(2)}, u32[]{:S(2)}) %collective-permute-start.8) | collective-permute-done | bytes 40992 | tf_op jit(solution)/shard_map/ppermute | solution.py:468
  23.2 1.3 %collective-permute-done.9.near = f32[5,16,128]{2,1,0:T(8,128)S(1)} collective-permute-done((f32[5,16,128]{2,1,0:T(8,128)S(1)}, f32[5,16,128]{2,1,0:T(8,128)S(1)}, u32[]{:S(2)}, u32[]{:S(2)}) %collective-permute-start.9) | collective-permute-done | bytes 40992 | tf_op jit(solution)/shard_map/ppermute | solution.py:468
  24.6 4.5 %collective-permute-start.11 = (f32[5,16,128]{2,1,0:T(8,128)S(1)}, f32[5,16,128]{2,1,0:T(8,128)S(1)}, u32[]{:S(2)}, u32[]{:S(2)}) collective-permute-start(f32[5,16,128]{2,1,0:T(8,128)S(1)} %get-tuple-element.61), channel_id=1, source_target_pairs={{0,4},{1,5},{2,6},{3,7},{4,0},{5,1},{6,2},{7,3},{8,12},{9,13},{10,... | collective-permute-start | bytes 122888 | tf_op jit(solution)/shard_map/ppermute | solution.py:468
  29.1 0.8 %collective-permute-start.12 = (f32[5,8,128]{2,1,0:T(8,128)S(1)}, f32[5,8,128]{2,1,0:T(8,128)S(1)}, u32[]{:S(2)}, u32[]{:S(2)}) collective-permute-start(f32[5,8,128]{2,1,0:T(8,128)S(1)} %get-tuple-element.60.mine), channel_id=1, source_target_pairs={{0,12},{1,13},{2,14},{3,15},{4,8},{5,9},{6,10},{7,11},{8,4},{9,5},... | collective-permute-start | bytes 61448 | tf_op jit(solution)/shard_map/ppermute | solution.py:468
  29.9 0.6 %collective-permute-done.11.value.far = f32[5,16,128]{2,1,0:T(8,128)S(1)} collective-permute-done((f32[5,16,128]{2,1,0:T(8,128)S(1)}, f32[5,16,128]{2,1,0:T(8,128)S(1)}, u32[]{:S(2)}, u32[]{:S(2)}) %collective-permute-start.11) | collective-permute-done | bytes 40992 | tf_op jit(solution)/shard_map/ppermute | solution.py:468
  30.5 2.4 %collective-permute-done.12.near = f32[5,8,128]{2,1,0:T(8,128)S(1)} collective-permute-done((f32[5,8,128]{2,1,0:T(8,128)S(1)}, f32[5,8,128]{2,1,0:T(8,128)S(1)}, u32[]{:S(2)}, u32[]{:S(2)}) %collective-permute-start.12) | collective-permute-done | bytes 20512 | tf_op jit(solution)/shard_map/ppermute | solution.py:468
  33.0 1.1 %shard_map.49 = f32[1024,128]{1,0:T(8,128)} custom-call(f32[5,8,128]{2,1,0:T(8,128)S(1)} %get-tuple-element.60.mine, f32[5,16,128]{2,1,0:T(8,128)S(1)} %collective-permute-done.11.value.far, f32[5,8,128]{2,1,0:T(8,128)S(1)} %collective-permute-done.12.near, f32[5,8,128]{2,1,0:T(8,128)S(1)} %collective-permute-done.13.shared, ...), custom_call_target="tpu_custom_call" | custom-call | flops 100000 | bytes 100000 | tf_op jit(solution)/shard_map/pallas_call | solution.py:399
  (17 shorter events, 0.4 us)
Async XLA Ops:
  1.5 7.6 %collective-permute-start = (f32[2,8,128]{2,1,0:T(8,128)S(1)}, f32[2,8,128]{2,1,0:T(8,128)S(1)}, u32[]{:S(2)}, u32[]{:S(2)}) collective-permute-start(f32[2,8,128]{2,1,0:T(8,128)S(1)} %get-tuple-element.34), channel_id=1, source_target_pairs={{0,16},{1,2},{2,1},{3,4},{4,3},{5,6},{6,5},{7,8},{8,7},{9,10},{10,... | collective-permute-start | bytes 24584 | tf_op jit(solution)/shard_map/ppermute | solution.py:442
  3.0 6.1 %collective-permute-start.1 = (f32[16,128]{1,0:T(8,128)S(1)}, f32[16,128]{1,0:T(8,128)S(1)}, u32[]{:S(2)}, u32[]{:S(2)}) collective-permute-start(f32[16,128]{1,0:T(8,128)S(1)} %get-tuple-element.35), channel_id=1, source_target_pairs={{0,16},{16,32},{32,48},{48,64},{64,80},{80,96},{96,112},{112,0},{1... | collective-permute-start | bytes 24584 | tf_op jit(solution)/shard_map/ppermute | solution.py:444
  4.2 4.9 %collective-permute-start.2 = (f32[2,8,128]{2,1,0:T(8,128)S(1)}, f32[2,8,128]{2,1,0:T(8,128)S(1)}, u32[]{:S(2)}, u32[]{:S(2)}) collective-permute-start(f32[2,8,128]{2,1,0:T(8,128)S(1)} %get-tuple-element.36), channel_id=1, source_target_pairs={{0,1},{1,0},{2,3},{3,2},{4,5},{5,4},{6,7},{7,6},{8,9},{9,8},{10,11... | collective-permute-start | bytes 24584 | tf_op jit(solution)/shard_map/ppermute | solution.py:443
  9.2 1.3 %collective-permute-start.3 = (f32[5,16,128]{2,1,0:T(8,128)S(1)}, f32[5,16,128]{2,1,0:T(8,128)S(1)}, u32[]{:S(2)}, u32[]{:S(2)}) collective-permute-start(f32[5,16,128]{2,1,0:T(8,128)S(1)} %get-tuple-element.43.own), channel_id=1, source_target_pairs={{0,16},{16,0},{32,48},{48,32},{64,80},{80,64},{96,112},{112,96},{1... | collective-permute-start | bytes 122888 | tf_op jit(solution)/shard_map/ppermute | solution.py:458
  10.5 5.1 %collective-permute-start.4 = (f32[5,16,128]{2,1,0:T(8,128)S(1)}, f32[5,16,128]{2,1,0:T(8,128)S(1)}, u32[]{:S(2)}, u32[]{:S(2)}) collective-permute-start(f32[5,16,128]{2,1,0:T(8,128)S(1)} %get-tuple-element.49.own), channel_id=1, source_target_pairs={{0,32},{1,33},{2,34},{3,35},{4,36},{5,37},{6,38},{7,39},{8,40},{9,... | collective-permute-start | bytes 122888 | tf_op jit(solution)/shard_map/ppermute | solution.py:468
  13.0 4.2 %collective-permute-start.5 = (f32[5,16,128]{2,1,0:T(8,128)S(1)}, f32[5,16,128]{2,1,0:T(8,128)S(1)}, u32[]{:S(2)}, u32[]{:S(2)}) collective-permute-start(f32[5,16,128]{2,1,0:T(8,128)S(1)} %get-tuple-element.49.own), channel_id=1, source_target_pairs={{0,96},{1,97},{2,98},{3,99},{4,100},{5,101},{6,102},{7,103},{8,104... | collective-permute-start | bytes 122888 | tf_op jit(solution)/shard_map/ppermute | solution.py:468
  15.6 1.6 %collective-permute-start.6 = (f32[5,16,128]{2,1,0:T(8,128)S(1)}, f32[5,16,128]{2,1,0:T(8,128)S(1)}, u32[]{:S(2)}, u32[]{:S(2)}) collective-permute-start(f32[5,16,128]{2,1,0:T(8,128)S(1)} %shard_map.43), channel_id=1, source_target_pairs={{0,16},{16,0},{32,48},{48,32},{64,80},{80,64},{96,112},{112,96},{1... | collective-permute-start | bytes 122888 | tf_op jit(solution)/shard_map/ppermute | solution.py:479
  17.5 1.3 %collective-permute-start.7 = (f32[5,8,128]{2,1,0:T(8,128)S(1)}, f32[5,8,128]{2,1,0:T(8,128)S(1)}, u32[]{:S(2)}, u32[]{:S(2)}) collective-permute-start(f32[5,8,128]{2,1,0:T(8,128)S(1)} %get-tuple-element.56.own), channel_id=1, source_target_pairs={{0,16},{16,0},{32,48},{48,32},{64,80},{80,64},{96,112},{112,96},{1... | collective-permute-start | bytes 61448 | tf_op jit(solution)/shard_map/ppermute | solution.py:479
  18.8 4.4 %collective-permute-start.8 = (f32[5,16,128]{2,1,0:T(8,128)S(1)}, f32[5,16,128]{2,1,0:T(8,128)S(1)}, u32[]{:S(2)}, u32[]{:S(2)}) collective-permute-start(f32[5,16,128]{2,1,0:T(8,128)S(1)} %shard_map.46.own), channel_id=1, source_target_pairs={{0,1},{1,0},{2,3},{3,2},{4,5},{5,4},{6,7},{7,6},{8,9},{9,8},{10,11... | collective-permute-start | bytes 122888 | tf_op jit(solution)/shard_map/ppermute | solution.py:468
  20.5 4.1 %collective-permute-start.9 = (f32[5,16,128]{2,1,0:T(8,128)S(1)}, f32[5,16,128]{2,1,0:T(8,128)S(1)}, u32[]{:S(2)}, u32[]{:S(2)}) collective-permute-start(f32[5,16,128]{2,1,0:T(8,128)S(1)} %shard_map.46.own), channel_id=1, source_target_pairs={{0,3},{1,2},{2,1},{3,0},{4,7},{5,6},{6,5},{7,4},{8,11},{9,10},{10,... | collective-permute-start | bytes 122888 | tf_op jit(solution)/shard_map/ppermute | solution.py:468
  23.2 1.3 %collective-permute-start.10 = (f32[5,16,128]{2,1,0:T(8,128)S(1)}, f32[5,16,128]{2,1,0:T(8,128)S(1)}, u32[]{:S(2)}, u32[]{:S(2)}) collective-permute-start(f32[5,16,128]{2,1,0:T(8,128)S(1)} %collective-permute-done.8.far), channel_id=1, source_target_pairs={{0,16},{16,0},{32,48},{48,32},{64,80},{80,64},{96,112},{112,96},{1... | collective-permute-start | bytes 122888 | tf_op jit(solution)/shard_map/ppermute | solution.py:479
  24.6 5.9 %collective-permute-start.11 = (f32[5,16,128]{2,1,0:T(8,128)S(1)}, f32[5,16,128]{2,1,0:T(8,128)S(1)}, u32[]{:S(2)}, u32[]{:S(2)}) collective-permute-start(f32[5,16,128]{2,1,0:T(8,128)S(1)} %get-tuple-element.61), channel_id=1, source_target_pairs={{0,4},{1,5},{2,6},{3,7},{4,0},{5,1},{6,2},{7,3},{8,12},{9,13},{10,... | collective-permute-start | bytes 122888 | tf_op jit(solution)/shard_map/ppermute | solution.py:468
  29.1 3.8 %collective-permute-start.12 = (f32[5,8,128]{2,1,0:T(8,128)S(1)}, f32[5,8,128]{2,1,0:T(8,128)S(1)}, u32[]{:S(2)}, u32[]{:S(2)}) collective-permute-start(f32[5,8,128]{2,1,0:T(8,128)S(1)} %get-tuple-element.60.mine), channel_id=1, source_target_pairs={{0,12},{1,13},{2,14},{3,15},{4,8},{5,9},{6,10},{7,11},{8,4},{9,5},... | collective-permute-start | bytes 61448 | tf_op jit(solution)/shard_map/ppermute | solution.py:468
  30.5 2.5 %collective-permute-start.13 = (f32[5,8,128]{2,1,0:T(8,128)S(1)}, f32[5,8,128]{2,1,0:T(8,128)S(1)}, u32[]{:S(2)}, u32[]{:S(2)}) collective-permute-start(f32[5,8,128]{2,1,0:T(8,128)S(1)} %shard_map.48), channel_id=1, source_target_pairs={{0,16},{16,0},{32,48},{48,32},{64,80},{80,64},{96,112},{112,96},{1... | collective-permute-start | bytes 61448 | tf_op jit(solution)/shard_map/ppermute | solution.py:479

commit v14 on v10

--- a/solution.py
+++ b/solution.py
@@ -259,7 +259,7 @@
     my[2] = trail + jnp.where(me == last, (2.0 / (y_row(ky_t, BY - 1))), 0.0)
 
 
-def x_ends_kernel(came1, came2, mine, part, edges, send, flux, rows):
+def x_ends_kernel(came2, came1, mine, part, edges, send, flux, rows):
     me = lax.axis_index("gy")
     even = lax.rem(me, 2) == 0
     below = jnp.where(me == 0, 0.0, jnp.where(even, came2[...], came1[...]))
@@ -352,13 +352,13 @@
     send[4] = last
 
 
-def y_pack_kernel(own, other, both):
+def y_pack_kernel(own, other, after, both):
     on_low = lax.rem(lax.axis_index("gx"), 2) == 0
     both[:, 0:GROUPS] = jnp.where(on_low, own[...], other[...])
     both[:, GROUPS : 2 * GROUPS] = jnp.where(on_low, other[...], own[...])
 
 
-def y_local_kernel(v_t, f, u, after, g_t):
+def y_local_kernel(v_t, f, u, g_t):
     total = y_row(v_t, 0)
     g_t[0] = total
     for j in range(1, BY):
@@ -397,7 +397,7 @@
 
 
 def y_solve_kernel(
-    mine, far, near, shared, coefs, g_t, yf, yl, st, out_hbm, blocks, slots, inner, work, out, sems
+    mine, far, near, shared, coefs, g_t, yf, yl, st, out_hbm, blocks, slots, inner, work, out, sem
 ):
     me = lax.axis_index("gy")
     place, depth = lax.div(me, SIDE), lax.rem(me, SIDE)
@@ -414,15 +414,11 @@
     enter, leave = inner[depth], inner[depth + 1]
     for j in range(BY):
         work[pl.ds(j * GROUPS, GROUPS), :] = 2.0 * (g_t[j] + yf[j] * enter - yl[j] * leave)
-    moves = []
     for g in range(GROUPS):
         rows = pl.ds(g * 128, 128)
         out[rows, :] = group(st, g) + work[pl.ds(g, BY, stride=GROUPS), :].T
-        move = pltpu.make_async_copy(out.at[rows], out_hbm.at[rows], sems.at[g])
-        move.start()
-        moves.append(move)
-    for move in moves:
-        move.wait()
+        pltpu.make_async_copy(out.at[rows], out_hbm.at[rows], sem).start()
+    pltpu.make_async_copy(out, out_hbm, sem).wait()
 
 
 def call(kernel, outs, args, scratch=(), cost=100_000):
@@ -483,7 +479,7 @@
     ends, flux = call(
         x_ends_kernel,
         near(x_block, (3, GROUPS, 128)),
-        near(came1, came2, mine, part, edges),
+        near(came2, came1, mine, part, edges),
         [pltpu.VMEM((2, NZ, BY), F32)],
     )
     other = lax.ppermute(ends, "gx", [(i, i ^ 1) for i in range(nx)])
@@ -529,15 +525,14 @@
             pltpu.VMEM((2, NZ, BY), F32),
         ],
     )
-    (both,) = call(y_pack_kernel, near(wide), near(own, share(own)))
+    (g_t,) = call(y_local_kernel, near(ys), near(v_t, f, u), cost=3_000_000)
+    (both,) = call(y_pack_kernel, near(wide), near(own, share(own), g_t))
     far = swap("y", (1, 2), both)
     near_y = swap("y", (3, 3), both)
-    (g_t,) = call(y_local_kernel, near(ys), near(v_t, f, u, both), cost=3_000_000)
-    (relayed,) = call(relay_kernel, near(wide), near(far, g_t))
     quad, mine, coefs = call(
         y_merge_kernel,
         near(wide, (5, GROUPS, 128), (SIDE - 1, 3, 2 * GROUPS, 128)),
-        near(both, far, near_y, share(relayed)),
+        near(both, far, near_y, share(far)),
         [pltpu.VMEM((SIDE,) + wide, F32)],
     )
     far = swap("y", (4, 8), quad)
@@ -553,7 +548,7 @@
             pltpu.VMEM((SIDE + 1, GROUPS, 128), F32),
             pltpu.VMEM(plane, F32),
             pltpu.VMEM(plane, F32),
-            pltpu.SemaphoreType.DMA((GROUPS,)),
+            pltpu.SemaphoreType.DMA,
         ],
     )
     return out.reshape(state.shape)

time: 34.5 us -> 34.5 us (level)
  waiting for transfers between devices: 7.76 us -> 6.85 us
  starting transfers between devices: 19.5 us -> 20.4 us
    ppermute x1, starting transfers between devices: 0.31 us -> 1.51 us  [on_device(): other = lax.ppermute(ends, 'gx', [(i, i ^ 1) for i in range(nx)])]
    ppermute x6, starting transfers between devices: 14.2 us -> 13.5 us  [swap(): lax.ppermute(value, ('gx', 'gy'), [(i * ny + j, (i ^ 2 * bits[i % 2]) * n...]
    ppermute x1, starting transfers between devices: 0.96 us -> 1.5 us  [on_device(): came2 = lax.ppermute(second, ('gx', 'gy'), pairs)]
    ppermute x4, waiting for transfers between devices: 0.87 us -> 0.33 us  [share(): return lax.ppermute(value, 'gx', [(i, i ^ 1) for i in range(nx)])]
    pallas_call x14 -> x13, Pallas kernels: 7.06 us -> 6.99 us  [call(): pl.pallas_call(kernel, out_shape=[jax.ShapeDtypeStruct(shape, F32) if far...]
  transfers between devices with their start and end apart: 13 -> 13, of which waited for: 6 -> 7; matrix products, arithmetic and copies ran while one was open for 0% -> 0% of each run, Pallas kernels for 11% -> 11%
where the time goes in v14:
time: 34.5 us; the launch traced here: 34.4 us
  starting transfers between devices  20.4 us (59%)
  Pallas kernels  6.99 us (20%)
  waiting for transfers between devices  6.85 us (20%)
    ppermute x6, starting transfers between devices, swap(): lax.ppermute(value, ('gx', 'gy'), [(i * ny + j, (i ^ 2 * bits[i % 2]) * n...  13.5 us
    pallas_call x13, Pallas kernels, call(): pl.pallas_call(kernel, out_shape=[jax.ShapeDtypeStruct(shape, F32) if far...  6.99 us
    ppermute x6, waiting for transfers between devices, swap(): lax.ppermute(value, ('gx', 'gy'), [(i * ny + j, (i ^ 2 * bits[i % 2]) * n...  6.16 us
    ppermute x1, starting transfers between devices, on_device(): came1 = lax.ppermute(first, 'gy', [(i, i ^ 1) for i in range(ny)])  2.68 us
    ppermute x1, starting transfers between devices, on_device(): other = lax.ppermute(ends, 'gx', [(i, i ^ 1) for i in range(nx)])  1.51 us
    ppermute x1, starting transfers between devices, on_device(): came2 = lax.ppermute(second, ('gx', 'gy'), pairs)  1.5 us
    ppermute x4, starting transfers between devices, share(): return lax.ppermute(value, 'gx', [(i, i ^ 1) for i in range(nx)])  1.23 us
  transfers between devices with their start and end apart: 13, of which 7 were waited for; matrix products, arithmetic and copies ran while one was open for 0% of the time, Pallas kernels for 11%

profile of v14, /device:TPU:1, one launch (start us, length us, event | category | flops | bytes accessed | tf_op | source)
XLA Modules:
  0.0 34.4 jit_solution(5051738027367163655)
XLA Ops:
  0.0 1.5 %shard_map.37 = (f32[16,72,128]{2,1,0:T(8,128)S(1)}, f32[16,72,128]{2,1,0:T(8,128)S(1)}, f32[1024,128]{1,0:T(8,128)S(1)}, f32[1024,128]{1,0:T(8,128)S(1)}, f32[4...) custom-call(f32[16,64,128]{2,1,0:T(8,128)} %st_hbm.1, f32[16,64,128]{2,1,0:T(8,128)} %kx_hbm.1, ...), custom_call_target="tpu_custom_call" | custom-call | flops 100000 | bytes 100000 | tf_op jit(solution)/shard_map/pallas_call | solution.py:427
  1.5 1.5 %collective-permute-start = (f32[2,8,128]{2,1,0:T(8,128)S(1)}, f32[2,8,128]{2,1,0:T(8,128)S(1)}, u32[]{:S(2)}, u32[]{:S(2)}) collective-permute-start(f32[2,8,128]{2,1,0:T(8,128)S(1)} %get-tuple-element.33), channel_id=1, source_target_pairs={{0,16},{1,2},{2,1},{3,4},{4,3},{5,6},{6,5},{7,8},{8,7},{9,10},{10,... | collective-permute-start | bytes 24584 | tf_op jit(solution)/shard_map/ppermute | solution.py:470
  3.0 2.7 %collective-permute-start.1 = (f32[2,8,128]{2,1,0:T(8,128)S(1)}, f32[2,8,128]{2,1,0:T(8,128)S(1)}, u32[]{:S(2)}, u32[]{:S(2)}) collective-permute-start(f32[2,8,128]{2,1,0:T(8,128)S(1)} %get-tuple-element.34), channel_id=1, source_target_pairs={{0,1},{1,0},{2,3},{3,2},{4,5},{5,4},{6,7},{7,6},{8,9},{9,8},{10,11... | collective-permute-start | bytes 24584 | tf_op jit(solution)/shard_map/ppermute | solution.py:471
  5.7 1.4 %shard_map.38 = (f32[64,16,128]{2,1,0:T(8,128)S(1)}, f32[64,16,128]{2,1,0:T(8,128)S(1)}, f32[1152,128]{1,0:T(8,128)S(1)}, f32[1152,128]{1,0:T(8,128)S(1)}, f32[7...) custom-call(f32[1024,128]{1,0:T(8,128)S(1)} %get-tuple-element.36.st_t, ...), custom_call_target="tpu_custom_call" | custom-call | flops 5000000 | bytes 5000000 | tf_op jit(solution)/shard_map/pallas_call | solution.py:427
  7.2 1.5 %collective-permute-start.2 = (f32[7,16,128]{2,1,0:T(8,128)S(1)}, f32[7,16,128]{2,1,0:T(8,128)S(1)}, u32[]{:S(2)}, u32[]{:S(2)}) collective-permute-start(f32[7,16,128]{2,1,0:T(8,128)S(1)} %get-tuple-element.41.own), channel_id=1, source_target_pairs={{0,16},{16,0},{32,48},{48,32},{64,80},{80,64},{96,112},{112,96},{1... | collective-permute-start | bytes 172040 | tf_op jit(solution)/shard_map/ppermute | solution.py:485
  8.7 0.5 %shard_map.40.after.d = f32[1152,128]{1,0:T(8,128)S(1)} custom-call(f32[1024,128]{1,0:T(8,128)S(1)} %get-tuple-element.42.base_t, f32[3,8,128]{2,1,0:T(8,128)S(1)} %get-tuple-element.43.flux, f32[1152,128]{1,0:T(8,128)S(1)} %bitcast.3, f32[64,16,128]{2,1,0:T(8,128)S(1)} %get-tuple-element.45.fx, f32[64,16,128]{2,1,0:T(8,128)S(1)} %get-tuple-element.46.ux), custom_call_target="tpu_custom_call" | custom-call | flops 3000000 | bytes 3000000 | tf_op jit(solution)/shard_map/pallas_call | solution.py:427
  9.2 0.4 %collective-permute-done.2.other = f32[7,16,128]{2,1,0:T(8,128)S(1)} collective-permute-done((f32[7,16,128]{2,1,0:T(8,128)S(1)}, f32[7,16,128]{2,1,0:T(8,128)S(1)}, u32[]{:S(2)}, u32[]{:S(2)}) %collective-permute-start.2) | collective-permute-done | bytes 57376 | tf_op jit(solution)/shard_map/ppermute | solution.py:485
  9.6 2.8 %collective-permute-start.3 = (f32[7,16,128]{2,1,0:T(8,128)S(1)}, f32[7,16,128]{2,1,0:T(8,128)S(1)}, u32[]{:S(2)}, u32[]{:S(2)}) collective-permute-start(f32[7,16,128]{2,1,0:T(8,128)S(1)} %get-tuple-element.47.own), channel_id=1, source_target_pairs={{0,32},{1,33},{2,34},{3,35},{4,36},{5,37},{6,38},{7,39},{8,40},{9,... | collective-permute-start | bytes 172040 | tf_op jit(solution)/shard_map/ppermute | solution.py:495
  12.4 0.9 %collective-permute-start.4 = (f32[7,16,128]{2,1,0:T(8,128)S(1)}, f32[7,16,128]{2,1,0:T(8,128)S(1)}, u32[]{:S(2)}, u32[]{:S(2)}) collective-permute-start(f32[7,16,128]{2,1,0:T(8,128)S(1)} %get-tuple-element.47.own), channel_id=1, source_target_pairs={{0,96},{1,97},{2,98},{3,99},{4,100},{5,101},{6,102},{7,103},{8,104... | collective-permute-start | bytes 172040 | tf_op jit(solution)/shard_map/ppermute | solution.py:495
  13.3 1.4 %shard_map.42 = (f32[128,8,128]{2,1,0:T(8,128)S(1)}, f32[128,8,128]{2,1,0:T(8,128)S(1)}, f32[128,8,128]{2,1,0:T(8,128)S(1)}, f32[128,8,128]{2,1,0:T(8,128)S(1)}, f32[3,8,128]{2,1,0:T(8,128)S(1)}) custom-call(f32[1024,128]{1,0:T(8,128)S(1)} %get-tuple-element.38.ky_t, f32[3,16,128]{2,1,0:T(8,128)S(1)} %get-tuple-element.48.after.coefs), custom_call_target="tpu_custom_call" | custom-call | flops 5000000 | bytes 5000000 | tf_op jit(solution)/shard_map/pallas_call | solution.py:427
  14.7 0.4 %collective-permute-start.5 = (f32[7,16,128]{2,1,0:T(8,128)S(1)}, f32[7,16,128]{2,1,0:T(8,128)S(1)}, u32[]{:S(2)}, u32[]{:S(2)}) collective-permute-start(f32[7,16,128]{2,1,0:T(8,128)S(1)} %shard_map.43), channel_id=1, source_target_pairs={{0,16},{16,0},{32,48},{48,32},{64,80},{80,64},{96,112},{112,96},{1... | collective-permute-start | bytes 172040 | tf_op jit(solution)/shard_map/ppermute | solution.py:506
  15.1 1.7 %collective-permute-done.4.near = f32[7,16,128]{2,1,0:T(8,128)S(1)} collective-permute-done((f32[7,16,128]{2,1,0:T(8,128)S(1)}, f32[7,16,128]{2,1,0:T(8,128)S(1)}, u32[]{:S(2)}, u32[]{:S(2)}) %collective-permute-start.4) | collective-permute-done | bytes 57376 | tf_op jit(solution)/shard_map/ppermute | solution.py:495
  16.8 0.4 %shard_map.44 = (f32[1024,128]{1,0:T(8,128)S(1)}, f32[5,8,128]{2,1,0:T(8,128)S(1)}) custom-call(f32[7,16,128]{2,1,0:T(8,128)S(1)} %get-tuple-element.47.own, f32[7,16,128]{2,1,0:T(8,128)S(1)} %collective-permute-done.3.value.far, f32[7,16,128]{2,1,0:T(8,128)S(1)} %collective-permute-done.4.near, f32[7,16,128]{2,1,0:T(8,128)S(1)} %collective-permute-done.5.shared, ...), custom_call_target="tpu_custom_call" | custom-call | flops 100000 | bytes 100000 | tf_op jit(solution)/shard_map/pallas_call | solution.py:427
  17.2 0.4 %collective-permute-start.6 = (f32[5,8,128]{2,1,0:T(8,128)S(1)}, f32[5,8,128]{2,1,0:T(8,128)S(1)}, u32[]{:S(2)}, u32[]{:S(2)}) collective-permute-start(f32[5,8,128]{2,1,0:T(8,128)S(1)} %get-tuple-element.54.own), channel_id=1, source_target_pairs={{0,16},{16,0},{32,48},{48,32},{64,80},{80,64},{96,112},{112,96},{1... | collective-permute-start | bytes 61448 | tf_op jit(solution)/shard_map/ppermute | solution.py:506
  17.7 0.5 %shard_map.45.after.g_t = f32[128,8,128]{2,1,0:T(8,128)S(1)} custom-call(f32[1024,128]{1,0:T(8,128)S(1)} %get-tuple-element.55.v_t, f32[128,8,128]{2,1,0:T(8,128)S(1)} %get-tuple-element.56.f, f32[128,8,128]{2,1,0:T(8,128)S(1)} %get-tuple-element.57.u), custom_call_target="tpu_custom_call" | custom-call | flops 3000000 | bytes 3000000 | tf_op jit(solution)/shard_map/pallas_call | solution.py:427
  18.5 2.0 %collective-permute-start.7 = (f32[5,16,128]{2,1,0:T(8,128)S(1)}, f32[5,16,128]{2,1,0:T(8,128)S(1)}, u32[]{:S(2)}, u32[]{:S(2)}) collective-permute-start(f32[5,16,128]{2,1,0:T(8,128)S(1)} %shard_map.46.own), channel_id=1, source_target_pairs={{0,1},{1,0},{2,3},{3,2},{4,5},{5,4},{6,7},{7,6},{8,9},{9,8},{10,11... | collective-permute-start | bytes 122888 | tf_op jit(solution)/shard_map/ppermute | solution.py:495
  20.5 2.3 %collective-permute-start.8 = (f32[5,16,128]{2,1,0:T(8,128)S(1)}, f32[5,16,128]{2,1,0:T(8,128)S(1)}, u32[]{:S(2)}, u32[]{:S(2)}) collective-permute-start(f32[5,16,128]{2,1,0:T(8,128)S(1)} %shard_map.46.own), channel_id=1, source_target_pairs={{0,3},{1,2},{2,1},{3,0},{4,7},{5,6},{6,5},{7,4},{8,11},{9,10},{10,... | collective-permute-start | bytes 122888 | tf_op jit(solution)/shard_map/ppermute | solution.py:495
  23.0 0.4 %collective-permute-start.9 = (f32[5,16,128]{2,1,0:T(8,128)S(1)}, f32[5,16,128]{2,1,0:T(8,128)S(1)}, u32[]{:S(2)}, u32[]{:S(2)}) collective-permute-start(f32[5,16,128]{2,1,0:T(8,128)S(1)} %collective-permute-done.7.far), channel_id=1, source_target_pairs={{0,16},{16,0},{32,48},{48,32},{64,80},{80,64},{96,112},{112,96},{1... | collective-permute-start | bytes 122888 | tf_op jit(solution)/shard_map/ppermute | solution.py:506
  23.4 1.2 %collective-permute-done.8.near = f32[5,16,128]{2,1,0:T(8,128)S(1)} collective-permute-done((f32[5,16,128]{2,1,0:T(8,128)S(1)}, f32[5,16,128]{2,1,0:T(8,128)S(1)}, u32[]{:S(2)}, u32[]{:S(2)}) %collective-permute-start.8) | collective-permute-done | bytes 40992 | tf_op jit(solution)/shard_map/ppermute | solution.py:495
  24.6 4.8 %collective-permute-start.10 = (f32[5,16,128]{2,1,0:T(8,128)S(1)}, f32[5,16,128]{2,1,0:T(8,128)S(1)}, u32[]{:S(2)}, u32[]{:S(2)}) collective-permute-start(f32[5,16,128]{2,1,0:T(8,128)S(1)} %get-tuple-element.59), channel_id=1, source_target_pairs={{0,4},{1,5},{2,6},{3,7},{4,0},{5,1},{6,2},{7,3},{8,12},{9,13},{10,... | collective-permute-start | bytes 122888 | tf_op jit(solution)/shard_map/ppermute | solution.py:495
  29.4 0.8 %collective-permute-start.11 = (f32[5,8,128]{2,1,0:T(8,128)S(1)}, f32[5,8,128]{2,1,0:T(8,128)S(1)}, u32[]{:S(2)}, u32[]{:S(2)}) collective-permute-start(f32[5,8,128]{2,1,0:T(8,128)S(1)} %get-tuple-element.58.mine), channel_id=1, source_target_pairs={{0,12},{1,13},{2,14},{3,15},{4,8},{5,9},{6,10},{7,11},{8,4},{9,5},... | collective-permute-start | bytes 61448 | tf_op jit(solution)/shard_map/ppermute | solution.py:495
  30.2 0.6 %collective-permute-done.10.value.far = f32[5,16,128]{2,1,0:T(8,128)S(1)} collective-permute-done((f32[5,16,128]{2,1,0:T(8,128)S(1)}, f32[5,16,128]{2,1,0:T(8,128)S(1)}, u32[]{:S(2)}, u32[]{:S(2)}) %collective-permute-start.10) | collective-permute-done | bytes 40992 | tf_op jit(solution)/shard_map/ppermute | solution.py:495
  30.8 2.4 %collective-permute-done.11.near = f32[5,8,128]{2,1,0:T(8,128)S(1)} collective-permute-done((f32[5,8,128]{2,1,0:T(8,128)S(1)}, f32[5,8,128]{2,1,0:T(8,128)S(1)}, u32[]{:S(2)}, u32[]{:S(2)}) %collective-permute-start.11) | collective-permute-done | bytes 20512 | tf_op jit(solution)/shard_map/ppermute | solution.py:495
  33.3 1.1 %shard_map.49 = f32[1024,128]{1,0:T(8,128)} custom-call(f32[5,8,128]{2,1,0:T(8,128)S(1)} %get-tuple-element.58.mine, f32[5,16,128]{2,1,0:T(8,128)S(1)} %collective-permute-done.10.value.far, f32[5,8,128]{2,1,0:T(8,128)S(1)} %collective-permute-done.11.near, f32[5,8,128]{2,1,0:T(8,128)S(1)} %collective-permute-done.12.shared, ...), custom_call_target="tpu_custom_call" | custom-call | flops 100000 | bytes 100000 | tf_op jit(solution)/shard_map/pallas_call | solution.py:427
  (15 shorter events, 0.7 us)
Async XLA Ops:
  1.5 5.6 %collective-permute-start = (f32[2,8,128]{2,1,0:T(8,128)S(1)}, f32[2,8,128]{2,1,0:T(8,128)S(1)}, u32[]{:S(2)}, u32[]{:S(2)}) collective-permute-start(f32[2,8,128]{2,1,0:T(8,128)S(1)} %get-tuple-element.33), channel_id=1, source_target_pairs={{0,16},{1,2},{2,1},{3,4},{4,3},{5,6},{6,5},{7,8},{8,7},{9,10},{10,... | collective-permute-start | bytes 24584 | tf_op jit(solution)/shard_map/ppermute | solution.py:470
  3.0 4.1 %collective-permute-start.1 = (f32[2,8,128]{2,1,0:T(8,128)S(1)}, f32[2,8,128]{2,1,0:T(8,128)S(1)}, u32[]{:S(2)}, u32[]{:S(2)}) collective-permute-start(f32[2,8,128]{2,1,0:T(8,128)S(1)} %get-tuple-element.34), channel_id=1, source_target_pairs={{0,1},{1,0},{2,3},{3,2},{4,5},{5,4},{6,7},{7,6},{8,9},{9,8},{10,11... | collective-permute-start | bytes 24584 | tf_op jit(solution)/shard_map/ppermute | solution.py:471
  7.2 2.4 %collective-permute-start.2 = (f32[7,16,128]{2,1,0:T(8,128)S(1)}, f32[7,16,128]{2,1,0:T(8,128)S(1)}, u32[]{:S(2)}, u32[]{:S(2)}) collective-permute-start(f32[7,16,128]{2,1,0:T(8,128)S(1)} %get-tuple-element.41.own), channel_id=1, source_target_pairs={{0,16},{16,0},{32,48},{48,32},{64,80},{80,64},{96,112},{112,96},{1... | collective-permute-start | bytes 172040 | tf_op jit(solution)/shard_map/ppermute | solution.py:485
  9.6 5.1 %collective-permute-start.3 = (f32[7,16,128]{2,1,0:T(8,128)S(1)}, f32[7,16,128]{2,1,0:T(8,128)S(1)}, u32[]{:S(2)}, u32[]{:S(2)}) collective-permute-start(f32[7,16,128]{2,1,0:T(8,128)S(1)} %get-tuple-element.47.own), channel_id=1, source_target_pairs={{0,32},{1,33},{2,34},{3,35},{4,36},{5,37},{6,38},{7,39},{8,40},{9,... | collective-permute-start | bytes 172040 | tf_op jit(solution)/shard_map/ppermute | solution.py:495
  12.4 4.4 %collective-permute-start.4 = (f32[7,16,128]{2,1,0:T(8,128)S(1)}, f32[7,16,128]{2,1,0:T(8,128)S(1)}, u32[]{:S(2)}, u32[]{:S(2)}) collective-permute-start(f32[7,16,128]{2,1,0:T(8,128)S(1)} %get-tuple-element.47.own), channel_id=1, source_target_pairs={{0,96},{1,97},{2,98},{3,99},{4,100},{5,101},{6,102},{7,103},{8,104... | collective-permute-start | bytes 172040 | tf_op jit(solution)/shard_map/ppermute | solution.py:495
  14.7 2.1 %collective-permute-start.5 = (f32[7,16,128]{2,1,0:T(8,128)S(1)}, f32[7,16,128]{2,1,0:T(8,128)S(1)}, u32[]{:S(2)}, u32[]{:S(2)}) collective-permute-start(f32[7,16,128]{2,1,0:T(8,128)S(1)} %shard_map.43), channel_id=1, source_target_pairs={{0,16},{16,0},{32,48},{48,32},{64,80},{80,64},{96,112},{112,96},{1... | collective-permute-start | bytes 172040 | tf_op jit(solution)/shard_map/ppermute | solution.py:506
  17.2 1.3 %collective-permute-start.6 = (f32[5,8,128]{2,1,0:T(8,128)S(1)}, f32[5,8,128]{2,1,0:T(8,128)S(1)}, u32[]{:S(2)}, u32[]{:S(2)}) collective-permute-start(f32[5,8,128]{2,1,0:T(8,128)S(1)} %get-tuple-element.54.own), channel_id=1, source_target_pairs={{0,16},{16,0},{32,48},{48,32},{64,80},{80,64},{96,112},{112,96},{1... | collective-permute-start | bytes 61448 | tf_op jit(solution)/shard_map/ppermute | solution.py:506
  18.5 4.4 %collective-permute-start.7 = (f32[5,16,128]{2,1,0:T(8,128)S(1)}, f32[5,16,128]{2,1,0:T(8,128)S(1)}, u32[]{:S(2)}, u32[]{:S(2)}) collective-permute-start(f32[5,16,128]{2,1,0:T(8,128)S(1)} %shard_map.46.own), channel_id=1, source_target_pairs={{0,1},{1,0},{2,3},{3,2},{4,5},{5,4},{6,7},{7,6},{8,9},{9,8},{10,11... | collective-permute-start | bytes 122888 | tf_op jit(solution)/shard_map/ppermute | solution.py:495
  20.5 4.1 %collective-permute-start.8 = (f32[5,16,128]{2,1,0:T(8,128)S(1)}, f32[5,16,128]{2,1,0:T(8,128)S(1)}, u32[]{:S(2)}, u32[]{:S(2)}) collective-permute-start(f32[5,16,128]{2,1,0:T(8,128)S(1)} %shard_map.46.own), channel_id=1, source_target_pairs={{0,3},{1,2},{2,1},{3,0},{4,7},{5,6},{6,5},{7,4},{8,11},{9,10},{10,... | collective-permute-start | bytes 122888 | tf_op jit(solution)/shard_map/ppermute | solution.py:495
  23.0 1.6 %collective-permute-start.9 = (f32[5,16,128]{2,1,0:T(8,128)S(1)}, f32[5,16,128]{2,1,0:T(8,128)S(1)}, u32[]{:S(2)}, u32[]{:S(2)}) collective-permute-start(f32[5,16,128]{2,1,0:T(8,128)S(1)} %collective-permute-done.7.far), channel_id=1, source_target_pairs={{0,16},{16,0},{32,48},{48,32},{64,80},{80,64},{96,112},{112,96},{1... | collective-permute-start | bytes 122888 | tf_op jit(solution)/shard_map/ppermute | solution.py:506
  24.6 6.2 %collective-permute-start.10 = (f32[5,16,128]{2,1,0:T(8,128)S(1)}, f32[5,16,128]{2,1,0:T(8,128)S(1)}, u32[]{:S(2)}, u32[]{:S(2)}) collective-permute-start(f32[5,16,128]{2,1,0:T(8,128)S(1)} %get-tuple-element.59), channel_id=1, source_target_pairs={{0,4},{1,5},{2,6},{3,7},{4,0},{5,1},{6,2},{7,3},{8,12},{9,13},{10,... | collective-permute-start | bytes 122888 | tf_op jit(solution)/shard_map/ppermute | solution.py:495
  29.4 3.8 %collective-permute-start.11 = (f32[5,8,128]{2,1,0:T(8,128)S(1)}, f32[5,8,128]{2,1,0:T(8,128)S(1)}, u32[]{:S(2)}, u32[]{:S(2)}) collective-permute-start(f32[5,8,128]{2,1,0:T(8,128)S(1)} %get-tuple-element.58.mine), channel_id=1, source_target_pairs={{0,12},{1,13},{2,14},{3,15},{4,8},{5,9},{6,10},{7,11},{8,4},{9,5},... | collective-permute-start | bytes 61448 | tf_op jit(solution)/shard_map/ppermute | solution.py:495
  30.8 2.5 %collective-permute-start.12 = (f32[5,8,128]{2,1,0:T(8,128)S(1)}, f32[5,8,128]{2,1,0:T(8,128)S(1)}, u32[]{:S(2)}, u32[]{:S(2)}) collective-permute-start(f32[5,8,128]{2,1,0:T(8,128)S(1)} %shard_map.48), channel_id=1, source_target_pairs={{0,16},{16,0},{32,48},{48,32},{64,80},{80,64},{96,112},{112,96},{1... | collective-permute-start | bytes 61448 | tf_op jit(solution)/shard_map/ppermute | solution.py:506
